TPU v7x, 256 devices: a whole 4x4x8 slice. The times are simulated.
256 devices in a mesh: seq: 64 (over z, x, core), tp: 4 (over y).
Axes of the slice: x: 4, y: 4, z: 8, core: 2. Of those that a mesh axis runs over, the one named last changes fastest.
Arguments:
- queries: bfloat16 [16384, 4096], P('seq', 'tp'), may hold values from -16 to 16
- key_states: bfloat16 [16384, 1024], P('seq', 'tp'), may hold values from -4 to 4
- value_states: bfloat16 [16384, 1024], P('seq', 'tp'), may hold values from -4 to 4
- vert_blocks: int32 [32, 16], P('tp'), may hold values from 0 to 127, as said below
- window_size: int32 [32], P('tp'), may hold values from 1 to 64
- slash_offsets: int32 [32, 8], P('tp'), may hold values from 1 to 128, as said below
- out_weight: bfloat16 [4096, 4096], P('tp'), may hold values from -0.59765625 to 0.59765625
Outputs:
- mixed: bfloat16 [16384, 4096], P('seq', 'tp')
Inputs may be any that keep to these rules, and one draw needn't show every extreme that they name: `vert_blocks`: each row names 16 distinct blocks. For each key head, the blocks named by its 4 query heads include at most 1 of the 2 blocks of one index of seq, and exactly 1 for some index. `slash_offsets`: each head's 8 offsets are distinct and no smaller than that head's window_size.
All inputs are finite; a program needn't handle non-finite values.
Results may differ from a plain program's by a relative error of at most 0.0055.
Values may be sent and summed in bfloat16 or wider, within the bound.
No kernel may reach another device: no remote copies, remote signals or barrier semaphores. Data moves between devices by JAX's collectives and lax.ppermute only.
A program may use at most 128 MiB of HBM per device.

v0:
```python
import math

import jax
import jax.numpy as jnp
from jax import lax
from jax.sharding import PartitionSpec as P

HD = 128
BLK = 128


NEG_FILL = -1e30


def passed_along(value, axis, steps):
    count = lax.axis_size(axis)
    initial, last = (max(0, -steps), min(count, count - steps))
    return lax.ppermute(value, axis, [(source, source + steps) for source in range(initial, last)])


def slash_match(gap, slash_offsets):
    slash_mask = gap == slash_offsets[:, 0][:, None, None]
    for column in range(1, slash_offsets.shape[1]):
        slash_mask = slash_mask | (gap == slash_offsets[:, column][:, None, None])
    return slash_mask


def attend_context(
    query_rows,
    local_keys,
    local_values,
    vert_keys,
    vert_values,
    vert_blocks,
    window_size,
    slash_offsets,
    start_row,
):
    row_count = query_rows.shape[0]
    head_count = vert_blocks.shape[0]
    kv_heads = local_keys.shape[1]
    group_size = head_count // kv_heads
    head_dim = local_keys.shape[2]
    key_span = local_keys.shape[0]
    score_scale = 1.0 / math.sqrt(head_dim)
    grouped = query_rows.reshape(row_count, kv_heads, group_size, head_dim)
    local_scores = (
        jnp.einsum(
            "sgeh,tgh->gest", grouped, local_keys, preferred_element_type=jnp.float32
        ).reshape(head_count, row_count, key_span)
        * score_scale
    )
    per_head = query_rows.reshape(row_count, head_count, head_dim).transpose(1, 0, 2)
    vert_scores = (
        jnp.einsum("hsd,hkd->hsk", per_head, vert_keys, preferred_element_type=jnp.float32)
        * score_scale
    )
    query_pos = start_row + jnp.arange(row_count, dtype=jnp.int32)
    local_pos = start_row - (key_span - row_count) + jnp.arange(key_span, dtype=jnp.int32)
    local_gap = (query_pos[:, None] - local_pos[None, :])[None]
    window_col = window_size[:, None, None]
    local_ok = (local_pos[None, None, :] >= 0) & (
        (local_gap >= 0) & (local_gap < window_col) | slash_match(local_gap, slash_offsets)
    )
    block_rows = vert_keys.shape[1] // vert_blocks.shape[1]
    vert_pos = (
        vert_blocks[:, :, None] * block_rows
        + jnp.arange(block_rows, dtype=jnp.int32)[None, None, :]
    ).reshape(head_count, -1)
    vert_gap = query_pos[None, :, None] - vert_pos[:, None, :]
    vert_ok = (vert_gap >= window_col) & jnp.logical_not(slash_match(vert_gap, slash_offsets))
    local_scores = jnp.where(local_ok, local_scores, NEG_FILL)
    vert_scores = jnp.where(vert_ok, vert_scores, NEG_FILL)
    row_max = jnp.maximum(jnp.max(local_scores, axis=2), jnp.max(vert_scores, axis=2))[:, :, None]
    local_weights = jnp.where(local_ok, jnp.exp(local_scores - row_max), 0.0)
    vert_weights = jnp.where(vert_ok, jnp.exp(vert_scores - row_max), 0.0)
    denominator = jnp.sum(local_weights, axis=2) + jnp.sum(vert_weights, axis=2)
    local_part = jnp.einsum(
        "gest,tgh->gesh",
        local_weights.astype(jnp.bfloat16).reshape(kv_heads, group_size, row_count, key_span),
        local_values,
        preferred_element_type=jnp.float32,
    ).reshape(head_count, row_count, head_dim)
    vert_part = jnp.einsum(
        "hsk,hkd->hsd",
        vert_weights.astype(jnp.bfloat16),
        vert_values,
        preferred_element_type=jnp.float32,
    )
    context = (local_part + vert_part) / denominator[:, :, None]
    return context.transpose(1, 0, 2).reshape(row_count, head_count * head_dim).astype(jnp.bfloat16)


def local(queries, key_states, value_states, vert_blocks, window_size, slash_offsets, out_weight):
    row_count = queries.shape[0]
    head_count = vert_blocks.shape[0]
    pick_count = vert_blocks.shape[1]
    head_dim = HD
    kv_width = key_states.shape[1]
    kv_heads = kv_width // head_dim
    group_size = head_count // kv_heads
    seq_count = lax.axis_size("seq")
    own_blocks = row_count // BLK
    total_blocks = own_blocks * seq_count
    position = lax.axis_index("seq")
    start_row = position * row_count
    half_rows = row_count // 2
    tail_rows = jnp.concatenate(
        [key_states[row_count - half_rows :], value_states[row_count - half_rows :]], axis=1
    )
    earlier = passed_along(tail_rows, "seq", 1)
    local_keys = jnp.concatenate([earlier[:, :kv_width], key_states], axis=0).reshape(
        half_rows + row_count, kv_heads, head_dim
    )
    local_values = jnp.concatenate([earlier[:, kv_width:], value_states], axis=0).reshape(
        half_rows + row_count, kv_heads, head_dim
    )
    head_group = jnp.arange(head_count, dtype=jnp.int32) // group_size
    gathered_keys, gathered_values = (
        lax.all_gather(key_states, "seq", axis=0, tiled=True),
        lax.all_gather(value_states, "seq", axis=0, tiled=True),
    )
    gathered_keys = gathered_keys.reshape(total_blocks, BLK, kv_heads, head_dim)
    gathered_values = gathered_values.reshape(total_blocks, BLK, kv_heads, head_dim)
    vert_keys = gathered_keys[vert_blocks, :, head_group[:, None], :].reshape(
        head_count, pick_count * BLK, head_dim
    )
    vert_values = gathered_values[vert_blocks, :, head_group[:, None], :].reshape(
        head_count, pick_count * BLK, head_dim
    )
    context = attend_context(
        queries,
        local_keys,
        local_values,
        vert_keys,
        vert_values,
        vert_blocks,
        window_size,
        slash_offsets,
        start_row,
    )
    partial_value = jnp.dot(context, out_weight, preferred_element_type=jnp.float32)
    return lax.psum_scatter(partial_value, "tp", scatter_dimension=1, tiled=True).astype(
        jnp.bfloat16
    )


def solution(mesh):
    return jax.shard_map(
        local,
        mesh=mesh,
        in_specs=(
            P("seq", "tp"),
            P("seq", "tp"),
            P("seq", "tp"),
            P("tp", None),
            P("tp"),
            P("tp", None),
            P("tp", None),
        ),
        out_specs=P("seq", "tp"),
        check_vma=False,
    )
```

profile of v0, /device:TPU:192, one launch (start us, length us, event | category | flops | bytes accessed | tf_op | source)
XLA Modules:
  0.0 346.3 jit_solution(10504840127347969599)
XLA Ops:
  6.5 0.7 all-gather.3.cloned.1.call-update
  8.1 0.8 slice.53
  8.9 1.0 copy.27
  10.1 1.9 collective-permute-start
  12.8 0.8 fusion.31
  13.6 0.8 broadcast_compare_fusion
  14.4 0.7 bitcast_add_fusion
  15.2 1.3 slice_reduce_fusion.7
  16.5 1.3 lt.32
  23.1 2.2 reshape.247
  26.1 0.9 pad_maximum_fusion
  27.0 0.8 copy.37
  27.9 4.3 %fusion.14 = (f32[2,4,256]{2,1,0:T(4,128)S(1)}, f32[2,384,256,4]{2,1,3,0:T(8,128)S(1)}) fusion(s32[2,4]{1,0:T(2,128)} %eq.229, s32[2,4]{1,0:T(2,128)} %eq.226, s32[2,4]{1,0:T(2,128)} %eq.223, s32[2,4]{1,0:T(2,128)} %eq.220, s32[2,4]{1,0:T(2,128)} %eq.217, s32[2,4]{1,0:T(2,128)} %eq.214, s32[2,4]{1,0:T(2,128)} %eq.211, s32[2,4]{1,0:T(2,128)} %eq.208, ...), kind=kOutput, calls=%fused_computation.29 | convolution fusion | flops 218626048 | bytes 4367008 | tf_op jit(solution)/shard_map/sgeh,tgh->gest/dot_general | solution.py:48
  32.8 59.5 %all-gather.3.cloned.1.call-done = bf16[16384,256]{1,0:T(8,128)(2,1)} async-done(((bf16[256,256]{1,0:T(8,128)(2,1)}), bf16[16384,256]{1,0:T(8,128)(2,1)}) %all-gather.3.cloned.1.call-update) | async-done | bytes 8388624 | tf_op jit(solution)/shard_map/all_gather | solution.py:120
  92.4 12.5 %reshape.276 = bf16[128,128,2,128]{3,2,1,0:T(2,128)(2,1)} reshape(bf16[16384,256]{1,0:T(8,128)(2,1)} %all-gather.3.cloned.1.call-done) | data formatting | bytes 16777216 | tf_op jit(solution)/shard_map/reshape | solution.py:123
  104.9 9.3 %copy.34 = bf16[128,128,2,128]{3,1,2,0:T(8,128)(2,1)} copy(bf16[128,128,2,128]{3,2,1,0:T(2,128)(2,1)} %reshape.276) | data formatting | bytes 16777216 | tf_op jit(solution)/shard_map/reshape | solution.py:123
  114.2 61.2 %all-gather.5.cloned.1.call-done = bf16[16384,256]{1,0:T(8,128)(2,1)} async-done(((bf16[256,256]{1,0:T(8,128)(2,1)}), bf16[16384,256]{1,0:T(8,128)(2,1)}) %all-gather.5.cloned.1.call-update) | async-done | bytes 8388624 | tf_op jit(solution)/shard_map/all_gather | solution.py:121
  175.4 12.5 %reshape.277 = bf16[128,128,2,128]{3,2,1,0:T(2,128)(2,1)} reshape(bf16[16384,256]{1,0:T(8,128)(2,1)} %all-gather.5.cloned.1.call-done) | data formatting | bytes 16777216 | tf_op jit(solution)/shard_map/reshape | solution.py:124
  188.0 9.2 %copy.40 = bf16[128,128,2,128]{3,1,2,0:T(8,128)(2,1)} copy(bf16[128,128,2,128]{3,2,1,0:T(2,128)(2,1)} %reshape.277) | data formatting | bytes 16777216 | tf_op jit(solution)/shard_map/reshape | solution.py:124
  197.1 6.4 %gather_fusion.1 = bf16[128,128,128]{2,1,0:T(8,128)(2,1)} fusion(bf16[128,128,2,128]{3,1,2,0:T(8,128)(2,1)} %copy.40, s32[128]{0:T(128)S(1)} %reshape.255), kind=kCustom, calls=%fused_computation.1 | custom fusion | bytes 8389632 | tf_op jit(solution)/shard_map/gather | solution.py:128
  203.6 6.5 %gather_fusion = bf16[128,128,128]{2,1,0:T(8,128)(2,1)} fusion(bf16[128,128,2,128]{3,1,2,0:T(8,128)(2,1)} %copy.34, s32[128]{0:T(128)S(1)} %reshape.255), kind=kCustom, calls=%fused_computation | custom fusion | bytes 8389632 | tf_op jit(solution)/shard_map/gather | solution.py:125
  210.1 19.5 %fusion.9 = (f32[8,256]{1,0:T(8,128)S(1)}, f32[8,2048,256]{2,1,0:T(8,128)}) fusion(s32[8]{0:T(128)} %copy-done.16, s32[8]{0:T(128)} %copy-done.18, s32[8]{0:T(128)} %copy-done.6, s32[8]{0:T(128)} %copy-done.8, s32[8]{0:T(128)} %copy-done.10, s32[8]{0:T(128)} %copy-done.12, s32[8]{0:T(128)} %copy-done.14, s32[8]{0:T(128)} %copy-done.4, s32[8]{0:T(128)} %param.11, ...), kind=kOutput, calls=%fused_computation.22 | convolution fusion | flops 1166014464 | bytes 21570848 | tf_op jit(solution)/shard_map/hsd,hkd->hsk/dot_general | solution.py:55
  230.7 0.7 max.11
  231.5 0.7 max.10
  232.2 4.8 %fusion.15 = f32[2,4,256]{2,1,0:T(4,128)} fusion(f32[2,384,256,4]{2,1,3,0:T(8,128)S(1)} %get-tuple-element.16, f32[2,4,256]{2,1,0:T(4,128)S(1)} %max.10, s32[2,4]{1,0:T(2,128)} %eq.229, s32[2,4]{1,0:T(2,128)} %eq.226, s32[2,4]{1,0:T(2,128)} %eq.223, s32[2,4]{1,0:T(2,128)} %eq.220, s32[2,4]{1,0:T(2,128)} %eq.217, s32[2,4]{1,0:T(2,128)} %eq.214, ...), kind=kLoop, calls=%fused_computation.30 | loop fusion | flops 18872320 | bytes 3654304 | tf_op jit(solution)/shard_map/reduce_sum | solution.py:77
  237.0 5.4 %fusion.17 = f32[2,4,256,128]{2,3,1,0:T(8,128)} fusion(bf16[384,2,128,1]{0,2,3,1:T(8,128)(2,1)} %bitcast.77, f32[2,384,256,4]{2,1,3,0:T(8,128)S(1)} %get-tuple-element.16, f32[2,4,256]{2,1,0:T(4,128)S(1)} %max.10, s32[2,4]{1,0:T(2,128)} %eq.229, s32[2,4]{1,0:T(2,128)} %eq.226, s32[2,4]{1,0:T(2,128)} %eq.223, s32[2,4]{1,0:T(2,128)} %eq.220, ...), kind=kOutput, calls=%fused_computation.32 | convolution fusion | flops 220200960 | bytes 4891296 | tf_op jit(solution)/shard_map/gest,tgh->gesh/dot_general | solution.py:78
  242.4 0.7 reduce_sum.21
  243.2 21.2 %fusion.10 = f32[8,256]{1,0:T(8,128)S(1)} fusion(f32[8,2048,256]{2,1,0:T(8,128)} %get-tuple-element.18, f32[8,256]{1,0:T(8,128)S(1)} %max.11, s32[8]{0:T(128)} %copy-done.16, s32[8]{0:T(128)} %copy-done.18, s32[8]{0:T(128)} %copy-done.6, s32[8]{0:T(128)} %copy-done.8, s32[8]{0:T(128)} %copy-done.10, s32[8]{0:T(128)} %copy-done.12, s32[8]{0:T(128)} %copy-done.14, ...), kind=kLoop, calls=%fused_computation.23 | loop fusion | flops 100661248 | bytes 16860448 | tf_op jit(solution)/shard_map/reduce_sum | solution.py:77
  264.6 20.2 %divide_convert_fusion = bf16[8,256,128]{1,2,0:T(8,128)(2,1)S(1)} fusion(f32[8,256,128]{1,2,0:T(8,128)S(1)} %bitcast.79, bf16[8,2048,128]{2,1,0:T(8,128)(2,1)S(1)} %bitcast.74, f32[8,2048,256]{2,1,0:T(8,128)} %get-tuple-element.18, f32[8,256]{1,0:T(8,128)S(1)} %max.11, f32[8,256]{1,0:T(8,128)S(1)} %add.95, s32[8]{0:T(128)S(1)} %copy-done.17, ...), kind=kOutput, calls=%fused_computation.34 | convolution fusion | flops 1175191552 | bytes 22627616 | tf_op jit(solution)/shard_map/hsk,hkd->hsd/dot_general | solution.py:84
  284.8 4.5 %fusion.42 = f32[256,4096]{1,0:T(8,128)} fusion(bf16[256,1024]{0,1:T(8,128)(2,1)S(1)} %bitcast.76, bf16[1024,4096]{1,0:T(8,128)(2,1)S(1)} %bitcast.73), kind=kOutput, calls=%fused_computation.78 | convolution fusion | flops 2147483648 | bytes 13107200 | tf_op jit(solution)/shard_map/dot_general | solution.py:142
  289.3 48.4 %reduce-scatter.2.cloned.1.call-done = f32[256,1024]{1,0:T(8,128)} async-done(((f32[256,4096]{1,0:T(8,128)}), f32[256,1024]{1,0:T(8,128)}) %reduce-scatter.2.cloned.1.call-update) | async-done | bytes 1048592 | tf_op jit(solution)/shard_map/reduce_scatter | solution.py:143
  337.7 2.1 convert_element_type.24
  (83 shorter events, 9.8 us)
Async XLA Ops:
  6.5 85.8 %all-gather.3.cloned.1.call-start = ((), (), s32[]{:S(2)}) async-start(), calls=%async_computation.1 | async-start | bytes 8519680 | tf_op jit(solution)/shard_map/all_gather | solution.py:120
  7.3 168.2 %all-gather.5.cloned.1.call-start = ((), (), s32[]{:S(2)}) async-start(), calls=%async_computation.2 | async-start | bytes 8519680 | tf_op jit(solution)/shard_map/all_gather | solution.py:121
  8.0 329.7 %reduce-scatter.2.cloned.1.call-start = ((), (), s32[]{:S(2)}) async-start(), calls=%async_computation.3 | async-start | bytes 5242880 | tf_op jit(solution)/shard_map/reduce_scatter | solution.py:143
  10.1 15.9 %collective-permute-start = (bf16[128,512]{0,1:T(8,128)(2,1)S(1)}, bf16[128,512]{0,1:T(8,128)(2,1)S(1)}, u32[]{:S(2)}, u32[]{:S(2)}) collective-permute-start(bf16[128,512]{0,1:T(8,128)(2,1)S(1)} %pad_maximum_fusion.2), channel_id=1, source_target_pairs={{0,4},{4,8},{8,12},{12,16},{16,20},{20,24},{24,28},{28,32},{32,36}... | collective-permute-start | bytes 393224 | tf_op jit(solution)/shard_map/ppermute | solution.py:18
  16.4 9.5 %copy-start.8 = (s32[8]{0:T(128)}, s32[8]{0:T(128)S(1)}, u32[]{:S(2)}) copy-start(s32[8]{0:T(128)S(1)} %get-tuple-element.7) | copy-start | bytes 100
  16.4 9.5 %copy-start.10 = (s32[8]{0:T(128)}, s32[8]{0:T(128)S(1)}, u32[]{:S(2)}) copy-start(s32[8]{0:T(128)S(1)} %get-tuple-element.8) | copy-start | bytes 100
  16.4 9.5 %copy-start.12 = (s32[8]{0:T(128)}, s32[8]{0:T(128)S(1)}, u32[]{:S(2)}) copy-start(s32[8]{0:T(128)S(1)} %get-tuple-element.9) | copy-start | bytes 100
  16.5 9.5 %copy-start.14 = (s32[8]{0:T(128)}, s32[8]{0:T(128)S(1)}, u32[]{:S(2)}) copy-start(s32[8]{0:T(128)S(1)} %get-tuple-element.10) | copy-start | bytes 100
  16.5 9.5 %copy-start.16 = (s32[8]{0:T(128)}, s32[8]{0:T(128)S(1)}, u32[]{:S(2)}) copy-start(s32[8]{0:T(128)S(1)} %get-tuple-element.11) | copy-start | bytes 100
  16.5 9.5 %copy-start.18 = (s32[8]{0:T(128)}, s32[8]{0:T(128)S(1)}, u32[]{:S(2)}) copy-start(s32[8]{0:T(128)S(1)} %get-tuple-element.12) | copy-start | bytes 100
  16.5 11.4 %copy-start.4 = (s32[8]{0:T(128)}, s32[8]{0:T(128)S(1)}, u32[]{:S(2)}) copy-start(s32[8]{0:T(128)S(1)} %get-tuple-element.5) | copy-start | bytes 100
  16.5 11.4 %copy-start.6 = (s32[8]{0:T(128)}, s32[8]{0:T(128)S(1)}, u32[]{:S(2)}) copy-start(s32[8]{0:T(128)S(1)} %get-tuple-element.6) | copy-start | bytes 100
  32.2 72.7 %copy-start.2 = (f32[2,4,256]{2,1,0:T(4,128)}, f32[2,4,256]{2,1,0:T(4,128)S(1)}, u32[]{:S(2)}) copy-start(f32[2,4,256]{2,1,0:T(4,128)S(1)} %get-tuple-element.15) | copy-start | bytes 24580
  210.1 22.1 %copy-start.20 = (s32[2,4]{1,0:T(2,128)S(1)}, s32[2,4]{1,0:T(2,128)}, u32[]{:S(2)}) copy-start(s32[2,4]{1,0:T(2,128)} %lt.32) | copy-start | bytes 100
  229.5 0.6 copy-start.3
  243.1 21.3 %copy-start = (bf16[128,128,128]{2,1,0:T(8,128)(2,1)S(1)}, bf16[128,128,128]{2,1,0:T(8,128)(2,1)}, u32[]{:S(2)}) copy-start(bf16[128,128,128]{2,1,0:T(8,128)(2,1)} %gather_fusion.1) | copy-start | bytes 12582916
  243.1 21.3 %copy-start.1 = (s32[8,2048]{1,0:T(8,128)S(1)}, s32[8,2048]{1,0:T(8,128)}, u32[]{:S(2)}) copy-start(s32[8,2048]{1,0:T(8,128)} %bitcast_add_fusion) | copy-start | bytes 196612
  243.1 21.3 %copy-start.5 = (s32[8]{0:T(128)S(1)}, s32[8]{0:T(128)}, u32[]{:S(2)}) copy-start(s32[8]{0:T(128)} %copy-done.4) | copy-start | bytes 100
  243.1 21.3 %copy-start.7 = (s32[8]{0:T(128)S(1)}, s32[8]{0:T(128)}, u32[]{:S(2)}) copy-start(s32[8]{0:T(128)} %copy-done.6) | copy-start | bytes 100
  243.1 21.3 %copy-start.9 = (s32[8]{0:T(128)S(1)}, s32[8]{0:T(128)}, u32[]{:S(2)}) copy-start(s32[8]{0:T(128)} %copy-done.8) | copy-start | bytes 100
  243.1 21.3 %copy-start.11 = (s32[8]{0:T(128)S(1)}, s32[8]{0:T(128)}, u32[]{:S(2)}) copy-start(s32[8]{0:T(128)} %copy-done.10) | copy-start | bytes 100
  243.1 21.3 %copy-start.13 = (s32[8]{0:T(128)S(1)}, s32[8]{0:T(128)}, u32[]{:S(2)}) copy-start(s32[8]{0:T(128)} %copy-done.12) | copy-start | bytes 100
  243.2 21.3 %copy-start.15 = (s32[8]{0:T(128)S(1)}, s32[8]{0:T(128)}, u32[]{:S(2)}) copy-start(s32[8]{0:T(128)} %copy-done.14) | copy-start | bytes 100
  243.2 21.3 %copy-start.17 = (s32[8]{0:T(128)S(1)}, s32[8]{0:T(128)}, u32[]{:S(2)}) copy-start(s32[8]{0:T(128)} %copy-done.16) | copy-start | bytes 100
  243.2 21.3 %copy-start.19 = (s32[8]{0:T(128)S(1)}, s32[8]{0:T(128)}, u32[]{:S(2)}) copy-start(s32[8]{0:T(128)} %copy-done.18) | copy-start | bytes 100
  243.2 21.3 %copy-start.21 = (s32[8]{0:T(128)S(1)}, s32[8]{0:T(128)}, u32[]{:S(2)}) copy-start(s32[8]{0:T(128)} %param.11) | copy-start | bytes 100
  243.2 21.3 %copy-start.22 = (f32[2,4,256,128]{2,3,1,0:T(8,128)S(1)}, f32[2,4,256,128]{2,3,1,0:T(8,128)}, u32[]{:S(2)}) copy-start(f32[2,4,256,128]{2,3,1,0:T(8,128)} %fusion.17) | copy-start | bytes 3145732
  243.2 41.6 %slice-start = ((s8[8388608]{0:T(1024)(128)(4,1)}), s8[4194304]{0:T(1024)(128)(4,1)S(1)}, s32[]{:S(2)}) async-start(s8[8388608]{0:T(1024)(128)(4,1)} %bitcast.72), calls=%async_computation.4 | async-start | bytes 8388608
  264.5 20.2 %slice-start.1 = ((s8[8388608]{0:T(1024)(128)(4,1)}), s8[4194304]{0:T(1024)(128)(4,1)S(1)}, s32[]{:S(2)}) async-start(s8[8388608]{0:T(1024)(128)(4,1)} %bitcast.72), calls=%async_computation.5 | async-start | bytes 8388608
Sparse Core Ops, SparseCore 0:
  10.1 82.1 all-gather.2
  95.1 80.2 all-gather.4
  289.4 48.2 reduce-scatter.1
where the time goes:
time: 351 us; the launch traced here: 346 us
  waiting for transfers between devices  171 us (49%)
  local copies, waits for them, and re-layouts  72.2 us (21%)
  matrix products  53.9 us (15%)
  other arithmetic  34.2 us (10%)
  between operations  13.6 us (4%)
    all_gather x1, waiting for transfers between devices, local(): lax.all_gather(value_states, 'seq', axis=0, tiled=True)  61.2 us
    all_gather x1, waiting for transfers between devices, local(): lax.all_gather(key_states, 'seq', axis=0, tiled=True)  59.5 us
    reduce_scatter x1, waiting for transfers between devices, local(): lax.psum_scatter(partial_value, 'tp', scatter_dimension=1, tiled=True)  48.4 us
    reduce_sum x2, other arithmetic, attend_context(): denominator = jnp.sum(local_weights, axis=2) + jnp.sum(vert_weights, axis=2)  26 us
    reshape x2, local copies, waits for them, and re-layouts, local(): gathered_keys = gathered_keys.reshape(total_blocks, BLK, kv_heads, head_dim)  21.9 us
    reshape x2, local copies, waits for them, and re-layouts, local(): gathered_values.reshape(total_blocks, BLK, kv_heads, head_dim)  21.7 us
    dot_general x1, matrix products, attend_context(): jnp.einsum('hsk,hkd->hsd', vert_weights.astype(jnp.bfloat16), vert_values...  20.2 us
    dot_general x1, matrix products, attend_context(): jnp.einsum('hsd,hkd->hsk', per_head, vert_keys, preferred_element_type=jn...  19.5 us
  transfers between devices with their start and end apart: 4, of which 3 were waited for; matrix products, arithmetic and copies ran while one was open for 13% of the time, Pallas kernels for 0%

commit v1 on v0

v1 whole, which is shorter than its diff:
```python
import functools
import math

import jax
import jax.numpy as jnp
from jax import lax
from jax.experimental import pallas as pl
from jax.experimental.pallas import tpu as pltpu
from jax.sharding import PartitionSpec as P

HD = 128
BLK = 128
GROUP = 4
NX, NZ = 4, 8
NEG = -1e30
C2 = math.log2(math.e) / math.sqrt(HD)
VMEM_BYTES = 48 * 1024 * 1024


def seq_at(z, x, core):
    return ((z % NZ) * NX + (x % NX)) * 2 + core


def shift(value, dz, dx, flip=0):
    pairs = [
        (seq_at(z, x, c), seq_at(z + dz, x + dx, c ^ flip))
        for z in range(NZ)
        for x in range(NX)
        for c in range(2)
    ]
    return lax.ppermute(value, "seq", pairs)


def tp_shift(value, step):
    return lax.ppermute(value, "tp", [(i, (i + step) % 4) for i in range(4)])


def dot_t(a, b, dims):
    return lax.dot_general(a, b, (dims, ((), ())), preferred_element_type=jnp.float32)


def local_kernel(scal, win, slash, named, q_ref, kv_ref, halo_ref, m_ref, l_ref, acc_ref):
    has_prev = scal[0] > 0
    kj = lax.broadcasted_iota(jnp.int32, (BLK, BLK), 0)
    qi = lax.broadcasted_iota(jnp.int32, (BLK, BLK), 1)
    diag_gap = qi - kj
    prev_gap = diag_gap + BLK
    keys = jnp.concatenate([halo_ref[:, :HD], kv_ref[:, :HD]], axis=0)
    values = jnp.concatenate([halo_ref[:, HD:], kv_ref[:, HD:]], axis=0)
    for h in range(GROUP):
        diag_ok = diag_gap < win[h]
        prev_ok = prev_gap < win[h]
        for n in range(8):
            diag_ok = diag_ok | (diag_gap == slash[h, n])
            prev_ok = prev_ok | (prev_gap == slash[h, n])
        for i in range(4):
            span = (i + 2) * BLK
            s = dot_t(keys[:span], q_ref[h, i * BLK : (i + 1) * BLK, :], ((1,), (1,)))
            tiles = []
            for t in range(i + 2):
                tile = s[t * BLK : (t + 1) * BLK]
                is_named = named[h, t] > 0
                if t == i + 1:
                    ok = (diag_gap >= 0) & (diag_ok | is_named)
                elif t == i:
                    ok = prev_ok | is_named
                    if t == 0:
                        ok = ok & has_prev
                else:
                    ok = jnp.broadcast_to(is_named, (BLK, BLK))
                tiles.append(jnp.where(ok, tile, NEG))
            s = jnp.concatenate(tiles, axis=0)
            m = jnp.max(s, axis=0, keepdims=True)
            w = jnp.exp2((s - m) * C2)
            m_ref[h, :, i * BLK : (i + 1) * BLK] = m
            l_ref[h, :, i * BLK : (i + 1) * BLK] = jnp.sum(w, axis=0, keepdims=True)
            acc_ref[h, :, i * BLK : (i + 1) * BLK] = dot_t(
                values[:span], w.astype(jnp.bfloat16), ((0,), (0,))
            )


def far_kernel(first, sizes, final, act, q_ref, m_in, l_in, acc_in, *rest):
    pieces = rest[: len(sizes)]
    if final:
        out_ref, m_ref, l_ref, acc_ref, kv, todo, sem = rest[len(sizes) :]
    else:
        m_ref, l_ref, acc_ref, kv, todo, sem = rest[len(sizes) :]
    copies = []
    at = 0
    for k, (piece, size) in enumerate(zip(pieces, sizes)):
        copies.append(pltpu.make_async_copy(piece, kv.at[pl.ds(at, size)], sem.at[k]))
        at += size
    for copy in copies:
        copy.start()

    def note(k, count):
        slot = k // GROUP
        todo[count] = k
        return count + act[k - slot * GROUP, first + slot]

    count = lax.fori_loop(0, at * GROUP, note, 0)
    m_ref[...] = m_in[...]
    l_ref[...] = l_in[...]
    acc_ref[...] = acc_in[...]
    for copy in copies:
        copy.wait()

    def scores(k):
        slot = k // GROUP
        h = k - slot * GROUP
        return slot, h, dot_t(kv[slot, :, :HD], q_ref[h], ((1,), (1,)))

    def merge(slot, h, s):
        m_old = m_ref[h]
        m_new = jnp.maximum(m_old, jnp.max(s, axis=0, keepdims=True))
        alpha = jnp.exp2((m_old - m_new) * C2)
        w = jnp.exp2((s - m_new) * C2)
        m_ref[h] = m_new
        l_ref[h] = l_ref[h] * alpha + jnp.sum(w, axis=0, keepdims=True)
        acc_ref[h] = acc_ref[h] * alpha + dot_t(
            kv[slot, :, HD:], w.astype(jnp.bfloat16), ((0,), (0,))
        )

    def two(k, carry):
        one = scores(todo[2 * k])
        other = scores(todo[2 * k + 1])
        merge(*one)
        merge(*other)
        return carry

    lax.fori_loop(0, count // 2, two, 0)

    @pl.when(count % 2 == 1)
    def _():
        merge(*scores(todo[count - 1]))

    if final:
        for h in range(GROUP):
            done = acc_ref[h] / l_ref[h]
            out_ref[:, h * HD : (h + 1) * HD] = done.T.astype(jnp.bfloat16)


def spec(space):
    return pl.BlockSpec(memory_space=space)


def state_shapes(rows):
    return [
        jax.ShapeDtypeStruct((GROUP, 1, rows), jnp.float32),
        jax.ShapeDtypeStruct((GROUP, 1, rows), jnp.float32),
        jax.ShapeDtypeStruct((GROUP, HD, rows), jnp.float32),
    ]


def attend_local(scal, win, slash, named, q4, kv, halo):
    rows = kv.shape[0]
    return pl.pallas_call(
        local_kernel,
        out_shape=state_shapes(rows),
        in_specs=[spec(pltpu.SMEM)] * 4 + [spec(pltpu.VMEM)] * 3,
        out_specs=[spec(pltpu.VMEM)] * 3,
        compiler_params=pltpu.CompilerParams(vmem_limit_bytes=VMEM_BYTES),
        cost_estimate=pl.CostEstimate(flops=500_000_000, bytes_accessed=4_000_000, transcendentals=0),
        name="local_part",
    )(scal, win, slash, named, q4, kv, halo)


def attend_far(act, q4, state, pieces, first, final):
    rows = q4.shape[1]
    sizes = [p.shape[0] for p in pieces]
    total = sum(sizes)
    outs = state_shapes(rows)
    scratch = [
        pltpu.VMEM((total, BLK, 2 * HD), jnp.bfloat16),
        pltpu.SMEM((total * GROUP + 8,), jnp.int32),
        pltpu.SemaphoreType.DMA((len(sizes),)),
    ]
    if final:
        scratch = [pltpu.VMEM(o.shape, o.dtype) for o in outs] + scratch
        outs = [jax.ShapeDtypeStruct((rows, GROUP * HD), jnp.bfloat16)]
    return pl.pallas_call(
        functools.partial(far_kernel, first, sizes, final),
        out_shape=outs,
        in_specs=[spec(pltpu.SMEM)] + [spec(pltpu.VMEM)] * 4 + [spec(pl.ANY)] * len(sizes),
        out_specs=[spec(pltpu.VMEM)] * len(outs),
        scratch_shapes=scratch,
        compiler_params=pltpu.CompilerParams(vmem_limit_bytes=VMEM_BYTES),
        cost_estimate=pl.CostEstimate(
            flops=total * 30_000_000, bytes_accessed=4_000_000, transcendentals=0
        ),
        name="far_part",
    )(act, q4, *state, *pieces)


def local(queries, key_states, value_states, vert_blocks, window_size, slash_offsets, out_weight):
    place = lax.axis_index("seq")
    core = place % 2
    chip = place // 2
    z, x = chip // NX, chip % NX
    first_core = core == 0

    def mine_other(a, axis):
        half = a.shape[axis] // 2
        low = lax.slice_in_dim(a, 0, half, axis=axis)
        high = lax.slice_in_dim(a, half, 2 * half, axis=axis)
        return jnp.where(first_core, low, high), jnp.where(first_core, high, low)

    k_mine, k_other = mine_other(key_states, 1)
    v_mine, v_other = mine_other(value_states, 1)
    q_mine, q_other = mine_other(queries, 1)
    blocks = mine_other(vert_blocks, 0)[0]
    window = mine_other(window_size, 0)[0]
    slashes = mine_other(slash_offsets, 0)[0]

    kv_mine = jnp.concatenate([k_mine, v_mine], axis=1)
    kv_sib = shift(jnp.concatenate([k_other, v_other], axis=1), 0, 0, 1)
    q_sib = shift(q_other, 0, 0, 1)

    def chosen(kv, shard):
        second = jnp.any(blocks == 2 * shard + 1)
        return jnp.where(second, kv[BLK:], kv[:BLK])[None]

    a0 = chosen(kv_mine, place)
    b0 = chosen(kv_sib, place + 1 - 2 * core)

    a = jnp.concatenate([a0, shift(a0, 0, 1), shift(a0, 0, -1), shift(a0, 0, 2)], axis=0)
    ups, downs = [a], [a]
    for _ in range(3):
        ups.append(shift(ups[-1], 1, 0))
        downs.append(shift(downs[-1], -1, 0))
    up4 = shift(ups[3][:2], 1, 0)
    down4 = shift(downs[3][2:], -1, 0)

    bu, bd = [b0], [b0]
    for _ in range(3):
        bu.append(shift(bu[-1], 1, 0))
        bd.append(shift(bd[-1], -1, 0))
    bu4 = shift(bu[3], 1, 0)
    b = jnp.concatenate(bu + [bu4] + bd[1:], axis=0)
    b_right = shift(b, 0, 1)
    b_left = shift(b, 0, -1)
    b_right2 = shift(b_right[:4], 0, 1)
    b_left2 = shift(b_left[4:], 0, -1)

    ax = [0, -1, 1, 2]
    bz = [0, -1, -2, -3, -4, 1, 2, 3]

    def a_slots(dz, xs=ax):
        return [(dz, dx, 0) for dx in xs]

    def b_slots(dx, zs=bz):
        return [(dz, dx, 1) for dz in zs]

    groups = [
        ([a, ups[1], downs[1], b], a_slots(0) + a_slots(-1) + a_slots(1) + b_slots(0)),
        (
            [ups[2], downs[2], ups[3], downs[3], b_right, b_left],
            a_slots(-2) + a_slots(2) + a_slots(-3) + a_slots(3) + b_slots(-1) + b_slots(1),
        ),
        (
            [up4, down4, b_right2, b_left2],
            a_slots(-4, ax[:2]) + a_slots(4, ax[2:]) + b_slots(-2, bz[:4]) + b_slots(2, bz[4:]),
        ),
    ]
    slots = jnp.array([s for _, ss in groups for s in ss], dtype=jnp.int32)
    slot_z = (z + slots[:, 0] + NZ) % NZ
    slot_x = (x + slots[:, 1] + NX) % NX
    slot_core = jnp.where(slots[:, 2] == 0, core, 1 - core)
    slot_shard = (slot_z * NX + slot_x) * 2 + slot_core
    far = blocks <= 4 * chip - 2
    act = jnp.any(
        (blocks[:, :, None] // 2 == slot_shard[None, None, :]) & far[:, :, None], axis=1
    ).astype(jnp.int32)
    near = 4 * chip - 1 + jnp.arange(5, dtype=jnp.int32)
    named = jnp.any(blocks[:, :, None] == near[None, None, :], axis=1).astype(jnp.int32)

    def in_order(mine, sib):
        return jnp.where(
            first_core, jnp.concatenate([mine, sib], axis=0), jnp.concatenate([sib, mine], axis=0)
        )

    kv_chip = in_order(kv_mine, kv_sib)
    tail = jnp.where(first_core, kv_sib[BLK:], kv_mine[BLK:])
    halo = lax.ppermute(tail, "seq", [(i, i + 2) for i in range(2 * NX * NZ - 2)])
    q_chip = in_order(q_mine, q_sib)
    q4 = jnp.stack([q_chip[:, h * HD : (h + 1) * HD] for h in range(GROUP)], axis=0)

    state = attend_local(chip.reshape(1), window, slashes, named, q4, kv_chip, halo)
    first = 0
    for n, (pieces, ss) in enumerate(groups):
        state = attend_far(act, q4, state, pieces, first, n == len(groups) - 1)
        first += len(ss)
    context = state[0]

    rows = queries.shape[0]
    ctx_mine = jnp.where(first_core, context[:rows], context[rows:])
    ctx_sib = shift(jnp.where(first_core, context[rows:], context[:rows]), 0, 0, 1)
    ctx = jnp.where(
        first_core,
        jnp.concatenate([ctx_mine, ctx_sib], axis=1),
        jnp.concatenate([ctx_sib, ctx_mine], axis=1),
    )
    partial_value = jnp.dot(ctx, out_weight, preferred_element_type=jnp.float32)

    me = lax.axis_index("tp")
    width = out_weight.shape[1] // 4
    half = width // 2

    def share(step):
        return lax.dynamic_slice_in_dim(partial_value, ((me + step + 4) % 4) * width, width, 1)

    opposite, after, before = share(2), share(1), share(-1)
    via_after = tp_shift(opposite[:, :half].astype(jnp.bfloat16), 1)
    via_before = tp_shift(opposite[:, half:].astype(jnp.bfloat16), -1)
    to_after = jnp.concatenate(
        [after[:, :half] + via_after.astype(jnp.float32), after[:, half:]], axis=1
    ).astype(jnp.bfloat16)
    to_before = jnp.concatenate(
        [before[:, :half], before[:, half:] + via_before.astype(jnp.float32)], axis=1
    ).astype(jnp.bfloat16)
    from_before = tp_shift(to_after, 1)
    from_after = tp_shift(to_before, -1)
    total = share(0) + from_before.astype(jnp.float32) + from_after.astype(jnp.float32)
    return total.astype(jnp.bfloat16)


def solution(mesh):
    return jax.shard_map(
        local,
        mesh=mesh,
        in_specs=(
            P("seq", "tp"),
            P("seq", "tp"),
            P("seq", "tp"),
            P("tp", None),
            P("tp"),
            P("tp", None),
            P("tp", None),
        ),
        out_specs=P("seq", "tp"),
        check_vma=False,
    )
```

time: 351 us -> 120 us (0.34)
  the two profiles are of different devices: /device:TPU:192 before, /device:TPU:248 now
where the time goes in v1:
time: 120 us; the launch traced here: 119 us
  starting transfers between devices  40.3 us (34%)
  waiting for transfers between devices  32.6 us (27%)
  Pallas kernels  23.4 us (20%)
  other arithmetic  13.3 us (11%)
  matrix products  5.72 us (5%)
  local copies, waits for them, and re-layouts  3.63 us (3%)
    ppermute x25, starting transfers between devices, shift(): return lax.ppermute(value, 'seq', pairs)  34.1 us
    pallas_call x3, Pallas kernels, attend_far(): pl.pallas_call(functools.partial(far_kernel, first, sizes, final), out_sh...  20.4 us
    ppermute x4, waiting for transfers between devices, tp_shift(): return lax.ppermute(value, 'tp', [(i, (i + step) % 4) for i in range(4)])  18.6 us
    ppermute x25, waiting for transfers between devices, shift(): return lax.ppermute(value, 'seq', pairs)  14 us
    dot_general x1, matrix products, local(): partial_value = jnp.dot(ctx, out_weight, preferred_element_type=jnp.float32)  5.72 us
    select_n x4, other arithmetic, mine_other(): return (jnp.where(first_core, low, high), jnp.where(first_core, high, low))  4.3 us
    ppermute x4, starting transfers between devices, tp_shift(): return lax.ppermute(value, 'tp', [(i, (i + step) % 4) for i in range(4)])  4.28 us
    pallas_call x1, Pallas kernels, attend_local(): pl.pallas_call(local_kernel, out_shape=state_shapes(rows), in_specs=[spec...  2.95 us
  transfers between devices with their start and end apart: 30, of which 11 were waited for; matrix products, arithmetic and copies ran while one was open for 9% of the time, Pallas kernels for 16%

profile of v1, /device:TPU:248, one launch (start us, length us, event | category | flops | bytes accessed | tf_op | source)
XLA Modules:
  0.0 119.4 jit_solution(6963602191393100938)
XLA Ops:
  1.1 1.8 %broadcast_select_fusion.3 = (bf16[256,512]{1,0:T(8,128)(2,1)S(1)}, bf16[256,512]{1,0:T(8,128)(2,1)}) fusion(pred[]{:T(512)S(6)} %eq.60, bf16[256,1024]{1,0:T(8,128)(2,1)} %param.8), kind=kLoop, calls=%fused_computation.25 | loop fusion | flops 262144 | bytes 1048577 | tf_op jit(solution)/shard_map/jit(_where)/select_n | solution.py:206
  4.9 1.5 %compare_reduce_fusion.1 = (pred[]{:T(512)}, pred[]{:T(512)}, s32[4,16]{1,0:T(4,128)S(1)}) fusion(s32[]{:T(128)S(6)} %add.188, s32[]{:T(128)S(6)} %add.186, s32[8,16]{1,0:T(8,128)} %param.11, pred[]{:T(512)S(6)} %eq.60), kind=kLoop, calls=%fused_computation.67 | loop fusion | flops 318 | bytes 779 | tf_op jit(solution)/shard_map/reduce_or | solution.py:220
  7.9 1.6 %collective-permute-start.3 = (bf16[1,128,256]{2,1,0:T(8,128)(2,1)S(1)}, bf16[1,128,256]{2,1,0:T(8,128)(2,1)S(1)}, u32[]{:S(2)}, u32[]{:S(2)}) collective-permute-start(bf16[1,128,256]{2,1,0:T(8,128)(2,1)S(1)} %get-tuple-element.42), channel_id=1, source_target_pairs={{0,8},{4,12},{8,16},{12,20},{16,24},{20,28},{24,0},{28,4},{32,40},... | collective-permute-start | bytes 196616 | tf_op jit(solution)/shard_map/ppermute | solution.py:31
  9.5 1.7 %collective-permute-start.4 = (bf16[1,128,256]{2,1,0:T(8,128)(2,1)S(1)}, bf16[1,128,256]{2,1,0:T(8,128)(2,1)S(1)}, u32[]{:S(2)}, u32[]{:S(2)}) collective-permute-start(bf16[1,128,256]{2,1,0:T(8,128)(2,1)S(1)} %get-tuple-element.42), channel_id=1, source_target_pairs={{0,24},{4,28},{8,0},{12,4},{16,8},{20,12},{24,16},{28,20},{32,56},... | collective-permute-start | bytes 196616 | tf_op jit(solution)/shard_map/ppermute | solution.py:31
  11.2 1.8 %collective-permute-start.5 = (bf16[1,128,256]{2,1,0:T(8,128)(2,1)S(1)}, bf16[1,128,256]{2,1,0:T(8,128)(2,1)S(1)}, u32[]{:S(2)}, u32[]{:S(2)}) collective-permute-start(bf16[1,128,256]{2,1,0:T(8,128)(2,1)S(1)} %get-tuple-element.42), channel_id=1, source_target_pairs={{0,16},{4,20},{8,24},{12,28},{16,0},{20,4},{24,8},{28,12},{32,48},... | collective-permute-start | bytes 196616 | tf_op jit(solution)/shard_map/ppermute | solution.py:31
  13.8 2.0 %collective-permute-start.12 = (bf16[1,128,256]{2,1,0:T(8,128)(2,1)S(1)}, bf16[1,128,256]{2,1,0:T(8,128)(2,1)S(1)}, u32[]{:S(2)}, u32[]{:S(2)}) collective-permute-start(bf16[1,128,256]{2,1,0:T(8,128)(2,1)S(1)} %get-tuple-element.26), channel_id=1, source_target_pairs={{0,224},{4,228},{8,232},{12,236},{16,240},{20,244},{24,248},{28,25... | collective-permute-start | bytes 196616 | tf_op jit(solution)/shard_map/ppermute | solution.py:31
  17.3 1.9 %collective-permute-start.7 = (bf16[4,128,256]{2,1,0:T(8,128)(2,1)S(1)}, bf16[4,128,256]{2,1,0:T(8,128)(2,1)S(1)}, u32[]{:S(2)}, u32[]{:S(2)}) collective-permute-start(bf16[4,128,256]{2,1,0:T(8,128)(2,1)S(1)} %pad_maximum_fusion.3.rest_0_), channel_id=1, source_target_pairs={{0,224},{4,228},{8,232},{12,236},{16,240},{20,244},{24,248},{28,25... | collective-permute-start | bytes 786440 | tf_op jit(solution)/shard_map/ppermute | solution.py:31
  21.2 3.9 %collective-permute-done.9 = bf16[1,128,256]{2,1,0:T(8,128)(2,1)S(1)} collective-permute-done((bf16[1,128,256]{2,1,0:T(8,128)(2,1)S(1)}, bf16[1,128,256]{2,1,0:T(8,128)(2,1)S(1)}, u32[]{:S(2)}, u32[]{:S(2)}) %collective-permute-start.9) | collective-permute-done | bytes 65568 | tf_op jit(solution)/shard_map/ppermute | solution.py:31
  25.1 1.9 %collective-permute-start.10 = (bf16[1,128,256]{2,1,0:T(8,128)(2,1)S(1)}, bf16[1,128,256]{2,1,0:T(8,128)(2,1)S(1)}, u32[]{:S(2)}, u32[]{:S(2)}) collective-permute-start(bf16[1,128,256]{2,1,0:T(8,128)(2,1)S(1)} %collective-permute-done.9), channel_id=1, source_target_pairs={{0,32},{4,36},{8,40},{12,44},{16,48},{20,52},{24,56},{28,60},{32,6... | collective-permute-start | bytes 196616 | tf_op jit(solution)/shard_map/ppermute | solution.py:31
  27.1 2.9 %collective-permute-done.10 = bf16[1,128,256]{2,1,0:T(8,128)(2,1)S(1)} collective-permute-done((bf16[1,128,256]{2,1,0:T(8,128)(2,1)S(1)}, bf16[1,128,256]{2,1,0:T(8,128)(2,1)S(1)}, u32[]{:S(2)}, u32[]{:S(2)}) %collective-permute-start.10) | collective-permute-done | bytes 65568 | tf_op jit(solution)/shard_map/ppermute | solution.py:31
  30.0 2.5 %collective-permute-start.11 = (bf16[1,128,256]{2,1,0:T(8,128)(2,1)S(1)}, bf16[1,128,256]{2,1,0:T(8,128)(2,1)S(1)}, u32[]{:S(2)}, u32[]{:S(2)}) collective-permute-start(bf16[1,128,256]{2,1,0:T(8,128)(2,1)S(1)} %collective-permute-done.10), channel_id=1, source_target_pairs={{0,32},{4,36},{8,40},{12,44},{16,48},{20,52},{24,56},{28,60},{32,6... | collective-permute-start | bytes 196616 | tf_op jit(solution)/shard_map/ppermute | solution.py:31
  32.5 1.9 %collective-permute-done.11 = bf16[1,128,256]{2,1,0:T(8,128)(2,1)S(1)} collective-permute-done((bf16[1,128,256]{2,1,0:T(8,128)(2,1)S(1)}, bf16[1,128,256]{2,1,0:T(8,128)(2,1)S(1)}, u32[]{:S(2)}, u32[]{:S(2)}) %collective-permute-start.11) | collective-permute-done | bytes 65568 | tf_op jit(solution)/shard_map/ppermute | solution.py:31
  35.1 2.6 %collective-permute-start.20 = (bf16[8,128,256]{2,1,0:T(8,128)(2,1)S(1)}, bf16[8,128,256]{2,1,0:T(8,128)(2,1)S(1)}, u32[]{:S(2)}, u32[]{:S(2)}) collective-permute-start(bf16[8,128,256]{2,1,0:T(8,128)(2,1)S(1)} %constant_dynamic-update-slice_fusion.rest_3_), channel_id=1, source_target_pairs={{0,24},{4,28},{8,0},{12,4},{16,8},{20,12},{24,16},{28,20},{32,56},... | collective-permute-start | bytes 1572872 | tf_op jit(solution)/shard_map/ppermute | solution.py:31
  37.7 3.6 %collective-permute-start.15 = (bf16[4,128,256]{2,1,0:T(8,128)(2,1)S(1)}, bf16[4,128,256]{2,1,0:T(8,128)(2,1)S(1)}, u32[]{:S(2)}, u32[]{:S(2)}) collective-permute-start(bf16[4,128,256]{2,1,0:T(8,128)(2,1)S(1)} %collective-permute-done.6.rest_1_), channel_id=1, source_target_pairs={{0,32},{4,36},{8,40},{12,44},{16,48},{20,52},{24,56},{28,60},{32,6... | collective-permute-start | bytes 786440 | tf_op jit(solution)/shard_map/ppermute | solution.py:31
  41.8 1.9 %collective-permute-start.2 = (bf16[128,256]{1,0:T(8,128)(2,1)S(1)}, bf16[128,256]{1,0:T(8,128)(2,1)S(1)}, u32[]{:S(2)}, u32[]{:S(2)}) collective-permute-start(bf16[128,256]{1,0:T(8,128)(2,1)S(1)} %get-tuple-element.43), channel_id=1, source_target_pairs={{0,8},{4,12},{8,16},{12,20},{16,24},{20,28},{24,32},{28,36},{32,40... | collective-permute-start | bytes 196616 | tf_op jit(solution)/shard_map/ppermute | solution.py:284
  44.9 2.2 %collective-permute-done.15.rest_0_ = bf16[4,128,256]{2,1,0:T(8,128)(2,1)S(1)} collective-permute-done((bf16[4,128,256]{2,1,0:T(8,128)(2,1)S(1)}, bf16[4,128,256]{2,1,0:T(8,128)(2,1)S(1)}, u32[]{:S(2)}, u32[]{:S(2)}) %collective-permute-start.15) | collective-permute-done | bytes 262176 | tf_op jit(solution)/shard_map/ppermute | solution.py:31
  47.1 3.7 %collective-permute-start.17 = (bf16[4,128,256]{2,1,0:T(8,128)(2,1)S(1)}, bf16[4,128,256]{2,1,0:T(8,128)(2,1)S(1)}, u32[]{:S(2)}, u32[]{:S(2)}) collective-permute-start(bf16[4,128,256]{2,1,0:T(8,128)(2,1)S(1)} %collective-permute-done.15.rest_0_), channel_id=1, source_target_pairs={{0,32},{4,36},{8,40},{12,44},{16,48},{20,52},{24,56},{28,60},{32,6... | collective-permute-start | bytes 786440 | tf_op jit(solution)/shard_map/ppermute | solution.py:31
  51.4 3.3 %collective-permute-start.24 = (bf16[4,128,256]{2,1,0:T(8,128)(2,1)S(1)}, bf16[4,128,256]{2,1,0:T(8,128)(2,1)S(1)}, u32[]{:S(2)}, u32[]{:S(2)}) collective-permute-start(bf16[4,128,256]{2,1,0:T(8,128)(2,1)S(1)} %slice.159), channel_id=1, source_target_pairs={{0,24},{4,28},{8,0},{12,4},{16,8},{20,12},{24,16},{28,20},{32,56},... | collective-permute-start | bytes 786440 | tf_op jit(solution)/shard_map/ppermute | solution.py:31
  54.8 2.9 %local_part.1 = (f32[4,1,512]{2,1,0:T(1,128)S(1)}, f32[4,1,512]{2,1,0:T(1,128)S(1)}, f32[4,128,512]{2,1,0:T(8,128)S(1)}) custom-call(s32[1]{0:T(128)} %bitcast.7.scal, s32[4]{0:T(128)S(1)} %broadcast_select_fusion.9.win, s32[4,8]{1,0:T(4,128)S(1)} %slice_select_fusion.1.slash, s32[4,5]{1,0:T(4,128)S(1)} %convert_element_type.26.named, ...), custom_call_target="tpu_custom_call" | custom-call | flops 500000000 | bytes 4000000 | tf_op jit(solution)/shard_map/local_part/pallas_call | solution.py:157
  57.8 3.3 %collective-permute-start.21 = (bf16[2,128,256]{2,1,0:T(8,128)(2,1)S(1)}, bf16[2,128,256]{2,1,0:T(8,128)(2,1)S(1)}, u32[]{:S(2)}, u32[]{:S(2)}) collective-permute-start(bf16[2,128,256]{2,1,0:T(8,128)(2,1)S(1)} %slice.156), channel_id=1, source_target_pairs={{0,32},{4,36},{8,40},{12,44},{16,48},{20,52},{24,56},{28,60},{32,6... | collective-permute-start | bytes 393224 | tf_op jit(solution)/shard_map/ppermute | solution.py:31
  61.2 5.7 %far_part.3 = (f32[4,1,512]{2,1,0:T(1,128)S(1)}, f32[4,1,512]{2,1,0:T(1,128)S(1)}, f32[4,128,512]{2,1,0:T(8,128)S(1)}) custom-call(s32[4,64]{1,0:T(4,128)S(1)} %convert_element_type.25.act, bf16[4,512,128]{2,1,0:T(8,128)(2,1)S(1)} %pad_maximum_fusion.q_ref, f32[4,1,512]{2,1,0:T(1,128)S(1)} %get-tuple-element.14.m_in, ...), custom_call_target="tpu_custom_call" | custom-call | flops 600000000 | bytes 4000000 | tf_op jit(solution)/shard_map/far_part/pallas_call | solution.py:181
  66.9 9.9 %far_part.4 = (f32[4,1,512]{2,1,0:T(1,128)S(1)}, f32[4,1,512]{2,1,0:T(1,128)S(1)}, f32[4,128,512]{2,1,0:T(8,128)S(1)}) custom-call(s32[4,64]{1,0:T(4,128)S(1)} %convert_element_type.25.act, bf16[4,512,128]{2,1,0:T(8,128)(2,1)S(1)} %pad_maximum_fusion.q_ref, f32[4,1,512]{2,1,0:T(1,128)S(1)} %get-tuple-element.17.m_in, ...), custom_call_target="tpu_custom_call" | custom-call | flops 960000000 | bytes 4000000 | tf_op jit(solution)/shard_map/far_part/pallas_call | solution.py:181
  76.9 4.8 %far_part.5 = bf16[512,512]{1,0:T(8,128)(2,1)S(1)} custom-call(s32[4,64]{1,0:T(4,128)S(1)} %convert_element_type.25.act, bf16[4,512,128]{2,1,0:T(8,128)(2,1)S(1)} %pad_maximum_fusion.q_ref, f32[4,1,512]{2,1,0:T(1,128)S(1)} %get-tuple-element.20.m_in, f32[4,1,512]{2,1,0:T(1,128)S(1)} %get-tuple-element.21.l_in, f32[4,128,512]{2,1,0:T(8,128)S(1)} %get-tuple-element.22.acc_in, ...), custom_call_target="tpu_custom_call" | custom-call | flops 360000000 | bytes 4000000 | tf_op jit(solution)/shard_map/far_part/pallas_call | solution.py:181
  82.1 1.5 %collective-permute-done.25 = bf16[256,512]{1,0:T(8,128)(2,1)S(1)} collective-permute-done((bf16[256,512]{1,0:T(8,128)(2,1)S(1)}, bf16[256,512]{1,0:T(8,128)(2,1)S(1)}, u32[]{:S(2)}, u32[]{:S(2)}) %collective-permute-start.25) | collective-permute-done | bytes 262176 | tf_op jit(solution)/shard_map/ppermute | solution.py:31
  83.6 5.7 %fusion.2 = f32[256,4096]{1,0:T(8,128)S(1)} fusion(bf16[1024,4096]{1,0:T(8,128)(2,1)} %param.14, bf16[256,512]{1,0:T(8,128)(2,1)S(1)} %collective-permute-done.25, bf16[256,512]{1,0:T(8,128)(2,1)S(1)} %get-tuple-element.34, pred[]{:T(512)S(6)} %eq.60), kind=kOutput, calls=%fused_computation.11 | convolution fusion | flops 2149842944 | bytes 13107201 | tf_op jit(solution)/shard_map/dot_general | solution.py:303
  89.3 2.0 %copy-done = f32[256,4096]{1,0:T(8,128)} copy-done((f32[256,4096]{1,0:T(8,128)}, f32[256,4096]{1,0:T(8,128)S(1)}, u32[]{:S(2)}) %copy-start) | copy-done | bytes 4194328
  91.7 1.8 %collective-permute-start.28 = (bf16[256,512]{1,0:T(8,128)(2,1)S(1)}, bf16[256,512]{1,0:T(8,128)(2,1)S(1)}, u32[]{:S(2)}, u32[]{:S(2)}) collective-permute-start(bf16[256,512]{1,0:T(8,128)(2,1)S(1)} %get-tuple-element.33), channel_id=1, source_target_pairs={{0,3},{1,0},{2,1},{3,2},{4,7},{5,4},{6,5},{7,6},{8,11},{9,8},{10,9... | collective-permute-start | bytes 786440 | tf_op jit(solution)/shard_map/ppermute | solution.py:35
  94.8 5.0 %collective-permute-done.26 = bf16[256,512]{1,0:T(8,128)(2,1)S(1)} collective-permute-done((bf16[256,512]{1,0:T(8,128)(2,1)S(1)}, bf16[256,512]{1,0:T(8,128)(2,1)S(1)}, u32[]{:S(2)}, u32[]{:S(2)}) %collective-permute-start.26) | collective-permute-done | bytes 262176 | tf_op jit(solution)/shard_map/ppermute | solution.py:35
  103.0 1.8 %collective-permute-start.29 = (bf16[256,1024]{1,0:T(8,128)(2,1)S(1)}, bf16[256,1024]{1,0:T(8,128)(2,1)S(1)}, u32[]{:S(2)}, u32[]{:S(2)}) collective-permute-start(bf16[256,1024]{1,0:T(8,128)(2,1)S(1)} %pad_maximum_fusion.2), channel_id=1, source_target_pairs={{0,3},{1,0},{2,1},{3,2},{4,7},{5,4},{6,5},{7,6},{8,11},{9,8},{10,9... | collective-permute-start | bytes 1572872 | tf_op jit(solution)/shard_map/ppermute | solution.py:35
  104.8 10.8 %collective-permute-done.27 = bf16[256,1024]{1,0:T(8,128)(2,1)S(1)} collective-permute-done((bf16[256,1024]{1,0:T(8,128)(2,1)S(1)}, bf16[256,1024]{1,0:T(8,128)(2,1)S(1)}, u32[]{:S(2)}, u32[]{:S(2)}) %collective-permute-start.27) | collective-permute-done | bytes 524320 | tf_op jit(solution)/shard_map/ppermute | solution.py:35
  115.6 1.5 %collective-permute-done.29 = bf16[256,1024]{1,0:T(8,128)(2,1)S(1)} collective-permute-done((bf16[256,1024]{1,0:T(8,128)(2,1)S(1)}, bf16[256,1024]{1,0:T(8,128)(2,1)S(1)}, u32[]{:S(2)}, u32[]{:S(2)}) %collective-permute-start.29) | collective-permute-done | bytes 524320 | tf_op jit(solution)/shard_map/ppermute | solution.py:35
  117.1 2.3 %add_convert_fusion = bf16[256,1024]{1,0:T(8,128)(2,1)} fusion(bf16[256,1024]{1,0:T(8,128)(2,1)S(1)} %collective-permute-done.29, bf16[256,1024]{1,0:T(8,128)(2,1)S(1)} %collective-permute-done.27, f32[256,4096]{1,0:T(8,128)} %copy-done, s32[]{:T(128)S(6)} %select_n.227), kind=kLoop, calls=%fused_computation | loop fusion | flops 1310720 | bytes 2621444 | tf_op jit(solution)/shard_map/convert_element_type | solution.py:324
  (76 shorter events, 17.2 us)
Async XLA Ops:
  1.0 6.3 %collective-permute-start.1 = (bf16[256,256]{1,0:T(8,128)(2,1)S(1)}, bf16[256,256]{1,0:T(8,128)(2,1)S(1)}, u32[]{:S(2)}, u32[]{:S(2)}) collective-permute-start(bf16[256,256]{1,0:T(8,128)(2,1)S(1)} %pad_maximum_fusion.4), channel_id=1, source_target_pairs={{0,4},{4,0},{8,12},{12,8},{16,20},{20,16},{24,28},{28,24},{32,36},... | collective-permute-start | bytes 393224 | tf_op jit(solution)/shard_map/ppermute | solution.py:31
  2.9 39.0 %collective-permute-start = (bf16[256,512]{1,0:T(8,128)(2,1)}, bf16[256,512]{1,0:T(8,128)(2,1)}, u32[]{:S(2)}, u32[]{:S(2)}) collective-permute-start(bf16[256,512]{1,0:T(8,128)(2,1)} %get-tuple-element.41), channel_id=1, source_target_pairs={{0,4},{4,0},{8,12},{12,8},{16,20},{20,16},{24,28},{28,24},{32,36},... | collective-permute-start | bytes 786440 | tf_op jit(solution)/shard_map/ppermute | solution.py:31
  7.9 5.9 %collective-permute-start.3 = (bf16[1,128,256]{2,1,0:T(8,128)(2,1)S(1)}, bf16[1,128,256]{2,1,0:T(8,128)(2,1)S(1)}, u32[]{:S(2)}, u32[]{:S(2)}) collective-permute-start(bf16[1,128,256]{2,1,0:T(8,128)(2,1)S(1)} %get-tuple-element.42), channel_id=1, source_target_pairs={{0,8},{4,12},{8,16},{12,20},{16,24},{20,28},{24,0},{28,4},{32,40},... | collective-permute-start | bytes 196616 | tf_op jit(solution)/shard_map/ppermute | solution.py:31
  9.5 6.3 %collective-permute-start.4 = (bf16[1,128,256]{2,1,0:T(8,128)(2,1)S(1)}, bf16[1,128,256]{2,1,0:T(8,128)(2,1)S(1)}, u32[]{:S(2)}, u32[]{:S(2)}) collective-permute-start(bf16[1,128,256]{2,1,0:T(8,128)(2,1)S(1)} %get-tuple-element.42), channel_id=1, source_target_pairs={{0,24},{4,28},{8,0},{12,4},{16,8},{20,12},{24,16},{28,20},{32,56},... | collective-permute-start | bytes 196616 | tf_op jit(solution)/shard_map/ppermute | solution.py:31
  11.2 5.8 %collective-permute-start.5 = (bf16[1,128,256]{2,1,0:T(8,128)(2,1)S(1)}, bf16[1,128,256]{2,1,0:T(8,128)(2,1)S(1)}, u32[]{:S(2)}, u32[]{:S(2)}) collective-permute-start(bf16[1,128,256]{2,1,0:T(8,128)(2,1)S(1)} %get-tuple-element.42), channel_id=1, source_target_pairs={{0,16},{4,20},{8,24},{12,28},{16,0},{20,4},{24,8},{28,12},{32,48},... | collective-permute-start | bytes 196616 | tf_op jit(solution)/shard_map/ppermute | solution.py:31
  13.7 5.4 %collective-permute-start.8 = (bf16[1,128,256]{2,1,0:T(8,128)(2,1)S(1)}, bf16[1,128,256]{2,1,0:T(8,128)(2,1)S(1)}, u32[]{:S(2)}, u32[]{:S(2)}) collective-permute-start(bf16[1,128,256]{2,1,0:T(8,128)(2,1)S(1)} %get-tuple-element.26), channel_id=1, source_target_pairs={{0,32},{4,36},{8,40},{12,44},{16,48},{20,52},{24,56},{28,60},{32,6... | collective-permute-start | bytes 196616 | tf_op jit(solution)/shard_map/ppermute | solution.py:31
  13.8 6.7 %collective-permute-start.12 = (bf16[1,128,256]{2,1,0:T(8,128)(2,1)S(1)}, bf16[1,128,256]{2,1,0:T(8,128)(2,1)S(1)}, u32[]{:S(2)}, u32[]{:S(2)}) collective-permute-start(bf16[1,128,256]{2,1,0:T(8,128)(2,1)S(1)} %get-tuple-element.26), channel_id=1, source_target_pairs={{0,224},{4,228},{8,232},{12,236},{16,240},{20,244},{24,248},{28,25... | collective-permute-start | bytes 196616 | tf_op jit(solution)/shard_map/ppermute | solution.py:31
  17.0 20.7 %collective-permute-start.6 = (bf16[4,128,256]{2,1,0:T(8,128)(2,1)S(1)}, bf16[4,128,256]{2,1,0:T(8,128)(2,1)S(1)}, u32[]{:S(2)}, u32[]{:S(2)}) collective-permute-start(bf16[4,128,256]{2,1,0:T(8,128)(2,1)S(1)} %pad_maximum_fusion.3.rest_0_), channel_id=1, source_target_pairs={{0,32},{4,36},{8,40},{12,44},{16,48},{20,52},{24,56},{28,60},{32,6... | collective-permute-start | bytes 786440 | tf_op jit(solution)/shard_map/ppermute | solution.py:31
  17.3 24.1 %collective-permute-start.7 = (bf16[4,128,256]{2,1,0:T(8,128)(2,1)S(1)}, bf16[4,128,256]{2,1,0:T(8,128)(2,1)S(1)}, u32[]{:S(2)}, u32[]{:S(2)}) collective-permute-start(bf16[4,128,256]{2,1,0:T(8,128)(2,1)S(1)} %pad_maximum_fusion.3.rest_0_), channel_id=1, source_target_pairs={{0,224},{4,228},{8,232},{12,236},{16,240},{20,244},{24,248},{28,25... | collective-permute-start | bytes 786440 | tf_op jit(solution)/shard_map/ppermute | solution.py:31
  19.2 5.9 %collective-permute-start.9 = (bf16[1,128,256]{2,1,0:T(8,128)(2,1)S(1)}, bf16[1,128,256]{2,1,0:T(8,128)(2,1)S(1)}, u32[]{:S(2)}, u32[]{:S(2)}) collective-permute-start(bf16[1,128,256]{2,1,0:T(8,128)(2,1)S(1)} %collective-permute-done.8), channel_id=1, source_target_pairs={{0,32},{4,36},{8,40},{12,44},{16,48},{20,52},{24,56},{28,60},{32,6... | collective-permute-start | bytes 196616 | tf_op jit(solution)/shard_map/ppermute | solution.py:31
  20.5 6.5 %collective-permute-start.13 = (bf16[1,128,256]{2,1,0:T(8,128)(2,1)S(1)}, bf16[1,128,256]{2,1,0:T(8,128)(2,1)S(1)}, u32[]{:S(2)}, u32[]{:S(2)}) collective-permute-start(bf16[1,128,256]{2,1,0:T(8,128)(2,1)S(1)} %collective-permute-done.12), channel_id=1, source_target_pairs={{0,224},{4,228},{8,232},{12,236},{16,240},{20,244},{24,248},{28,25... | collective-permute-start | bytes 196616 | tf_op jit(solution)/shard_map/ppermute | solution.py:31
  25.1 4.9 %collective-permute-start.10 = (bf16[1,128,256]{2,1,0:T(8,128)(2,1)S(1)}, bf16[1,128,256]{2,1,0:T(8,128)(2,1)S(1)}, u32[]{:S(2)}, u32[]{:S(2)}) collective-permute-start(bf16[1,128,256]{2,1,0:T(8,128)(2,1)S(1)} %collective-permute-done.9), channel_id=1, source_target_pairs={{0,32},{4,36},{8,40},{12,44},{16,48},{20,52},{24,56},{28,60},{32,6... | collective-permute-start | bytes 196616 | tf_op jit(solution)/shard_map/ppermute | solution.py:31
  27.0 7.4 %collective-permute-start.14 = (bf16[1,128,256]{2,1,0:T(8,128)(2,1)S(1)}, bf16[1,128,256]{2,1,0:T(8,128)(2,1)S(1)}, u32[]{:S(2)}, u32[]{:S(2)}) collective-permute-start(bf16[1,128,256]{2,1,0:T(8,128)(2,1)S(1)} %collective-permute-done.13), channel_id=1, source_target_pairs={{0,224},{4,228},{8,232},{12,236},{16,240},{20,244},{24,248},{28,25... | collective-permute-start | bytes 196616 | tf_op jit(solution)/shard_map/ppermute | solution.py:31
  30.0 4.4 %collective-permute-start.11 = (bf16[1,128,256]{2,1,0:T(8,128)(2,1)S(1)}, bf16[1,128,256]{2,1,0:T(8,128)(2,1)S(1)}, u32[]{:S(2)}, u32[]{:S(2)}) collective-permute-start(bf16[1,128,256]{2,1,0:T(8,128)(2,1)S(1)} %collective-permute-done.10), channel_id=1, source_target_pairs={{0,32},{4,36},{8,40},{12,44},{16,48},{20,52},{24,56},{28,60},{32,6... | collective-permute-start | bytes 196616 | tf_op jit(solution)/shard_map/ppermute | solution.py:31
  34.4 16.8 %collective-permute-start.19 = (bf16[8,128,256]{2,1,0:T(8,128)(2,1)S(1)}, bf16[8,128,256]{2,1,0:T(8,128)(2,1)S(1)}, u32[]{:S(2)}, u32[]{:S(2)}) collective-permute-start(bf16[8,128,256]{2,1,0:T(8,128)(2,1)S(1)} %constant_dynamic-update-slice_fusion.rest_3_), channel_id=1, source_target_pairs={{0,8},{4,12},{8,16},{12,20},{16,24},{20,28},{24,0},{28,4},{32,40},... | collective-permute-start | bytes 1572872 | tf_op jit(solution)/shard_map/ppermute | solution.py:31
  35.1 16.3 %collective-permute-start.20 = (bf16[8,128,256]{2,1,0:T(8,128)(2,1)S(1)}, bf16[8,128,256]{2,1,0:T(8,128)(2,1)S(1)}, u32[]{:S(2)}, u32[]{:S(2)}) collective-permute-start(bf16[8,128,256]{2,1,0:T(8,128)(2,1)S(1)} %constant_dynamic-update-slice_fusion.rest_3_), channel_id=1, source_target_pairs={{0,24},{4,28},{8,0},{12,4},{16,8},{20,12},{24,16},{28,20},{32,56},... | collective-permute-start | bytes 1572872 | tf_op jit(solution)/shard_map/ppermute | solution.py:31
  37.7 9.4 %collective-permute-start.15 = (bf16[4,128,256]{2,1,0:T(8,128)(2,1)S(1)}, bf16[4,128,256]{2,1,0:T(8,128)(2,1)S(1)}, u32[]{:S(2)}, u32[]{:S(2)}) collective-permute-start(bf16[4,128,256]{2,1,0:T(8,128)(2,1)S(1)} %collective-permute-done.6.rest_1_), channel_id=1, source_target_pairs={{0,32},{4,36},{8,40},{12,44},{16,48},{20,52},{24,56},{28,60},{32,6... | collective-permute-start | bytes 786440 | tf_op jit(solution)/shard_map/ppermute | solution.py:31
  41.3 9.9 %collective-permute-start.16 = (bf16[4,128,256]{2,1,0:T(8,128)(2,1)S(1)}, bf16[4,128,256]{2,1,0:T(8,128)(2,1)S(1)}, u32[]{:S(2)}, u32[]{:S(2)}) collective-permute-start(bf16[4,128,256]{2,1,0:T(8,128)(2,1)S(1)} %collective-permute-done.7.rest_2_), channel_id=1, source_target_pairs={{0,224},{4,228},{8,232},{12,236},{16,240},{20,244},{24,248},{28,25... | collective-permute-start | bytes 786440 | tf_op jit(solution)/shard_map/ppermute | solution.py:31
  41.8 13.0 %collective-permute-start.2 = (bf16[128,256]{1,0:T(8,128)(2,1)S(1)}, bf16[128,256]{1,0:T(8,128)(2,1)S(1)}, u32[]{:S(2)}, u32[]{:S(2)}) collective-permute-start(bf16[128,256]{1,0:T(8,128)(2,1)S(1)} %get-tuple-element.43), channel_id=1, source_target_pairs={{0,8},{4,12},{8,16},{12,20},{16,24},{20,28},{24,32},{28,36},{32,40... | collective-permute-start | bytes 196616 | tf_op jit(solution)/shard_map/ppermute | solution.py:284
  47.1 10.6 %collective-permute-start.17 = (bf16[4,128,256]{2,1,0:T(8,128)(2,1)S(1)}, bf16[4,128,256]{2,1,0:T(8,128)(2,1)S(1)}, u32[]{:S(2)}, u32[]{:S(2)}) collective-permute-start(bf16[4,128,256]{2,1,0:T(8,128)(2,1)S(1)} %collective-permute-done.15.rest_0_), channel_id=1, source_target_pairs={{0,32},{4,36},{8,40},{12,44},{16,48},{20,52},{24,56},{28,60},{32,6... | collective-permute-start | bytes 786440 | tf_op jit(solution)/shard_map/ppermute | solution.py:31
  51.2 9.9 %collective-permute-start.18 = (bf16[4,128,256]{2,1,0:T(8,128)(2,1)S(1)}, bf16[4,128,256]{2,1,0:T(8,128)(2,1)S(1)}, u32[]{:S(2)}, u32[]{:S(2)}) collective-permute-start(bf16[4,128,256]{2,1,0:T(8,128)(2,1)S(1)} %collective-permute-done.16.rest_1_), channel_id=1, source_target_pairs={{0,224},{4,228},{8,232},{12,236},{16,240},{20,244},{24,248},{28,25... | collective-permute-start | bytes 786440 | tf_op jit(solution)/shard_map/ppermute | solution.py:31
  51.3 25.6 %collective-permute-start.23 = (bf16[4,128,256]{2,1,0:T(8,128)(2,1)S(1)}, bf16[4,128,256]{2,1,0:T(8,128)(2,1)S(1)}, u32[]{:S(2)}, u32[]{:S(2)}) collective-permute-start(bf16[4,128,256]{2,1,0:T(8,128)(2,1)S(1)} %slice.158), channel_id=1, source_target_pairs={{0,8},{4,12},{8,16},{12,20},{16,24},{20,28},{24,0},{28,4},{32,40},... | collective-permute-start | bytes 786440 | tf_op jit(solution)/shard_map/ppermute | solution.py:31
  51.4 25.5 %collective-permute-start.24 = (bf16[4,128,256]{2,1,0:T(8,128)(2,1)S(1)}, bf16[4,128,256]{2,1,0:T(8,128)(2,1)S(1)}, u32[]{:S(2)}, u32[]{:S(2)}) collective-permute-start(bf16[4,128,256]{2,1,0:T(8,128)(2,1)S(1)} %slice.159), channel_id=1, source_target_pairs={{0,24},{4,28},{8,0},{12,4},{16,8},{20,12},{24,16},{28,20},{32,56},... | collective-permute-start | bytes 786440 | tf_op jit(solution)/shard_map/ppermute | solution.py:31
  57.8 19.1 %collective-permute-start.21 = (bf16[2,128,256]{2,1,0:T(8,128)(2,1)S(1)}, bf16[2,128,256]{2,1,0:T(8,128)(2,1)S(1)}, u32[]{:S(2)}, u32[]{:S(2)}) collective-permute-start(bf16[2,128,256]{2,1,0:T(8,128)(2,1)S(1)} %slice.156), channel_id=1, source_target_pairs={{0,32},{4,36},{8,40},{12,44},{16,48},{20,52},{24,56},{28,60},{32,6... | collective-permute-start | bytes 393224 | tf_op jit(solution)/shard_map/ppermute | solution.py:31
  61.1 15.8 %collective-permute-start.22 = (bf16[2,128,256]{2,1,0:T(8,128)(2,1)S(1)}, bf16[2,128,256]{2,1,0:T(8,128)(2,1)S(1)}, u32[]{:S(2)}, u32[]{:S(2)}) collective-permute-start(bf16[2,128,256]{2,1,0:T(8,128)(2,1)S(1)} %slice.157), channel_id=1, source_target_pairs={{0,224},{4,228},{8,232},{12,236},{16,240},{20,244},{24,248},{28,25... | collective-permute-start | bytes 393224 | tf_op jit(solution)/shard_map/ppermute | solution.py:31
  81.7 1.8 %collective-permute-start.25 = (bf16[256,512]{1,0:T(8,128)(2,1)S(1)}, bf16[256,512]{1,0:T(8,128)(2,1)S(1)}, u32[]{:S(2)}, u32[]{:S(2)}) collective-permute-start(bf16[256,512]{1,0:T(8,128)(2,1)S(1)} %get-tuple-element.35), channel_id=1, source_target_pairs={{0,4},{4,0},{8,12},{12,8},{16,20},{20,16},{24,28},{28,24},{32,36},... | collective-permute-start | bytes 786440 | tf_op jit(solution)/shard_map/ppermute | solution.py:31
  89.3 2.0 %copy-start = (f32[256,4096]{1,0:T(8,128)}, f32[256,4096]{1,0:T(8,128)S(1)}, u32[]{:S(2)}) copy-start(f32[256,4096]{1,0:T(8,128)S(1)} %fusion.2) | copy-start | bytes 12582916
  91.4 8.4 %collective-permute-start.26 = (bf16[256,512]{1,0:T(8,128)(2,1)S(1)}, bf16[256,512]{1,0:T(8,128)(2,1)S(1)}, u32[]{:S(2)}, u32[]{:S(2)}) collective-permute-start(bf16[256,512]{1,0:T(8,128)(2,1)S(1)} %get-tuple-element.32), channel_id=1, source_target_pairs={{0,1},{1,2},{2,3},{3,0},{4,5},{5,6},{6,7},{7,4},{8,9},{9,10},{10,1... | collective-permute-start | bytes 786440 | tf_op jit(solution)/shard_map/ppermute | solution.py:35
  91.7 9.4 %collective-permute-start.28 = (bf16[256,512]{1,0:T(8,128)(2,1)S(1)}, bf16[256,512]{1,0:T(8,128)(2,1)S(1)}, u32[]{:S(2)}, u32[]{:S(2)}) collective-permute-start(bf16[256,512]{1,0:T(8,128)(2,1)S(1)} %get-tuple-element.33), channel_id=1, source_target_pairs={{0,3},{1,0},{2,1},{3,2},{4,7},{5,4},{6,5},{7,6},{8,11},{9,8},{10,9... | collective-permute-start | bytes 786440 | tf_op jit(solution)/shard_map/ppermute | solution.py:35
  102.6 13.0 %collective-permute-start.27 = (bf16[256,1024]{1,0:T(8,128)(2,1)S(1)}, bf16[256,1024]{1,0:T(8,128)(2,1)S(1)}, u32[]{:S(2)}, u32[]{:S(2)}) collective-permute-start(bf16[256,1024]{1,0:T(8,128)(2,1)S(1)} %pad_maximum_fusion.1), channel_id=1, source_target_pairs={{0,1},{1,2},{2,3},{3,0},{4,5},{5,6},{6,7},{7,4},{8,9},{9,10},{10,1... | collective-permute-start | bytes 1572872 | tf_op jit(solution)/shard_map/ppermute | solution.py:35
  103.0 14.1 %collective-permute-start.29 = (bf16[256,1024]{1,0:T(8,128)(2,1)S(1)}, bf16[256,1024]{1,0:T(8,128)(2,1)S(1)}, u32[]{:S(2)}, u32[]{:S(2)}) collective-permute-start(bf16[256,1024]{1,0:T(8,128)(2,1)S(1)} %pad_maximum_fusion.2), channel_id=1, source_target_pairs={{0,3},{1,0},{2,1},{3,2},{4,7},{5,4},{6,5},{7,6},{8,11},{9,8},{10,9... | collective-permute-start | bytes 1572872 | tf_op jit(solution)/shard_map/ppermute | solution.py:35

commit v2 on v0

v2 whole, which is shorter than its diff:
```python
import functools
import math

import jax
import jax.numpy as jnp
import numpy as np
from jax import lax
from jax.experimental import pallas as pl
from jax.experimental.pallas import tpu as pltpu
from jax.sharding import PartitionSpec as P

HD = 128
BLK = 128
GROUP = 4
PICKS = 16
NX, NZ = 4, 8
NEG = -1e30
C2 = math.log2(math.e) / math.sqrt(HD)
LIMIT = 100.0
VMEM_BYTES = 40 * 1024 * 1024
SLOT_BITS = 6
BF16, F32, I32 = jnp.bfloat16, jnp.float32, jnp.int32

AX = (0, 3, 1, 2)


def slot_table():
    table = np.zeros((2, NZ, NX), np.int32)

    def put(group, base, same, z, x, at):
        table[same, z % NZ, x % NX] = (group << SLOT_BITS) | (base + at)

    for i, dx in enumerate(AX):
        put(0, 0, 1, 0, dx, i)
        put(0, 4, 1, -1, dx, i)
        put(0, 8, 1, 1, dx, i)
        put(1, 0, 1, -2, dx, i)
        put(1, 4, 1, 2, dx, i)
        put(2, 0, 1, -3, dx, i)
        put(2, 4, 1, 3, dx, i)
        put(2, 8, 1, 4, dx, i)
    for z in range(NZ):
        put(0, 12, 0, z, 0, z)
        put(1, 8, 0, z, -1, z)
        put(1, 16, 0, z, 1, z)
        put(2, 12, 0, z, 2, z)
    return table.reshape(-1)


def seq_at(z, x, core):
    return (z * NX + x) * 2 + core


def along_x(value, dx):
    pairs = [
        (seq_at(z, x, c), seq_at(z, (x + dx) % NX, c))
        for z in range(NZ)
        for x in range(NX)
        for c in range(2)
    ]
    return lax.ppermute(value, "seq", pairs)


def up(value, hop):
    pairs = [
        (seq_at(z, x, c), seq_at(z + 1, x, c))
        for z in range(hop - 1, NZ - 1)
        for x in range(NX)
        for c in range(2)
    ]
    return lax.ppermute(value, "seq", pairs)


def down(value, hop):
    pairs = []
    for source in range(4):
        z = (source - (hop - 1)) % NZ
        pairs += [(z, (z - 1) % NZ)]
    pairs = [
        (seq_at(a, x, c), seq_at(b, x, c)) for a, b in pairs for x in range(NX) for c in range(2)
    ]
    return lax.ppermute(value, "seq", pairs)


def swap_cores(value):
    return lax.ppermute(value, "seq", [(i, i ^ 1) for i in range(2 * NX * NZ)])


def tp_shift(value, step):
    return lax.ppermute(value, "tp", [(i, (i + step) % 4) for i in range(4)])


def dot_f32(a, b, dims):
    return lax.dot_general(a, b, (dims, ((), ())), preferred_element_type=F32)


def lanes(core, width=HD):
    return pl.ds(pl.multiple_of(core * width, width), width)


def chosen_half(blocks, core, shard):
    def look(n, found):
        h = n // PICKS
        hit = blocks[core * GROUP + h, n - h * PICKS] == 2 * shard + 1
        return found | hit.astype(I32)

    return lax.fori_loop(0, GROUP * PICKS, look, 0)


def pick_kernel(of_sibling, scal, blocks, k_ref, v_ref, *outs):
    core, place = scal[0], scal[1]
    shard = place + 1 - 2 * core if of_sibling else place
    half = chosen_half(blocks, core, shard)
    rows = pl.ds(pl.multiple_of(half * BLK, BLK), BLK)
    outs[0][0, :, :HD] = k_ref[rows, lanes(core)]
    outs[0][0, :, HD:] = v_ref[rows, lanes(core)]


def tail_kernel(scal, k_ref, v_ref, k_sib, v_sib, out_ref):
    core = scal[0]

    @pl.when(core == 1)
    def _():
        out_ref[:, :HD] = k_ref[BLK:, HD:]
        out_ref[:, HD:] = v_ref[BLK:, HD:]

    @pl.when(core == 0)
    def _():
        out_ref[:, :HD] = k_sib[BLK:, :HD]
        out_ref[:, HD:] = v_sib[BLK:, :HD]


def split3(m):
    a = m.astype(BF16)
    rest = m - a.astype(F32)
    b = rest.astype(BF16)
    c = (rest - b.astype(F32)).astype(BF16)
    return a, b, c


def extra_columns(m):
    rows = m.shape[0]
    lane = lax.broadcasted_iota(I32, (rows, HD), 1)
    a, b, c = (jnp.broadcast_to(-part.astype(F32), (rows, HD)) for part in split3(m))
    wide = jnp.where(lane == 0, a, jnp.where(lane == 1, b, jnp.where(lane == 2, c, 0.0)))
    return jnp.where(lane == 3, 1.0, wide).astype(BF16)


def local_kernel(
    scal, blocks, win, slash, table, q, q_sib, k, k_sib, v, v_sib, halo,
    qa_ref, acc_ref, list_ref, count_ref, qs, ks, vs, named,
):
    core, place = scal[0], scal[1]
    chip = place // 2
    z, x = chip // NX, chip % NX

    for g in range(16):
        count_ref[g] = 0
    for n in range(GROUP * 8):
        named[n] = 0

    def note(n, carry):
        h = n // PICKS
        b = blocks[core * GROUP + h, n - h * PICKS]
        shard = b // 2
        same = jnp.where(shard % 2 == core, 1, 0)
        from_z = shard // (2 * NX)
        from_x = (shard // 2) % NX
        at_z = jnp.where(same == 1, (from_z - z + NZ) % NZ, from_z)
        entry = table[(same * NZ + at_z) * NX + (from_x - x + NX) % NX]
        group = entry // (1 << SLOT_BITS)
        key = group * GROUP + h
        count = count_ref[key]
        list_ref[key * PICKS + count] = entry - group * (1 << SLOT_BITS)
        count_ref[key] = count + jnp.where(b <= 4 * chip - 2, 1, 0)
        near = b - (4 * chip - 1)
        inside = (near >= 0) & (near < 5)
        at = h * 8 + jnp.where(inside, near, 7)
        named[at] = 1
        return carry

    lax.fori_loop(0, GROUP * PICKS, note, 0)

    mine, sib = core * 2 * BLK, (1 - core) * 2 * BLK
    ks[:BLK] = halo[:, :HD]
    vs[:BLK] = halo[:, HD:]
    for ref, own, other in ((ks, k, k_sib), (vs, v, v_sib)):
        ref[pl.ds(pl.multiple_of(BLK + mine, BLK), 2 * BLK)] = own[:, lanes(core)]
        ref[pl.ds(pl.multiple_of(BLK + sib, BLK), 2 * BLK)] = other[:, lanes(core)]
    for h in range(GROUP):
        cols = pl.ds(pl.multiple_of(core * GROUP * HD + h * HD, HD), HD)
        qs[h, pl.ds(pl.multiple_of(mine, BLK), 2 * BLK)] = q[:, cols]
        qs[h, pl.ds(pl.multiple_of(sib, BLK), 2 * BLK)] = q_sib[:, cols]

    qi = lax.broadcasted_iota(I32, (BLK, BLK), 0)
    kj = lax.broadcasted_iota(I32, (BLK, BLK), 1)
    diag_gap = qi - kj
    prev_gap = diag_gap + BLK
    for h in range(GROUP):
        head = core * GROUP + h
        diag_ok = diag_gap < win[head]
        prev_ok = prev_gap < win[head]
        for n in range(8):
            diag_ok = diag_ok | (diag_gap == slash[head, n])
            prev_ok = prev_ok | (prev_gap == slash[head, n])
        for i in range(4):
            span = (i + 2) * BLK
            rows = slice(i * BLK, (i + 1) * BLK)
            s = dot_f32(qs[h, rows, :], ks[:span], ((1,), (1,)))
            tiles = []
            for t in range(i + 2):
                is_named = named[h * 8 + t] > 0
                if t == i + 1:
                    ok = (diag_gap >= 0) & (diag_ok | is_named)
                elif t == i:
                    ok = prev_ok | is_named
                    if t == 0:
                        ok = ok & (chip > 0)
                else:
                    ok = jnp.broadcast_to(is_named, (BLK, BLK))
                    if t == 0:
                        ok = ok & (chip > 0)
                tiles.append(jnp.where(ok, s[:, t * BLK : (t + 1) * BLK], NEG))
            s = jnp.concatenate(tiles, axis=1)
            m = jnp.max(s, axis=1, keepdims=True)
            w = jnp.exp2((s - m) * C2)
            total = jnp.sum(w, axis=1, keepdims=True)
            acc_ref[h, rows, :HD] = dot_f32(w.astype(BF16), vs[:span], ((1,), (0,)))
            acc_ref[h, rows, HD:] = jnp.broadcast_to(total, (BLK, HD))
            qa_ref[h, rows, :HD] = qs[h, rows, :]
            qa_ref[h, rows, HD:] = extra_columns(m)


def far_kernel(group, sizes, final, scal, lists, counts, qa_in, acc_in, *rest):
    pieces = rest[: len(sizes)]
    if final:
        mine_ref, other_ref, qa_ref, acc_ref, kv, aug, sem = rest[len(sizes) :]
    else:
        qa_ref, acc_ref, kv, aug, sem = rest[len(sizes) :]
    copies = []
    spare = 0
    for n, (piece, size) in enumerate(zip(pieces, sizes)):
        copies.append(pltpu.make_async_copy(piece, kv.at[pl.ds(spare, size)], sem.at[n]))
        spare += size
    for copy in copies:
        copy.start()
    kv[spare] = jnp.zeros((BLK, 2 * HD), BF16)
    lane = lax.broadcasted_iota(I32, (BLK, HD), 1)
    aug[0] = jnp.where(lane < 3, 1.0, jnp.where(lane == 3, NEG, 0.0)).astype(BF16)
    aug[1] = jnp.where(lane < 3, 1.0, 0.0).astype(BF16)
    qa_ref[...] = qa_in[...]
    acc_ref[...] = acc_in[...]
    for copy in copies:
        copy.wait()

    def pair(h, j):
        base = (group * GROUP + h) * PICKS
        count = counts[group * GROUP + h]
        real = jnp.where(2 * j + 1 < count, 1, 0)
        one = lists[base + 2 * j]
        two = jnp.where(real == 1, lists[base + 2 * j + real], spare)
        keys = jnp.concatenate([kv[one, :, :HD], kv[two, :, :HD]], axis=0)
        more = jnp.concatenate([aug[1], aug[real]], axis=0)
        return one, two, dot_f32(qa_ref[h], jnp.concatenate([keys, more], axis=1), ((1,), (1,)))

    def pairs_of(h):
        return (counts[group * GROUP + h] + 1) // 2

    ones = jnp.ones((2 * BLK, HD), BF16)

    def accumulate():
        def head(h, high):
            def step(j, high):
                one, two, s = pair(h, j)
                s = s * C2
                values = jnp.concatenate([kv[one, :, HD:], kv[two, :, HD:]], axis=0)
                acc_ref[h] += dot_f32(
                    jnp.exp2(s).astype(BF16), jnp.concatenate([values, ones], axis=1), ((1,), (0,))
                )
                return jnp.maximum(high, jnp.max(s.reshape(-1, 8, 2 * BLK), axis=0))

            return lax.fori_loop(0, pairs_of(h), step, high)

        return jnp.max(lax.fori_loop(0, GROUP, head, jnp.zeros((8, 2 * BLK), F32)))

    highest = accumulate()

    @pl.when(highest > LIMIT)
    def _():
        def raise_head(h, carry):
            def step(j, gain):
                return jnp.maximum(gain, jnp.max(pair(h, j)[2], axis=1, keepdims=True))

            rows = qa_ref.shape[1]
            gain = lax.fori_loop(0, pairs_of(h), step, jnp.zeros((rows, 1), F32))
            parts = qa_ref[h, :, HD:].astype(F32)
            old = -(parts[:, 0:1] + parts[:, 1:2] + parts[:, 2:3])
            new = old + gain
            qa_ref[h, :, HD:] = extra_columns(new)
            acc_ref[h] = acc_in[h] * jnp.exp2((old - new) * C2)
            return carry

        lax.fori_loop(0, GROUP, raise_head, 0)
        accumulate()

    if final:
        core = scal[0]
        for out, first in ((mine_ref, core * 2 * BLK), (other_ref, (1 - core) * 2 * BLK)):
            rows = pl.ds(pl.multiple_of(first, BLK), 2 * BLK)
            for h in range(GROUP):
                both = acc_ref[h, rows, :]
                out[:, h * HD : (h + 1) * HD] = (both[:, :HD] / both[:, HD:]).astype(BF16)


def weight_tiles(scal, w_ref, w_buf, sem, sibling, rel_tiles):
    core, me = scal[0], scal[2]
    rows, cols = w_buf.shape[1:]
    first = jnp.where(core == (1 if sibling else 0), 0, rows)
    copies = []
    for n, tile in enumerate(rel_tiles):
        step = (2, 1, 3, 0)[tile // 2]
        col = ((me + step) % 4) * (2 * cols) + (tile % 2) * cols
        copies.append(
            pltpu.make_async_copy(
                w_ref.at[pl.ds(pl.multiple_of(first, rows), rows), pl.ds(pl.multiple_of(col, cols), cols)],
                w_buf.at[n],
                sem.at[n],
            )
        )
    for copy in copies:
        copy.start()
    return copies


def own_part_kernel(scal, ctx, w_ref, opp_ref, rest_ref, w_buf, sem):
    copies = weight_tiles(scal, w_ref, w_buf, sem, False, range(8))
    for n, copy in enumerate(copies):
        copy.wait()
        out = opp_ref.at[n] if n < 2 else rest_ref.at[n - 2]
        out[...] = dot_f32(ctx[...], w_buf[n], ((1,), (0,)))


def sib_part_kernel(tiles, scal, ctx, part, w_ref, *rest):
    outs, (w_buf, sem) = rest[: len(tiles)], rest[len(tiles) :]
    copies = weight_tiles(scal, w_ref, w_buf, sem, True, tiles)
    for n, copy in enumerate(copies):
        copy.wait()
        outs[n][...] = (part[n] + dot_f32(ctx[...], w_buf[n], ((1,), (0,)))).astype(outs[n].dtype)


def spec(space):
    return pl.BlockSpec(memory_space=space)


def call(kernel, name, outs, args, spaces, scratch=(), out_spaces=None, flops=0, moved=0):
    return pl.pallas_call(
        kernel,
        out_shape=outs,
        in_specs=[spec(s) for s in spaces],
        out_specs=[spec(s) for s in (out_spaces or [pltpu.VMEM] * len(outs))],
        scratch_shapes=list(scratch),
        compiler_params=pltpu.CompilerParams(vmem_limit_bytes=VMEM_BYTES),
        cost_estimate=pl.CostEstimate(flops=flops, bytes_accessed=moved, transcendentals=0),
        name=name,
    )(*args)


def shape(dims, dtype):
    return jax.ShapeDtypeStruct(dims, dtype)


def local(queries, key_states, value_states, vert_blocks, window_size, slash_offsets, out_weight):
    smem, vmem, anywhere = pltpu.SMEM, pltpu.VMEM, pl.ANY
    place = lax.axis_index("seq").astype(I32)
    me = lax.axis_index("tp").astype(I32)
    core = place % 2
    scal = jnp.stack([core, place, me])
    block = shape((1, BLK, 2 * HD), BF16)

    k_sib = swap_cores(key_states)
    v_sib = swap_cores(value_states)
    q_sib = swap_cores(queries)

    def pick(of_sibling, k, v):
        return call(
            functools.partial(pick_kernel, of_sibling), "pick", [block],
            (scal, vert_blocks, k, v), [smem, smem, vmem, vmem], moved=1_000_000,
        )[0]

    a0 = pick(False, key_states, value_states)
    a = jnp.concatenate([a0, along_x(a0, 1), along_x(a0, -1), along_x(a0, 2)], axis=0)
    b0 = pick(True, k_sib, v_sib)
    b = lax.all_gather(
        b0,
        "seq",
        axis=0,
        tiled=True,
        axis_index_groups=[
            [seq_at(z, x, c) for z in range(NZ)] for x in range(NX) for c in range(2)
        ],
    )
    up1, down1 = up(a, 1), down(a, 1)
    up2, down2 = up(up1, 2), down(down1, 2)
    up3, down3 = up(up2, 3), down(down2, 3)
    up4, down4 = up(up3[:2], 4), down(down3[2:], 4)
    b_right, b_left = along_x(b, 1), along_x(b, -1)
    b_right2, b_left2 = along_x(b_right[:4], 1), along_x(b_left[4:], -1)

    tail = call(
        tail_kernel, "tail", [shape((BLK, 2 * HD), BF16)],
        (scal, key_states, value_states, k_sib, v_sib), [smem] + [vmem] * 4, moved=1_000_000,
    )[0]
    halo = lax.ppermute(tail, "seq", [(i, i + 2) for i in range(2 * NX * NZ - 2)])

    rows = 2 * queries.shape[0]
    wide = (GROUP, rows, 2 * HD)
    qa, acc, lists, counts = call(
        local_kernel,
        "near_part",
        [shape(wide, BF16), shape(wide, F32), shape((16 * PICKS,), I32), shape((16,), I32)],
        (
            scal, vert_blocks, window_size, slash_offsets, jnp.asarray(slot_table()),
            queries, q_sib, key_states, k_sib, value_states, v_sib, halo,
        ),
        [smem] * 5 + [vmem] * 7,
        [
            pltpu.VMEM((GROUP, rows, HD), BF16),
            pltpu.VMEM((rows + BLK, HD), BF16),
            pltpu.VMEM((rows + BLK, HD), BF16),
            pltpu.SMEM((GROUP * 8,), I32),
        ],
        [vmem, vmem, smem, smem],
        flops=1_000_000_000,
        moved=8_000_000,
    )

    groups = [
        [a, up1, down1, b],
        [up2, down2, b_right, b_left],
        [up3, down3, up4, down4, b_right2, b_left2],
    ]
    for n, pieces in enumerate(groups):
        sizes = [p.shape[0] for p in pieces]
        scratch = [
            pltpu.VMEM((sum(sizes) + 1, BLK, 2 * HD), BF16),
            pltpu.VMEM((2, BLK, HD), BF16),
            pltpu.SemaphoreType.DMA((len(sizes),)),
        ]
        final = n == len(groups) - 1
        outs = [shape(wide, BF16), shape(wide, F32)]
        if final:
            scratch = [pltpu.VMEM(wide, BF16), pltpu.VMEM(wide, F32)] + scratch
            outs = [shape((rows // 2, GROUP * HD), BF16)] * 2
        qa, acc = call(
            functools.partial(far_kernel, n, sizes, final),
            "far_part",
            outs,
            (scal, lists, counts, qa, acc, *pieces),
            [smem] * 3 + [vmem] * 2 + [anywhere] * len(sizes),
            scratch,
            flops=1_500_000_000,
            moved=6_000_000,
        )
    ctx_mine, ctx_other = qa, acc
    ctx_sib = swap_cores(ctx_other)

    half_rows, half = rows // 2, out_weight.shape[1] // 8
    depth = GROUP * HD

    def tiles(count, dtype):
        return shape((count, half_rows, half), dtype)

    def w_scratch(count):
        return [pltpu.VMEM((count, depth, half), BF16), pltpu.SemaphoreType.DMA((count,))]

    opp, rest = call(
        own_part_kernel, "own_part", [tiles(2, F32), tiles(6, F32)],
        (scal, ctx_mine, out_weight), [smem, vmem, anywhere], w_scratch(8),
        flops=1_000_000_000, moved=9_000_000,
    )
    tile_bf, tile_f = shape((half_rows, half), BF16), shape((half_rows, half), F32)
    opp0, opp1 = call(
        functools.partial(sib_part_kernel, (0, 1)), "sib_part", [tile_bf] * 2,
        (scal, ctx_sib, opp, out_weight), [smem, vmem, vmem, anywhere], w_scratch(2),
        flops=300_000_000, moved=3_000_000,
    )
    via_before = tp_shift(opp0, 1)
    via_after = tp_shift(opp1, -1)
    after0, after1, before0, before1, own0, own1 = call(
        functools.partial(sib_part_kernel, (2, 3, 4, 5, 6, 7)), "sib_rest",
        [tile_f, tile_bf, tile_bf, tile_f, tile_f, tile_f],
        (scal, ctx_sib, rest, out_weight), [smem, vmem, vmem, anywhere], w_scratch(6),
        flops=800_000_000, moved=9_000_000,
    )
    direct1 = tp_shift(after1, 1)
    direct0 = tp_shift(before0, -1)
    summed0 = tp_shift((after0 + via_before.astype(F32)).astype(BF16), 1)
    summed1 = tp_shift((before1 + via_after.astype(F32)).astype(BF16), -1)
    return jnp.concatenate(
        [
            own0 + direct0.astype(F32) + summed0.astype(F32),
            own1 + direct1.astype(F32) + summed1.astype(F32),
        ],
        axis=1,
    ).astype(BF16)


def solution(mesh):
    return jax.shard_map(
        local,
        mesh=mesh,
        in_specs=(
            P("seq", "tp"),
            P("seq", "tp"),
            P("seq", "tp"),
            P("tp", None),
            P("tp"),
            P("tp", None),
            P("tp", None),
        ),
        out_specs=P("seq", "tp"),
        check_vma=False,
    )
```

time: 351 us -> 134 us (0.38)
  waiting for transfers between devices: 171 us -> 22.8 us
  local copies, waits for them, and re-layouts: 72.2 us -> 2.59 us
  matrix products: 53.9 us -> 0 us
  starting transfers between devices: 2 us -> 42.9 us
  Pallas kernels: 0 us -> 36.4 us
  other arithmetic: 34.2 us -> 1.35 us
  blocking collectives: 0 us -> 26 us
  between operations: 13.6 us -> 0.44 us
    all_gather x2 -> x0, waiting for transfers between devices: 121 us -> none  [the longest x1 61.2 us: local(): lax.all_gather(value_states, 'seq', axis=0, tiled=True)]
    dot_general x5 -> x0, matrix products: 53.9 us -> none  [the longest x1 20.2 us: attend_context(): jnp.einsum('hsk,hkd->hsd', vert_weights.astype(jnp.bfloat16), vert_values...]
    reduce_scatter x1 -> x0, waiting for transfers between devices: 48.4 us -> none  [local(): lax.psum_scatter(partial_value, 'tp', scatter_dimension=1, tiled=True)]
    reshape x5 -> x0, local copies, waits for them, and re-layouts: 45.8 us -> none  [the longest x2 21.9 us: local(): gathered_keys = gathered_keys.reshape(total_blocks, BLK, kv_heads, head_dim)]
    ppermute x1 -> x26, starting transfers between devices: 1.92 us -> 42.9 us  [the longest x7 11.9 us: along_x(): return lax.ppermute(value, 'seq', pairs)]
    pallas_call x0 -> x10, Pallas kernels: none -> 36.4 us  [call(): pl.pallas_call(kernel, out_shape=outs, in_specs=[spec(s) for s in spaces]...]
    all_gather x0 -> x1, blocking collectives: none -> 26 us  [local(): lax.all_gather(b0, 'seq', axis=0, tiled=True, axis_index_groups=[[seq_at(...]
    reduce_sum x2 -> x0, other arithmetic: 26 us -> none  [attend_context(): denominator = jnp.sum(local_weights, axis=2) + jnp.sum(vert_weights, axis=2)]
  transfers between devices with their start and end apart: 4 -> 26, of which waited for: 3 -> 7; matrix products, arithmetic and copies ran while one was open for 13% -> 0% of each run, Pallas kernels for 0% -> 21%
where the time goes in v2:
time: 134 us; the launch traced here: 133 us
  starting transfers between devices  42.9 us (32%)
  Pallas kernels  36.4 us (27%)
  blocking collectives  26 us (19%)
  waiting for transfers between devices  22.8 us (17%)
  local copies, waits for them, and re-layouts  2.59 us (2%)
  other arithmetic  1.35 us (1%)
    pallas_call x10, Pallas kernels, call(): pl.pallas_call(kernel, out_shape=outs, in_specs=[spec(s) for s in spaces]...  36.4 us
    all_gather x1, blocking collectives, local(): lax.all_gather(b0, 'seq', axis=0, tiled=True, axis_index_groups=[[seq_at(...  26 us
    ppermute x6, waiting for transfers between devices, tp_shift(): return lax.ppermute(value, 'tp', [(i, (i + step) % 4) for i in range(4)])  13.3 us
    ppermute x7, starting transfers between devices, along_x(): return lax.ppermute(value, 'seq', pairs)  11.9 us
    ppermute x4, starting transfers between devices, up(): return lax.ppermute(value, 'seq', pairs)  10.3 us
    ppermute x6, starting transfers between devices, tp_shift(): return lax.ppermute(value, 'tp', [(i, (i + step) % 4) for i in range(4)])  9.57 us
    ppermute x4, starting transfers between devices, down(): return lax.ppermute(value, 'seq', pairs)  8.36 us
    ppermute x4, waiting for transfers between devices, up(): return lax.ppermute(value, 'seq', pairs)  5.99 us
  transfers between devices with their start and end apart: 26, of which 7 were waited for; matrix products, arithmetic and copies ran while one was open for 0% of the time, Pallas kernels for 21%

profile of v2, /device:TPU:192, one launch (start us, length us, event | category | flops | bytes accessed | tf_op | source)
XLA Modules:
  0.0 132.5 jit_solution(12055267279057411522)
XLA Ops:
  2.6 1.7 %pick.2 = bf16[1,128,256]{2,1,0:T(8,128)(2,1)S(1)} custom-call(s32[3]{0:T(128)S(1)} %pad_add_fusion.scal, s32[8,16]{1,0:T(8,128)S(1)} %copy-done.4, bf16[256,256]{1,0:T(8,128)(2,1)S(1)} %copy-done, bf16[256,256]{1,0:T(8,128)(2,1)S(1)} %copy-done.2), custom_call_target="tpu_custom_call" | custom-call | bytes 1000000 | tf_op jit(solution)/shard_map/pick/pallas_call | solution.py:356
  4.3 1.6 %collective-permute-start.4 = (bf16[1,128,256]{2,1,0:T(8,128)(2,1)S(1)}, bf16[1,128,256]{2,1,0:T(8,128)(2,1)S(1)}, u32[]{:S(2)}, u32[]{:S(2)}) collective-permute-start(bf16[1,128,256]{2,1,0:T(8,128)(2,1)S(1)} %pick.2), channel_id=1, source_target_pairs={{0,8},{4,12},{8,16},{12,20},{16,24},{20,28},{24,0},{28,4},{32,40},... | collective-permute-start | bytes 196616 | tf_op jit(solution)/shard_map/ppermute | solution.py:61
  5.8 1.7 %collective-permute-start.5 = (bf16[1,128,256]{2,1,0:T(8,128)(2,1)S(1)}, bf16[1,128,256]{2,1,0:T(8,128)(2,1)S(1)}, u32[]{:S(2)}, u32[]{:S(2)}) collective-permute-start(bf16[1,128,256]{2,1,0:T(8,128)(2,1)S(1)} %pick.2), channel_id=1, source_target_pairs={{0,24},{4,28},{8,0},{12,4},{16,8},{20,12},{24,16},{28,20},{32,56},... | collective-permute-start | bytes 196616 | tf_op jit(solution)/shard_map/ppermute | solution.py:61
  7.6 1.8 %collective-permute-start.6 = (bf16[1,128,256]{2,1,0:T(8,128)(2,1)S(1)}, bf16[1,128,256]{2,1,0:T(8,128)(2,1)S(1)}, u32[]{:S(2)}, u32[]{:S(2)}) collective-permute-start(bf16[1,128,256]{2,1,0:T(8,128)(2,1)S(1)} %pick.2), channel_id=1, source_target_pairs={{0,16},{4,20},{8,24},{12,28},{16,0},{20,4},{24,8},{28,12},{32,48},... | collective-permute-start | bytes 196616 | tf_op jit(solution)/shard_map/ppermute | solution.py:61
  10.5 2.9 %collective-permute-done.6 = bf16[1,128,256]{2,1,0:T(8,128)(2,1)S(1)} collective-permute-done((bf16[1,128,256]{2,1,0:T(8,128)(2,1)S(1)}, bf16[1,128,256]{2,1,0:T(8,128)(2,1)S(1)}, u32[]{:S(2)}, u32[]{:S(2)}) %collective-permute-start.6) | collective-permute-done | bytes 65568 | tf_op jit(solution)/shard_map/ppermute | solution.py:61
  13.4 2.9 %collective-permute-start.7 = (bf16[4,128,256]{2,1,0:T(8,128)(2,1)S(1)}, bf16[4,128,256]{2,1,0:T(8,128)(2,1)S(1)}, u32[]{:S(2)}, u32[]{:S(2)}) collective-permute-start(bf16[4,128,256]{2,1,0:T(8,128)(2,1)S(1)} %pad_maximum_fusion.1.rest_0_), channel_id=1, source_target_pairs={{0,32},{4,36},{8,40},{12,44},{16,48},{20,52},{24,56},{28,60},{32,6... | collective-permute-start | bytes 786440 | tf_op jit(solution)/shard_map/ppermute | solution.py:71
  17.6 2.2 %collective-permute-start.3 = (bf16[128,256]{1,0:T(8,128)(2,1)S(1)}, bf16[128,256]{1,0:T(8,128)(2,1)S(1)}, u32[]{:S(2)}, u32[]{:S(2)}) collective-permute-start(bf16[128,256]{1,0:T(8,128)(2,1)S(1)} %tail.1), channel_id=1, source_target_pairs={{0,8},{4,12},{8,16},{12,20},{16,24},{20,28},{24,32},{28,36},{32,40... | collective-permute-start | bytes 196616 | tf_op jit(solution)/shard_map/ppermute | solution.py:413
  19.8 1.7 %pick.3 = bf16[1,128,256]{2,1,0:T(8,128)(2,1)S(1)} custom-call(s32[3]{0:T(128)S(1)} %pad_add_fusion.scal, s32[8,16]{1,0:T(8,128)S(1)} %copy-done.4, bf16[256,256]{1,0:T(8,128)(2,1)S(1)} %collective-permute-done.1.k_sib.k_ref, bf16[256,256]{1,0:T(8,128)(2,1)S(1)} %collective-permute-done.2.v_sib.v_ref), custom_call_target="tpu_custom_call" | custom-call | bytes 1000000 | tf_op jit(solution)/shard_map/pick/pallas_call | solution.py:356
  21.5 26.0 %all_gather.3.rest_3_ = bf16[8,128,256]{2,1,0:T(8,128)(2,1)S(1)} all-gather(bf16[1,128,256]{2,1,0:T(8,128)(2,1)S(1)} %pick.3), channel_id=1, replica_groups={{0,32,64,96,128,160,192,224},{4,36,68,100,132,164,196,228},{8,40,72,104..., dimensions={0}, use_global_device_ids=true | all-gather | bytes 589824 | tf_op jit(solution)/shard_map/all_gather | solution.py:393
  47.5 1.5 %collective-permute-start.11 = (bf16[8,128,256]{2,1,0:T(8,128)(2,1)S(1)}, bf16[8,128,256]{2,1,0:T(8,128)(2,1)S(1)}, u32[]{:S(2)}, u32[]{:S(2)}) collective-permute-start(bf16[8,128,256]{2,1,0:T(8,128)(2,1)S(1)} %all_gather.3.rest_3_), channel_id=1, source_target_pairs={{0,8},{4,12},{8,16},{12,20},{16,24},{20,28},{24,0},{28,4},{32,40},... | collective-permute-start | bytes 1572872 | tf_op jit(solution)/shard_map/ppermute | solution.py:61
  49.0 1.8 %collective-permute-start.12 = (bf16[8,128,256]{2,1,0:T(8,128)(2,1)S(1)}, bf16[8,128,256]{2,1,0:T(8,128)(2,1)S(1)}, u32[]{:S(2)}, u32[]{:S(2)}) collective-permute-start(bf16[8,128,256]{2,1,0:T(8,128)(2,1)S(1)} %all_gather.3.rest_3_), channel_id=1, source_target_pairs={{0,24},{4,28},{8,0},{12,4},{16,8},{20,12},{24,16},{28,20},{32,56},... | collective-permute-start | bytes 1572872 | tf_op jit(solution)/shard_map/ppermute | solution.py:61
  50.7 2.0 %collective-permute-start.9 = (bf16[4,128,256]{2,1,0:T(8,128)(2,1)S(1)}, bf16[4,128,256]{2,1,0:T(8,128)(2,1)S(1)}, u32[]{:S(2)}, u32[]{:S(2)}) collective-permute-start(bf16[4,128,256]{2,1,0:T(8,128)(2,1)S(1)} %collective-permute-done.7.rest_1_), channel_id=1, source_target_pairs={{32,64},{36,68},{40,72},{44,76},{48,80},{52,84},{56,88},{60,92},{6... | collective-permute-start | bytes 786440 | tf_op jit(solution)/shard_map/ppermute | solution.py:71
  54.1 6.0 %collective-permute-done.9.rest_0_ = bf16[4,128,256]{2,1,0:T(8,128)(2,1)S(1)} collective-permute-done((bf16[4,128,256]{2,1,0:T(8,128)(2,1)S(1)}, bf16[4,128,256]{2,1,0:T(8,128)(2,1)S(1)}, u32[]{:S(2)}, u32[]{:S(2)}) %collective-permute-start.9) | collective-permute-done | bytes 262176 | tf_op jit(solution)/shard_map/ppermute | solution.py:71
  60.1 2.2 %collective-permute-start.13 = (bf16[4,128,256]{2,1,0:T(8,128)(2,1)S(1)}, bf16[4,128,256]{2,1,0:T(8,128)(2,1)S(1)}, u32[]{:S(2)}, u32[]{:S(2)}) collective-permute-start(bf16[4,128,256]{2,1,0:T(8,128)(2,1)S(1)} %collective-permute-done.9.rest_0_), channel_id=1, source_target_pairs={{64,96},{68,100},{72,104},{76,108},{80,112},{84,116},{88,120},{92,... | collective-permute-start | bytes 786440 | tf_op jit(solution)/shard_map/ppermute | solution.py:71
  62.3 3.6 %collective-permute-start.14 = (bf16[4,128,256]{2,1,0:T(8,128)(2,1)S(1)}, bf16[4,128,256]{2,1,0:T(8,128)(2,1)S(1)}, u32[]{:S(2)}, u32[]{:S(2)}) collective-permute-start(bf16[4,128,256]{2,1,0:T(8,128)(2,1)S(1)} %collective-permute-done.10.rest_1_), channel_id=1, source_target_pairs={{192,160},{196,164},{200,168},{204,172},{208,176},{212,180},{216,1... | collective-permute-start | bytes 786440 | tf_op jit(solution)/shard_map/ppermute | solution.py:82
  66.0 9.4 %near_part.1 = (bf16[4,512,256]{2,1,0:T(8,128)(2,1)S(1)}, f32[4,512,256]{2,1,0:T(8,128)S(1)}, s32[256]{0:T(256)S(1)}, s32[16]{0:T(128)S(1)}) custom-call(s32[3]{0:T(128)S(1)} %pad_add_fusion.scal, s32[8,16]{1,0:T(8,128)S(1)} %copy-done.4, s32[8]{0:T(128)S(1)} %copy-done.7, s32[8,8]{1,0:T(8,128)S(1)} %copy-done.6, s32[64]{0:T(128)S(1)} %copy-done.8, ...), custom_call_target="tpu_custom_call" | custom-call | flops 1000000000 | bytes 8000000 | tf_op jit(solution)/shard_map/near_part/pallas_call | solution.py:356
  75.6 3.5 %collective-permute-start.18 = (bf16[4,128,256]{2,1,0:T(8,128)(2,1)S(1)}, bf16[4,128,256]{2,1,0:T(8,128)(2,1)S(1)}, u32[]{:S(2)}, u32[]{:S(2)}) collective-permute-start(bf16[4,128,256]{2,1,0:T(8,128)(2,1)S(1)} %slice.19), channel_id=1, source_target_pairs={{0,24},{4,28},{8,0},{12,4},{16,8},{20,12},{24,16},{28,20},{32,56},... | collective-permute-start | bytes 786440 | tf_op jit(solution)/shard_map/ppermute | solution.py:61
  79.1 3.8 %far_part.3 = (bf16[4,512,256]{2,1,0:T(8,128)(2,1)S(1)}, f32[4,512,256]{2,1,0:T(8,128)S(1)}) custom-call(s32[3]{0:T(128)S(1)} %pad_add_fusion.scal, s32[256]{0:T(256)S(1)} %get-tuple-element.25.lists, s32[16]{0:T(128)S(1)} %get-tuple-element.26.counts, bf16[4,512,256]{2,1,0:T(8,128)(2,1)S(1)} %get-tuple-element.27.qa_in, ...), custom_call_target="tpu_custom_call" | custom-call | flops 1500000000 | bytes 6000000 | tf_op jit(solution)/shard_map/far_part/pallas_call | solution.py:356
  82.9 3.1 %collective-permute-start.15 = (bf16[2,128,256]{2,1,0:T(8,128)(2,1)S(1)}, bf16[2,128,256]{2,1,0:T(8,128)(2,1)S(1)}, u32[]{:S(2)}, u32[]{:S(2)}) collective-permute-start(bf16[2,128,256]{2,1,0:T(8,128)(2,1)S(1)} %slice.16), channel_id=1, source_target_pairs={{96,128},{100,132},{104,136},{108,140},{112,144},{116,148},{120,15... | collective-permute-start | bytes 393224 | tf_op jit(solution)/shard_map/ppermute | solution.py:71
  86.0 2.7 %collective-permute-start.16 = (bf16[2,128,256]{2,1,0:T(8,128)(2,1)S(1)}, bf16[2,128,256]{2,1,0:T(8,128)(2,1)S(1)}, u32[]{:S(2)}, u32[]{:S(2)}) collective-permute-start(bf16[2,128,256]{2,1,0:T(8,128)(2,1)S(1)} %slice.17), channel_id=1, source_target_pairs={{160,128},{164,132},{168,136},{172,140},{176,144},{180,148},{184,1... | collective-permute-start | bytes 393224 | tf_op jit(solution)/shard_map/ppermute | solution.py:82
  88.8 6.0 %far_part.4 = (bf16[4,512,256]{2,1,0:T(8,128)(2,1)S(1)}, f32[4,512,256]{2,1,0:T(8,128)S(1)}) custom-call(s32[3]{0:T(128)S(1)} %pad_add_fusion.scal, s32[256]{0:T(256)S(1)} %get-tuple-element.25.lists, s32[16]{0:T(128)S(1)} %get-tuple-element.26.counts, bf16[4,512,256]{2,1,0:T(8,128)(2,1)S(1)} %get-tuple-element.29.qa_in, ...), custom_call_target="tpu_custom_call" | custom-call | flops 1500000000 | bytes 6000000 | tf_op jit(solution)/shard_map/far_part/pallas_call | solution.py:356
  94.8 5.6 %far_part.5 = (bf16[256,512]{1,0:T(8,128)(2,1)S(1)}, bf16[256,512]{1,0:T(8,128)(2,1)S(1)}) custom-call(s32[3]{0:T(128)S(1)} %pad_add_fusion.scal, s32[256]{0:T(256)S(1)} %get-tuple-element.25.lists, s32[16]{0:T(128)S(1)} %get-tuple-element.26.counts, bf16[4,512,256]{2,1,0:T(8,128)(2,1)S(1)} %get-tuple-element.31.qa_in, ...), custom_call_target="tpu_custom_call" | custom-call | flops 1500000000 | bytes 6000000 | tf_op jit(solution)/shard_map/far_part/pallas_call | solution.py:356
  100.5 3.6 %own_part.1 = (f32[2,256,512]{2,1,0:T(8,128)S(1)}, f32[6,256,512]{2,1,0:T(8,128)S(1)}) custom-call(s32[3]{0:T(128)S(1)} %pad_add_fusion.scal, bf16[256,512]{1,0:T(8,128)(2,1)S(1)} %get-tuple-element.34.ctx, bf16[1024,4096]{1,0:T(8,128)(2,1)S(1)} %bitcast.4), custom_call_target="tpu_custom_call" | custom-call | flops 1000000000 | bytes 9000000 | tf_op jit(solution)/shard_map/own_part/pallas_call | solution.py:356
  105.5 2.1 %collective-permute-start.21 = (bf16[256,512]{1,0:T(8,128)(2,1)S(1)}, bf16[256,512]{1,0:T(8,128)(2,1)S(1)}, u32[]{:S(2)}, u32[]{:S(2)}) collective-permute-start(bf16[256,512]{1,0:T(8,128)(2,1)S(1)} %get-tuple-element.40), channel_id=1, source_target_pairs={{0,1},{1,2},{2,3},{3,0},{4,5},{5,6},{6,7},{7,4},{8,9},{9,10},{10,1... | collective-permute-start | bytes 786440 | tf_op jit(solution)/shard_map/ppermute | solution.py:90
  107.6 2.0 %collective-permute-start.24 = (bf16[256,512]{1,0:T(8,128)(2,1)S(1)}, bf16[256,512]{1,0:T(8,128)(2,1)S(1)}, u32[]{:S(2)}, u32[]{:S(2)}) collective-permute-start(bf16[256,512]{1,0:T(8,128)(2,1)S(1)} %get-tuple-element.44), channel_id=1, source_target_pairs={{0,3},{1,0},{2,1},{3,2},{4,7},{5,4},{6,5},{7,6},{8,11},{9,8},{10,9... | collective-permute-start | bytes 786440 | tf_op jit(solution)/shard_map/ppermute | solution.py:90
  109.6 2.9 %sib_rest.1 = (f32[256,512]{1,0:T(8,128)S(1)}, bf16[256,512]{1,0:T(8,128)(2,1)S(1)}, bf16[256,512]{1,0:T(8,128)(2,1)S(1)}, f32[256,512]{1,0:T(8,128)S(1)}, f32[2...) custom-call(s32[3]{0:T(128)S(1)} %pad_add_fusion.scal, bf16[256,512]{1,0:T(8,128)(2,1)S(1)} %collective-permute-done.19.ctx, ...), custom_call_target="tpu_custom_call" | custom-call | flops 800000000 | bytes 9000000 | tf_op jit(solution)/shard_map/sib_rest/pallas_call | solution.py:356
  112.5 2.0 %collective-permute-start.20 = (bf16[256,512]{1,0:T(8,128)(2,1)S(1)}, bf16[256,512]{1,0:T(8,128)(2,1)S(1)}, u32[]{:S(2)}, u32[]{:S(2)}) collective-permute-start(bf16[256,512]{1,0:T(8,128)(2,1)S(1)} %get-tuple-element.37), channel_id=1, source_target_pairs={{0,3},{1,0},{2,1},{3,2},{4,7},{5,4},{6,5},{7,6},{8,11},{9,8},{10,9... | collective-permute-start | bytes 786440 | tf_op jit(solution)/shard_map/ppermute | solution.py:90
  114.5 2.0 %collective-permute-done.21 = bf16[256,512]{1,0:T(8,128)(2,1)S(1)} collective-permute-done((bf16[256,512]{1,0:T(8,128)(2,1)S(1)}, bf16[256,512]{1,0:T(8,128)(2,1)S(1)}, u32[]{:S(2)}, u32[]{:S(2)}) %collective-permute-start.21) | collective-permute-done | bytes 262176 | tf_op jit(solution)/shard_map/ppermute | solution.py:90
  118.1 2.0 %collective-permute-start.25 = (bf16[256,512]{1,0:T(8,128)(2,1)S(1)}, bf16[256,512]{1,0:T(8,128)(2,1)S(1)}, u32[]{:S(2)}, u32[]{:S(2)}) collective-permute-start(bf16[256,512]{1,0:T(8,128)(2,1)S(1)} %add_convert_fusion.1), channel_id=1, source_target_pairs={{0,3},{1,0},{2,1},{3,2},{4,7},{5,4},{6,5},{7,6},{8,11},{9,8},{10,9... | collective-permute-start | bytes 786440 | tf_op jit(solution)/shard_map/ppermute | solution.py:90
  120.1 2.2 %collective-permute-done.20 = bf16[256,512]{1,0:T(8,128)(2,1)S(1)} collective-permute-done((bf16[256,512]{1,0:T(8,128)(2,1)S(1)}, bf16[256,512]{1,0:T(8,128)(2,1)S(1)}, u32[]{:S(2)}, u32[]{:S(2)}) %collective-permute-start.20) | collective-permute-done | bytes 262176 | tf_op jit(solution)/shard_map/ppermute | solution.py:90
  122.3 4.7 %collective-permute-done.22 = bf16[256,512]{1,0:T(8,128)(2,1)S(1)} collective-permute-done((bf16[256,512]{1,0:T(8,128)(2,1)S(1)}, bf16[256,512]{1,0:T(8,128)(2,1)S(1)}, u32[]{:S(2)}, u32[]{:S(2)}) %collective-permute-start.22) | collective-permute-done | bytes 262176 | tf_op jit(solution)/shard_map/ppermute | solution.py:90
  127.1 4.4 %collective-permute-done.23 = bf16[256,512]{1,0:T(8,128)(2,1)S(1)} collective-permute-done((bf16[256,512]{1,0:T(8,128)(2,1)S(1)}, bf16[256,512]{1,0:T(8,128)(2,1)S(1)}, u32[]{:S(2)}, u32[]{:S(2)}) %collective-permute-start.23) | collective-permute-done | bytes 262176 | tf_op jit(solution)/shard_map/ppermute | solution.py:90
  (65 shorter events, 10.6 us)
Async XLA Ops:
  0.0 66.0 %copy-start.8 = (s32[64]{0:T(128)S(1)}, s32[64]{0:T(128)}, u32[]{:S(2)}) copy-start(s32[64]{0:T(128)} %constant.24.clone.table) | copy-start | bytes 772
  0.0 66.0 %copy-start.7 = (s32[8]{0:T(128)S(1)}, s32[8]{0:T(128)}, u32[]{:S(2)}) copy-start(s32[8]{0:T(128)} %win.1) | copy-start | bytes 100
  0.0 66.0 %copy-start.6 = (s32[8,8]{1,0:T(8,128)S(1)}, s32[8,8]{1,0:T(8,128)}, u32[]{:S(2)}) copy-start(s32[8,8]{1,0:T(8,128)} %slash.1) | copy-start | bytes 772
  2.6 63.4 %copy-start.1 = (bf16[256,256]{1,0:T(8,128)(2,1)S(1)}, bf16[256,256]{1,0:T(8,128)(2,1)}, u32[]{:S(2)}) copy-start(bf16[256,256]{1,0:T(8,128)(2,1)} %k_ref.3) | copy-start | bytes 393220
  2.6 63.4 %copy-start.3 = (bf16[256,256]{1,0:T(8,128)(2,1)S(1)}, bf16[256,256]{1,0:T(8,128)(2,1)}, u32[]{:S(2)}) copy-start(bf16[256,256]{1,0:T(8,128)(2,1)} %v_ref.3) | copy-start | bytes 393220
  2.6 63.4 %copy-start.5 = (bf16[256,1024]{1,0:T(8,128)(2,1)S(1)}, bf16[256,1024]{1,0:T(8,128)(2,1)}, u32[]{:S(2)}) copy-start(bf16[256,1024]{1,0:T(8,128)(2,1)} %q.1) | copy-start | bytes 1572868
  4.3 5.6 %collective-permute-start.4 = (bf16[1,128,256]{2,1,0:T(8,128)(2,1)S(1)}, bf16[1,128,256]{2,1,0:T(8,128)(2,1)S(1)}, u32[]{:S(2)}, u32[]{:S(2)}) collective-permute-start(bf16[1,128,256]{2,1,0:T(8,128)(2,1)S(1)} %pick.2), channel_id=1, source_target_pairs={{0,8},{4,12},{8,16},{12,20},{16,24},{20,28},{24,0},{28,4},{32,40},... | collective-permute-start | bytes 196616 | tf_op jit(solution)/shard_map/ppermute | solution.py:61
  5.8 4.6 %collective-permute-start.5 = (bf16[1,128,256]{2,1,0:T(8,128)(2,1)S(1)}, bf16[1,128,256]{2,1,0:T(8,128)(2,1)S(1)}, u32[]{:S(2)}, u32[]{:S(2)}) collective-permute-start(bf16[1,128,256]{2,1,0:T(8,128)(2,1)S(1)} %pick.2), channel_id=1, source_target_pairs={{0,24},{4,28},{8,0},{12,4},{16,8},{20,12},{24,16},{28,20},{32,56},... | collective-permute-start | bytes 196616 | tf_op jit(solution)/shard_map/ppermute | solution.py:61
  7.6 5.8 %collective-permute-start.6 = (bf16[1,128,256]{2,1,0:T(8,128)(2,1)S(1)}, bf16[1,128,256]{2,1,0:T(8,128)(2,1)S(1)}, u32[]{:S(2)}, u32[]{:S(2)}) collective-permute-start(bf16[1,128,256]{2,1,0:T(8,128)(2,1)S(1)} %pick.2), channel_id=1, source_target_pairs={{0,16},{4,20},{8,24},{12,28},{16,0},{20,4},{24,8},{28,12},{32,48},... | collective-permute-start | bytes 196616 | tf_op jit(solution)/shard_map/ppermute | solution.py:61
  9.4 7.6 %collective-permute-start.1 = (bf16[256,256]{1,0:T(8,128)(2,1)S(1)}, bf16[256,256]{1,0:T(8,128)(2,1)S(1)}, u32[]{:S(2)}, u32[]{:S(2)}) collective-permute-start(bf16[256,256]{1,0:T(8,128)(2,1)S(1)} %copy-done), channel_id=1, source_target_pairs={{0,4},{4,0},{8,12},{12,8},{16,20},{20,16},{24,28},{28,24},{32,36},... | collective-permute-start | bytes 393224 | tf_op jit(solution)/shard_map/ppermute | solution.py:86
  9.4 7.6 %collective-permute-start.2 = (bf16[256,256]{1,0:T(8,128)(2,1)S(1)}, bf16[256,256]{1,0:T(8,128)(2,1)S(1)}, u32[]{:S(2)}, u32[]{:S(2)}) collective-permute-start(bf16[256,256]{1,0:T(8,128)(2,1)S(1)} %copy-done.2), channel_id=1, source_target_pairs={{0,4},{4,0},{8,12},{12,8},{16,20},{20,16},{24,28},{28,24},{32,36},... | collective-permute-start | bytes 393224 | tf_op jit(solution)/shard_map/ppermute | solution.py:86
  9.9 56.0 %collective-permute-start = (bf16[256,1024]{1,0:T(8,128)(2,1)}, bf16[256,1024]{1,0:T(8,128)(2,1)S(1)}, u32[]{:S(2)}, u32[]{:S(2)}) collective-permute-start(bf16[256,1024]{1,0:T(8,128)(2,1)} %q.1), channel_id=1, source_target_pairs={{0,4},{4,0},{8,12},{12,8},{16,20},{20,16},{24,28},{28,24},{32,36},... | collective-permute-start | bytes 1572872 | tf_op jit(solution)/shard_map/ppermute | solution.py:86
  13.4 37.3 %collective-permute-start.7 = (bf16[4,128,256]{2,1,0:T(8,128)(2,1)S(1)}, bf16[4,128,256]{2,1,0:T(8,128)(2,1)S(1)}, u32[]{:S(2)}, u32[]{:S(2)}) collective-permute-start(bf16[4,128,256]{2,1,0:T(8,128)(2,1)S(1)} %pad_maximum_fusion.1.rest_0_), channel_id=1, source_target_pairs={{0,32},{4,36},{8,40},{12,44},{16,48},{20,52},{24,56},{28,60},{32,6... | collective-permute-start | bytes 786440 | tf_op jit(solution)/shard_map/ppermute | solution.py:71
  16.3 36.5 %collective-permute-start.8 = (bf16[4,128,256]{2,1,0:T(8,128)(2,1)S(1)}, bf16[4,128,256]{2,1,0:T(8,128)(2,1)S(1)}, u32[]{:S(2)}, u32[]{:S(2)}) collective-permute-start(bf16[4,128,256]{2,1,0:T(8,128)(2,1)S(1)} %pad_maximum_fusion.1.rest_0_), channel_id=1, source_target_pairs={{0,224},{4,228},{8,232},{12,236},{16,240},{20,244},{24,248},{28,25... | collective-permute-start | bytes 786440 | tf_op jit(solution)/shard_map/ppermute | solution.py:82
  17.6 31.4 %collective-permute-start.3 = (bf16[128,256]{1,0:T(8,128)(2,1)S(1)}, bf16[128,256]{1,0:T(8,128)(2,1)S(1)}, u32[]{:S(2)}, u32[]{:S(2)}) collective-permute-start(bf16[128,256]{1,0:T(8,128)(2,1)S(1)} %tail.1), channel_id=1, source_target_pairs={{0,8},{4,12},{8,16},{12,20},{16,24},{20,28},{24,32},{28,36},{32,40... | collective-permute-start | bytes 196616 | tf_op jit(solution)/shard_map/ppermute | solution.py:413
  47.5 27.9 %collective-permute-start.11 = (bf16[8,128,256]{2,1,0:T(8,128)(2,1)S(1)}, bf16[8,128,256]{2,1,0:T(8,128)(2,1)S(1)}, u32[]{:S(2)}, u32[]{:S(2)}) collective-permute-start(bf16[8,128,256]{2,1,0:T(8,128)(2,1)S(1)} %all_gather.3.rest_3_), channel_id=1, source_target_pairs={{0,8},{4,12},{8,16},{12,20},{16,24},{20,28},{24,0},{28,4},{32,40},... | collective-permute-start | bytes 1572872 | tf_op jit(solution)/shard_map/ppermute | solution.py:61
  49.0 26.6 %collective-permute-start.12 = (bf16[8,128,256]{2,1,0:T(8,128)(2,1)S(1)}, bf16[8,128,256]{2,1,0:T(8,128)(2,1)S(1)}, u32[]{:S(2)}, u32[]{:S(2)}) collective-permute-start(bf16[8,128,256]{2,1,0:T(8,128)(2,1)S(1)} %all_gather.3.rest_3_), channel_id=1, source_target_pairs={{0,24},{4,28},{8,0},{12,4},{16,8},{20,12},{24,16},{28,20},{32,56},... | collective-permute-start | bytes 1572872 | tf_op jit(solution)/shard_map/ppermute | solution.py:61
  50.7 9.4 %collective-permute-start.9 = (bf16[4,128,256]{2,1,0:T(8,128)(2,1)S(1)}, bf16[4,128,256]{2,1,0:T(8,128)(2,1)S(1)}, u32[]{:S(2)}, u32[]{:S(2)}) collective-permute-start(bf16[4,128,256]{2,1,0:T(8,128)(2,1)S(1)} %collective-permute-done.7.rest_1_), channel_id=1, source_target_pairs={{32,64},{36,68},{40,72},{44,76},{48,80},{52,84},{56,88},{60,92},{6... | collective-permute-start | bytes 786440 | tf_op jit(solution)/shard_map/ppermute | solution.py:71
  52.8 9.5 %collective-permute-start.10 = (bf16[4,128,256]{2,1,0:T(8,128)(2,1)S(1)}, bf16[4,128,256]{2,1,0:T(8,128)(2,1)S(1)}, u32[]{:S(2)}, u32[]{:S(2)}) collective-permute-start(bf16[4,128,256]{2,1,0:T(8,128)(2,1)S(1)} %collective-permute-done.8.rest_2_), channel_id=1, source_target_pairs={{224,192},{228,196},{232,200},{236,204},{240,208},{244,212},{248,2... | collective-permute-start | bytes 786440 | tf_op jit(solution)/shard_map/ppermute | solution.py:82
  60.1 22.7 %collective-permute-start.13 = (bf16[4,128,256]{2,1,0:T(8,128)(2,1)S(1)}, bf16[4,128,256]{2,1,0:T(8,128)(2,1)S(1)}, u32[]{:S(2)}, u32[]{:S(2)}) collective-permute-start(bf16[4,128,256]{2,1,0:T(8,128)(2,1)S(1)} %collective-permute-done.9.rest_0_), channel_id=1, source_target_pairs={{64,96},{68,100},{72,104},{76,108},{80,112},{84,116},{88,120},{92,... | collective-permute-start | bytes 786440 | tf_op jit(solution)/shard_map/ppermute | solution.py:71
  62.3 23.7 %collective-permute-start.14 = (bf16[4,128,256]{2,1,0:T(8,128)(2,1)S(1)}, bf16[4,128,256]{2,1,0:T(8,128)(2,1)S(1)}, u32[]{:S(2)}, u32[]{:S(2)}) collective-permute-start(bf16[4,128,256]{2,1,0:T(8,128)(2,1)S(1)} %collective-permute-done.10.rest_1_), channel_id=1, source_target_pairs={{192,160},{196,164},{200,168},{204,172},{208,176},{212,180},{216,1... | collective-permute-start | bytes 786440 | tf_op jit(solution)/shard_map/ppermute | solution.py:82
  75.5 19.3 %collective-permute-start.17 = (bf16[4,128,256]{2,1,0:T(8,128)(2,1)S(1)}, bf16[4,128,256]{2,1,0:T(8,128)(2,1)S(1)}, u32[]{:S(2)}, u32[]{:S(2)}) collective-permute-start(bf16[4,128,256]{2,1,0:T(8,128)(2,1)S(1)} %slice.18), channel_id=1, source_target_pairs={{0,8},{4,12},{8,16},{12,20},{16,24},{20,28},{24,0},{28,4},{32,40},... | collective-permute-start | bytes 786440 | tf_op jit(solution)/shard_map/ppermute | solution.py:61
  75.6 19.2 %collective-permute-start.18 = (bf16[4,128,256]{2,1,0:T(8,128)(2,1)S(1)}, bf16[4,128,256]{2,1,0:T(8,128)(2,1)S(1)}, u32[]{:S(2)}, u32[]{:S(2)}) collective-permute-start(bf16[4,128,256]{2,1,0:T(8,128)(2,1)S(1)} %slice.19), channel_id=1, source_target_pairs={{0,24},{4,28},{8,0},{12,4},{16,8},{20,12},{24,16},{28,20},{32,56},... | collective-permute-start | bytes 786440 | tf_op jit(solution)/shard_map/ppermute | solution.py:61
  82.9 11.9 %collective-permute-start.15 = (bf16[2,128,256]{2,1,0:T(8,128)(2,1)S(1)}, bf16[2,128,256]{2,1,0:T(8,128)(2,1)S(1)}, u32[]{:S(2)}, u32[]{:S(2)}) collective-permute-start(bf16[2,128,256]{2,1,0:T(8,128)(2,1)S(1)} %slice.16), channel_id=1, source_target_pairs={{96,128},{100,132},{104,136},{108,140},{112,144},{116,148},{120,15... | collective-permute-start | bytes 393224 | tf_op jit(solution)/shard_map/ppermute | solution.py:71
  86.0 8.8 %collective-permute-start.16 = (bf16[2,128,256]{2,1,0:T(8,128)(2,1)S(1)}, bf16[2,128,256]{2,1,0:T(8,128)(2,1)S(1)}, u32[]{:S(2)}, u32[]{:S(2)}) collective-permute-start(bf16[2,128,256]{2,1,0:T(8,128)(2,1)S(1)} %slice.17), channel_id=1, source_target_pairs={{160,128},{164,132},{168,136},{172,140},{176,144},{180,148},{184,1... | collective-permute-start | bytes 393224 | tf_op jit(solution)/shard_map/ppermute | solution.py:82
  100.4 3.8 %collective-permute-start.19 = (bf16[256,512]{1,0:T(8,128)(2,1)S(1)}, bf16[256,512]{1,0:T(8,128)(2,1)S(1)}, u32[]{:S(2)}, u32[]{:S(2)}) collective-permute-start(bf16[256,512]{1,0:T(8,128)(2,1)S(1)} %get-tuple-element.33), channel_id=1, source_target_pairs={{0,4},{4,0},{8,12},{12,8},{16,20},{20,16},{24,28},{28,24},{32,36},... | collective-permute-start | bytes 786440 | tf_op jit(solution)/shard_map/ppermute | solution.py:86
  105.5 10.9 %collective-permute-start.21 = (bf16[256,512]{1,0:T(8,128)(2,1)S(1)}, bf16[256,512]{1,0:T(8,128)(2,1)S(1)}, u32[]{:S(2)}, u32[]{:S(2)}) collective-permute-start(bf16[256,512]{1,0:T(8,128)(2,1)S(1)} %get-tuple-element.40), channel_id=1, source_target_pairs={{0,1},{1,2},{2,3},{3,0},{4,5},{5,6},{6,7},{7,4},{8,9},{9,10},{10,1... | collective-permute-start | bytes 786440 | tf_op jit(solution)/shard_map/ppermute | solution.py:90
  107.6 10.4 %collective-permute-start.24 = (bf16[256,512]{1,0:T(8,128)(2,1)S(1)}, bf16[256,512]{1,0:T(8,128)(2,1)S(1)}, u32[]{:S(2)}, u32[]{:S(2)}) collective-permute-start(bf16[256,512]{1,0:T(8,128)(2,1)S(1)} %get-tuple-element.44), channel_id=1, source_target_pairs={{0,3},{1,0},{2,1},{3,2},{4,7},{5,4},{6,5},{7,6},{8,11},{9,8},{10,9... | collective-permute-start | bytes 786440 | tf_op jit(solution)/shard_map/ppermute | solution.py:90
  112.5 9.8 %collective-permute-start.20 = (bf16[256,512]{1,0:T(8,128)(2,1)S(1)}, bf16[256,512]{1,0:T(8,128)(2,1)S(1)}, u32[]{:S(2)}, u32[]{:S(2)}) collective-permute-start(bf16[256,512]{1,0:T(8,128)(2,1)S(1)} %get-tuple-element.37), channel_id=1, source_target_pairs={{0,3},{1,0},{2,1},{3,2},{4,7},{5,4},{6,5},{7,6},{8,11},{9,8},{10,9... | collective-permute-start | bytes 786440 | tf_op jit(solution)/shard_map/ppermute | solution.py:90
  116.5 10.5 %collective-permute-start.22 = (bf16[256,512]{1,0:T(8,128)(2,1)S(1)}, bf16[256,512]{1,0:T(8,128)(2,1)S(1)}, u32[]{:S(2)}, u32[]{:S(2)}) collective-permute-start(bf16[256,512]{1,0:T(8,128)(2,1)S(1)} %add_convert_fusion.3), channel_id=1, source_target_pairs={{0,1},{1,2},{2,3},{3,0},{4,5},{5,6},{6,7},{7,4},{8,9},{9,10},{10,1... | collective-permute-start | bytes 786440 | tf_op jit(solution)/shard_map/ppermute | solution.py:90
  116.6 14.9 %collective-permute-start.23 = (bf16[256,512]{1,0:T(8,128)(2,1)S(1)}, bf16[256,512]{1,0:T(8,128)(2,1)S(1)}, u32[]{:S(2)}, u32[]{:S(2)}) collective-permute-start(bf16[256,512]{1,0:T(8,128)(2,1)S(1)} %get-tuple-element.42), channel_id=1, source_target_pairs={{0,1},{1,2},{2,3},{3,0},{4,5},{5,6},{6,7},{7,4},{8,9},{9,10},{10,1... | collective-permute-start | bytes 786440 | tf_op jit(solution)/shard_map/ppermute | solution.py:90
  118.1 13.4 %collective-permute-start.25 = (bf16[256,512]{1,0:T(8,128)(2,1)S(1)}, bf16[256,512]{1,0:T(8,128)(2,1)S(1)}, u32[]{:S(2)}, u32[]{:S(2)}) collective-permute-start(bf16[256,512]{1,0:T(8,128)(2,1)S(1)} %add_convert_fusion.1), channel_id=1, source_target_pairs={{0,3},{1,0},{2,1},{3,2},{4,7},{5,4},{6,5},{7,6},{8,11},{9,8},{10,9... | collective-permute-start | bytes 786440 | tf_op jit(solution)/shard_map/ppermute | solution.py:90
  (5 other events, 35.7 us)

commit v3 on v2

v3 whole, which is shorter than its diff:
```python
import functools
import math

import jax
import jax.numpy as jnp
import numpy as np
from jax import lax
from jax.experimental import pallas as pl
from jax.experimental.pallas import tpu as pltpu
from jax.sharding import PartitionSpec as P

HD = 128
BLK = 128
GROUP = 4
PICKS = 16
NX, NZ = 4, 8
NEG = -1e30
C2 = math.log2(math.e) / math.sqrt(HD)
LIMIT = 100.0
VMEM_BYTES = 40 * 1024 * 1024
SLOT_BITS = 6
AT_ONCE = 4
BF16, F32, I32 = jnp.bfloat16, jnp.float32, jnp.int32

STACKS = ((-1, -2, 1), (-3, -4, 2, 3))


def slot_table():
    table = np.zeros((NZ, NX), np.int32)

    def put(group, base, zs, dx):
        for i, dz in enumerate(zs):
            table[dz % NZ, dx % NX] = (group << SLOT_BITS) | (base + 2 * i)

    first, second = STACKS
    put(0, 0, (0,), 0)
    put(0, 2, first, 0)
    put(0, 8, (0,), -1)
    put(0, 10, (0,), 1)
    put(0, 12, (0,), 2)
    put(0, 14, second, 0)
    put(0, 22, first, -1)
    put(0, 28, first, 1)
    put(1, 0, second, -1)
    put(1, 8, second, 1)
    put(2, 0, first, 2)
    put(2, 6, second, 2)
    return table.reshape(-1)


def seq_at(z, x, core):
    return (z * NX + x) * 2 + core


def along_x(value, dx, lowest):
    pairs = [
        (seq_at(z, x, c), seq_at(z, (x + dx) % NX, c))
        for z in range(lowest, NZ)
        for x in range(NX)
        for c in range(2)
    ]
    return lax.ppermute(value, "seq", pairs)


def along_z(value, dz, lowest, count):
    pairs = [
        (seq_at(z, x, c), seq_at((z + dz) % NZ, x, c))
        for z in range(lowest, lowest + count)
        for x in range(NX)
        for c in range(2)
    ]
    return lax.ppermute(value, "seq", pairs)


def swap_cores(value):
    return lax.ppermute(value, "seq", [(i, i ^ 1) for i in range(2 * NX * NZ)])


def tp_shift(value, step):
    return lax.ppermute(value, "tp", [(i, (i + step) % 4) for i in range(4)])


def dot_f32(a, b, dims):
    return lax.dot_general(a, b, (dims, ((), ())), preferred_element_type=F32)


def lanes(core, width=HD):
    return pl.ds(pl.multiple_of(core * width, width), width)


def pick_kernel(scal, blocks, k_ref, v_ref, k_sib, v_sib, out_ref):
    core, place = scal[0], scal[1]
    head = lax.broadcasted_iota(I32, blocks.shape, 0)
    of_core = (head >= core * GROUP) & (head < (core + 1) * GROUP)
    for k, v, parity in ((k_ref, v_ref, core), (k_sib, v_sib, 1 - core)):
        shard = place - core + parity
        hit = jnp.where(of_core & (blocks[...] == 2 * shard + 1), 1.0, 0.0)
        half = (jnp.max(hit) > 0.5).astype(I32)
        rows = pl.ds(pl.multiple_of(half * BLK, BLK), BLK)
        out_ref[parity, :, :HD] = k[rows, lanes(core)]
        out_ref[parity, :, HD:] = v[rows, lanes(core)]


def tail_kernel(scal, k_ref, v_ref, k_sib, v_sib, out_ref):
    core = scal[0]

    @pl.when(core == 1)
    def _():
        out_ref[:, :HD] = k_ref[BLK:, HD:]
        out_ref[:, HD:] = v_ref[BLK:, HD:]

    @pl.when(core == 0)
    def _():
        out_ref[:, :HD] = k_sib[BLK:, :HD]
        out_ref[:, HD:] = v_sib[BLK:, :HD]


def split3(m):
    a = m.astype(BF16)
    rest = m - a.astype(F32)
    b = rest.astype(BF16)
    c = (rest - b.astype(F32)).astype(BF16)
    return a, b, c


def extra_columns(m):
    rows = m.shape[0]
    lane = lax.broadcasted_iota(I32, (rows, HD), 1)
    a, b, c = (jnp.broadcast_to(-part.astype(F32), (rows, HD)) for part in split3(m))
    wide = jnp.where(lane == 0, a, jnp.where(lane == 1, b, jnp.where(lane == 2, c, 0.0)))
    return jnp.where(lane == 3, 1.0, wide).astype(BF16)


def local_kernel(
    scal, blocks, win, slash, table, q, q_sib, k, k_sib, v, v_sib, halo,
    qa_ref, acc_ref, list_ref, count_ref, qs, ks, vs, named,
):
    core, place = scal[0], scal[1]
    chip = place >> 1
    z, x = chip >> 2, chip & 3

    for g in range(16):
        count_ref[g] = 0
    for n in range(GROUP * 8):
        named[n] = 0

    def note(n, carry):
        h, column = n >> 4, n & 15
        b = blocks[core * GROUP + h, column]
        entry = table[((((b >> 4) - z) & 7) << 2) + (((b >> 2) - x) & 3)]
        key = ((entry >> SLOT_BITS) << 2) + h
        count = count_ref[key]
        list_ref[(key << 4) + count] = (entry & ((1 << SLOT_BITS) - 1)) + ((b >> 1) & 1)
        near = b - (4 * chip - 1)
        count_ref[key] = count + jnp.where(near < 0, 1, 0)
        inside = (near >= 0) & (near < 5)
        named[(h << 3) + jnp.where(inside, near, 7)] = 1
        return carry

    lax.fori_loop(0, GROUP * PICKS, note, 0, unroll=4)

    mine, sib = core * 2 * BLK, (1 - core) * 2 * BLK
    ks[:BLK] = halo[:, :HD]
    vs[:BLK] = halo[:, HD:]
    for ref, own, other in ((ks, k, k_sib), (vs, v, v_sib)):
        ref[pl.ds(pl.multiple_of(BLK + mine, BLK), 2 * BLK)] = own[:, lanes(core)]
        ref[pl.ds(pl.multiple_of(BLK + sib, BLK), 2 * BLK)] = other[:, lanes(core)]
    for h in range(GROUP):
        cols = pl.ds(pl.multiple_of(core * GROUP * HD + h * HD, HD), HD)
        qs[h, pl.ds(pl.multiple_of(mine, BLK), 2 * BLK)] = q[:, cols]
        qs[h, pl.ds(pl.multiple_of(sib, BLK), 2 * BLK)] = q_sib[:, cols]

    qi = lax.broadcasted_iota(I32, (BLK, BLK), 0)
    kj = lax.broadcasted_iota(I32, (BLK, BLK), 1)
    diag_gap = qi - kj
    prev_gap = diag_gap + BLK
    for h in range(GROUP):
        head = core * GROUP + h
        diag_ok = diag_gap < win[head]
        prev_ok = prev_gap < win[head]
        for n in range(8):
            diag_ok = diag_ok | (diag_gap == slash[head, n])
            prev_ok = prev_ok | (prev_gap == slash[head, n])
        scores = dot_f32(qs[h], ks[...], ((1,), (1,)))
        weights = []
        for i in range(4):
            rows = slice(i * BLK, (i + 1) * BLK)
            tiles = []
            for t in range(i + 2):
                is_named = named[h * 8 + t] > 0
                if t == i + 1:
                    ok = (diag_gap >= 0) & (diag_ok | is_named)
                elif t == i:
                    ok = prev_ok | is_named
                else:
                    ok = jnp.broadcast_to(is_named, (BLK, BLK))
                if t == 0:
                    ok = ok & (chip > 0)
                tiles.append(jnp.where(ok, scores[rows, t * BLK : (t + 1) * BLK], NEG))
            m = jnp.max(functools.reduce(jnp.maximum, tiles), axis=1, keepdims=True)
            tiles = [jnp.exp2((tile - m) * C2) for tile in tiles]
            total = jnp.sum(functools.reduce(jnp.add, tiles), axis=1, keepdims=True)
            acc_ref[h, rows, HD:] = jnp.broadcast_to(total, (BLK, HD))
            qa_ref[h, rows, :HD] = qs[h, rows, :]
            qa_ref[h, rows, HD:] = extra_columns(m)
            tiles += [jnp.zeros((BLK, BLK), F32)] * (3 - i)
            weights.append(jnp.concatenate([tile.astype(BF16) for tile in tiles], axis=1))
        acc_ref[h, :, :HD] = dot_f32(jnp.concatenate(weights, axis=0), vs[...], ((1,), (0,)))


def far_kernel(group, sizes, final, scal, lists, counts, qa_in, acc_in, *rest):
    pieces = rest[: len(sizes)]
    if final:
        mine_ref, other_ref, qa_ref, acc_ref, kv, aug, todo, sem = rest[len(sizes) :]
    else:
        qa_ref, acc_ref, kv, aug, todo, sem = rest[len(sizes) :]
    copies = []
    spare = 0
    for n, (piece, size) in enumerate(zip(pieces, sizes)):
        copies.append(pltpu.make_async_copy(piece, kv.at[pl.ds(spare, size)], sem.at[n]))
        spare += size
    for copy in copies:
        copy.start()
    kv[spare] = jnp.zeros((BLK, 2 * HD), BF16)
    lane = lax.broadcasted_iota(I32, (BLK, HD), 1)
    aug[0] = jnp.where(lane < 3, 1.0, jnp.where(lane == 3, NEG, 0.0)).astype(BF16)
    aug[1] = jnp.where(lane < 3, 1.0, 0.0).astype(BF16)
    qa_ref[...] = qa_in[...]
    acc_ref[...] = acc_in[...]

    total = jnp.int32(0)
    for h in range(GROUP):
        base = (group * GROUP + h) * PICKS
        count = counts[group * GROUP + h]

        def note(j, at, h=h, base=base, count=count):
            todo[3 * at] = h
            todo[3 * at + 1] = lists[base + 2 * j]
            more = 2 * j + 1 < count
            todo[3 * at + 2] = jnp.where(more, lists[base + 2 * j + jnp.where(more, 1, 0)], spare)
            return at + 1

        total = lax.fori_loop(0, (count + 1) >> 1, note, total)
    for n in range(AT_ONCE - 1):
        todo[3 * (total + n)] = n
        todo[3 * (total + n) + 1] = spare
        todo[3 * (total + n) + 2] = spare
    steps = (total + AT_ONCE - 1) // AT_ONCE
    for copy in copies:
        copy.wait()

    def entries(i):
        first = 3 * AT_ONCE * i
        return [tuple(todo[first + 3 * n + k] for k in range(3)) for n in range(AT_ONCE)]

    def scores(h, one, two):
        keys = jnp.concatenate([kv[one, :, :HD], kv[two, :, :HD]], axis=0)
        real = [jnp.where(slot == spare, 0, 1) for slot in (one, two)]
        more = jnp.concatenate([aug[real[0]], aug[real[1]]], axis=0)
        return dot_f32(qa_ref[h], jnp.concatenate([keys, more], axis=1), ((1,), (1,)))

    ones = jnp.ones((2 * BLK, HD), BF16)

    def accumulate():
        def step(i, high):
            work = entries(i)
            for h, one, two in work:
                s = scores(h, one, two) * C2
                values = jnp.concatenate([kv[one, :, HD:], kv[two, :, HD:]], axis=0)
                acc_ref[h] += dot_f32(
                    jnp.exp2(s).astype(BF16), jnp.concatenate([values, ones], axis=1), ((1,), (0,))
                )
                high = jnp.maximum(high, jnp.max(s.reshape(-1, 8, 2 * BLK), axis=0))
            return high

        return jnp.max(lax.fori_loop(0, steps, step, jnp.zeros((8, 2 * BLK), F32)))

    highest = accumulate()

    @pl.when(highest > LIMIT)
    def _():
        rows = qa_ref.shape[1]
        for h in range(GROUP):

            def step(n, gain, h=h):
                mine = todo[3 * n] == h
                s = scores(todo[3 * n], todo[3 * n + 1], todo[3 * n + 2])
                top = jnp.max(s, axis=1, keepdims=True)
                return jnp.maximum(gain, jnp.where(mine, top, 0.0))

            gain = lax.fori_loop(0, total, step, jnp.zeros((rows, 1), F32))
            parts = qa_ref[h, :, HD:].astype(F32)
            old = -(parts[:, 0:1] + parts[:, 1:2] + parts[:, 2:3])
            new = old + gain
            qa_ref[h, :, HD:] = extra_columns(new)
            acc_ref[h] = acc_in[h] * jnp.exp2((old - new) * C2)
        accumulate()

    if final:
        core = scal[0]
        for out, first in ((other_ref, (1 - core) * 2 * BLK), (mine_ref, core * 2 * BLK)):
            rows = pl.ds(pl.multiple_of(first, BLK), 2 * BLK)
            for h in range(GROUP):
                both = acc_ref[h, rows, :]
                out[:, h * HD : (h + 1) * HD] = (both[:, :HD] / both[:, HD:]).astype(BF16)


def weight_tiles(scal, w_ref, w_buf, sem, sibling, rel_tiles):
    core, me = scal[0], scal[2]
    rows, cols = w_buf.shape[1:]
    first = jnp.where(core == (1 if sibling else 0), 0, rows)
    copies = []
    for n, tile in enumerate(rel_tiles):
        step = (2, 1, 3, 0)[tile // 2]
        col = ((me + step) % 4) * (2 * cols) + (tile % 2) * cols
        copies.append(
            pltpu.make_async_copy(
                w_ref.at[pl.ds(pl.multiple_of(first, rows), rows), pl.ds(pl.multiple_of(col, cols), cols)],
                w_buf.at[n],
                sem.at[n],
            )
        )
    for copy in copies:
        copy.start()
    return copies


def part_kernel(sibling, tiles, scal, ctx, w_ref, out_ref, w_buf, sem):
    copies = weight_tiles(scal, w_ref, w_buf, sem, sibling, tiles)
    for n, copy in enumerate(copies):
        copy.wait()
        out_ref[n] = dot_f32(ctx[...], w_buf[n], ((1,), (0,)))


def add_part_kernel(sibling, tiles, scal, ctx, part, w_ref, *rest):
    outs, (w_buf, sem) = rest[: len(tiles)], rest[len(tiles) :]
    copies = weight_tiles(scal, w_ref, w_buf, sem, sibling, tiles)
    for n, copy in enumerate(copies):
        copy.wait()
        outs[n][...] = (part[n] + dot_f32(ctx[...], w_buf[n], ((1,), (0,)))).astype(outs[n].dtype)


def both_parts_kernel(tiles, scal, ctx, ctx_sib, w_ref, *rest):
    outs, (w_own, w_sib, sem_own, sem_sib) = rest[: len(tiles)], rest[len(tiles) :]
    own = weight_tiles(scal, w_ref, w_own, sem_own, False, tiles)
    sib = weight_tiles(scal, w_ref, w_sib, sem_sib, True, tiles)
    for n in range(len(tiles)):
        own[n].wait()
        part = dot_f32(ctx[...], w_own[n], ((1,), (0,)))
        sib[n].wait()
        outs[n][...] = (part + dot_f32(ctx_sib[...], w_sib[n], ((1,), (0,)))).astype(outs[n].dtype)


def spec(space):
    return pl.BlockSpec(memory_space=space)


def call(kernel, name, outs, args, spaces, scratch=(), out_spaces=None, flops=0, moved=0):
    return pl.pallas_call(
        kernel,
        out_shape=outs,
        in_specs=[spec(s) for s in spaces],
        out_specs=[spec(s) for s in (out_spaces or [pltpu.VMEM] * len(outs))],
        scratch_shapes=list(scratch),
        compiler_params=pltpu.CompilerParams(vmem_limit_bytes=VMEM_BYTES),
        cost_estimate=pl.CostEstimate(flops=flops, bytes_accessed=moved, transcendentals=0),
        name=name,
    )(*args)


def shape(dims, dtype):
    return jax.ShapeDtypeStruct(dims, dtype)


def local(queries, key_states, value_states, vert_blocks, window_size, slash_offsets, out_weight):
    smem, vmem, anywhere = pltpu.SMEM, pltpu.VMEM, pl.ANY
    place = lax.axis_index("seq").astype(I32)
    me = lax.axis_index("tp").astype(I32)
    core = place % 2
    scal = jnp.stack([core, place, me])
    block = shape((1, BLK, 2 * HD), BF16)

    k_sib = swap_cores(key_states)
    v_sib = swap_cores(value_states)
    q_sib = swap_cores(queries)
    unit = call(
        pick_kernel, "pick", [shape((2, BLK, 2 * HD), BF16)],
        (scal, vert_blocks, key_states, value_states, k_sib, v_sib), [smem] + [vmem] * 5,
        moved=1_000_000,
    )[0]

    up1 = along_z(unit, 1, 0, NZ - 1)
    down1 = along_z(unit, -1, 0, 1)
    up2 = along_z(unit, 2, 0, NZ - 2)
    down2 = along_z(unit, -2, 0, 2)
    down3 = along_z(unit, -3, 0, 3)
    right0, left0 = along_x(unit, 1, 0), along_x(unit, -1, 0)
    up3 = along_z(up2, 1, 2, NZ - 3)
    up4 = along_z(up2, 2, 2, NZ - 4)
    opposite0 = along_x(right0, 1, 0)
    first = jnp.concatenate([up1, up2, down1], axis=0)
    right1, left1 = along_x(first, 1, 1), along_x(first, -1, 1)
    second = jnp.concatenate([up3, up4, down2, down3], axis=0)

    tail = call(
        tail_kernel, "tail", [shape((BLK, 2 * HD), BF16)],
        (scal, key_states, value_states, k_sib, v_sib), [smem] + [vmem] * 4, moved=1_000_000,
    )[0]
    halo = lax.ppermute(tail, "seq", [(i, i + 2) for i in range(2 * NX * NZ - 2)])

    rows = 2 * queries.shape[0]
    wide = (GROUP, rows, 2 * HD)
    qa, acc, lists, counts = call(
        local_kernel,
        "near_part",
        [shape(wide, BF16), shape(wide, F32), shape((16 * PICKS,), I32), shape((16,), I32)],
        (
            scal, vert_blocks, window_size, slash_offsets, jnp.asarray(slot_table()),
            queries, q_sib, key_states, k_sib, value_states, v_sib, halo,
        ),
        [smem] * 5 + [vmem] * 7,
        [
            pltpu.VMEM((GROUP, rows, HD), BF16),
            pltpu.VMEM((rows + BLK, HD), BF16),
            pltpu.VMEM((rows + BLK, HD), BF16),
            pltpu.SMEM((GROUP * 8,), I32),
        ],
        [vmem, vmem, smem, smem],
        flops=1_000_000_000,
        moved=8_000_000,
    )

    def far(n, pieces, qa, acc):
        sizes = [p.shape[0] for p in pieces]
        scratch = [
            pltpu.VMEM((sum(sizes) + 1, BLK, 2 * HD), BF16),
            pltpu.VMEM((2, BLK, HD), BF16),
            pltpu.SMEM((3 * (GROUP * PICKS + AT_ONCE),), I32),
            pltpu.SemaphoreType.DMA((len(sizes),)),
        ]
        final = n == 2
        outs = [shape(wide, BF16), shape(wide, F32)]
        if final:
            scratch = [pltpu.VMEM(wide, BF16), pltpu.VMEM(wide, F32)] + scratch
            outs = [shape((rows // 2, GROUP * HD), BF16)] * 2
        return call(
            functools.partial(far_kernel, n, sizes, final),
            "far_part",
            outs,
            (scal, lists, counts, qa, acc, *pieces),
            [smem] * 3 + [vmem] * 2 + [anywhere] * len(sizes),
            scratch,
            flops=1_500_000_000,
            moved=6_000_000,
        )

    second, acc = lax.optimization_barrier((second, acc))
    right2, left2 = along_x(second, 1, 3), along_x(second, -1, 3)
    opposite1 = along_x(right1, 1, 1)
    qa, acc = far(0, [unit, first, right0, left0, opposite0, second, right1, left1], qa, acc)
    relayed, acc = lax.optimization_barrier((left2, acc))
    opposite2 = along_x(relayed, -1, 3)
    qa, acc = far(1, [right2, left2], qa, acc)
    ctx_mine, ctx_other = far(2, [opposite1, opposite2], qa, acc)
    ctx_sib = swap_cores(ctx_other)

    half_rows, half = rows // 2, out_weight.shape[1] // 8
    depth = GROUP * HD

    def w_scratch(count):
        return [pltpu.VMEM((count, depth, half), BF16)], [pltpu.SemaphoreType.DMA((count,))]

    tile_bf, tile_f = shape((half_rows, half), BF16), shape((half_rows, half), F32)
    opp = call(
        functools.partial(part_kernel, False, (0, 1)), "own_part",
        [shape((2, half_rows, half), F32)], (scal, ctx_mine, out_weight), [smem, vmem, anywhere],
        sum(w_scratch(2), []), flops=300_000_000, moved=3_000_000,
    )[0]
    opp0, opp1 = call(
        functools.partial(add_part_kernel, True, (0, 1)), "sib_part", [tile_bf] * 2,
        (scal, ctx_sib, opp, out_weight), [smem, vmem, vmem, anywhere],
        sum(w_scratch(2), []), flops=300_000_000, moved=3_000_000,
    )
    via_before = tp_shift(opp0, 1)
    via_after = tp_shift(opp1, -1)
    bufs, sems = w_scratch(6)
    after0, after1, before0, before1, own0, own1 = call(
        functools.partial(both_parts_kernel, (2, 3, 4, 5, 6, 7)), "other_shares",
        [tile_f, tile_bf, tile_bf, tile_f, tile_f, tile_f],
        (scal, ctx_mine, ctx_sib, out_weight), [smem, vmem, vmem, anywhere],
        bufs * 2 + sems * 2, flops=1_600_000_000, moved=9_000_000,
    )
    direct1 = tp_shift(after1, 1)
    direct0 = tp_shift(before0, -1)
    summed0 = tp_shift((after0 + via_before.astype(F32)).astype(BF16), 1)
    summed1 = tp_shift((before1 + via_after.astype(F32)).astype(BF16), -1)
    return jnp.concatenate(
        [
            own0 + direct0.astype(F32) + summed0.astype(F32),
            own1 + direct1.astype(F32) + summed1.astype(F32),
        ],
        axis=1,
    ).astype(BF16)


def solution(mesh):
    return jax.shard_map(
        local,
        mesh=mesh,
        in_specs=(
            P("seq", "tp"),
            P("seq", "tp"),
            P("seq", "tp"),
            P("tp", None),
            P("tp"),
            P("tp", None),
            P("tp", None),
        ),
        out_specs=P("seq", "tp"),
        check_vma=False,
    )
```

time: 134 us -> 121 us (0.903)
  blocking collectives: 26 us -> 0 us
  waiting for transfers between devices: 22.8 us -> 42.3 us
  Pallas kernels: 36.4 us -> 25.8 us
  starting transfers between devices: 42.9 us -> 46.9 us
    all_gather x1 -> x0, blocking collectives: 26 us -> none  [local(): lax.all_gather(b0, 'seq', axis=0, tiled=True, axis_index_groups=[[seq_at(...]
    ppermute x7 -> x9, waiting for transfers between devices: 3.45 us -> 17.7 us  [along_x(): return lax.ppermute(value, 'seq', pairs)]
    ppermute x7 -> x9, starting transfers between devices: 11.9 us -> 23.1 us  [along_x(): return lax.ppermute(value, 'seq', pairs)]
    pallas_call x10 -> x9, Pallas kernels: 36.4 us -> 25.8 us  [call(): pl.pallas_call(kernel, out_shape=outs, in_specs=[spec(s) for s in spaces]...]
    ppermute x8 -> x7, starting transfers between devices: 18.6 us -> 10.8 us  [along_z(): return lax.ppermute(value, 'seq', pairs)]
    ppermute x8 -> x7, waiting for transfers between devices: 6 us -> 12.3 us  [along_z(): return lax.ppermute(value, 'seq', pairs)]
    ppermute x6, waiting for transfers between devices: 13.3 us -> 11 us  [tp_shift(): return lax.ppermute(value, 'tp', [(i, (i + step) % 4) for i in range(4)])]
  transfers between devices with their start and end apart: 26 -> 27, of which waited for: 7 -> 13; matrix products, arithmetic and copies ran while one was open for 0% -> 0% of each run, Pallas kernels for 21% -> 17%
where the time goes in v3:
time: 121 us; the launch traced here: 119 us
  starting transfers between devices  46.9 us (39%)
  waiting for transfers between devices  42.3 us (35%)
  Pallas kernels  25.8 us (21%)
  local copies, waits for them, and re-layouts  2.56 us (2%)
  other arithmetic  1.37 us (1%)
    pallas_call x9, Pallas kernels, call(): pl.pallas_call(kernel, out_shape=outs, in_specs=[spec(s) for s in spaces]...  25.8 us
    ppermute x9, starting transfers between devices, along_x(): return lax.ppermute(value, 'seq', pairs)  23.1 us
    ppermute x9, waiting for transfers between devices, along_x(): return lax.ppermute(value, 'seq', pairs)  17.7 us
    ppermute x7, waiting for transfers between devices, along_z(): return lax.ppermute(value, 'seq', pairs)  12.3 us
    ppermute x6, waiting for transfers between devices, tp_shift(): return lax.ppermute(value, 'tp', [(i, (i + step) % 4) for i in range(4)])  11 us
    ppermute x7, starting transfers between devices, along_z(): return lax.ppermute(value, 'seq', pairs)  10.8 us
    ppermute x6, starting transfers between devices, tp_shift(): return lax.ppermute(value, 'tp', [(i, (i + step) % 4) for i in range(4)])  8.88 us
    ppermute x1, starting transfers between devices, local(): lax.ppermute(tail, 'seq', [(i, i + 2) for i in range(2 * NX * NZ - 2)])  3.39 us
  transfers between devices with their start and end apart: 27, of which 13 were waited for; matrix products, arithmetic and copies ran while one was open for 0% of the time, Pallas kernels for 17%

profile of v3, /device:TPU:192, one launch (start us, length us, event | category | flops | bytes accessed | tf_op | source)
XLA Modules:
  0.0 119.4 jit_solution(4170433462169766315)
XLA Ops:
  5.0 1.3 %collective-permute-start.4 = (bf16[2,128,256]{2,1,0:T(8,128)(2,1)S(1)}, bf16[2,128,256]{2,1,0:T(8,128)(2,1)S(1)}, u32[]{:S(2)}, u32[]{:S(2)}) collective-permute-start(bf16[2,128,256]{2,1,0:T(8,128)(2,1)S(1)} %pick.1.rest_0_), channel_id=1, source_target_pairs={{0,64},{4,68},{8,72},{12,76},{16,80},{20,84},{24,88},{28,92},{32,9... | collective-permute-start | bytes 393224 | tf_op jit(solution)/shard_map/ppermute | solution.py:72
  6.3 2.9 %collective-permute-start.9 = (bf16[2,128,256]{2,1,0:T(8,128)(2,1)S(1)}, bf16[2,128,256]{2,1,0:T(8,128)(2,1)S(1)}, u32[]{:S(2)}, u32[]{:S(2)}) collective-permute-start(bf16[2,128,256]{2,1,0:T(8,128)(2,1)S(1)} %pick.1.rest_0_), channel_id=1, source_target_pairs={{0,32},{4,36},{8,40},{12,44},{16,48},{20,52},{24,56},{28,60},{32,6... | collective-permute-start | bytes 393224 | tf_op jit(solution)/shard_map/ppermute | solution.py:72
  10.1 1.3 %collective-permute-start.7 = (bf16[2,128,256]{2,1,0:T(8,128)(2,1)S(1)}, bf16[2,128,256]{2,1,0:T(8,128)(2,1)S(1)}, u32[]{:S(2)}, u32[]{:S(2)}) collective-permute-start(bf16[2,128,256]{2,1,0:T(8,128)(2,1)S(1)} %pick.1.rest_0_), channel_id=1, source_target_pairs={{0,192},{4,196},{8,200},{12,204},{16,208},{20,212},{24,216},{28,22... | collective-permute-start | bytes 393224 | tf_op jit(solution)/shard_map/ppermute | solution.py:72
  11.9 5.0 %collective-permute-done.4 = bf16[2,128,256]{2,1,0:T(8,128)(2,1)S(1)} collective-permute-done((bf16[2,128,256]{2,1,0:T(8,128)(2,1)S(1)}, bf16[2,128,256]{2,1,0:T(8,128)(2,1)S(1)}, u32[]{:S(2)}, u32[]{:S(2)}) %collective-permute-start.4) | collective-permute-done | bytes 131104 | tf_op jit(solution)/shard_map/ppermute | solution.py:72
  18.7 2.0 %collective-permute-start.5 = (bf16[2,128,256]{2,1,0:T(8,128)(2,1)S(1)}, bf16[2,128,256]{2,1,0:T(8,128)(2,1)S(1)}, u32[]{:S(2)}, u32[]{:S(2)}) collective-permute-start(bf16[2,128,256]{2,1,0:T(8,128)(2,1)S(1)} %collective-permute-done.4), channel_id=1, source_target_pairs={{64,96},{68,100},{72,104},{76,108},{80,112},{84,116},{88,120},{92,... | collective-permute-start | bytes 393224 | tf_op jit(solution)/shard_map/ppermute | solution.py:72
  22.1 6.8 %collective-permute-done.7 = bf16[2,128,256]{2,1,0:T(8,128)(2,1)S(1)} collective-permute-done((bf16[2,128,256]{2,1,0:T(8,128)(2,1)S(1)}, bf16[2,128,256]{2,1,0:T(8,128)(2,1)S(1)}, u32[]{:S(2)}, u32[]{:S(2)}) %collective-permute-start.7) | collective-permute-done | bytes 131104 | tf_op jit(solution)/shard_map/ppermute | solution.py:72
  28.9 3.4 %collective-permute-start.3 = (bf16[128,256]{1,0:T(8,128)(2,1)S(1)}, bf16[128,256]{1,0:T(8,128)(2,1)S(1)}, u32[]{:S(2)}, u32[]{:S(2)}) collective-permute-start(bf16[128,256]{1,0:T(8,128)(2,1)S(1)} %tail.1), channel_id=1, source_target_pairs={{0,8},{4,12},{8,16},{12,20},{16,24},{20,28},{24,32},{28,36},{32,40... | collective-permute-start | bytes 196616 | tf_op jit(solution)/shard_map/ppermute | solution.py:409
  32.3 3.4 %collective-permute-start.14 = (bf16[6,128,256]{2,1,0:T(8,128)(2,1)S(1)}, bf16[6,128,256]{2,1,0:T(8,128)(2,1)S(1)}, u32[]{:S(2)}, u32[]{:S(2)}) collective-permute-start(bf16[6,128,256]{2,1,0:T(8,128)(2,1)S(1)} %constant_dynamic-update-slice_fusion.rest_1_), channel_id=1, source_target_pairs={{32,40},{36,44},{40,48},{44,52},{48,56},{52,60},{56,32},{60,36},{6... | collective-permute-start | bytes 1179656 | tf_op jit(solution)/shard_map/ppermute | solution.py:62
  35.7 3.7 %collective-permute-start.15 = (bf16[6,128,256]{2,1,0:T(8,128)(2,1)S(1)}, bf16[6,128,256]{2,1,0:T(8,128)(2,1)S(1)}, u32[]{:S(2)}, u32[]{:S(2)}) collective-permute-start(bf16[6,128,256]{2,1,0:T(8,128)(2,1)S(1)} %constant_dynamic-update-slice_fusion.rest_1_), channel_id=1, source_target_pairs={{32,56},{36,60},{40,32},{44,36},{48,40},{52,44},{56,48},{60,52},{6... | collective-permute-start | bytes 1179656 | tf_op jit(solution)/shard_map/ppermute | solution.py:62
  39.5 4.5 %near_part.1 = (bf16[4,512,256]{2,1,0:T(8,128)(2,1)S(1)}, f32[4,512,256]{2,1,0:T(8,128)S(1)}, s32[256]{0:T(256)S(1)}, s32[16]{0:T(128)S(1)}) custom-call(s32[3]{0:T(128)S(1)} %pad_add_fusion.scal, s32[8,16]{1,0:T(8,128)S(1)} %copy-done.2, s32[8]{0:T(128)S(1)} %copy-done.5, s32[8,8]{1,0:T(8,128)S(1)} %copy-done.4, s32[32]{0:T(128)S(1)} %copy-done.6, ...), custom_call_target="tpu_custom_call" | custom-call | flops 1000000000 | bytes 8000000 | tf_op jit(solution)/shard_map/near_part/pallas_call | solution.py:359
  44.0 2.0 %collective-permute-start.16 = (bf16[8,128,256]{2,1,0:T(8,128)(2,1)S(1)}, bf16[8,128,256]{2,1,0:T(8,128)(2,1)S(1)}, u32[]{:S(2)}, u32[]{:S(2)}) collective-permute-start(bf16[8,128,256]{2,1,0:T(8,128)(2,1)S(1)} %pad_maximum_fusion.rest_5_), channel_id=1, source_target_pairs={{96,120},{100,124},{104,96},{108,100},{112,104},{116,108},{120,112... | collective-permute-start | bytes 1572872 | tf_op jit(solution)/shard_map/ppermute | solution.py:62
  46.0 2.0 %collective-permute-start.11 = (bf16[2,128,256]{2,1,0:T(8,128)(2,1)S(1)}, bf16[2,128,256]{2,1,0:T(8,128)(2,1)S(1)}, u32[]{:S(2)}, u32[]{:S(2)}) collective-permute-start(bf16[2,128,256]{2,1,0:T(8,128)(2,1)S(1)} %pick.1.rest_0_), channel_id=1, source_target_pairs={{0,8},{4,12},{8,16},{12,20},{16,24},{20,28},{24,0},{28,4},{32,40},... | collective-permute-start | bytes 393224 | tf_op jit(solution)/shard_map/ppermute | solution.py:62
  49.3 2.9 %collective-permute-done.11.rest_2_ = bf16[2,128,256]{2,1,0:T(8,128)(2,1)S(1)} collective-permute-done((bf16[2,128,256]{2,1,0:T(8,128)(2,1)S(1)}, bf16[2,128,256]{2,1,0:T(8,128)(2,1)S(1)}, u32[]{:S(2)}, u32[]{:S(2)}) %collective-permute-start.11) | collective-permute-done | bytes 131104 | tf_op jit(solution)/shard_map/ppermute | solution.py:62
  53.0 8.8 %collective-permute-done.12.rest_3_ = bf16[2,128,256]{2,1,0:T(8,128)(2,1)S(1)} collective-permute-done((bf16[2,128,256]{2,1,0:T(8,128)(2,1)S(1)}, bf16[2,128,256]{2,1,0:T(8,128)(2,1)S(1)}, u32[]{:S(2)}, u32[]{:S(2)}) %collective-permute-start.12) | collective-permute-done | bytes 131104 | tf_op jit(solution)/shard_map/ppermute | solution.py:62
  61.8 3.1 %collective-permute-start.17 = (bf16[8,128,256]{2,1,0:T(8,128)(2,1)S(1)}, bf16[8,128,256]{2,1,0:T(8,128)(2,1)S(1)}, u32[]{:S(2)}, u32[]{:S(2)}) collective-permute-start(bf16[8,128,256]{2,1,0:T(8,128)(2,1)S(1)} %pad_maximum_fusion.rest_5_), channel_id=1, source_target_pairs={{96,104},{100,108},{104,112},{108,116},{112,120},{116,124},{120,96... | collective-permute-start | bytes 1572872 | tf_op jit(solution)/shard_map/ppermute | solution.py:62
  64.9 5.5 %far_part.3 = (bf16[4,512,256]{2,1,0:T(8,128)(2,1)S(1)}, f32[4,512,256]{2,1,0:T(8,128)S(1)}) custom-call(s32[3]{0:T(128)S(1)} %pad_add_fusion.scal, s32[256]{0:T(256)S(1)} %get-tuple-element.27.lists, s32[16]{0:T(128)S(1)} %get-tuple-element.28.counts, bf16[4,512,256]{2,1,0:T(8,128)(2,1)S(1)} %get-tuple-element.29.qa_in, ...), custom_call_target="tpu_custom_call" | custom-call | flops 1500000000 | bytes 6000000 | tf_op jit(solution)/shard_map/far_part/pallas_call | solution.py:359
  70.5 5.0 %collective-permute-start.19 = (bf16[8,128,256]{2,1,0:T(8,128)(2,1)S(1)}, bf16[8,128,256]{2,1,0:T(8,128)(2,1)S(1)}, u32[]{:S(2)}, u32[]{:S(2)}) collective-permute-start(bf16[8,128,256]{2,1,0:T(8,128)(2,1)S(1)} %collective-permute-done.16.rest_1_), channel_id=1, source_target_pairs={{96,120},{100,124},{104,96},{108,100},{112,104},{116,108},{120,112... | collective-permute-start | bytes 1572872 | tf_op jit(solution)/shard_map/ppermute | solution.py:62
  75.5 1.9 %collective-permute-start.18 = (bf16[6,128,256]{2,1,0:T(8,128)(2,1)S(1)}, bf16[6,128,256]{2,1,0:T(8,128)(2,1)S(1)}, u32[]{:S(2)}, u32[]{:S(2)}) collective-permute-start(bf16[6,128,256]{2,1,0:T(8,128)(2,1)S(1)} %collective-permute-done.14.rest_6_), channel_id=1, source_target_pairs={{32,40},{36,44},{40,48},{44,52},{48,56},{52,60},{56,32},{60,36},{6... | collective-permute-start | bytes 1179656 | tf_op jit(solution)/shard_map/ppermute | solution.py:62
  77.4 4.1 %far_part.4 = (bf16[4,512,256]{2,1,0:T(8,128)(2,1)S(1)}, f32[4,512,256]{2,1,0:T(8,128)S(1)}) custom-call(s32[3]{0:T(128)S(1)} %pad_add_fusion.scal, s32[256]{0:T(256)S(1)} %get-tuple-element.27.lists, s32[16]{0:T(128)S(1)} %get-tuple-element.28.counts, bf16[4,512,256]{2,1,0:T(8,128)(2,1)S(1)} %get-tuple-element.33.qa_in, ...), custom_call_target="tpu_custom_call" | custom-call | flops 1500000000 | bytes 6000000 | tf_op jit(solution)/shard_map/far_part/pallas_call | solution.py:359
  81.5 5.9 %collective-permute-done.18.rest_0_ = bf16[6,128,256]{2,1,0:T(8,128)(2,1)S(1)} collective-permute-done((bf16[6,128,256]{2,1,0:T(8,128)(2,1)S(1)}, bf16[6,128,256]{2,1,0:T(8,128)(2,1)S(1)}, u32[]{:S(2)}, u32[]{:S(2)}) %collective-permute-start.18) | collective-permute-done | bytes 393248 | tf_op jit(solution)/shard_map/ppermute | solution.py:62
  87.4 3.4 %far_part.5 = (bf16[256,512]{1,0:T(8,128)(2,1)S(1)}, bf16[256,512]{1,0:T(8,128)(2,1)S(1)}) custom-call(s32[3]{0:T(128)S(1)} %pad_add_fusion.scal, s32[256]{0:T(256)S(1)} %get-tuple-element.27.lists, s32[16]{0:T(128)S(1)} %get-tuple-element.28.counts, bf16[4,512,256]{2,1,0:T(8,128)(2,1)S(1)} %get-tuple-element.36.qa_in, ...), custom_call_target="tpu_custom_call" | custom-call | flops 1500000000 | bytes 6000000 | tf_op jit(solution)/shard_map/far_part/pallas_call | solution.py:359
  90.9 1.3 %own_part.1.part = f32[2,256,512]{2,1,0:T(8,128)S(1)} custom-call(s32[3]{0:T(128)S(1)} %pad_add_fusion.scal, bf16[256,512]{1,0:T(8,128)(2,1)S(1)} %get-tuple-element.39.ctx, bf16[1024,4096]{1,0:T(8,128)(2,1)S(1)} %bitcast.4), custom_call_target="tpu_custom_call" | custom-call | flops 300000000 | bytes 3000000 | tf_op jit(solution)/shard_map/own_part/pallas_call | solution.py:359
  92.4 1.3 %sib_part.1 = (bf16[256,512]{1,0:T(8,128)(2,1)S(1)}, bf16[256,512]{1,0:T(8,128)(2,1)S(1)}) custom-call(s32[3]{0:T(128)S(1)} %pad_add_fusion.scal, bf16[256,512]{1,0:T(8,128)(2,1)S(1)} %collective-permute-done.20.ctx_sib.ctx, f32[2,256,512]{2,1,0:T(8,128)S(1)} %own_part.1.part, bf16[1024,4096]{1,0:T(8,128)(2,1)S(1)} %bitcast.4), custom_call_target="tpu_custom_call" | custom-call | flops 300000000 | bytes 3000000 | tf_op jit(solution)/shard_map/sib_part/pallas_call | solution.py:359
  93.7 1.7 %collective-permute-start.22 = (bf16[256,512]{1,0:T(8,128)(2,1)S(1)}, bf16[256,512]{1,0:T(8,128)(2,1)S(1)}, u32[]{:S(2)}, u32[]{:S(2)}) collective-permute-start(bf16[256,512]{1,0:T(8,128)(2,1)S(1)} %get-tuple-element.44), channel_id=1, source_target_pairs={{0,1},{1,2},{2,3},{3,0},{4,5},{5,6},{6,7},{7,4},{8,9},{9,10},{10,1... | collective-permute-start | bytes 786440 | tf_op jit(solution)/shard_map/ppermute | solution.py:80
  95.4 1.7 %collective-permute-start.25 = (bf16[256,512]{1,0:T(8,128)(2,1)S(1)}, bf16[256,512]{1,0:T(8,128)(2,1)S(1)}, u32[]{:S(2)}, u32[]{:S(2)}) collective-permute-start(bf16[256,512]{1,0:T(8,128)(2,1)S(1)} %get-tuple-element.48), channel_id=1, source_target_pairs={{0,3},{1,0},{2,1},{3,2},{4,7},{5,4},{6,5},{7,6},{8,11},{9,8},{10,9... | collective-permute-start | bytes 786440 | tf_op jit(solution)/shard_map/ppermute | solution.py:80
  97.1 4.5 %other_shares.1 = (f32[256,512]{1,0:T(8,128)S(1)}, bf16[256,512]{1,0:T(8,128)(2,1)S(1)}, bf16[256,512]{1,0:T(8,128)(2,1)S(1)}, f32[256,512]{1,0:T(8,128)S(1)}, f...) custom-call(s32[3]{0:T(128)S(1)} %pad_add_fusion.scal, bf16[256,512]{1,0:T(8,128)(2,1)S(1)} %get-tuple-element.39.ctx, ...), custom_call_target="tpu_custom_call" | custom-call | flops 1600000000 | bytes 9000000 | tf_op jit(solution)/shard_map/other_shares/pallas_call | solution.py:359
  101.6 1.8 %collective-permute-start.21 = (bf16[256,512]{1,0:T(8,128)(2,1)S(1)}, bf16[256,512]{1,0:T(8,128)(2,1)S(1)}, u32[]{:S(2)}, u32[]{:S(2)}) collective-permute-start(bf16[256,512]{1,0:T(8,128)(2,1)S(1)} %get-tuple-element.42), channel_id=1, source_target_pairs={{0,3},{1,0},{2,1},{3,2},{4,7},{5,4},{6,5},{7,6},{8,11},{9,8},{10,9... | collective-permute-start | bytes 786440 | tf_op jit(solution)/shard_map/ppermute | solution.py:80
  104.1 1.6 %collective-permute-start.24 = (bf16[256,512]{1,0:T(8,128)(2,1)S(1)}, bf16[256,512]{1,0:T(8,128)(2,1)S(1)}, u32[]{:S(2)}, u32[]{:S(2)}) collective-permute-start(bf16[256,512]{1,0:T(8,128)(2,1)S(1)} %get-tuple-element.46), channel_id=1, source_target_pairs={{0,1},{1,2},{2,3},{3,0},{4,5},{5,6},{6,7},{7,4},{8,9},{9,10},{10,1... | collective-permute-start | bytes 786440 | tf_op jit(solution)/shard_map/ppermute | solution.py:80
  105.7 1.7 %collective-permute-start.26 = (bf16[256,512]{1,0:T(8,128)(2,1)S(1)}, bf16[256,512]{1,0:T(8,128)(2,1)S(1)}, u32[]{:S(2)}, u32[]{:S(2)}) collective-permute-start(bf16[256,512]{1,0:T(8,128)(2,1)S(1)} %add_convert_fusion.1), channel_id=1, source_target_pairs={{0,3},{1,0},{2,1},{3,2},{4,7},{5,4},{6,5},{7,6},{8,11},{9,8},{10,9... | collective-permute-start | bytes 786440 | tf_op jit(solution)/shard_map/ppermute | solution.py:80
  107.5 3.4 %collective-permute-done.21 = bf16[256,512]{1,0:T(8,128)(2,1)S(1)} collective-permute-done((bf16[256,512]{1,0:T(8,128)(2,1)S(1)}, bf16[256,512]{1,0:T(8,128)(2,1)S(1)}, u32[]{:S(2)}, u32[]{:S(2)}) %collective-permute-start.21) | collective-permute-done | bytes 262176 | tf_op jit(solution)/shard_map/ppermute | solution.py:80
  110.8 3.4 %collective-permute-done.23 = bf16[256,512]{1,0:T(8,128)(2,1)S(1)} collective-permute-done((bf16[256,512]{1,0:T(8,128)(2,1)S(1)}, bf16[256,512]{1,0:T(8,128)(2,1)S(1)}, u32[]{:S(2)}, u32[]{:S(2)}) %collective-permute-start.23) | collective-permute-done | bytes 262176 | tf_op jit(solution)/shard_map/ppermute | solution.py:80
  114.3 4.1 %collective-permute-done.24 = bf16[256,512]{1,0:T(8,128)(2,1)S(1)} collective-permute-done((bf16[256,512]{1,0:T(8,128)(2,1)S(1)}, bf16[256,512]{1,0:T(8,128)(2,1)S(1)}, u32[]{:S(2)}, u32[]{:S(2)}) %collective-permute-start.24) | collective-permute-done | bytes 262176 | tf_op jit(solution)/shard_map/ppermute | solution.py:80
  (60 shorter events, 13.7 us)
Async XLA Ops:
  0.0 39.5 %copy-start.6 = (s32[32]{0:T(128)S(1)}, s32[32]{0:T(128)}, u32[]{:S(2)}) copy-start(s32[32]{0:T(128)} %constant.24.clone.table) | copy-start | bytes 388
  0.0 39.5 %copy-start.5 = (s32[8]{0:T(128)S(1)}, s32[8]{0:T(128)}, u32[]{:S(2)}) copy-start(s32[8]{0:T(128)} %win.1) | copy-start | bytes 100
  0.0 39.5 %copy-start.4 = (s32[8,8]{1,0:T(8,128)S(1)}, s32[8,8]{1,0:T(8,128)}, u32[]{:S(2)}) copy-start(s32[8,8]{1,0:T(8,128)} %slash.1) | copy-start | bytes 772
  0.0 1.6 %collective-permute-start.1 = (bf16[256,256]{1,0:T(8,128)(2,1)}, bf16[256,256]{1,0:T(8,128)(2,1)S(1)}, u32[]{:S(2)}, u32[]{:S(2)}) collective-permute-start(bf16[256,256]{1,0:T(8,128)(2,1)} %k_ref.3), channel_id=1, source_target_pairs={{0,4},{4,0},{8,12},{12,8},{16,20},{20,16},{24,28},{28,24},{32,36},... | collective-permute-start | bytes 393224 | tf_op jit(solution)/shard_map/ppermute | solution.py:76
  0.1 1.7 %collective-permute-start.2 = (bf16[256,256]{1,0:T(8,128)(2,1)}, bf16[256,256]{1,0:T(8,128)(2,1)S(1)}, u32[]{:S(2)}, u32[]{:S(2)}) collective-permute-start(bf16[256,256]{1,0:T(8,128)(2,1)} %v_ref.3), channel_id=1, source_target_pairs={{0,4},{4,0},{8,12},{12,8},{16,20},{20,16},{24,28},{28,24},{32,36},... | collective-permute-start | bytes 393224 | tf_op jit(solution)/shard_map/ppermute | solution.py:76
  4.3 35.2 %copy-start.3 = (bf16[256,1024]{1,0:T(8,128)(2,1)S(1)}, bf16[256,1024]{1,0:T(8,128)(2,1)}, u32[]{:S(2)}) copy-start(bf16[256,1024]{1,0:T(8,128)(2,1)} %q.1) | copy-start | bytes 1572868
  5.0 11.9 %collective-permute-start.4 = (bf16[2,128,256]{2,1,0:T(8,128)(2,1)S(1)}, bf16[2,128,256]{2,1,0:T(8,128)(2,1)S(1)}, u32[]{:S(2)}, u32[]{:S(2)}) collective-permute-start(bf16[2,128,256]{2,1,0:T(8,128)(2,1)S(1)} %pick.1.rest_0_), channel_id=1, source_target_pairs={{0,64},{4,68},{8,72},{12,76},{16,80},{20,84},{24,88},{28,92},{32,9... | collective-permute-start | bytes 393224 | tf_op jit(solution)/shard_map/ppermute | solution.py:72
  6.3 12.4 %collective-permute-start.9 = (bf16[2,128,256]{2,1,0:T(8,128)(2,1)S(1)}, bf16[2,128,256]{2,1,0:T(8,128)(2,1)S(1)}, u32[]{:S(2)}, u32[]{:S(2)}) collective-permute-start(bf16[2,128,256]{2,1,0:T(8,128)(2,1)S(1)} %pick.1.rest_0_), channel_id=1, source_target_pairs={{0,32},{4,36},{8,40},{12,44},{16,48},{20,52},{24,56},{28,60},{32,6... | collective-permute-start | bytes 393224 | tf_op jit(solution)/shard_map/ppermute | solution.py:72
  9.3 30.2 %collective-permute-start = (bf16[256,1024]{1,0:T(8,128)(2,1)}, bf16[256,1024]{1,0:T(8,128)(2,1)S(1)}, u32[]{:S(2)}, u32[]{:S(2)}) collective-permute-start(bf16[256,1024]{1,0:T(8,128)(2,1)} %q.1), channel_id=1, source_target_pairs={{0,4},{4,0},{8,12},{12,8},{16,20},{20,16},{24,28},{28,24},{32,36},... | collective-permute-start | bytes 1572872 | tf_op jit(solution)/shard_map/ppermute | solution.py:76
  9.4 11.4 %collective-permute-start.10 = (bf16[2,128,256]{2,1,0:T(8,128)(2,1)S(1)}, bf16[2,128,256]{2,1,0:T(8,128)(2,1)S(1)}, u32[]{:S(2)}, u32[]{:S(2)}) collective-permute-start(bf16[2,128,256]{2,1,0:T(8,128)(2,1)S(1)} %pick.1.rest_0_), channel_id=1, source_target_pairs={{0,224},{4,228},{8,232},{12,236},{16,240},{20,244},{24,248},{28,25... | collective-permute-start | bytes 393224 | tf_op jit(solution)/shard_map/ppermute | solution.py:72
  10.1 18.8 %collective-permute-start.7 = (bf16[2,128,256]{2,1,0:T(8,128)(2,1)S(1)}, bf16[2,128,256]{2,1,0:T(8,128)(2,1)S(1)}, u32[]{:S(2)}, u32[]{:S(2)}) collective-permute-start(bf16[2,128,256]{2,1,0:T(8,128)(2,1)S(1)} %pick.1.rest_0_), channel_id=1, source_target_pairs={{0,192},{4,196},{8,200},{12,204},{16,208},{20,212},{24,216},{28,22... | collective-permute-start | bytes 393224 | tf_op jit(solution)/shard_map/ppermute | solution.py:72
  17.0 15.3 %collective-permute-start.8 = (bf16[2,128,256]{2,1,0:T(8,128)(2,1)S(1)}, bf16[2,128,256]{2,1,0:T(8,128)(2,1)S(1)}, u32[]{:S(2)}, u32[]{:S(2)}) collective-permute-start(bf16[2,128,256]{2,1,0:T(8,128)(2,1)S(1)} %pick.1.rest_0_), channel_id=1, source_target_pairs={{0,160},{4,164},{8,168},{12,172},{16,176},{20,180},{24,184},{28,18... | collective-permute-start | bytes 393224 | tf_op jit(solution)/shard_map/ppermute | solution.py:72
  18.7 17.0 %collective-permute-start.5 = (bf16[2,128,256]{2,1,0:T(8,128)(2,1)S(1)}, bf16[2,128,256]{2,1,0:T(8,128)(2,1)S(1)}, u32[]{:S(2)}, u32[]{:S(2)}) collective-permute-start(bf16[2,128,256]{2,1,0:T(8,128)(2,1)S(1)} %collective-permute-done.4), channel_id=1, source_target_pairs={{64,96},{68,100},{72,104},{76,108},{80,112},{84,116},{88,120},{92,... | collective-permute-start | bytes 393224 | tf_op jit(solution)/shard_map/ppermute | solution.py:72
  20.8 18.6 %collective-permute-start.6 = (bf16[2,128,256]{2,1,0:T(8,128)(2,1)S(1)}, bf16[2,128,256]{2,1,0:T(8,128)(2,1)S(1)}, u32[]{:S(2)}, u32[]{:S(2)}) collective-permute-start(bf16[2,128,256]{2,1,0:T(8,128)(2,1)S(1)} %collective-permute-done.4), channel_id=1, source_target_pairs={{64,128},{68,132},{72,136},{76,140},{80,144},{84,148},{88,152},{92... | collective-permute-start | bytes 393224 | tf_op jit(solution)/shard_map/ppermute | solution.py:72
  28.9 10.6 %collective-permute-start.3 = (bf16[128,256]{1,0:T(8,128)(2,1)S(1)}, bf16[128,256]{1,0:T(8,128)(2,1)S(1)}, u32[]{:S(2)}, u32[]{:S(2)}) collective-permute-start(bf16[128,256]{1,0:T(8,128)(2,1)S(1)} %tail.1), channel_id=1, source_target_pairs={{0,8},{4,12},{8,16},{12,20},{16,24},{20,28},{24,32},{28,36},{32,40... | collective-permute-start | bytes 196616 | tf_op jit(solution)/shard_map/ppermute | solution.py:409
  32.3 32.6 %collective-permute-start.14 = (bf16[6,128,256]{2,1,0:T(8,128)(2,1)S(1)}, bf16[6,128,256]{2,1,0:T(8,128)(2,1)S(1)}, u32[]{:S(2)}, u32[]{:S(2)}) collective-permute-start(bf16[6,128,256]{2,1,0:T(8,128)(2,1)S(1)} %constant_dynamic-update-slice_fusion.rest_1_), channel_id=1, source_target_pairs={{32,40},{36,44},{40,48},{44,52},{48,56},{52,60},{56,32},{60,36},{6... | collective-permute-start | bytes 1179656 | tf_op jit(solution)/shard_map/ppermute | solution.py:62
  35.7 29.2 %collective-permute-start.15 = (bf16[6,128,256]{2,1,0:T(8,128)(2,1)S(1)}, bf16[6,128,256]{2,1,0:T(8,128)(2,1)S(1)}, u32[]{:S(2)}, u32[]{:S(2)}) collective-permute-start(bf16[6,128,256]{2,1,0:T(8,128)(2,1)S(1)} %constant_dynamic-update-slice_fusion.rest_1_), channel_id=1, source_target_pairs={{32,56},{36,60},{40,32},{44,36},{48,40},{52,44},{56,48},{60,52},{6... | collective-permute-start | bytes 1179656 | tf_op jit(solution)/shard_map/ppermute | solution.py:62
  44.0 26.4 %collective-permute-start.16 = (bf16[8,128,256]{2,1,0:T(8,128)(2,1)S(1)}, bf16[8,128,256]{2,1,0:T(8,128)(2,1)S(1)}, u32[]{:S(2)}, u32[]{:S(2)}) collective-permute-start(bf16[8,128,256]{2,1,0:T(8,128)(2,1)S(1)} %pad_maximum_fusion.rest_5_), channel_id=1, source_target_pairs={{96,120},{100,124},{104,96},{108,100},{112,104},{116,108},{120,112... | collective-permute-start | bytes 1572872 | tf_op jit(solution)/shard_map/ppermute | solution.py:62
  46.0 6.3 %collective-permute-start.11 = (bf16[2,128,256]{2,1,0:T(8,128)(2,1)S(1)}, bf16[2,128,256]{2,1,0:T(8,128)(2,1)S(1)}, u32[]{:S(2)}, u32[]{:S(2)}) collective-permute-start(bf16[2,128,256]{2,1,0:T(8,128)(2,1)S(1)} %pick.1.rest_0_), channel_id=1, source_target_pairs={{0,8},{4,12},{8,16},{12,20},{16,24},{20,28},{24,0},{28,4},{32,40},... | collective-permute-start | bytes 393224 | tf_op jit(solution)/shard_map/ppermute | solution.py:62
  48.0 13.7 %collective-permute-start.12 = (bf16[2,128,256]{2,1,0:T(8,128)(2,1)S(1)}, bf16[2,128,256]{2,1,0:T(8,128)(2,1)S(1)}, u32[]{:S(2)}, u32[]{:S(2)}) collective-permute-start(bf16[2,128,256]{2,1,0:T(8,128)(2,1)S(1)} %pick.1.rest_0_), channel_id=1, source_target_pairs={{0,24},{4,28},{8,0},{12,4},{16,8},{20,12},{24,16},{28,20},{32,56},... | collective-permute-start | bytes 393224 | tf_op jit(solution)/shard_map/ppermute | solution.py:62
  52.3 12.6 %collective-permute-start.13 = (bf16[2,128,256]{2,1,0:T(8,128)(2,1)S(1)}, bf16[2,128,256]{2,1,0:T(8,128)(2,1)S(1)}, u32[]{:S(2)}, u32[]{:S(2)}) collective-permute-start(bf16[2,128,256]{2,1,0:T(8,128)(2,1)S(1)} %collective-permute-done.11.rest_2_), channel_id=1, source_target_pairs={{0,8},{4,12},{8,16},{12,20},{16,24},{20,28},{24,0},{28,4},{32,40},... | collective-permute-start | bytes 393224 | tf_op jit(solution)/shard_map/ppermute | solution.py:62
  61.8 15.6 %collective-permute-start.17 = (bf16[8,128,256]{2,1,0:T(8,128)(2,1)S(1)}, bf16[8,128,256]{2,1,0:T(8,128)(2,1)S(1)}, u32[]{:S(2)}, u32[]{:S(2)}) collective-permute-start(bf16[8,128,256]{2,1,0:T(8,128)(2,1)S(1)} %pad_maximum_fusion.rest_5_), channel_id=1, source_target_pairs={{96,104},{100,108},{104,112},{108,116},{112,120},{116,124},{120,96... | collective-permute-start | bytes 1572872 | tf_op jit(solution)/shard_map/ppermute | solution.py:62
  64.9 26.0 %slice-start = ((s8[8388608]{0:T(1024)(128)(4,1)}), s8[4194304]{0:T(1024)(128)(4,1)S(1)}, s32[]{:S(2)}) async-start(s8[8388608]{0:T(1024)(128)(4,1)} %bitcast.3), calls=%async_computation | async-start | bytes 8388608
  70.5 17.0 %collective-permute-start.19 = (bf16[8,128,256]{2,1,0:T(8,128)(2,1)S(1)}, bf16[8,128,256]{2,1,0:T(8,128)(2,1)S(1)}, u32[]{:S(2)}, u32[]{:S(2)}) collective-permute-start(bf16[8,128,256]{2,1,0:T(8,128)(2,1)S(1)} %collective-permute-done.16.rest_1_), channel_id=1, source_target_pairs={{96,120},{100,124},{104,96},{108,100},{112,104},{116,108},{120,112... | collective-permute-start | bytes 1572872 | tf_op jit(solution)/shard_map/ppermute | solution.py:62
  75.5 12.0 %collective-permute-start.18 = (bf16[6,128,256]{2,1,0:T(8,128)(2,1)S(1)}, bf16[6,128,256]{2,1,0:T(8,128)(2,1)S(1)}, u32[]{:S(2)}, u32[]{:S(2)}) collective-permute-start(bf16[6,128,256]{2,1,0:T(8,128)(2,1)S(1)} %collective-permute-done.14.rest_6_), channel_id=1, source_target_pairs={{32,40},{36,44},{40,48},{44,52},{48,56},{52,60},{56,32},{60,36},{6... | collective-permute-start | bytes 1179656 | tf_op jit(solution)/shard_map/ppermute | solution.py:62
  90.8 1.6 %collective-permute-start.20 = (bf16[256,512]{1,0:T(8,128)(2,1)S(1)}, bf16[256,512]{1,0:T(8,128)(2,1)S(1)}, u32[]{:S(2)}, u32[]{:S(2)}) collective-permute-start(bf16[256,512]{1,0:T(8,128)(2,1)S(1)} %get-tuple-element.40), channel_id=1, source_target_pairs={{0,4},{4,0},{8,12},{12,8},{16,20},{20,16},{24,28},{28,24},{32,36},... | collective-permute-start | bytes 786440 | tf_op jit(solution)/shard_map/ppermute | solution.py:76
  93.7 9.9 %collective-permute-start.22 = (bf16[256,512]{1,0:T(8,128)(2,1)S(1)}, bf16[256,512]{1,0:T(8,128)(2,1)S(1)}, u32[]{:S(2)}, u32[]{:S(2)}) collective-permute-start(bf16[256,512]{1,0:T(8,128)(2,1)S(1)} %get-tuple-element.44), channel_id=1, source_target_pairs={{0,1},{1,2},{2,3},{3,0},{4,5},{5,6},{6,7},{7,4},{8,9},{9,10},{10,1... | collective-permute-start | bytes 786440 | tf_op jit(solution)/shard_map/ppermute | solution.py:80
  95.4 10.3 %collective-permute-start.25 = (bf16[256,512]{1,0:T(8,128)(2,1)S(1)}, bf16[256,512]{1,0:T(8,128)(2,1)S(1)}, u32[]{:S(2)}, u32[]{:S(2)}) collective-permute-start(bf16[256,512]{1,0:T(8,128)(2,1)S(1)} %get-tuple-element.48), channel_id=1, source_target_pairs={{0,3},{1,0},{2,1},{3,2},{4,7},{5,4},{6,5},{7,6},{8,11},{9,8},{10,9... | collective-permute-start | bytes 786440 | tf_op jit(solution)/shard_map/ppermute | solution.py:80
  101.6 9.2 %collective-permute-start.21 = (bf16[256,512]{1,0:T(8,128)(2,1)S(1)}, bf16[256,512]{1,0:T(8,128)(2,1)S(1)}, u32[]{:S(2)}, u32[]{:S(2)}) collective-permute-start(bf16[256,512]{1,0:T(8,128)(2,1)S(1)} %get-tuple-element.42), channel_id=1, source_target_pairs={{0,3},{1,0},{2,1},{3,2},{4,7},{5,4},{6,5},{7,6},{8,11},{9,8},{10,9... | collective-permute-start | bytes 786440 | tf_op jit(solution)/shard_map/ppermute | solution.py:80
  103.7 10.5 %collective-permute-start.23 = (bf16[256,512]{1,0:T(8,128)(2,1)S(1)}, bf16[256,512]{1,0:T(8,128)(2,1)S(1)}, u32[]{:S(2)}, u32[]{:S(2)}) collective-permute-start(bf16[256,512]{1,0:T(8,128)(2,1)S(1)} %add_convert_fusion.3), channel_id=1, source_target_pairs={{0,1},{1,2},{2,3},{3,0},{4,5},{5,6},{6,7},{7,4},{8,9},{9,10},{10,1... | collective-permute-start | bytes 786440 | tf_op jit(solution)/shard_map/ppermute | solution.py:80
  104.1 14.3 %collective-permute-start.24 = (bf16[256,512]{1,0:T(8,128)(2,1)S(1)}, bf16[256,512]{1,0:T(8,128)(2,1)S(1)}, u32[]{:S(2)}, u32[]{:S(2)}) collective-permute-start(bf16[256,512]{1,0:T(8,128)(2,1)S(1)} %get-tuple-element.46), channel_id=1, source_target_pairs={{0,1},{1,2},{2,3},{3,0},{4,5},{5,6},{6,7},{7,4},{8,9},{9,10},{10,1... | collective-permute-start | bytes 786440 | tf_op jit(solution)/shard_map/ppermute | solution.py:80
  105.7 12.7 %collective-permute-start.26 = (bf16[256,512]{1,0:T(8,128)(2,1)S(1)}, bf16[256,512]{1,0:T(8,128)(2,1)S(1)}, u32[]{:S(2)}, u32[]{:S(2)}) collective-permute-start(bf16[256,512]{1,0:T(8,128)(2,1)S(1)} %add_convert_fusion.1), channel_id=1, source_target_pairs={{0,3},{1,0},{2,1},{3,2},{4,7},{5,4},{6,5},{7,6},{8,11},{9,8},{10,9... | collective-permute-start | bytes 786440 | tf_op jit(solution)/shard_map/ppermute | solution.py:80
  (4 other events, 16.0 us)

commit v4 on v3

--- a/solution.py
+++ b/solution.py
@@ -19,10 +19,11 @@
 LIMIT = 100.0
 VMEM_BYTES = 40 * 1024 * 1024
 SLOT_BITS = 6
+AT_BLOCKS, AT_WINDOW, AT_SLASH, AT_TABLE = 8, 136, 144, 208
 AT_ONCE = 4
 BF16, F32, I32 = jnp.bfloat16, jnp.float32, jnp.int32
 
-STACKS = ((-1, -2, 1), (-3, -4, 2, 3))
+STACKS = ((0, -1, -2, 1), (-3, -4, 2, 3))
 
 
 def slot_table():
@@ -33,18 +34,16 @@
             table[dz % NZ, dx % NX] = (group << SLOT_BITS) | (base + 2 * i)
 
     first, second = STACKS
-    put(0, 0, (0,), 0)
-    put(0, 2, first, 0)
-    put(0, 8, (0,), -1)
-    put(0, 10, (0,), 1)
-    put(0, 12, (0,), 2)
-    put(0, 14, second, 0)
-    put(0, 22, first, -1)
-    put(0, 28, first, 1)
-    put(1, 0, second, -1)
-    put(1, 8, second, 1)
-    put(2, 0, first, 2)
-    put(2, 6, second, 2)
+    put(0, 0, first, 0)
+    put(0, 8, first, -1)
+    put(0, 16, first, 1)
+    put(0, 24, (0,), 2)
+    for at, dz in ((4, -3), (8, -4), (14, 2), (18, 3)):
+        put(1, at, (dz,), 0)
+    for at, dz in ((2, -1), (6, -2), (10, -3), (12, -4), (16, 1), (20, 2), (22, 3)):
+        put(1, at, (dz,), 2)
+    put(2, 0, second, -1)
+    put(2, 8, second, 1)
     return table.reshape(-1)
 
 
@@ -62,16 +61,22 @@
     return lax.ppermute(value, "seq", pairs)
 
 
-def along_z(value, dz, lowest, count):
+def up(value, lowest):
     pairs = [
-        (seq_at(z, x, c), seq_at((z + dz) % NZ, x, c))
-        for z in range(lowest, lowest + count)
+        (seq_at(z, x, c), seq_at(z + 1, x, c))
+        for z in range(lowest, NZ - 1)
         for x in range(NX)
         for c in range(2)
     ]
     return lax.ppermute(value, "seq", pairs)
 
 
+def down(value, hops):
+    steps = sorted({((s - n + 1) % NZ, (s - n) % NZ) for s in range(3) for n in hops})
+    pairs = [(seq_at(a, x, c), seq_at(b, x, c)) for a, b in steps for x in range(NX) for c in range(2)]
+    return lax.ppermute(value, "seq", pairs)
+
+
 def swap_cores(value):
     return lax.ppermute(value, "seq", [(i, i ^ 1) for i in range(2 * NX * NZ)])
 
@@ -88,31 +93,31 @@
     return pl.ds(pl.multiple_of(core * width, width), width)
 
 
-def pick_kernel(scal, blocks, k_ref, v_ref, k_sib, v_sib, out_ref):
+def pick_kernel(scal, blocks, k_ref, v_ref, k_sib, v_sib, out_ref, tail_ref, buf, sem):
     core, place = scal[0], scal[1]
-    head = lax.broadcasted_iota(I32, blocks.shape, 0)
-    of_core = (head >= core * GROUP) & (head < (core + 1) * GROUP)
-    for k, v, parity in ((k_ref, v_ref, core), (k_sib, v_sib, 1 - core)):
-        shard = place - core + parity
-        hit = jnp.where(of_core & (blocks[...] == 2 * shard + 1), 1.0, 0.0)
-        half = (jnp.max(hit) > 0.5).astype(I32)
-        rows = pl.ds(pl.multiple_of(half * BLK, BLK), BLK)
-        out_ref[parity, :, :HD] = k[rows, lanes(core)]
-        out_ref[parity, :, HD:] = v[rows, lanes(core)]
-
-
-def tail_kernel(scal, k_ref, v_ref, k_sib, v_sib, out_ref):
-    core = scal[0]
-
-    @pl.when(core == 1)
-    def _():
-        out_ref[:, :HD] = k_ref[BLK:, HD:]
-        out_ref[:, HD:] = v_ref[BLK:, HD:]
-
-    @pl.when(core == 0)
-    def _():
-        out_ref[:, :HD] = k_sib[BLK:, :HD]
-        out_ref[:, HD:] = v_sib[BLK:, :HD]
+    copies = []
+    for n, ref in enumerate((k_ref, v_ref, k_sib, v_sib)):
+        copies.append(pltpu.make_async_copy(ref, buf.at[n], sem.at[n]))
+    for copy in copies:
+        copy.start()
+    own, sib = 2 * place + 1, 2 * (place + 1 - 2 * core) + 1
+
+    def look(n, found):
+        h = n >> 4
+        b = blocks[core * GROUP + h, n & 15]
+        return found[0] | (b == own).astype(I32), found[1] | (b == sib).astype(I32)
+
+    zero = jnp.int32(0)
+    halves = lax.fori_loop(0, GROUP * PICKS, look, (zero, zero), unroll=8)
+    for copy in copies:
+        copy.wait()
+    for n, parity in enumerate((core, 1 - core)):
+        rows = pl.ds(pl.multiple_of(halves[n] * BLK, BLK), BLK)
+        out_ref[parity, :, :HD] = buf[2 * n, rows, lanes(core)]
+        out_ref[parity, :, HD:] = buf[2 * n + 1, rows, lanes(core)]
+    later = 2 * (1 - core)
+    tail_ref[:, :HD] = buf[later, BLK:, lanes(core)]
+    tail_ref[:, HD:] = buf[later + 1, BLK:, lanes(core)]
 
 
 def split3(m):
@@ -132,10 +137,23 @@
 
 
 def local_kernel(
-    scal, blocks, win, slash, table, q, q_sib, k, k_sib, v, v_sib, halo,
-    qa_ref, acc_ref, list_ref, count_ref, qs, ks, vs, named,
+    ints, q_ref, q_sib_ref, k_ref, k_sib_ref, v_ref, v_sib_ref, halo_ref,
+    qa_ref, acc_ref, list_ref, count_ref, q_buf, kv_buf, halo, qs, ks, vs, named, sem,
 ):
-    core, place = scal[0], scal[1]
+    q, q_sib = q_buf.at[0], q_buf.at[1]
+    k, k_sib, v, v_sib = (kv_buf.at[n] for n in range(4))
+    copies = [
+        pltpu.make_async_copy(source, into, sem.at[n])
+        for n, (source, into) in enumerate(
+            (
+                (q_ref, q), (q_sib_ref, q_sib), (k_ref, k), (k_sib_ref, k_sib),
+                (v_ref, v), (v_sib_ref, v_sib), (halo_ref, halo),
+            )
+        )
+    ]
+    for copy in copies:
+        copy.start()
+    core, place = ints[0], ints[1]
     chip = place >> 1
     z, x = chip >> 2, chip & 3
 
@@ -145,9 +163,9 @@
         named[n] = 0
 
     def note(n, carry):
-        h, column = n >> 4, n & 15
-        b = blocks[core * GROUP + h, column]
-        entry = table[((((b >> 4) - z) & 7) << 2) + (((b >> 2) - x) & 3)]
+        h = n >> 4
+        b = ints[AT_BLOCKS + core * (GROUP * PICKS) + n]
+        entry = ints[AT_TABLE + ((((b >> 4) - z) & 7) << 2) + (((b >> 2) - x) & 3)]
         key = ((entry >> SLOT_BITS) << 2) + h
         count = count_ref[key]
         list_ref[(key << 4) + count] = (entry & ((1 << SLOT_BITS) - 1)) + ((b >> 1) & 1)
@@ -159,6 +177,8 @@
 
     lax.fori_loop(0, GROUP * PICKS, note, 0, unroll=4)
 
+    for copy in copies:
+        copy.wait()
     mine, sib = core * 2 * BLK, (1 - core) * 2 * BLK
     ks[:BLK] = halo[:, :HD]
     vs[:BLK] = halo[:, HD:]
@@ -176,11 +196,11 @@
     prev_gap = diag_gap + BLK
     for h in range(GROUP):
         head = core * GROUP + h
-        diag_ok = diag_gap < win[head]
-        prev_ok = prev_gap < win[head]
+        diag_ok = diag_gap < ints[AT_WINDOW + head]
+        prev_ok = prev_gap < ints[AT_WINDOW + head]
         for n in range(8):
-            diag_ok = diag_ok | (diag_gap == slash[head, n])
-            prev_ok = prev_ok | (prev_gap == slash[head, n])
+            diag_ok = diag_ok | (diag_gap == ints[AT_SLASH + head * 8 + n])
+            prev_ok = prev_ok | (prev_gap == ints[AT_SLASH + head * 8 + n])
         scores = dot_f32(qs[h], ks[...], ((1,), (1,)))
         weights = []
         for i in range(4):
@@ -355,14 +375,16 @@
     return pl.BlockSpec(memory_space=space)
 
 
-def call(kernel, name, outs, args, spaces, scratch=(), out_spaces=None, flops=0, moved=0):
+def call(
+    kernel, name, outs, args, spaces, scratch=(), out_spaces=None, flops=0, moved=0, vmem_bytes=VMEM_BYTES
+):
     return pl.pallas_call(
         kernel,
         out_shape=outs,
         in_specs=[spec(s) for s in spaces],
         out_specs=[spec(s) for s in (out_spaces or [pltpu.VMEM] * len(outs))],
         scratch_shapes=list(scratch),
-        compiler_params=pltpu.CompilerParams(vmem_limit_bytes=VMEM_BYTES),
+        compiler_params=pltpu.CompilerParams(vmem_limit_bytes=vmem_bytes),
         cost_estimate=pl.CostEstimate(flops=flops, bytes_accessed=moved, transcendentals=0),
         name=name,
     )(*args)
@@ -378,35 +400,39 @@
     me = lax.axis_index("tp").astype(I32)
     core = place % 2
     scal = jnp.stack([core, place, me])
+    ints = jnp.concatenate(
+        [
+            jnp.pad(scal, (0, AT_BLOCKS - 3)),
+            vert_blocks.reshape(-1),
+            window_size,
+            slash_offsets.reshape(-1),
+            jnp.asarray(slot_table()),
+        ]
+    )
     block = shape((1, BLK, 2 * HD), BF16)
 
     k_sib = swap_cores(key_states)
     v_sib = swap_cores(value_states)
     q_sib = swap_cores(queries)
-    unit = call(
-        pick_kernel, "pick", [shape((2, BLK, 2 * HD), BF16)],
-        (scal, vert_blocks, key_states, value_states, k_sib, v_sib), [smem] + [vmem] * 5,
+    unit, tail = call(
+        pick_kernel, "pick", [shape((2, BLK, 2 * HD), BF16), shape((BLK, 2 * HD), BF16)],
+        (scal, vert_blocks, key_states, value_states, k_sib, v_sib),
+        [smem] * 2 + [anywhere] * 4,
+        [pltpu.VMEM((4,) + key_states.shape, BF16), pltpu.SemaphoreType.DMA((4,))],
         moved=1_000_000,
-    )[0]
-
-    up1 = along_z(unit, 1, 0, NZ - 1)
-    down1 = along_z(unit, -1, 0, 1)
-    up2 = along_z(unit, 2, 0, NZ - 2)
-    down2 = along_z(unit, -2, 0, 2)
-    down3 = along_z(unit, -3, 0, 3)
-    right0, left0 = along_x(unit, 1, 0), along_x(unit, -1, 0)
-    up3 = along_z(up2, 1, 2, NZ - 3)
-    up4 = along_z(up2, 2, 2, NZ - 4)
-    opposite0 = along_x(right0, 1, 0)
-    first = jnp.concatenate([up1, up2, down1], axis=0)
-    right1, left1 = along_x(first, 1, 1), along_x(first, -1, 1)
-    second = jnp.concatenate([up3, up4, down2, down3], axis=0)
-
-    tail = call(
-        tail_kernel, "tail", [shape((BLK, 2 * HD), BF16)],
-        (scal, key_states, value_states, k_sib, v_sib), [smem] + [vmem] * 4, moved=1_000_000,
-    )[0]
+        vmem_bytes=60 * 1024 * 1024,
+    )
+
     halo = lax.ppermute(tail, "seq", [(i, i + 2) for i in range(2 * NX * NZ - 2)])
+
+    up1, down1 = up(unit, 0), down(unit, (1,))
+    opposite = along_x(unit, 2, 0)
+    up1, halo = lax.optimization_barrier((up1, halo))
+    up2 = up(jnp.concatenate([up1, opposite], axis=0), 0)
+    down2 = down(jnp.concatenate([down1, opposite], axis=0), (2, 1))
+    up3, down3 = up(up2, 1), down(down2, (3, 2))
+    first = jnp.concatenate([unit, up1, up2[:2], down1], axis=0)
+    right1, left1 = along_x(first, 1, 0), along_x(first, -1, 0)
 
     rows = 2 * queries.shape[0]
     wide = (GROUP, rows, 2 * HD)
@@ -415,19 +441,22 @@
         "near_part",
         [shape(wide, BF16), shape(wide, F32), shape((16 * PICKS,), I32), shape((16,), I32)],
         (
-            scal, vert_blocks, window_size, slash_offsets, jnp.asarray(slot_table()),
-            queries, q_sib, key_states, k_sib, value_states, v_sib, halo,
+            ints, queries, q_sib, key_states, k_sib, value_states, v_sib, halo,
         ),
-        [smem] * 5 + [vmem] * 7,
+        [smem] + [anywhere] * 7,
         [
+            pltpu.VMEM((2,) + queries.shape, BF16),
+            pltpu.VMEM((4,) + key_states.shape, BF16),
+            pltpu.VMEM((BLK, 2 * HD), BF16),
             pltpu.VMEM((GROUP, rows, HD), BF16),
             pltpu.VMEM((rows + BLK, HD), BF16),
             pltpu.VMEM((rows + BLK, HD), BF16),
             pltpu.SMEM((GROUP * 8,), I32),
+            pltpu.SemaphoreType.DMA((7,)),
         ],
         [vmem, vmem, smem, smem],
-        flops=1_000_000_000,
-        moved=8_000_000,
+        flops=5_000_000_000,
+        moved=100_000,
     )
 
     def far(n, pieces, qa, acc):
@@ -450,18 +479,18 @@
             (scal, lists, counts, qa, acc, *pieces),
             [smem] * 3 + [vmem] * 2 + [anywhere] * len(sizes),
             scratch,
-            flops=1_500_000_000,
-            moved=6_000_000,
+            flops=6_000_000_000,
+            moved=100_000,
         )
 
+    up4 = up(up3, 2)
+    second = jnp.concatenate([up3[:2], up4[:2], down2[:2], down3[:2]], axis=0)
+    up5, down4 = up(up4[2:], 3), down(down3[2:], (3,))
+    qa, acc = far(0, [first, right1, left1, opposite], qa, acc)
     second, acc = lax.optimization_barrier((second, acc))
     right2, left2 = along_x(second, 1, 3), along_x(second, -1, 3)
-    opposite1 = along_x(right1, 1, 1)
-    qa, acc = far(0, [unit, first, right0, left0, opposite0, second, right1, left1], qa, acc)
-    relayed, acc = lax.optimization_barrier((left2, acc))
-    opposite2 = along_x(relayed, -1, 3)
-    qa, acc = far(1, [right2, left2], qa, acc)
-    ctx_mine, ctx_other = far(2, [opposite1, opposite2], qa, acc)
+    qa, acc = far(1, [up2, up3, up4, up5, down2, down3, down4], qa, acc)
+    ctx_mine, ctx_other = far(2, [right2, left2], qa, acc)
     ctx_sib = swap_cores(ctx_other)
 
     half_rows, half = rows // 2, out_weight.shape[1] // 8

time: 121 us -> 108 us (0.89)
  waiting for transfers between devices: 42.3 us -> 24.3 us
  local copies, waits for them, and re-layouts: 2.56 us -> 4.3 us
  other arithmetic: 1.37 us -> 2.96 us
    ppermute x9 -> x5, waiting for transfers between devices: 17.7 us -> 2.56 us  [along_x(): return lax.ppermute(value, 'seq', pairs)]
    ppermute x7 -> x9, starting transfers between devices: 10.8 us -> 20.8 us  [the longest x5 11.6 us: up(): return lax.ppermute(value, 'seq', pairs)]
    ppermute x9 -> x5, starting transfers between devices: 23.1 us -> 13.5 us  [along_x(): return lax.ppermute(value, 'seq', pairs)]
    ppermute x7 -> x9, waiting for transfers between devices: 12.3 us -> 5.23 us  [the longest x5 5.22 us: up(): return lax.ppermute(value, 'seq', pairs)]
    ppermute x1, waiting for transfers between devices: 0.01 us -> 5.97 us  [local(): lax.ppermute(tail, 'seq', [(i, i + 2) for i in range(2 * NX * NZ - 2)])]
    reshape x0 -> x2, local copies, waits for them, and re-layouts: none -> 1.53 us  [the longest x1 0.77 us: local(): slash_offsets.reshape(-1)]
    ppermute x6, starting transfers between devices: 8.88 us -> 10.2 us  [tp_shift(): return lax.ppermute(value, 'tp', [(i, (i + step) % 4) for i in range(4)])]
    unnamed x20, local copies, waits for them, and re-layouts: 2.55 us -> 1.28 us
  transfers between devices with their start and end apart: 27 -> 25, of which waited for: 13 -> 12; matrix products, arithmetic and copies ran while one was open for 0% -> 5% of each run, Pallas kernels for 17% -> 18%
where the time goes in v4:
time: 108 us; the launch traced here: 106 us
  starting transfers between devices  47.8 us (44%)
  Pallas kernels  26.1 us (24%)
  waiting for transfers between devices  24.3 us (22%)
  local copies, waits for them, and re-layouts  4.3 us (4%)
  other arithmetic  2.96 us (3%)
    pallas_call x8, Pallas kernels, call(): pl.pallas_call(kernel, out_shape=outs, in_specs=[spec(s) for s in spaces]...  26.1 us
    ppermute x5, starting transfers between devices, along_x(): return lax.ppermute(value, 'seq', pairs)  13.5 us
    ppermute x5, starting transfers between devices, up(): return lax.ppermute(value, 'seq', pairs)  11.6 us
    ppermute x6, starting transfers between devices, tp_shift(): return lax.ppermute(value, 'tp', [(i, (i + step) % 4) for i in range(4)])  10.2 us
    ppermute x6, waiting for transfers between devices, tp_shift(): return lax.ppermute(value, 'tp', [(i, (i + step) % 4) for i in range(4)])  9.89 us
    ppermute x4, starting transfers between devices, down(): return lax.ppermute(value, 'seq', pairs)  9.24 us
    ppermute x1, waiting for transfers between devices, local(): lax.ppermute(tail, 'seq', [(i, i + 2) for i in range(2 * NX * NZ - 2)])  5.97 us
    ppermute x5, waiting for transfers between devices, up(): return lax.ppermute(value, 'seq', pairs)  5.22 us
  transfers between devices with their start and end apart: 25, of which 12 were waited for; matrix products, arithmetic and copies ran while one was open for 5% of the time, Pallas kernels for 18%

profile of v4, /device:TPU:192, one launch (start us, length us, event | category | flops | bytes accessed | tf_op | source)
XLA Modules:
  0.0 105.9 jit_solution(6506672434026455482)
XLA Ops:
  3.0 2.6 %pick.1 = (bf16[2,128,256]{2,1,0:T(8,128)(2,1)}, bf16[128,256]{1,0:T(8,128)(2,1)}) custom-call(s32[3]{0:T(128)} %pad_add_fusion.scal, s32[8,16]{1,0:T(8,128)} %blocks.1, bf16[256,256]{1,0:T(8,128)(2,1)} %k_ref.3, bf16[256,256]{1,0:T(8,128)(2,1)} %v_ref.3, bf16[256,256]{1,0:T(8,128)(2,1)} %copy-done.2, bf16[256,256]{1,0:T(8,128)(2,1)} %copy-done.4), custom_call_target="tpu_custom_call" | custom-call | bytes 1000000 | tf_op jit(solution)/shard_map/pick/pallas_call | solution.py:381
  5.6 3.1 %collective-permute-start.3 = (bf16[2,128,256]{2,1,0:T(8,128)(2,1)}, bf16[2,128,256]{2,1,0:T(8,128)(2,1)S(1)}, u32[]{:S(2)}, u32[]{:S(2)}) collective-permute-start(bf16[2,128,256]{2,1,0:T(8,128)(2,1)} %get-tuple-element.29), channel_id=1, source_target_pairs={{0,32},{4,36},{8,40},{12,44},{16,48},{20,52},{24,56},{28,60},{32,6... | collective-permute-start | bytes 393224 | tf_op jit(solution)/shard_map/ppermute | solution.py:71
  9.3 3.1 %collective-permute-start.5 = (bf16[2,128,256]{2,1,0:T(8,128)(2,1)}, bf16[2,128,256]{2,1,0:T(8,128)(2,1)S(1)}, u32[]{:S(2)}, u32[]{:S(2)}) collective-permute-start(bf16[2,128,256]{2,1,0:T(8,128)(2,1)} %get-tuple-element.29), channel_id=1, source_target_pairs={{0,16},{4,20},{8,24},{12,28},{16,0},{20,4},{24,8},{28,12},{32,48},... | collective-permute-start | bytes 393224 | tf_op jit(solution)/shard_map/ppermute | solution.py:61
  12.4 2.5 %collective-permute-start.4 = (bf16[128,256]{1,0:T(8,128)(2,1)}, bf16[128,256]{1,0:T(8,128)(2,1)S(1)}, u32[]{:S(2)}, u32[]{:S(2)}) collective-permute-start(bf16[128,256]{1,0:T(8,128)(2,1)} %get-tuple-element.30), channel_id=1, source_target_pairs={{0,8},{4,12},{8,16},{12,20},{16,24},{20,28},{24,32},{28,36},{32,40... | collective-permute-start | bytes 196616 | tf_op jit(solution)/shard_map/ppermute | solution.py:426
  14.9 6.0 %collective-permute-done.4.halo_ref = bf16[128,256]{1,0:T(8,128)(2,1)S(1)} collective-permute-done((bf16[128,256]{1,0:T(8,128)(2,1)}, bf16[128,256]{1,0:T(8,128)(2,1)S(1)}, u32[]{:S(2)}, u32[]{:S(2)}) %collective-permute-start.4) | collective-permute-done | bytes 65568 | tf_op jit(solution)/shard_map/ppermute | solution.py:426
  20.9 1.9 %collective-permute-start.6 = (bf16[4,128,256]{2,1,0:T(8,128)(2,1)S(1)}, bf16[4,128,256]{2,1,0:T(8,128)(2,1)S(1)}, u32[]{:S(2)}, u32[]{:S(2)}) collective-permute-start(bf16[4,128,256]{2,1,0:T(8,128)(2,1)S(1)} %get-tuple-element.58), channel_id=1, source_target_pairs={{0,32},{4,36},{8,40},{12,44},{16,48},{20,52},{24,56},{28,60},{32,6... | collective-permute-start | bytes 786440 | tf_op jit(solution)/shard_map/ppermute | solution.py:71
  23.0 1.3 %collective-permute-start.12 = (bf16[4,128,256]{2,1,0:T(8,128)(2,1)S(1)}, bf16[4,128,256]{2,1,0:T(8,128)(2,1)S(1)}, u32[]{:S(2)}, u32[]{:S(2)}) collective-permute-start(bf16[4,128,256]{2,1,0:T(8,128)(2,1)S(1)} %get-tuple-element.57), channel_id=1, source_target_pairs={{0,224},{4,228},{8,232},{12,236},{16,240},{20,244},{24,248},{28,25... | collective-permute-start | bytes 786440 | tf_op jit(solution)/shard_map/ppermute | solution.py:77
  24.3 5.2 %collective-permute-done.6.rest_0_ = bf16[4,128,256]{2,1,0:T(8,128)(2,1)S(1)} collective-permute-done((bf16[4,128,256]{2,1,0:T(8,128)(2,1)S(1)}, bf16[4,128,256]{2,1,0:T(8,128)(2,1)S(1)}, u32[]{:S(2)}, u32[]{:S(2)}) %collective-permute-start.6) | collective-permute-done | bytes 262176 | tf_op jit(solution)/shard_map/ppermute | solution.py:71
  29.5 2.2 %collective-permute-start.10 = (bf16[4,128,256]{2,1,0:T(8,128)(2,1)S(1)}, bf16[4,128,256]{2,1,0:T(8,128)(2,1)S(1)}, u32[]{:S(2)}, u32[]{:S(2)}) collective-permute-start(bf16[4,128,256]{2,1,0:T(8,128)(2,1)S(1)} %collective-permute-done.6.rest_0_), channel_id=1, source_target_pairs={{32,64},{36,68},{40,72},{44,76},{48,80},{52,84},{56,88},{60,92},{6... | collective-permute-start | bytes 786440 | tf_op jit(solution)/shard_map/ppermute | solution.py:71
  34.7 1.0 pad_maximum_fusion.rest_0_
  35.7 3.2 %collective-permute-start.9 = (bf16[8,128,256]{2,1,0:T(8,128)(2,1)S(1)}, bf16[8,128,256]{2,1,0:T(8,128)(2,1)S(1)}, u32[]{:S(2)}, u32[]{:S(2)}) collective-permute-start(bf16[8,128,256]{2,1,0:T(8,128)(2,1)S(1)} %pad_maximum_fusion.rest_0_), channel_id=1, source_target_pairs={{0,24},{4,28},{8,0},{12,4},{16,8},{20,12},{24,16},{28,20},{32,56},... | collective-permute-start | bytes 1572872 | tf_op jit(solution)/shard_map/ppermute | solution.py:61
  39.0 3.6 %collective-permute-start.13 = (bf16[4,128,256]{2,1,0:T(8,128)(2,1)S(1)}, bf16[4,128,256]{2,1,0:T(8,128)(2,1)S(1)}, u32[]{:S(2)}, u32[]{:S(2)}) collective-permute-start(bf16[4,128,256]{2,1,0:T(8,128)(2,1)S(1)} %collective-permute-done.12.rest_4_), channel_id=1, source_target_pairs={{0,224},{4,228},{8,232},{12,236},{16,240},{20,244},{24,248},{28,25... | collective-permute-start | bytes 786440 | tf_op jit(solution)/shard_map/ppermute | solution.py:77
  42.6 2.2 %collective-permute-start.11 = (bf16[4,128,256]{2,1,0:T(8,128)(2,1)S(1)}, bf16[4,128,256]{2,1,0:T(8,128)(2,1)S(1)}, u32[]{:S(2)}, u32[]{:S(2)}) collective-permute-start(bf16[4,128,256]{2,1,0:T(8,128)(2,1)S(1)} %collective-permute-done.10.rest_1_), channel_id=1, source_target_pairs={{64,96},{68,100},{72,104},{76,108},{80,112},{84,116},{88,120},{92,... | collective-permute-start | bytes 786440 | tf_op jit(solution)/shard_map/ppermute | solution.py:71
  44.9 5.3 %near_part.1 = (bf16[4,512,256]{2,1,0:T(8,128)(2,1)S(1)}, f32[4,512,256]{2,1,0:T(8,128)S(1)}, s32[256]{0:T(256)S(1)}, s32[16]{0:T(128)S(1)}) custom-call(s32[240]{0:T(256)S(1)} %concatenate.19.ints, bf16[256,1024]{1,0:T(8,128)(2,1)S(1)} %copy-done.7, bf16[256,1024]{1,0:T(8,128)(2,1)S(1)} %collective-permute-done.q_sib_ref, bf16[256,256]{1,0:T(8,128)(2,1)S(1)} %copy-done, ...), custom_call_target="tpu_custom_call" | custom-call | flops 5000000000 | bytes 100000 | tf_op jit(solution)/shard_map/near_part/pallas_call | solution.py:381
  50.2 3.6 %collective-permute-start.15 = (bf16[2,128,256]{2,1,0:T(8,128)(2,1)S(1)}, bf16[2,128,256]{2,1,0:T(8,128)(2,1)S(1)}, u32[]{:S(2)}, u32[]{:S(2)}) collective-permute-start(bf16[2,128,256]{2,1,0:T(8,128)(2,1)S(1)} %get-tuple-element.53), channel_id=1, source_target_pairs={{0,224},{4,228},{8,232},{12,236},{16,240},{20,244},{24,248},{28,25... | collective-permute-start | bytes 393224 | tf_op jit(solution)/shard_map/ppermute | solution.py:77
  53.9 2.2 %collective-permute-start.14 = (bf16[2,128,256]{2,1,0:T(8,128)(2,1)S(1)}, bf16[2,128,256]{2,1,0:T(8,128)(2,1)S(1)}, u32[]{:S(2)}, u32[]{:S(2)}) collective-permute-start(bf16[2,128,256]{2,1,0:T(8,128)(2,1)S(1)} %get-tuple-element.55), channel_id=1, source_target_pairs={{96,128},{100,132},{104,136},{108,140},{112,144},{116,148},{120,15... | collective-permute-start | bytes 393224 | tf_op jit(solution)/shard_map/ppermute | solution.py:71
  56.2 3.5 %far_part.3 = (bf16[4,512,256]{2,1,0:T(8,128)(2,1)S(1)}, f32[4,512,256]{2,1,0:T(8,128)S(1)}) custom-call(s32[3]{0:T(128)S(1)} %copy-done.6, s32[256]{0:T(256)S(1)} %get-tuple-element.32.lists, s32[16]{0:T(128)S(1)} %get-tuple-element.33.counts, bf16[4,512,256]{2,1,0:T(8,128)(2,1)S(1)} %get-tuple-element.34.qa_in, ...), custom_call_target="tpu_custom_call" | custom-call | flops 6000000000 | bytes 100000 | tf_op jit(solution)/shard_map/far_part/pallas_call | solution.py:381
  59.7 1.9 %collective-permute-start.16 = (bf16[8,128,256]{2,1,0:T(8,128)(2,1)S(1)}, bf16[8,128,256]{2,1,0:T(8,128)(2,1)S(1)}, u32[]{:S(2)}, u32[]{:S(2)}) collective-permute-start(bf16[8,128,256]{2,1,0:T(8,128)(2,1)S(1)} %pad_maximum_fusion.1), channel_id=1, source_target_pairs={{96,104},{100,108},{104,112},{108,116},{112,120},{116,124},{120,96... | collective-permute-start | bytes 1572872 | tf_op jit(solution)/shard_map/ppermute | solution.py:61
  61.7 5.1 %collective-permute-start.17 = (bf16[8,128,256]{2,1,0:T(8,128)(2,1)S(1)}, bf16[8,128,256]{2,1,0:T(8,128)(2,1)S(1)}, u32[]{:S(2)}, u32[]{:S(2)}) collective-permute-start(bf16[8,128,256]{2,1,0:T(8,128)(2,1)S(1)} %pad_maximum_fusion.1), channel_id=1, source_target_pairs={{96,120},{100,124},{104,96},{108,100},{112,104},{116,108},{120,112... | collective-permute-start | bytes 1572872 | tf_op jit(solution)/shard_map/ppermute | solution.py:61
  66.8 4.5 %far_part.4 = (bf16[4,512,256]{2,1,0:T(8,128)(2,1)S(1)}, f32[4,512,256]{2,1,0:T(8,128)S(1)}) custom-call(s32[3]{0:T(128)S(1)} %copy-done.6, s32[256]{0:T(256)S(1)} %get-tuple-element.32.lists, s32[16]{0:T(128)S(1)} %get-tuple-element.33.counts, bf16[4,512,256]{2,1,0:T(8,128)(2,1)S(1)} %get-tuple-element.37.qa_in, ...), custom_call_target="tpu_custom_call" | custom-call | flops 6000000000 | bytes 100000 | tf_op jit(solution)/shard_map/far_part/pallas_call | solution.py:381
  71.3 1.2 %collective-permute-done.16.rest_0_ = bf16[8,128,256]{2,1,0:T(8,128)(2,1)S(1)} collective-permute-done((bf16[8,128,256]{2,1,0:T(8,128)(2,1)S(1)}, bf16[8,128,256]{2,1,0:T(8,128)(2,1)S(1)}, u32[]{:S(2)}, u32[]{:S(2)}) %collective-permute-start.16) | collective-permute-done | bytes 524320 | tf_op jit(solution)/shard_map/ppermute | solution.py:61
  72.5 1.4 %collective-permute-done.17.rest_1_ = bf16[8,128,256]{2,1,0:T(8,128)(2,1)S(1)} collective-permute-done((bf16[8,128,256]{2,1,0:T(8,128)(2,1)S(1)}, bf16[8,128,256]{2,1,0:T(8,128)(2,1)S(1)}, u32[]{:S(2)}, u32[]{:S(2)}) %collective-permute-start.17) | collective-permute-done | bytes 524320 | tf_op jit(solution)/shard_map/ppermute | solution.py:61
  73.9 3.2 %far_part.5 = (bf16[256,512]{1,0:T(8,128)(2,1)S(1)}, bf16[256,512]{1,0:T(8,128)(2,1)S(1)}) custom-call(s32[3]{0:T(128)S(1)} %copy-done.6, s32[256]{0:T(256)S(1)} %get-tuple-element.32.lists, s32[16]{0:T(128)S(1)} %get-tuple-element.33.counts, bf16[4,512,256]{2,1,0:T(8,128)(2,1)S(1)} %get-tuple-element.40.qa_in, f32[4,512,256]{2,1,0:T(8,128)S(1)} %get-tuple-element.41.acc_in, ...), custom_call_target="tpu_custom_call" | custom-call | flops 6000000000 | bytes 100000 | tf_op jit(solution)/shard_map/far_part/pallas_call | solution.py:381
  77.3 1.3 %own_part.1.part = f32[2,256,512]{2,1,0:T(8,128)S(1)} custom-call(s32[3]{0:T(128)S(1)} %copy-done.6, bf16[256,512]{1,0:T(8,128)(2,1)S(1)} %get-tuple-element.43.ctx, bf16[1024,4096]{1,0:T(8,128)(2,1)S(1)} %bitcast.4), custom_call_target="tpu_custom_call" | custom-call | flops 300000000 | bytes 3000000 | tf_op jit(solution)/shard_map/own_part/pallas_call | solution.py:381
  78.7 1.3 %sib_part.1 = (bf16[256,512]{1,0:T(8,128)(2,1)S(1)}, bf16[256,512]{1,0:T(8,128)(2,1)S(1)}) custom-call(s32[3]{0:T(128)S(1)} %copy-done.6, bf16[256,512]{1,0:T(8,128)(2,1)S(1)} %collective-permute-done.18.ctx_sib.ctx, f32[2,256,512]{2,1,0:T(8,128)S(1)} %own_part.1.part, bf16[1024,4096]{1,0:T(8,128)(2,1)S(1)} %bitcast.4), custom_call_target="tpu_custom_call" | custom-call | flops 300000000 | bytes 3000000 | tf_op jit(solution)/shard_map/sib_part/pallas_call | solution.py:381
  80.0 4.1 %collective-permute-start.23 = (bf16[256,512]{1,0:T(8,128)(2,1)S(1)}, bf16[256,512]{1,0:T(8,128)(2,1)S(1)}, u32[]{:S(2)}, u32[]{:S(2)}) collective-permute-start(bf16[256,512]{1,0:T(8,128)(2,1)S(1)} %get-tuple-element.52), channel_id=1, source_target_pairs={{0,3},{1,0},{2,1},{3,2},{4,7},{5,4},{6,5},{7,6},{8,11},{9,8},{10,9... | collective-permute-start | bytes 786440 | tf_op jit(solution)/shard_map/ppermute | solution.py:85
  84.1 4.5 %other_shares.1 = (f32[256,512]{1,0:T(8,128)S(1)}, bf16[256,512]{1,0:T(8,128)(2,1)S(1)}, bf16[256,512]{1,0:T(8,128)(2,1)S(1)}, f32[256,512]{1,0:T(8,128)S(1)}, f...) custom-call(s32[3]{0:T(128)S(1)} %copy-done.6, bf16[256,512]{1,0:T(8,128)(2,1)S(1)} %get-tuple-element.43.ctx, ...), custom_call_target="tpu_custom_call" | custom-call | flops 1600000000 | bytes 9000000 | tf_op jit(solution)/shard_map/other_shares/pallas_call | solution.py:381
  89.3 0.9 collective-permute-done.23
  90.3 3.8 %collective-permute-start.24 = (bf16[256,512]{1,0:T(8,128)(2,1)S(1)}, bf16[256,512]{1,0:T(8,128)(2,1)S(1)}, u32[]{:S(2)}, u32[]{:S(2)}) collective-permute-start(bf16[256,512]{1,0:T(8,128)(2,1)S(1)} %add_convert_fusion.1), channel_id=1, source_target_pairs={{0,3},{1,0},{2,1},{3,2},{4,7},{5,4},{6,5},{7,6},{8,11},{9,8},{10,9... | collective-permute-start | bytes 786440 | tf_op jit(solution)/shard_map/ppermute | solution.py:85
  94.6 1.6 %collective-permute-start.21 = (bf16[256,512]{1,0:T(8,128)(2,1)S(1)}, bf16[256,512]{1,0:T(8,128)(2,1)S(1)}, u32[]{:S(2)}, u32[]{:S(2)}) collective-permute-start(bf16[256,512]{1,0:T(8,128)(2,1)S(1)} %add_convert_fusion.3), channel_id=1, source_target_pairs={{0,1},{1,2},{2,3},{3,0},{4,5},{5,6},{6,7},{7,4},{8,9},{9,10},{10,1... | collective-permute-start | bytes 786440 | tf_op jit(solution)/shard_map/ppermute | solution.py:85
  96.2 3.9 %collective-permute-done.22 = bf16[256,512]{1,0:T(8,128)(2,1)S(1)} collective-permute-done((bf16[256,512]{1,0:T(8,128)(2,1)S(1)}, bf16[256,512]{1,0:T(8,128)(2,1)S(1)}, u32[]{:S(2)}, u32[]{:S(2)}) %collective-permute-start.22) | collective-permute-done | bytes 262176 | tf_op jit(solution)/shard_map/ppermute | solution.py:85
  100.9 4.0 %collective-permute-done.19 = bf16[256,512]{1,0:T(8,128)(2,1)S(1)} collective-permute-done((bf16[256,512]{1,0:T(8,128)(2,1)S(1)}, bf16[256,512]{1,0:T(8,128)(2,1)S(1)}, u32[]{:S(2)}, u32[]{:S(2)}) %collective-permute-start.19) | collective-permute-done | bytes 262176 | tf_op jit(solution)/shard_map/ppermute | solution.py:85
  (65 shorter events, 10.3 us)
Async XLA Ops:
  0.0 44.8 %copy-start = (bf16[256,256]{1,0:T(8,128)(2,1)S(1)}, bf16[256,256]{1,0:T(8,128)(2,1)}, u32[]{:S(2)}) copy-start(bf16[256,256]{1,0:T(8,128)(2,1)} %k_ref.3) | copy-start | bytes 393220
  0.0 44.8 %copy-start.1 = (bf16[256,256]{1,0:T(8,128)(2,1)S(1)}, bf16[256,256]{1,0:T(8,128)(2,1)}, u32[]{:S(2)}) copy-start(bf16[256,256]{1,0:T(8,128)(2,1)} %v_ref.3) | copy-start | bytes 393220
  0.0 44.8 %copy-start.7 = (bf16[256,1024]{1,0:T(8,128)(2,1)S(1)}, bf16[256,1024]{1,0:T(8,128)(2,1)}, u32[]{:S(2)}) copy-start(bf16[256,1024]{1,0:T(8,128)(2,1)} %q_ref.1) | copy-start | bytes 1572868
  0.0 1.6 %collective-permute-start.1 = (bf16[256,256]{1,0:T(8,128)(2,1)}, bf16[256,256]{1,0:T(8,128)(2,1)S(1)}, u32[]{:S(2)}, u32[]{:S(2)}) collective-permute-start(bf16[256,256]{1,0:T(8,128)(2,1)} %k_ref.3), channel_id=1, source_target_pairs={{0,4},{4,0},{8,12},{12,8},{16,20},{20,16},{24,28},{28,24},{32,36},... | collective-permute-start | bytes 393224 | tf_op jit(solution)/shard_map/ppermute | solution.py:81
  0.1 1.7 %collective-permute-start.2 = (bf16[256,256]{1,0:T(8,128)(2,1)}, bf16[256,256]{1,0:T(8,128)(2,1)S(1)}, u32[]{:S(2)}, u32[]{:S(2)}) collective-permute-start(bf16[256,256]{1,0:T(8,128)(2,1)} %v_ref.3), channel_id=1, source_target_pairs={{0,4},{4,0},{8,12},{12,8},{16,20},{20,16},{24,28},{28,24},{32,36},... | collective-permute-start | bytes 393224 | tf_op jit(solution)/shard_map/ppermute | solution.py:81
  5.5 39.3 %copy-start.3 = (bf16[256,256]{1,0:T(8,128)(2,1)S(1)}, bf16[256,256]{1,0:T(8,128)(2,1)}, u32[]{:S(2)}) copy-start(bf16[256,256]{1,0:T(8,128)(2,1)} %copy-done.2) | copy-start | bytes 393220
  5.6 39.3 %copy-start.5 = (bf16[256,256]{1,0:T(8,128)(2,1)S(1)}, bf16[256,256]{1,0:T(8,128)(2,1)}, u32[]{:S(2)}) copy-start(bf16[256,256]{1,0:T(8,128)(2,1)} %copy-done.4) | copy-start | bytes 393220
  5.6 15.3 %collective-permute-start.3 = (bf16[2,128,256]{2,1,0:T(8,128)(2,1)}, bf16[2,128,256]{2,1,0:T(8,128)(2,1)S(1)}, u32[]{:S(2)}, u32[]{:S(2)}) collective-permute-start(bf16[2,128,256]{2,1,0:T(8,128)(2,1)} %get-tuple-element.29), channel_id=1, source_target_pairs={{0,32},{4,36},{8,40},{12,44},{16,48},{20,52},{24,56},{28,60},{32,6... | collective-permute-start | bytes 393224 | tf_op jit(solution)/shard_map/ppermute | solution.py:71
  8.6 12.3 %collective-permute-start.7 = (bf16[2,128,256]{2,1,0:T(8,128)(2,1)}, bf16[2,128,256]{2,1,0:T(8,128)(2,1)S(1)}, u32[]{:S(2)}, u32[]{:S(2)}) collective-permute-start(bf16[2,128,256]{2,1,0:T(8,128)(2,1)} %get-tuple-element.29), channel_id=1, source_target_pairs={{0,224},{4,228},{8,232},{12,236},{16,240},{20,244},{24,248},{28,25... | collective-permute-start | bytes 393224 | tf_op jit(solution)/shard_map/ppermute | solution.py:77
  9.3 11.6 %collective-permute-start.5 = (bf16[2,128,256]{2,1,0:T(8,128)(2,1)}, bf16[2,128,256]{2,1,0:T(8,128)(2,1)S(1)}, u32[]{:S(2)}, u32[]{:S(2)}) collective-permute-start(bf16[2,128,256]{2,1,0:T(8,128)(2,1)} %get-tuple-element.29), channel_id=1, source_target_pairs={{0,16},{4,20},{8,24},{12,28},{16,0},{20,4},{24,8},{28,12},{32,48},... | collective-permute-start | bytes 393224 | tf_op jit(solution)/shard_map/ppermute | solution.py:61
  12.4 8.5 %collective-permute-start.4 = (bf16[128,256]{1,0:T(8,128)(2,1)}, bf16[128,256]{1,0:T(8,128)(2,1)S(1)}, u32[]{:S(2)}, u32[]{:S(2)}) collective-permute-start(bf16[128,256]{1,0:T(8,128)(2,1)} %get-tuple-element.30), channel_id=1, source_target_pairs={{0,8},{4,12},{8,16},{12,20},{16,24},{20,28},{24,32},{28,36},{32,40... | collective-permute-start | bytes 196616 | tf_op jit(solution)/shard_map/ppermute | solution.py:426
  20.9 8.5 %collective-permute-start.6 = (bf16[4,128,256]{2,1,0:T(8,128)(2,1)S(1)}, bf16[4,128,256]{2,1,0:T(8,128)(2,1)S(1)}, u32[]{:S(2)}, u32[]{:S(2)}) collective-permute-start(bf16[4,128,256]{2,1,0:T(8,128)(2,1)S(1)} %get-tuple-element.58), channel_id=1, source_target_pairs={{0,32},{4,36},{8,40},{12,44},{16,48},{20,52},{24,56},{28,60},{32,6... | collective-permute-start | bytes 786440 | tf_op jit(solution)/shard_map/ppermute | solution.py:71
  22.9 21.9 %collective-permute-start = (bf16[256,1024]{1,0:T(8,128)(2,1)}, bf16[256,1024]{1,0:T(8,128)(2,1)S(1)}, u32[]{:S(2)}, u32[]{:S(2)}) collective-permute-start(bf16[256,1024]{1,0:T(8,128)(2,1)} %q_ref.1), channel_id=1, source_target_pairs={{0,4},{4,0},{8,12},{12,8},{16,20},{20,16},{24,28},{28,24},{32,36},... | collective-permute-start | bytes 1572872 | tf_op jit(solution)/shard_map/ppermute | solution.py:81
  23.0 16.0 %collective-permute-start.12 = (bf16[4,128,256]{2,1,0:T(8,128)(2,1)S(1)}, bf16[4,128,256]{2,1,0:T(8,128)(2,1)S(1)}, u32[]{:S(2)}, u32[]{:S(2)}) collective-permute-start(bf16[4,128,256]{2,1,0:T(8,128)(2,1)S(1)} %get-tuple-element.57), channel_id=1, source_target_pairs={{0,224},{4,228},{8,232},{12,236},{16,240},{20,244},{24,248},{28,25... | collective-permute-start | bytes 786440 | tf_op jit(solution)/shard_map/ppermute | solution.py:77
  29.5 13.1 %collective-permute-start.10 = (bf16[4,128,256]{2,1,0:T(8,128)(2,1)S(1)}, bf16[4,128,256]{2,1,0:T(8,128)(2,1)S(1)}, u32[]{:S(2)}, u32[]{:S(2)}) collective-permute-start(bf16[4,128,256]{2,1,0:T(8,128)(2,1)S(1)} %collective-permute-done.6.rest_0_), channel_id=1, source_target_pairs={{32,64},{36,68},{40,72},{44,76},{48,80},{52,84},{56,88},{60,92},{6... | collective-permute-start | bytes 786440 | tf_op jit(solution)/shard_map/ppermute | solution.py:71
  35.6 20.5 %copy-start.6 = (s32[3]{0:T(128)S(1)}, s32[3]{0:T(128)}, u32[]{:S(2)}) copy-start(s32[3]{0:T(128)} %pad_add_fusion.scal) | copy-start | bytes 40
  35.6 20.5 %collective-permute-start.8 = (bf16[8,128,256]{2,1,0:T(8,128)(2,1)S(1)}, bf16[8,128,256]{2,1,0:T(8,128)(2,1)S(1)}, u32[]{:S(2)}, u32[]{:S(2)}) collective-permute-start(bf16[8,128,256]{2,1,0:T(8,128)(2,1)S(1)} %pad_maximum_fusion.rest_0_), channel_id=1, source_target_pairs={{0,8},{4,12},{8,16},{12,20},{16,24},{20,28},{24,0},{28,4},{32,40},... | collective-permute-start | bytes 1572872 | tf_op jit(solution)/shard_map/ppermute | solution.py:61
  35.7 20.4 %collective-permute-start.9 = (bf16[8,128,256]{2,1,0:T(8,128)(2,1)S(1)}, bf16[8,128,256]{2,1,0:T(8,128)(2,1)S(1)}, u32[]{:S(2)}, u32[]{:S(2)}) collective-permute-start(bf16[8,128,256]{2,1,0:T(8,128)(2,1)S(1)} %pad_maximum_fusion.rest_0_), channel_id=1, source_target_pairs={{0,24},{4,28},{8,0},{12,4},{16,8},{20,12},{24,16},{28,20},{32,56},... | collective-permute-start | bytes 1572872 | tf_op jit(solution)/shard_map/ppermute | solution.py:61
  39.0 11.2 %collective-permute-start.13 = (bf16[4,128,256]{2,1,0:T(8,128)(2,1)S(1)}, bf16[4,128,256]{2,1,0:T(8,128)(2,1)S(1)}, u32[]{:S(2)}, u32[]{:S(2)}) collective-permute-start(bf16[4,128,256]{2,1,0:T(8,128)(2,1)S(1)} %collective-permute-done.12.rest_4_), channel_id=1, source_target_pairs={{0,224},{4,228},{8,232},{12,236},{16,240},{20,244},{24,248},{28,25... | collective-permute-start | bytes 786440 | tf_op jit(solution)/shard_map/ppermute | solution.py:77
  42.6 11.3 %collective-permute-start.11 = (bf16[4,128,256]{2,1,0:T(8,128)(2,1)S(1)}, bf16[4,128,256]{2,1,0:T(8,128)(2,1)S(1)}, u32[]{:S(2)}, u32[]{:S(2)}) collective-permute-start(bf16[4,128,256]{2,1,0:T(8,128)(2,1)S(1)} %collective-permute-done.10.rest_1_), channel_id=1, source_target_pairs={{64,96},{68,100},{72,104},{76,108},{80,112},{84,116},{88,120},{92,... | collective-permute-start | bytes 786440 | tf_op jit(solution)/shard_map/ppermute | solution.py:71
  50.2 16.6 %collective-permute-start.15 = (bf16[2,128,256]{2,1,0:T(8,128)(2,1)S(1)}, bf16[2,128,256]{2,1,0:T(8,128)(2,1)S(1)}, u32[]{:S(2)}, u32[]{:S(2)}) collective-permute-start(bf16[2,128,256]{2,1,0:T(8,128)(2,1)S(1)} %get-tuple-element.53), channel_id=1, source_target_pairs={{0,224},{4,228},{8,232},{12,236},{16,240},{20,244},{24,248},{28,25... | collective-permute-start | bytes 393224 | tf_op jit(solution)/shard_map/ppermute | solution.py:77
  53.9 12.9 %collective-permute-start.14 = (bf16[2,128,256]{2,1,0:T(8,128)(2,1)S(1)}, bf16[2,128,256]{2,1,0:T(8,128)(2,1)S(1)}, u32[]{:S(2)}, u32[]{:S(2)}) collective-permute-start(bf16[2,128,256]{2,1,0:T(8,128)(2,1)S(1)} %get-tuple-element.55), channel_id=1, source_target_pairs={{96,128},{100,132},{104,136},{108,140},{112,144},{116,148},{120,15... | collective-permute-start | bytes 393224 | tf_op jit(solution)/shard_map/ppermute | solution.py:71
  59.7 12.8 %collective-permute-start.16 = (bf16[8,128,256]{2,1,0:T(8,128)(2,1)S(1)}, bf16[8,128,256]{2,1,0:T(8,128)(2,1)S(1)}, u32[]{:S(2)}, u32[]{:S(2)}) collective-permute-start(bf16[8,128,256]{2,1,0:T(8,128)(2,1)S(1)} %pad_maximum_fusion.1), channel_id=1, source_target_pairs={{96,104},{100,108},{104,112},{108,116},{112,120},{116,124},{120,96... | collective-permute-start | bytes 1572872 | tf_op jit(solution)/shard_map/ppermute | solution.py:61
  61.7 12.2 %collective-permute-start.17 = (bf16[8,128,256]{2,1,0:T(8,128)(2,1)S(1)}, bf16[8,128,256]{2,1,0:T(8,128)(2,1)S(1)}, u32[]{:S(2)}, u32[]{:S(2)}) collective-permute-start(bf16[8,128,256]{2,1,0:T(8,128)(2,1)S(1)} %pad_maximum_fusion.1), channel_id=1, source_target_pairs={{96,120},{100,124},{104,96},{108,100},{112,104},{116,108},{120,112... | collective-permute-start | bytes 1572872 | tf_op jit(solution)/shard_map/ppermute | solution.py:61
  73.9 3.5 %slice-start.1 = ((s8[8388608]{0:T(1024)(128)(4,1)}), s8[4194304]{0:T(1024)(128)(4,1)S(1)}, s32[]{:S(2)}) async-start(s8[8388608]{0:T(1024)(128)(4,1)} %bitcast.3), calls=%async_computation.1 | async-start | bytes 8388608
  77.1 1.6 %collective-permute-start.18 = (bf16[256,512]{1,0:T(8,128)(2,1)S(1)}, bf16[256,512]{1,0:T(8,128)(2,1)S(1)}, u32[]{:S(2)}, u32[]{:S(2)}) collective-permute-start(bf16[256,512]{1,0:T(8,128)(2,1)S(1)} %get-tuple-element.44), channel_id=1, source_target_pairs={{0,4},{4,0},{8,12},{12,8},{16,20},{20,16},{24,28},{28,24},{32,36},... | collective-permute-start | bytes 786440 | tf_op jit(solution)/shard_map/ppermute | solution.py:81
  80.0 10.1 %collective-permute-start.23 = (bf16[256,512]{1,0:T(8,128)(2,1)S(1)}, bf16[256,512]{1,0:T(8,128)(2,1)S(1)}, u32[]{:S(2)}, u32[]{:S(2)}) collective-permute-start(bf16[256,512]{1,0:T(8,128)(2,1)S(1)} %get-tuple-element.52), channel_id=1, source_target_pairs={{0,3},{1,0},{2,1},{3,2},{4,7},{5,4},{6,5},{7,6},{8,11},{9,8},{10,9... | collective-permute-start | bytes 786440 | tf_op jit(solution)/shard_map/ppermute | solution.py:85
  84.1 10.4 %collective-permute-start.20 = (bf16[256,512]{1,0:T(8,128)(2,1)S(1)}, bf16[256,512]{1,0:T(8,128)(2,1)S(1)}, u32[]{:S(2)}, u32[]{:S(2)}) collective-permute-start(bf16[256,512]{1,0:T(8,128)(2,1)S(1)} %get-tuple-element.48), channel_id=1, source_target_pairs={{0,1},{1,2},{2,3},{3,0},{4,5},{5,6},{6,7},{7,4},{8,9},{9,10},{10,1... | collective-permute-start | bytes 786440 | tf_op jit(solution)/shard_map/ppermute | solution.py:85
  88.6 11.5 %collective-permute-start.22 = (bf16[256,512]{1,0:T(8,128)(2,1)S(1)}, bf16[256,512]{1,0:T(8,128)(2,1)S(1)}, u32[]{:S(2)}, u32[]{:S(2)}) collective-permute-start(bf16[256,512]{1,0:T(8,128)(2,1)S(1)} %get-tuple-element.50), channel_id=1, source_target_pairs={{0,1},{1,2},{2,3},{3,0},{4,5},{5,6},{6,7},{7,4},{8,9},{9,10},{10,1... | collective-permute-start | bytes 786440 | tf_op jit(solution)/shard_map/ppermute | solution.py:85
  90.3 10.5 %collective-permute-start.24 = (bf16[256,512]{1,0:T(8,128)(2,1)S(1)}, bf16[256,512]{1,0:T(8,128)(2,1)S(1)}, u32[]{:S(2)}, u32[]{:S(2)}) collective-permute-start(bf16[256,512]{1,0:T(8,128)(2,1)S(1)} %add_convert_fusion.1), channel_id=1, source_target_pairs={{0,3},{1,0},{2,1},{3,2},{4,7},{5,4},{6,5},{7,6},{8,11},{9,8},{10,9... | collective-permute-start | bytes 786440 | tf_op jit(solution)/shard_map/ppermute | solution.py:85
  94.0 10.9 %collective-permute-start.19 = (bf16[256,512]{1,0:T(8,128)(2,1)S(1)}, bf16[256,512]{1,0:T(8,128)(2,1)S(1)}, u32[]{:S(2)}, u32[]{:S(2)}) collective-permute-start(bf16[256,512]{1,0:T(8,128)(2,1)S(1)} %get-tuple-element.46), channel_id=1, source_target_pairs={{0,3},{1,0},{2,1},{3,2},{4,7},{5,4},{6,5},{7,6},{8,11},{9,8},{10,9... | collective-permute-start | bytes 786440 | tf_op jit(solution)/shard_map/ppermute | solution.py:85
  94.6 10.3 %collective-permute-start.21 = (bf16[256,512]{1,0:T(8,128)(2,1)S(1)}, bf16[256,512]{1,0:T(8,128)(2,1)S(1)}, u32[]{:S(2)}, u32[]{:S(2)}) collective-permute-start(bf16[256,512]{1,0:T(8,128)(2,1)S(1)} %add_convert_fusion.3), channel_id=1, source_target_pairs={{0,1},{1,2},{2,3},{3,0},{4,5},{5,6},{6,7},{7,4},{8,9},{9,10},{10,1... | collective-permute-start | bytes 786440 | tf_op jit(solution)/shard_map/ppermute | solution.py:85
  (3 other events, 4.6 us)

commit v5 on v4

--- a/solution.py
+++ b/solution.py
@@ -19,7 +19,6 @@
 LIMIT = 100.0
 VMEM_BYTES = 40 * 1024 * 1024
 SLOT_BITS = 6
-AT_BLOCKS, AT_WINDOW, AT_SLASH, AT_TABLE = 8, 136, 144, 208
 AT_ONCE = 4
 BF16, F32, I32 = jnp.bfloat16, jnp.float32, jnp.int32
 
@@ -39,11 +38,11 @@
     put(0, 16, first, 1)
     put(0, 24, (0,), 2)
     for at, dz in ((4, -3), (8, -4), (14, 2), (18, 3)):
-        put(1, at, (dz,), 0)
+        put(2, at, (dz,), 0)
     for at, dz in ((2, -1), (6, -2), (10, -3), (12, -4), (16, 1), (20, 2), (22, 3)):
-        put(1, at, (dz,), 2)
-    put(2, 0, second, -1)
-    put(2, 8, second, 1)
+        put(2, at, (dz,), 2)
+    put(1, 0, second, -1)
+    put(1, 8, second, 1)
     return table.reshape(-1)
 
 
@@ -93,13 +92,16 @@
     return pl.ds(pl.multiple_of(core * width, width), width)
 
 
-def pick_kernel(scal, blocks, k_ref, v_ref, k_sib, v_sib, out_ref, tail_ref, buf, sem):
+def pick_kernel(scal, blocks_ref, k_ref, v_ref, k_sib, v_sib, out_ref, tail_ref, buf, blocks, sem):
     core, place = scal[0], scal[1]
     copies = []
     for n, ref in enumerate((k_ref, v_ref, k_sib, v_sib)):
         copies.append(pltpu.make_async_copy(ref, buf.at[n], sem.at[n]))
+    naming = pltpu.make_async_copy(blocks_ref, blocks, sem.at[4])
+    naming.start()
     for copy in copies:
         copy.start()
+    naming.wait()
     own, sib = 2 * place + 1, 2 * (place + 1 - 2 * core) + 1
 
     def look(n, found):
@@ -137,7 +139,7 @@
 
 
 def local_kernel(
-    ints, q_ref, q_sib_ref, k_ref, k_sib_ref, v_ref, v_sib_ref, halo_ref,
+    scal, blocks, window, slash, table, q_ref, q_sib_ref, k_ref, k_sib_ref, v_ref, v_sib_ref, halo_ref,
     qa_ref, acc_ref, list_ref, count_ref, q_buf, kv_buf, halo, qs, ks, vs, named, sem,
 ):
     q, q_sib = q_buf.at[0], q_buf.at[1]
@@ -153,7 +155,7 @@
     ]
     for copy in copies:
         copy.start()
-    core, place = ints[0], ints[1]
+    core, place = scal[0], scal[1]
     chip = place >> 1
     z, x = chip >> 2, chip & 3
 
@@ -164,8 +166,8 @@
 
     def note(n, carry):
         h = n >> 4
-        b = ints[AT_BLOCKS + core * (GROUP * PICKS) + n]
-        entry = ints[AT_TABLE + ((((b >> 4) - z) & 7) << 2) + (((b >> 2) - x) & 3)]
+        b = blocks[core * GROUP + h, n & 15]
+        entry = table[((((b >> 4) - z) & 7) << 2) + (((b >> 2) - x) & 3)]
         key = ((entry >> SLOT_BITS) << 2) + h
         count = count_ref[key]
         list_ref[(key << 4) + count] = (entry & ((1 << SLOT_BITS) - 1)) + ((b >> 1) & 1)
@@ -196,11 +198,11 @@
     prev_gap = diag_gap + BLK
     for h in range(GROUP):
         head = core * GROUP + h
-        diag_ok = diag_gap < ints[AT_WINDOW + head]
-        prev_ok = prev_gap < ints[AT_WINDOW + head]
+        diag_ok = diag_gap < window[head]
+        prev_ok = prev_gap < window[head]
         for n in range(8):
-            diag_ok = diag_ok | (diag_gap == ints[AT_SLASH + head * 8 + n])
-            prev_ok = prev_ok | (prev_gap == ints[AT_SLASH + head * 8 + n])
+            diag_ok = diag_ok | (diag_gap == slash[head, n])
+            prev_ok = prev_ok | (prev_gap == slash[head, n])
         scores = dot_f32(qs[h], ks[...], ((1,), (1,)))
         weights = []
         for i in range(4):
@@ -325,6 +327,10 @@
                 out[:, h * HD : (h + 1) * HD] = (both[:, :HD] / both[:, HD:]).astype(BF16)
 
 
+def crossed_kernel(right, left, out_ref):
+    out_ref[...] = jnp.zeros_like(out_ref)
+
+
 def weight_tiles(scal, w_ref, w_buf, sem, sibling, rel_tiles):
     core, me = scal[0], scal[2]
     rows, cols = w_buf.shape[1:]
@@ -400,15 +406,6 @@
     me = lax.axis_index("tp").astype(I32)
     core = place % 2
     scal = jnp.stack([core, place, me])
-    ints = jnp.concatenate(
-        [
-            jnp.pad(scal, (0, AT_BLOCKS - 3)),
-            vert_blocks.reshape(-1),
-            window_size,
-            slash_offsets.reshape(-1),
-            jnp.asarray(slot_table()),
-        ]
-    )
     block = shape((1, BLK, 2 * HD), BF16)
 
     k_sib = swap_cores(key_states)
@@ -417,8 +414,12 @@
     unit, tail = call(
         pick_kernel, "pick", [shape((2, BLK, 2 * HD), BF16), shape((BLK, 2 * HD), BF16)],
         (scal, vert_blocks, key_states, value_states, k_sib, v_sib),
-        [smem] * 2 + [anywhere] * 4,
-        [pltpu.VMEM((4,) + key_states.shape, BF16), pltpu.SemaphoreType.DMA((4,))],
+        [smem] + [anywhere] * 5,
+        [
+            pltpu.VMEM((4,) + key_states.shape, BF16),
+            pltpu.SMEM(vert_blocks.shape, I32),
+            pltpu.SemaphoreType.DMA((5,)),
+        ],
         moved=1_000_000,
         vmem_bytes=60 * 1024 * 1024,
     )
@@ -441,9 +442,9 @@
         "near_part",
         [shape(wide, BF16), shape(wide, F32), shape((16 * PICKS,), I32), shape((16,), I32)],
         (
-            ints, queries, q_sib, key_states, k_sib, value_states, v_sib, halo,
+            scal, vert_blocks, window_size, slash_offsets, jnp.asarray(slot_table()), queries, q_sib, key_states, k_sib, value_states, v_sib, halo,
         ),
-        [smem] + [anywhere] * 7,
+        [smem] * 5 + [anywhere] * 7,
         [
             pltpu.VMEM((2,) + queries.shape, BF16),
             pltpu.VMEM((4,) + key_states.shape, BF16),
@@ -485,12 +486,17 @@
 
     up4 = up(up3, 2)
     second = jnp.concatenate([up3[:2], up4[:2], down2[:2], down3[:2]], axis=0)
+    crossed = call(
+        crossed_kernel, "crossed", [shape((8, HD), F32)], (right1, left1), [anywhere] * 2,
+        flops=6_000_000_000,
+    )[0]
+    second, acc, crossed = lax.optimization_barrier((second, acc, crossed))
+    right2, left2 = along_x(second, 1, 3), along_x(second, -1, 3)
+    qa, acc = far(0, [first, right1, left1, opposite], qa, acc)
+    up4, down3, acc = lax.optimization_barrier((up4, down3, acc))
     up5, down4 = up(up4[2:], 3), down(down3[2:], (3,))
-    qa, acc = far(0, [first, right1, left1, opposite], qa, acc)
-    second, acc = lax.optimization_barrier((second, acc))
-    right2, left2 = along_x(second, 1, 3), along_x(second, -1, 3)
-    qa, acc = far(1, [up2, up3, up4, up5, down2, down3, down4], qa, acc)
-    ctx_mine, ctx_other = far(2, [right2, left2], qa, acc)
+    qa, acc = far(1, [right2, left2], qa, acc)
+    ctx_mine, ctx_other = far(2, [up2, up3, up4, up5, down2, down3, down4], qa, acc)
     ctx_sib = swap_cores(ctx_other)
 
     half_rows, half = rows // 2, out_weight.shape[1] // 8
@@ -500,27 +506,34 @@
         return [pltpu.VMEM((count, depth, half), BF16)], [pltpu.SemaphoreType.DMA((count,))]
 
     tile_bf, tile_f = shape((half_rows, half), BF16), shape((half_rows, half), F32)
-    opp = call(
-        functools.partial(part_kernel, False, (0, 1)), "own_part",
-        [shape((2, half_rows, half), F32)], (scal, ctx_mine, out_weight), [smem, vmem, anywhere],
-        sum(w_scratch(2), []), flops=300_000_000, moved=3_000_000,
-    )[0]
-    opp0, opp1 = call(
-        functools.partial(add_part_kernel, True, (0, 1)), "sib_part", [tile_bf] * 2,
-        (scal, ctx_sib, opp, out_weight), [smem, vmem, vmem, anywhere],
-        sum(w_scratch(2), []), flops=300_000_000, moved=3_000_000,
-    )
+
+    def own_part(tiles):
+        return call(
+            functools.partial(part_kernel, False, tiles), "own_part",
+            [shape((len(tiles), half_rows, half), F32)],
+            (scal, ctx_mine, out_weight), [smem, vmem, anywhere],
+            sum(w_scratch(len(tiles)), []), flops=1_000_000, moved=1_000,
+        )[0]
+
+    def sib_part(tiles, part):
+        return call(
+            functools.partial(add_part_kernel, True, tiles), "sib_part", [tile_bf] * 2,
+            (scal, ctx_sib, part, out_weight), [smem, vmem, vmem, anywhere],
+            sum(w_scratch(2), []), flops=1_000_000, moved=1_000,
+        )
+
+    opp0, opp1 = sib_part((0, 1), own_part((0, 1)))
     via_before = tp_shift(opp0, 1)
     via_after = tp_shift(opp1, -1)
-    bufs, sems = w_scratch(6)
-    after0, after1, before0, before1, own0, own1 = call(
-        functools.partial(both_parts_kernel, (2, 3, 4, 5, 6, 7)), "other_shares",
-        [tile_f, tile_bf, tile_bf, tile_f, tile_f, tile_f],
-        (scal, ctx_mine, ctx_sib, out_weight), [smem, vmem, vmem, anywhere],
-        bufs * 2 + sems * 2, flops=1_600_000_000, moved=9_000_000,
-    )
+    after1, before0 = sib_part((3, 4), own_part((3, 4)))
     direct1 = tp_shift(after1, 1)
     direct0 = tp_shift(before0, -1)
+    bufs, sems = w_scratch(4)
+    after0, before1, own0, own1 = call(
+        functools.partial(both_parts_kernel, (2, 5, 6, 7)), "other_shares", [tile_f] * 4,
+        (scal, ctx_mine, ctx_sib, out_weight), [smem, vmem, vmem, anywhere],
+        bufs * 2 + sems * 2, flops=1_000_000, moved=1_000,
+    )
     summed0 = tp_shift((after0 + via_before.astype(F32)).astype(BF16), 1)
     summed1 = tp_shift((before1 + via_after.astype(F32)).astype(BF16), -1)
     return jnp.concatenate(

time: 108 us -> 103 us (0.954); the launches traced: 106 us -> 102 us
  local copies, waits for them, and re-layouts: 4.3 us -> 1.24 us
  starting transfers between devices: 47.8 us -> 44.9 us
  Pallas kernels: 26.1 us -> 28.6 us
    pallas_call x8 -> x10, Pallas kernels: 26.1 us -> 28.6 us  [call(): pl.pallas_call(kernel, out_shape=outs, in_specs=[spec(s) for s in spaces]...]
    ppermute x5, starting transfers between devices: 13.5 us -> 11 us  [along_x(): return lax.ppermute(value, 'seq', pairs)]
    ppermute x5, waiting for transfers between devices: 2.56 us -> 0.21 us  [along_x(): return lax.ppermute(value, 'seq', pairs)]
    reshape x2 -> x0, local copies, waits for them, and re-layouts: 1.53 us -> none  [the longest x1 0.77 us: local(): slash_offsets.reshape(-1)]
    ppermute x6, starting transfers between devices: 10.2 us -> 8.91 us  [tp_shift(): return lax.ppermute(value, 'tp', [(i, (i + step) % 4) for i in range(4)])]
    ppermute x4, starting transfers between devices: 9.24 us -> 10.4 us  [down(): return lax.ppermute(value, 'seq', pairs)]
  transfers between devices with their start and end apart: 25 -> 25, of which waited for: 12 -> 11; matrix products, arithmetic and copies ran while one was open for 5% -> 2% of each run, Pallas kernels for 18% -> 20%
where the time goes in v5:
time: 103 us; the launch traced here: 102 us
  starting transfers between devices  44.9 us (44%)
  Pallas kernels  28.6 us (28%)
  waiting for transfers between devices  23.9 us (23%)
  other arithmetic  2.96 us (3%)
  local copies, waits for them, and re-layouts  1.24 us (1%)
    pallas_call x10, Pallas kernels, call(): pl.pallas_call(kernel, out_shape=outs, in_specs=[spec(s) for s in spaces]...  28.6 us
    ppermute x5, starting transfers between devices, up(): return lax.ppermute(value, 'seq', pairs)  11.3 us
    ppermute x5, starting transfers between devices, along_x(): return lax.ppermute(value, 'seq', pairs)  11 us
    ppermute x6, waiting for transfers between devices, tp_shift(): return lax.ppermute(value, 'tp', [(i, (i + step) % 4) for i in range(4)])  10.7 us
    ppermute x4, starting transfers between devices, down(): return lax.ppermute(value, 'seq', pairs)  10.4 us
    ppermute x6, starting transfers between devices, tp_shift(): return lax.ppermute(value, 'tp', [(i, (i + step) % 4) for i in range(4)])  8.91 us
    ppermute x5, waiting for transfers between devices, up(): return lax.ppermute(value, 'seq', pairs)  6.27 us
    ppermute x1, waiting for transfers between devices, local(): lax.ppermute(tail, 'seq', [(i, i + 2) for i in range(2 * NX * NZ - 2)])  5.97 us
  transfers between devices with their start and end apart: 25, of which 11 were waited for; matrix products, arithmetic and copies ran while one was open for 2% of the time, Pallas kernels for 20%

profile of v5, /device:TPU:192, one launch (start us, length us, event | category | flops | bytes accessed | tf_op | source)
XLA Modules:
  0.0 102.2 jit_solution(2209793642272701967)
XLA Ops:
  3.0 2.5 %pick.1 = (bf16[2,128,256]{2,1,0:T(8,128)(2,1)}, bf16[128,256]{1,0:T(8,128)(2,1)}) custom-call(s32[3]{0:T(128)} %pad_add_fusion.scal, s32[8,16]{1,0:T(8,128)} %blocks.1, bf16[256,256]{1,0:T(8,128)(2,1)} %k_ref.3, bf16[256,256]{1,0:T(8,128)(2,1)} %v_ref.3, bf16[256,256]{1,0:T(8,128)(2,1)} %copy-done.2, bf16[256,256]{1,0:T(8,128)(2,1)} %copy-done.4), custom_call_target="tpu_custom_call" | custom-call | bytes 1000000 | tf_op jit(solution)/shard_map/pick/pallas_call | solution.py:387
  5.6 3.1 %collective-permute-start.3 = (bf16[2,128,256]{2,1,0:T(8,128)(2,1)}, bf16[2,128,256]{2,1,0:T(8,128)(2,1)S(1)}, u32[]{:S(2)}, u32[]{:S(2)}) collective-permute-start(bf16[2,128,256]{2,1,0:T(8,128)(2,1)} %get-tuple-element.32), channel_id=1, source_target_pairs={{0,32},{4,36},{8,40},{12,44},{16,48},{20,52},{24,56},{28,60},{32,6... | collective-permute-start | bytes 393224 | tf_op jit(solution)/shard_map/ppermute | solution.py:70
  9.3 3.1 %collective-permute-start.5 = (bf16[2,128,256]{2,1,0:T(8,128)(2,1)}, bf16[2,128,256]{2,1,0:T(8,128)(2,1)S(1)}, u32[]{:S(2)}, u32[]{:S(2)}) collective-permute-start(bf16[2,128,256]{2,1,0:T(8,128)(2,1)} %get-tuple-element.32), channel_id=1, source_target_pairs={{0,16},{4,20},{8,24},{12,28},{16,0},{20,4},{24,8},{28,12},{32,48},... | collective-permute-start | bytes 393224 | tf_op jit(solution)/shard_map/ppermute | solution.py:60
  12.4 2.5 %collective-permute-start.4 = (bf16[128,256]{1,0:T(8,128)(2,1)}, bf16[128,256]{1,0:T(8,128)(2,1)S(1)}, u32[]{:S(2)}, u32[]{:S(2)}) collective-permute-start(bf16[128,256]{1,0:T(8,128)(2,1)} %get-tuple-element.33), channel_id=1, source_target_pairs={{0,8},{4,12},{8,16},{12,20},{16,24},{20,28},{24,32},{28,36},{32,40... | collective-permute-start | bytes 196616 | tf_op jit(solution)/shard_map/ppermute | solution.py:427
  14.9 6.0 %collective-permute-done.4.halo_ref = bf16[128,256]{1,0:T(8,128)(2,1)S(1)} collective-permute-done((bf16[128,256]{1,0:T(8,128)(2,1)}, bf16[128,256]{1,0:T(8,128)(2,1)S(1)}, u32[]{:S(2)}, u32[]{:S(2)}) %collective-permute-start.4) | collective-permute-done | bytes 65568 | tf_op jit(solution)/shard_map/ppermute | solution.py:427
  20.9 1.9 %collective-permute-start.6 = (bf16[4,128,256]{2,1,0:T(8,128)(2,1)S(1)}, bf16[4,128,256]{2,1,0:T(8,128)(2,1)S(1)}, u32[]{:S(2)}, u32[]{:S(2)}) collective-permute-start(bf16[4,128,256]{2,1,0:T(8,128)(2,1)S(1)} %get-tuple-element.59), channel_id=1, source_target_pairs={{0,32},{4,36},{8,40},{12,44},{16,48},{20,52},{24,56},{28,60},{32,6... | collective-permute-start | bytes 786440 | tf_op jit(solution)/shard_map/ppermute | solution.py:70
  23.0 1.3 %collective-permute-start.10 = (bf16[4,128,256]{2,1,0:T(8,128)(2,1)S(1)}, bf16[4,128,256]{2,1,0:T(8,128)(2,1)S(1)}, u32[]{:S(2)}, u32[]{:S(2)}) collective-permute-start(bf16[4,128,256]{2,1,0:T(8,128)(2,1)S(1)} %get-tuple-element.60), channel_id=1, source_target_pairs={{0,224},{4,228},{8,232},{12,236},{16,240},{20,244},{24,248},{28,25... | collective-permute-start | bytes 786440 | tf_op jit(solution)/shard_map/ppermute | solution.py:76
  24.3 5.2 %collective-permute-done.6.rest_0_ = bf16[4,128,256]{2,1,0:T(8,128)(2,1)S(1)} collective-permute-done((bf16[4,128,256]{2,1,0:T(8,128)(2,1)S(1)}, bf16[4,128,256]{2,1,0:T(8,128)(2,1)S(1)}, u32[]{:S(2)}, u32[]{:S(2)}) %collective-permute-start.6) | collective-permute-done | bytes 262176 | tf_op jit(solution)/shard_map/ppermute | solution.py:70
  29.5 2.2 %collective-permute-start.7 = (bf16[4,128,256]{2,1,0:T(8,128)(2,1)S(1)}, bf16[4,128,256]{2,1,0:T(8,128)(2,1)S(1)}, u32[]{:S(2)}, u32[]{:S(2)}) collective-permute-start(bf16[4,128,256]{2,1,0:T(8,128)(2,1)S(1)} %collective-permute-done.6.rest_0_), channel_id=1, source_target_pairs={{32,64},{36,68},{40,72},{44,76},{48,80},{52,84},{56,88},{60,92},{6... | collective-permute-start | bytes 786440 | tf_op jit(solution)/shard_map/ppermute | solution.py:70
  32.8 2.0 %collective-permute-start.12 = (bf16[8,128,256]{2,1,0:T(8,128)(2,1)S(1)}, bf16[8,128,256]{2,1,0:T(8,128)(2,1)S(1)}, u32[]{:S(2)}, u32[]{:S(2)}) collective-permute-start(bf16[8,128,256]{2,1,0:T(8,128)(2,1)S(1)} %pad_maximum_fusion.1.rest_0_), channel_id=1, source_target_pairs={{0,8},{4,12},{8,16},{12,20},{16,24},{20,28},{24,0},{28,4},{32,40},... | collective-permute-start | bytes 1572872 | tf_op jit(solution)/shard_map/ppermute | solution.py:60
  34.8 3.6 %collective-permute-start.11 = (bf16[4,128,256]{2,1,0:T(8,128)(2,1)S(1)}, bf16[4,128,256]{2,1,0:T(8,128)(2,1)S(1)}, u32[]{:S(2)}, u32[]{:S(2)}) collective-permute-start(bf16[4,128,256]{2,1,0:T(8,128)(2,1)S(1)} %collective-permute-done.10.rest_4_), channel_id=1, source_target_pairs={{0,224},{4,228},{8,232},{12,236},{16,240},{20,244},{24,248},{28,25... | collective-permute-start | bytes 786440 | tf_op jit(solution)/shard_map/ppermute | solution.py:76
  38.5 2.2 %collective-permute-start.8 = (bf16[4,128,256]{2,1,0:T(8,128)(2,1)S(1)}, bf16[4,128,256]{2,1,0:T(8,128)(2,1)S(1)}, u32[]{:S(2)}, u32[]{:S(2)}) collective-permute-start(bf16[4,128,256]{2,1,0:T(8,128)(2,1)S(1)} %collective-permute-done.7.rest_1_), channel_id=1, source_target_pairs={{64,96},{68,100},{72,104},{76,108},{80,112},{84,116},{88,120},{92,... | collective-permute-start | bytes 786440 | tf_op jit(solution)/shard_map/ppermute | solution.py:70
  40.8 5.5 %near_part.1 = (bf16[4,512,256]{2,1,0:T(8,128)(2,1)S(1)}, f32[4,512,256]{2,1,0:T(8,128)S(1)}, s32[256]{0:T(256)S(1)}, s32[16]{0:T(128)S(1)}) custom-call(s32[3]{0:T(128)S(1)} %copy-done.6, s32[8,16]{1,0:T(8,128)S(1)} %copy-done.7, s32[8]{0:T(128)S(1)} %copy-done.10, s32[8,8]{1,0:T(8,128)S(1)} %copy-done.9, s32[32]{0:T(128)S(1)} %copy-done.11, ...), custom_call_target="tpu_custom_call" | custom-call | flops 5000000000 | bytes 100000 | tf_op jit(solution)/shard_map/near_part/pallas_call | solution.py:387
  46.8 3.2 %collective-permute-start.15 = (bf16[8,128,256]{2,1,0:T(8,128)(2,1)S(1)}, bf16[8,128,256]{2,1,0:T(8,128)(2,1)S(1)}, u32[]{:S(2)}, u32[]{:S(2)}) collective-permute-start(bf16[8,128,256]{2,1,0:T(8,128)(2,1)S(1)} %pad_maximum_fusion), channel_id=1, source_target_pairs={{96,120},{100,124},{104,96},{108,100},{112,104},{116,108},{120,112... | collective-permute-start | bytes 1572872 | tf_op jit(solution)/shard_map/ppermute | solution.py:60
  50.0 2.6 %collective-permute-start.14 = (bf16[8,128,256]{2,1,0:T(8,128)(2,1)S(1)}, bf16[8,128,256]{2,1,0:T(8,128)(2,1)S(1)}, u32[]{:S(2)}, u32[]{:S(2)}) collective-permute-start(bf16[8,128,256]{2,1,0:T(8,128)(2,1)S(1)} %pad_maximum_fusion), channel_id=1, source_target_pairs={{96,104},{100,108},{104,112},{108,116},{112,120},{116,124},{120,96... | collective-permute-start | bytes 1572872 | tf_op jit(solution)/shard_map/ppermute | solution.py:60
  52.7 3.5 %far_part.3 = (bf16[4,512,256]{2,1,0:T(8,128)(2,1)S(1)}, f32[4,512,256]{2,1,0:T(8,128)S(1)}) custom-call(s32[3]{0:T(128)S(1)} %copy-done.6, s32[256]{0:T(256)S(1)} %get-tuple-element.35.lists, s32[16]{0:T(128)S(1)} %get-tuple-element.36.counts, bf16[4,512,256]{2,1,0:T(8,128)(2,1)S(1)} %get-tuple-element.37.qa_in, ...), custom_call_target="tpu_custom_call" | custom-call | flops 6000000000 | bytes 100000 | tf_op jit(solution)/shard_map/far_part/pallas_call | solution.py:387
  56.2 4.8 %collective-permute-start.17 = (bf16[2,128,256]{2,1,0:T(8,128)(2,1)S(1)}, bf16[2,128,256]{2,1,0:T(8,128)(2,1)S(1)}, u32[]{:S(2)}, u32[]{:S(2)}) collective-permute-start(bf16[2,128,256]{2,1,0:T(8,128)(2,1)S(1)} %slice.27), channel_id=1, source_target_pairs={{0,224},{4,228},{8,232},{12,236},{16,240},{20,244},{24,248},{28,25... | collective-permute-start | bytes 393224 | tf_op jit(solution)/shard_map/ppermute | solution.py:76
  61.0 1.9 %collective-permute-start.16 = (bf16[2,128,256]{2,1,0:T(8,128)(2,1)S(1)}, bf16[2,128,256]{2,1,0:T(8,128)(2,1)S(1)}, u32[]{:S(2)}, u32[]{:S(2)}) collective-permute-start(bf16[2,128,256]{2,1,0:T(8,128)(2,1)S(1)} %slice.26), channel_id=1, source_target_pairs={{96,128},{100,132},{104,136},{108,140},{112,144},{116,148},{120,15... | collective-permute-start | bytes 393224 | tf_op jit(solution)/shard_map/ppermute | solution.py:70
  63.2 4.1 %far_part.4 = (bf16[4,512,256]{2,1,0:T(8,128)(2,1)S(1)}, f32[4,512,256]{2,1,0:T(8,128)S(1)}) custom-call(s32[3]{0:T(128)S(1)} %copy-done.6, s32[256]{0:T(256)S(1)} %get-tuple-element.35.lists, s32[16]{0:T(128)S(1)} %get-tuple-element.36.counts, bf16[4,512,256]{2,1,0:T(8,128)(2,1)S(1)} %get-tuple-element.41.qa_in, ...), custom_call_target="tpu_custom_call" | custom-call | flops 6000000000 | bytes 100000 | tf_op jit(solution)/shard_map/far_part/pallas_call | solution.py:387
  67.9 4.6 %far_part.5 = (bf16[256,512]{1,0:T(8,128)(2,1)S(1)}, bf16[256,512]{1,0:T(8,128)(2,1)S(1)}) custom-call(s32[3]{0:T(128)S(1)} %copy-done.6, s32[256]{0:T(256)S(1)} %get-tuple-element.35.lists, s32[16]{0:T(128)S(1)} %get-tuple-element.36.counts, bf16[4,512,256]{2,1,0:T(8,128)(2,1)S(1)} %get-tuple-element.45.qa_in, f32[4,512,256]{2,1,0:T(8,128)S(1)} %get-tuple-element.46.acc_in, ...), custom_call_target="tpu_custom_call" | custom-call | flops 6000000000 | bytes 100000 | tf_op jit(solution)/shard_map/far_part/pallas_call | solution.py:387
  72.7 1.3 %own_part.3.part = f32[2,256,512]{2,1,0:T(8,128)S(1)} custom-call(s32[3]{0:T(128)S(1)} %copy-done.6, bf16[256,512]{1,0:T(8,128)(2,1)S(1)} %get-tuple-element.49.ctx, bf16[1024,4096]{1,0:T(8,128)(2,1)S(1)} %bitcast.4), custom_call_target="tpu_custom_call" | custom-call | flops 1000000 | bytes 1000 | tf_op jit(solution)/shard_map/own_part/pallas_call | solution.py:387
  74.2 1.3 %sib_part.3 = (bf16[256,512]{1,0:T(8,128)(2,1)S(1)}, bf16[256,512]{1,0:T(8,128)(2,1)S(1)}) custom-call(s32[3]{0:T(128)S(1)} %copy-done.6, bf16[256,512]{1,0:T(8,128)(2,1)S(1)} %collective-permute-done.18.ctx_sib.ctx, f32[2,256,512]{2,1,0:T(8,128)S(1)} %own_part.3.part, bf16[1024,4096]{1,0:T(8,128)(2,1)S(1)} %bitcast.4), custom_call_target="tpu_custom_call" | custom-call | flops 1000000 | bytes 1000 | tf_op jit(solution)/shard_map/sib_part/pallas_call | solution.py:387
  75.5 1.7 %collective-permute-start.20 = (bf16[256,512]{1,0:T(8,128)(2,1)S(1)}, bf16[256,512]{1,0:T(8,128)(2,1)S(1)}, u32[]{:S(2)}, u32[]{:S(2)}) collective-permute-start(bf16[256,512]{1,0:T(8,128)(2,1)S(1)} %get-tuple-element.54), channel_id=1, source_target_pairs={{0,1},{1,2},{2,3},{3,0},{4,5},{5,6},{6,7},{7,4},{8,9},{9,10},{10,1... | collective-permute-start | bytes 786440 | tf_op jit(solution)/shard_map/ppermute | solution.py:84
  77.1 1.8 %collective-permute-start.23 = (bf16[256,512]{1,0:T(8,128)(2,1)S(1)}, bf16[256,512]{1,0:T(8,128)(2,1)S(1)}, u32[]{:S(2)}, u32[]{:S(2)}) collective-permute-start(bf16[256,512]{1,0:T(8,128)(2,1)S(1)} %get-tuple-element.58), channel_id=1, source_target_pairs={{0,3},{1,0},{2,1},{3,2},{4,7},{5,4},{6,5},{7,6},{8,11},{9,8},{10,9... | collective-permute-start | bytes 786440 | tf_op jit(solution)/shard_map/ppermute | solution.py:84
  78.9 1.3 %own_part.2.part = f32[2,256,512]{2,1,0:T(8,128)S(1)} custom-call(s32[3]{0:T(128)S(1)} %copy-done.6, bf16[256,512]{1,0:T(8,128)(2,1)S(1)} %get-tuple-element.49.ctx, bf16[1024,4096]{1,0:T(8,128)(2,1)S(1)} %bitcast.4), custom_call_target="tpu_custom_call" | custom-call | flops 1000000 | bytes 1000 | tf_op jit(solution)/shard_map/own_part/pallas_call | solution.py:387
  80.2 1.3 %sib_part.2 = (bf16[256,512]{1,0:T(8,128)(2,1)S(1)}, bf16[256,512]{1,0:T(8,128)(2,1)S(1)}) custom-call(s32[3]{0:T(128)S(1)} %copy-done.6, bf16[256,512]{1,0:T(8,128)(2,1)S(1)} %collective-permute-done.18.ctx_sib.ctx, f32[2,256,512]{2,1,0:T(8,128)S(1)} %own_part.2.part, bf16[1024,4096]{1,0:T(8,128)(2,1)S(1)} %bitcast.4), custom_call_target="tpu_custom_call" | custom-call | flops 1000000 | bytes 1000 | tf_op jit(solution)/shard_map/sib_part/pallas_call | solution.py:387
  81.6 1.8 %collective-permute-start.19 = (bf16[256,512]{1,0:T(8,128)(2,1)S(1)}, bf16[256,512]{1,0:T(8,128)(2,1)S(1)}, u32[]{:S(2)}, u32[]{:S(2)}) collective-permute-start(bf16[256,512]{1,0:T(8,128)(2,1)S(1)} %get-tuple-element.52), channel_id=1, source_target_pairs={{0,3},{1,0},{2,1},{3,2},{4,7},{5,4},{6,5},{7,6},{8,11},{9,8},{10,9... | collective-permute-start | bytes 786440 | tf_op jit(solution)/shard_map/ppermute | solution.py:84
  83.3 3.2 %other_shares.1 = (f32[256,512]{1,0:T(8,128)S(1)}, f32[256,512]{1,0:T(8,128)S(1)}, f32[256,512]{1,0:T(8,128)S(1)}, f32[256,512]{1,0:T(8,128)S(1)}) custom-call(s32[3]{0:T(128)S(1)} %copy-done.6, bf16[256,512]{1,0:T(8,128)(2,1)S(1)} %get-tuple-element.49.ctx, bf16[256,512]{1,0:T(8,128)(2,1)S(1)} %collective-permute-done.18.ctx_sib.ctx, ...), custom_call_target="tpu_custom_call" | custom-call | flops 1000000 | bytes 1000 | tf_op jit(solution)/shard_map/other_shares/pallas_call | solution.py:387
  87.5 2.9 %collective-permute-start.24 = (bf16[256,512]{1,0:T(8,128)(2,1)S(1)}, bf16[256,512]{1,0:T(8,128)(2,1)S(1)}, u32[]{:S(2)}, u32[]{:S(2)}) collective-permute-start(bf16[256,512]{1,0:T(8,128)(2,1)S(1)} %add_convert_fusion.1), channel_id=1, source_target_pairs={{0,3},{1,0},{2,1},{3,2},{4,7},{5,4},{6,5},{7,6},{8,11},{9,8},{10,9... | collective-permute-start | bytes 786440 | tf_op jit(solution)/shard_map/ppermute | solution.py:84
  90.4 1.5 %collective-permute-done.19 = bf16[256,512]{1,0:T(8,128)(2,1)S(1)} collective-permute-done((bf16[256,512]{1,0:T(8,128)(2,1)S(1)}, bf16[256,512]{1,0:T(8,128)(2,1)S(1)}, u32[]{:S(2)}, u32[]{:S(2)}) %collective-permute-start.19) | collective-permute-done | bytes 262176 | tf_op jit(solution)/shard_map/ppermute | solution.py:84
  91.9 5.2 %collective-permute-done.21 = bf16[256,512]{1,0:T(8,128)(2,1)S(1)} collective-permute-done((bf16[256,512]{1,0:T(8,128)(2,1)S(1)}, bf16[256,512]{1,0:T(8,128)(2,1)S(1)}, u32[]{:S(2)}, u32[]{:S(2)}) %collective-permute-start.21) | collective-permute-done | bytes 262176 | tf_op jit(solution)/shard_map/ppermute | solution.py:84
  97.2 4.0 %collective-permute-done.22 = bf16[256,512]{1,0:T(8,128)(2,1)S(1)} collective-permute-done((bf16[256,512]{1,0:T(8,128)(2,1)S(1)}, bf16[256,512]{1,0:T(8,128)(2,1)S(1)}, u32[]{:S(2)}, u32[]{:S(2)}) %collective-permute-start.22) | collective-permute-done | bytes 262176 | tf_op jit(solution)/shard_map/ppermute | solution.py:84
  (73 shorter events, 8.6 us)
Async XLA Ops:
  0.0 40.7 %copy-start.11 = (s32[32]{0:T(128)S(1)}, s32[32]{0:T(128)}, u32[]{:S(2)}) copy-start(s32[32]{0:T(128)} %constant.24.clone.table) | copy-start | bytes 388
  0.0 40.7 %copy-start = (bf16[256,256]{1,0:T(8,128)(2,1)S(1)}, bf16[256,256]{1,0:T(8,128)(2,1)}, u32[]{:S(2)}) copy-start(bf16[256,256]{1,0:T(8,128)(2,1)} %k_ref.3) | copy-start | bytes 393220
  0.0 40.7 %copy-start.1 = (bf16[256,256]{1,0:T(8,128)(2,1)S(1)}, bf16[256,256]{1,0:T(8,128)(2,1)}, u32[]{:S(2)}) copy-start(bf16[256,256]{1,0:T(8,128)(2,1)} %v_ref.3) | copy-start | bytes 393220
  0.0 40.7 %copy-start.7 = (s32[8,16]{1,0:T(8,128)S(1)}, s32[8,16]{1,0:T(8,128)}, u32[]{:S(2)}) copy-start(s32[8,16]{1,0:T(8,128)} %blocks.1) | copy-start | bytes 1540
  0.0 40.7 %copy-start.8 = (bf16[256,1024]{1,0:T(8,128)(2,1)S(1)}, bf16[256,1024]{1,0:T(8,128)(2,1)}, u32[]{:S(2)}) copy-start(bf16[256,1024]{1,0:T(8,128)(2,1)} %q_ref.1) | copy-start | bytes 1572868
  0.0 40.7 %copy-start.9 = (s32[8,8]{1,0:T(8,128)S(1)}, s32[8,8]{1,0:T(8,128)}, u32[]{:S(2)}) copy-start(s32[8,8]{1,0:T(8,128)} %slash.1) | copy-start | bytes 772
  0.0 40.7 %copy-start.10 = (s32[8]{0:T(128)S(1)}, s32[8]{0:T(128)}, u32[]{:S(2)}) copy-start(s32[8]{0:T(128)} %window.1) | copy-start | bytes 100
  0.1 1.6 %collective-permute-start.1 = (bf16[256,256]{1,0:T(8,128)(2,1)}, bf16[256,256]{1,0:T(8,128)(2,1)S(1)}, u32[]{:S(2)}, u32[]{:S(2)}) collective-permute-start(bf16[256,256]{1,0:T(8,128)(2,1)} %k_ref.3), channel_id=1, source_target_pairs={{0,4},{4,0},{8,12},{12,8},{16,20},{20,16},{24,28},{28,24},{32,36},... | collective-permute-start | bytes 393224 | tf_op jit(solution)/shard_map/ppermute | solution.py:80
  0.2 1.7 %collective-permute-start.2 = (bf16[256,256]{1,0:T(8,128)(2,1)}, bf16[256,256]{1,0:T(8,128)(2,1)S(1)}, u32[]{:S(2)}, u32[]{:S(2)}) collective-permute-start(bf16[256,256]{1,0:T(8,128)(2,1)} %v_ref.3), channel_id=1, source_target_pairs={{0,4},{4,0},{8,12},{12,8},{16,20},{20,16},{24,28},{28,24},{32,36},... | collective-permute-start | bytes 393224 | tf_op jit(solution)/shard_map/ppermute | solution.py:80
  5.6 15.3 %collective-permute-start.3 = (bf16[2,128,256]{2,1,0:T(8,128)(2,1)}, bf16[2,128,256]{2,1,0:T(8,128)(2,1)S(1)}, u32[]{:S(2)}, u32[]{:S(2)}) collective-permute-start(bf16[2,128,256]{2,1,0:T(8,128)(2,1)} %get-tuple-element.32), channel_id=1, source_target_pairs={{0,32},{4,36},{8,40},{12,44},{16,48},{20,52},{24,56},{28,60},{32,6... | collective-permute-start | bytes 393224 | tf_op jit(solution)/shard_map/ppermute | solution.py:70
  8.6 12.3 %collective-permute-start.9 = (bf16[2,128,256]{2,1,0:T(8,128)(2,1)}, bf16[2,128,256]{2,1,0:T(8,128)(2,1)S(1)}, u32[]{:S(2)}, u32[]{:S(2)}) collective-permute-start(bf16[2,128,256]{2,1,0:T(8,128)(2,1)} %get-tuple-element.32), channel_id=1, source_target_pairs={{0,224},{4,228},{8,232},{12,236},{16,240},{20,244},{24,248},{28,25... | collective-permute-start | bytes 393224 | tf_op jit(solution)/shard_map/ppermute | solution.py:76
  9.3 11.6 %collective-permute-start.5 = (bf16[2,128,256]{2,1,0:T(8,128)(2,1)}, bf16[2,128,256]{2,1,0:T(8,128)(2,1)S(1)}, u32[]{:S(2)}, u32[]{:S(2)}) collective-permute-start(bf16[2,128,256]{2,1,0:T(8,128)(2,1)} %get-tuple-element.32), channel_id=1, source_target_pairs={{0,16},{4,20},{8,24},{12,28},{16,0},{20,4},{24,8},{28,12},{32,48},... | collective-permute-start | bytes 393224 | tf_op jit(solution)/shard_map/ppermute | solution.py:60
  12.4 8.5 %collective-permute-start.4 = (bf16[128,256]{1,0:T(8,128)(2,1)}, bf16[128,256]{1,0:T(8,128)(2,1)S(1)}, u32[]{:S(2)}, u32[]{:S(2)}) collective-permute-start(bf16[128,256]{1,0:T(8,128)(2,1)} %get-tuple-element.33), channel_id=1, source_target_pairs={{0,8},{4,12},{8,16},{12,20},{16,24},{20,28},{24,32},{28,36},{32,40... | collective-permute-start | bytes 196616 | tf_op jit(solution)/shard_map/ppermute | solution.py:427
  20.9 8.5 %collective-permute-start.6 = (bf16[4,128,256]{2,1,0:T(8,128)(2,1)S(1)}, bf16[4,128,256]{2,1,0:T(8,128)(2,1)S(1)}, u32[]{:S(2)}, u32[]{:S(2)}) collective-permute-start(bf16[4,128,256]{2,1,0:T(8,128)(2,1)S(1)} %get-tuple-element.59), channel_id=1, source_target_pairs={{0,32},{4,36},{8,40},{12,44},{16,48},{20,52},{24,56},{28,60},{32,6... | collective-permute-start | bytes 786440 | tf_op jit(solution)/shard_map/ppermute | solution.py:70
  22.9 17.8 %collective-permute-start = (bf16[256,1024]{1,0:T(8,128)(2,1)}, bf16[256,1024]{1,0:T(8,128)(2,1)S(1)}, u32[]{:S(2)}, u32[]{:S(2)}) collective-permute-start(bf16[256,1024]{1,0:T(8,128)(2,1)} %q_ref.1), channel_id=1, source_target_pairs={{0,4},{4,0},{8,12},{12,8},{16,20},{20,16},{24,28},{28,24},{32,36},... | collective-permute-start | bytes 1572872 | tf_op jit(solution)/shard_map/ppermute | solution.py:80
  23.0 11.8 %collective-permute-start.10 = (bf16[4,128,256]{2,1,0:T(8,128)(2,1)S(1)}, bf16[4,128,256]{2,1,0:T(8,128)(2,1)S(1)}, u32[]{:S(2)}, u32[]{:S(2)}) collective-permute-start(bf16[4,128,256]{2,1,0:T(8,128)(2,1)S(1)} %get-tuple-element.60), channel_id=1, source_target_pairs={{0,224},{4,228},{8,232},{12,236},{16,240},{20,244},{24,248},{28,25... | collective-permute-start | bytes 786440 | tf_op jit(solution)/shard_map/ppermute | solution.py:76
  29.5 9.0 %collective-permute-start.7 = (bf16[4,128,256]{2,1,0:T(8,128)(2,1)S(1)}, bf16[4,128,256]{2,1,0:T(8,128)(2,1)S(1)}, u32[]{:S(2)}, u32[]{:S(2)}) collective-permute-start(bf16[4,128,256]{2,1,0:T(8,128)(2,1)S(1)} %collective-permute-done.6.rest_0_), channel_id=1, source_target_pairs={{32,64},{36,68},{40,72},{44,76},{48,80},{52,84},{56,88},{60,92},{6... | collective-permute-start | bytes 786440 | tf_op jit(solution)/shard_map/ppermute | solution.py:70
  32.7 20.0 %collective-permute-start.13 = (bf16[8,128,256]{2,1,0:T(8,128)(2,1)S(1)}, bf16[8,128,256]{2,1,0:T(8,128)(2,1)S(1)}, u32[]{:S(2)}, u32[]{:S(2)}) collective-permute-start(bf16[8,128,256]{2,1,0:T(8,128)(2,1)S(1)} %pad_maximum_fusion.1.rest_0_), channel_id=1, source_target_pairs={{0,24},{4,28},{8,0},{12,4},{16,8},{20,12},{24,16},{28,20},{32,56},... | collective-permute-start | bytes 1572872 | tf_op jit(solution)/shard_map/ppermute | solution.py:60
  32.8 19.9 %collective-permute-start.12 = (bf16[8,128,256]{2,1,0:T(8,128)(2,1)S(1)}, bf16[8,128,256]{2,1,0:T(8,128)(2,1)S(1)}, u32[]{:S(2)}, u32[]{:S(2)}) collective-permute-start(bf16[8,128,256]{2,1,0:T(8,128)(2,1)S(1)} %pad_maximum_fusion.1.rest_0_), channel_id=1, source_target_pairs={{0,8},{4,12},{8,16},{12,20},{16,24},{20,28},{24,0},{28,4},{32,40},... | collective-permute-start | bytes 1572872 | tf_op jit(solution)/shard_map/ppermute | solution.py:60
  34.8 11.5 %collective-permute-start.11 = (bf16[4,128,256]{2,1,0:T(8,128)(2,1)S(1)}, bf16[4,128,256]{2,1,0:T(8,128)(2,1)S(1)}, u32[]{:S(2)}, u32[]{:S(2)}) collective-permute-start(bf16[4,128,256]{2,1,0:T(8,128)(2,1)S(1)} %collective-permute-done.10.rest_4_), channel_id=1, source_target_pairs={{0,224},{4,228},{8,232},{12,236},{16,240},{20,244},{24,248},{28,25... | collective-permute-start | bytes 786440 | tf_op jit(solution)/shard_map/ppermute | solution.py:76
  38.5 8.3 %collective-permute-start.8 = (bf16[4,128,256]{2,1,0:T(8,128)(2,1)S(1)}, bf16[4,128,256]{2,1,0:T(8,128)(2,1)S(1)}, u32[]{:S(2)}, u32[]{:S(2)}) collective-permute-start(bf16[4,128,256]{2,1,0:T(8,128)(2,1)S(1)} %collective-permute-done.7.rest_1_), channel_id=1, source_target_pairs={{64,96},{68,100},{72,104},{76,108},{80,112},{84,116},{88,120},{92,... | collective-permute-start | bytes 786440 | tf_op jit(solution)/shard_map/ppermute | solution.py:70
  46.8 16.1 %collective-permute-start.15 = (bf16[8,128,256]{2,1,0:T(8,128)(2,1)S(1)}, bf16[8,128,256]{2,1,0:T(8,128)(2,1)S(1)}, u32[]{:S(2)}, u32[]{:S(2)}) collective-permute-start(bf16[8,128,256]{2,1,0:T(8,128)(2,1)S(1)} %pad_maximum_fusion), channel_id=1, source_target_pairs={{96,120},{100,124},{104,96},{108,100},{112,104},{116,108},{120,112... | collective-permute-start | bytes 1572872 | tf_op jit(solution)/shard_map/ppermute | solution.py:60
  50.0 13.1 %collective-permute-start.14 = (bf16[8,128,256]{2,1,0:T(8,128)(2,1)S(1)}, bf16[8,128,256]{2,1,0:T(8,128)(2,1)S(1)}, u32[]{:S(2)}, u32[]{:S(2)}) collective-permute-start(bf16[8,128,256]{2,1,0:T(8,128)(2,1)S(1)} %pad_maximum_fusion), channel_id=1, source_target_pairs={{96,104},{100,108},{104,112},{108,116},{112,120},{116,124},{120,96... | collective-permute-start | bytes 1572872 | tf_op jit(solution)/shard_map/ppermute | solution.py:60
  56.2 11.1 %collective-permute-start.17 = (bf16[2,128,256]{2,1,0:T(8,128)(2,1)S(1)}, bf16[2,128,256]{2,1,0:T(8,128)(2,1)S(1)}, u32[]{:S(2)}, u32[]{:S(2)}) collective-permute-start(bf16[2,128,256]{2,1,0:T(8,128)(2,1)S(1)} %slice.27), channel_id=1, source_target_pairs={{0,224},{4,228},{8,232},{12,236},{16,240},{20,244},{24,248},{28,25... | collective-permute-start | bytes 393224 | tf_op jit(solution)/shard_map/ppermute | solution.py:76
  61.0 6.9 %collective-permute-start.16 = (bf16[2,128,256]{2,1,0:T(8,128)(2,1)S(1)}, bf16[2,128,256]{2,1,0:T(8,128)(2,1)S(1)}, u32[]{:S(2)}, u32[]{:S(2)}) collective-permute-start(bf16[2,128,256]{2,1,0:T(8,128)(2,1)S(1)} %slice.26), channel_id=1, source_target_pairs={{96,128},{100,132},{104,136},{108,140},{112,144},{116,148},{120,15... | collective-permute-start | bytes 393224 | tf_op jit(solution)/shard_map/ppermute | solution.py:70
  72.5 1.6 %collective-permute-start.18 = (bf16[256,512]{1,0:T(8,128)(2,1)S(1)}, bf16[256,512]{1,0:T(8,128)(2,1)S(1)}, u32[]{:S(2)}, u32[]{:S(2)}) collective-permute-start(bf16[256,512]{1,0:T(8,128)(2,1)S(1)} %get-tuple-element.50), channel_id=1, source_target_pairs={{0,4},{4,0},{8,12},{12,8},{16,20},{20,16},{24,28},{28,24},{32,36},... | collective-permute-start | bytes 786440 | tf_op jit(solution)/shard_map/ppermute | solution.py:80
  75.5 11.0 %collective-permute-start.20 = (bf16[256,512]{1,0:T(8,128)(2,1)S(1)}, bf16[256,512]{1,0:T(8,128)(2,1)S(1)}, u32[]{:S(2)}, u32[]{:S(2)}) collective-permute-start(bf16[256,512]{1,0:T(8,128)(2,1)S(1)} %get-tuple-element.54), channel_id=1, source_target_pairs={{0,1},{1,2},{2,3},{3,0},{4,5},{5,6},{6,7},{7,4},{8,9},{9,10},{10,1... | collective-permute-start | bytes 786440 | tf_op jit(solution)/shard_map/ppermute | solution.py:84
  77.1 10.2 %collective-permute-start.23 = (bf16[256,512]{1,0:T(8,128)(2,1)S(1)}, bf16[256,512]{1,0:T(8,128)(2,1)S(1)}, u32[]{:S(2)}, u32[]{:S(2)}) collective-permute-start(bf16[256,512]{1,0:T(8,128)(2,1)S(1)} %get-tuple-element.58), channel_id=1, source_target_pairs={{0,3},{1,0},{2,1},{3,2},{4,7},{5,4},{6,5},{7,6},{8,11},{9,8},{10,9... | collective-permute-start | bytes 786440 | tf_op jit(solution)/shard_map/ppermute | solution.py:84
  81.6 10.4 %collective-permute-start.19 = (bf16[256,512]{1,0:T(8,128)(2,1)S(1)}, bf16[256,512]{1,0:T(8,128)(2,1)S(1)}, u32[]{:S(2)}, u32[]{:S(2)}) collective-permute-start(bf16[256,512]{1,0:T(8,128)(2,1)S(1)} %get-tuple-element.52), channel_id=1, source_target_pairs={{0,3},{1,0},{2,1},{3,2},{4,7},{5,4},{6,5},{7,6},{8,11},{9,8},{10,9... | collective-permute-start | bytes 786440 | tf_op jit(solution)/shard_map/ppermute | solution.py:84
  86.6 10.5 %collective-permute-start.21 = (bf16[256,512]{1,0:T(8,128)(2,1)S(1)}, bf16[256,512]{1,0:T(8,128)(2,1)S(1)}, u32[]{:S(2)}, u32[]{:S(2)}) collective-permute-start(bf16[256,512]{1,0:T(8,128)(2,1)S(1)} %add_convert_fusion.3), channel_id=1, source_target_pairs={{0,1},{1,2},{2,3},{3,0},{4,5},{5,6},{6,7},{7,4},{8,9},{9,10},{10,1... | collective-permute-start | bytes 786440 | tf_op jit(solution)/shard_map/ppermute | solution.py:84
  87.0 14.2 %collective-permute-start.22 = (bf16[256,512]{1,0:T(8,128)(2,1)S(1)}, bf16[256,512]{1,0:T(8,128)(2,1)S(1)}, u32[]{:S(2)}, u32[]{:S(2)}) collective-permute-start(bf16[256,512]{1,0:T(8,128)(2,1)S(1)} %get-tuple-element.56), channel_id=1, source_target_pairs={{0,1},{1,2},{2,3},{3,0},{4,5},{5,6},{6,7},{7,4},{8,9},{9,10},{10,1... | collective-permute-start | bytes 786440 | tf_op jit(solution)/shard_map/ppermute | solution.py:84
  87.5 13.7 %collective-permute-start.24 = (bf16[256,512]{1,0:T(8,128)(2,1)S(1)}, bf16[256,512]{1,0:T(8,128)(2,1)S(1)}, u32[]{:S(2)}, u32[]{:S(2)}) collective-permute-start(bf16[256,512]{1,0:T(8,128)(2,1)S(1)} %add_convert_fusion.1), channel_id=1, source_target_pairs={{0,3},{1,0},{2,1},{3,2},{4,7},{5,4},{6,5},{7,6},{8,11},{9,8},{10,9... | collective-permute-start | bytes 786440 | tf_op jit(solution)/shard_map/ppermute | solution.py:84
  (7 other events, 120.7 us)

commit v6 on v5

--- a/solution.py
+++ b/solution.py
@@ -37,9 +37,9 @@
     put(0, 8, first, -1)
     put(0, 16, first, 1)
     put(0, 24, (0,), 2)
-    for at, dz in ((4, -3), (8, -4), (14, 2), (18, 3)):
+    for at, dz in ((0, -3), (4, -4), (12, 2), (16, 3)):
         put(2, at, (dz,), 0)
-    for at, dz in ((2, -1), (6, -2), (10, -3), (12, -4), (16, 1), (20, 2), (22, 3)):
+    for at, dz in ((2, -1), (6, -2), (8, -3), (10, -4), (14, 1), (18, 2), (20, 3)):
         put(2, at, (dz,), 2)
     put(1, 0, second, -1)
     put(1, 8, second, 1)
@@ -60,10 +60,10 @@
     return lax.ppermute(value, "seq", pairs)
 
 
-def up(value, lowest):
+def up(value, lowest, levels=1):
     pairs = [
-        (seq_at(z, x, c), seq_at(z + 1, x, c))
-        for z in range(lowest, NZ - 1)
+        (seq_at(z, x, c), seq_at(z + levels, x, c))
+        for z in range(lowest, NZ - levels)
         for x in range(NX)
         for c in range(2)
     ]
@@ -426,13 +426,13 @@
 
     halo = lax.ppermute(tail, "seq", [(i, i + 2) for i in range(2 * NX * NZ - 2)])
 
-    up1, down1 = up(unit, 0), down(unit, (1,))
+    up1, up2, down1 = up(unit, 0), up(unit, 0, 2), down(unit, (1,))
     opposite = along_x(unit, 2, 0)
-    up1, halo = lax.optimization_barrier((up1, halo))
-    up2 = up(jnp.concatenate([up1, opposite], axis=0), 0)
+    up2, halo = lax.optimization_barrier((up2, halo))
+    up3 = up(jnp.concatenate([up2, opposite], axis=0), 0)
     down2 = down(jnp.concatenate([down1, opposite], axis=0), (2, 1))
-    up3, down3 = up(up2, 1), down(down2, (3, 2))
-    first = jnp.concatenate([unit, up1, up2[:2], down1], axis=0)
+    down3 = down(down2, (3, 2))
+    first = jnp.concatenate([unit, up1, up2, down1], axis=0)
     right1, left1 = along_x(first, 1, 0), along_x(first, -1, 0)
 
     rows = 2 * queries.shape[0]
@@ -484,7 +484,7 @@
             moved=100_000,
         )
 
-    up4 = up(up3, 2)
+    up4 = up(up3, 1)
     second = jnp.concatenate([up3[:2], up4[:2], down2[:2], down3[:2]], axis=0)
     crossed = call(
         crossed_kernel, "crossed", [shape((8, HD), F32)], (right1, left1), [anywhere] * 2,
@@ -493,10 +493,11 @@
     second, acc, crossed = lax.optimization_barrier((second, acc, crossed))
     right2, left2 = along_x(second, 1, 3), along_x(second, -1, 3)
     qa, acc = far(0, [first, right1, left1, opposite], qa, acc)
-    up4, down3, acc = lax.optimization_barrier((up4, down3, acc))
-    up5, down4 = up(up4[2:], 3), down(down3[2:], (3,))
+    down3, acc = lax.optimization_barrier((down3, acc))
+    up5 = up(jnp.concatenate([up3[2:], up4[2:]], axis=0), 1, 2)
+    down4 = down(down3[2:], (3,))
     qa, acc = far(1, [right2, left2], qa, acc)
-    ctx_mine, ctx_other = far(2, [up2, up3, up4, up5, down2, down3, down4], qa, acc)
+    ctx_mine, ctx_other = far(2, [up3, up4, up5, down2, down3, down4], qa, acc)
     ctx_sib = swap_cores(ctx_other)
 
     half_rows, half = rows // 2, out_weight.shape[1] // 8

time: 103 us -> 101 us (0.981)
  waiting for transfers between devices: 23.9 us -> 17.6 us
  local copies, waits for them, and re-layouts: 1.24 us -> 3.99 us
  starting transfers between devices: 44.9 us -> 47.4 us
    ppermute x1, waiting for transfers between devices: 5.97 us -> 0.27 us  [local(): lax.ppermute(tail, 'seq', [(i, i + 2) for i in range(2 * NX * NZ - 2)])]
    unnamed x28 -> x31, local copies, waits for them, and re-layouts: 1.17 us -> 3.91 us
    ppermute x5, waiting for transfers between devices: 6.27 us -> 4 us  [up(): return lax.ppermute(value, 'seq', pairs)]
    ppermute x5, waiting for transfers between devices: 0.21 us -> 1.28 us  [along_x(): return lax.ppermute(value, 'seq', pairs)]
where the time goes in v6:
time: 101 us; the launch traced here: 99.9 us
  starting transfers between devices  47.4 us (47%)
  Pallas kernels  28.4 us (28%)
  waiting for transfers between devices  17.6 us (17%)
  local copies, waits for them, and re-layouts  3.99 us (4%)
  other arithmetic  2.01 us (2%)
    pallas_call x10, Pallas kernels, call(): pl.pallas_call(kernel, out_shape=outs, in_specs=[spec(s) for s in spaces]...  28.4 us
    ppermute x5, starting transfers between devices, up(): return lax.ppermute(value, 'seq', pairs)  12.3 us
    ppermute x4, starting transfers between devices, down(): return lax.ppermute(value, 'seq', pairs)  11.1 us
    ppermute x5, starting transfers between devices, along_x(): return lax.ppermute(value, 'seq', pairs)  11.1 us
    ppermute x6, waiting for transfers between devices, tp_shift(): return lax.ppermute(value, 'tp', [(i, (i + step) % 4) for i in range(4)])  10.7 us
    ppermute x6, starting transfers between devices, tp_shift(): return lax.ppermute(value, 'tp', [(i, (i + step) % 4) for i in range(4)])  8.9 us
    ppermute x5, waiting for transfers between devices, up(): return lax.ppermute(value, 'seq', pairs)  4 us
    unnamed x31, local copies, waits for them, and re-layouts  3.91 us
  transfers between devices with their start and end apart: 25, of which 11 were waited for; matrix products, arithmetic and copies ran while one was open for 2% of the time, Pallas kernels for 20%

profile of v6, /device:TPU:192, one launch (start us, length us, event | category | flops | bytes accessed | tf_op | source)
XLA Modules:
  0.0 99.9 jit_solution(9195267998366879278)
XLA Ops:
  3.0 2.5 %pick.1 = (bf16[2,128,256]{2,1,0:T(8,128)(2,1)}, bf16[128,256]{1,0:T(8,128)(2,1)}) custom-call(s32[3]{0:T(128)} %pad_add_fusion.scal, s32[8,16]{1,0:T(8,128)} %blocks.1, bf16[256,256]{1,0:T(8,128)(2,1)} %k_ref.3, bf16[256,256]{1,0:T(8,128)(2,1)} %v_ref.3, bf16[256,256]{1,0:T(8,128)(2,1)} %copy-done.2, bf16[256,256]{1,0:T(8,128)(2,1)} %copy-done.4), custom_call_target="tpu_custom_call" | custom-call | bytes 1000000 | tf_op jit(solution)/shard_map/pick/pallas_call | solution.py:387
  5.5 3.4 %collective-permute-start.4 = (bf16[128,256]{1,0:T(8,128)(2,1)}, bf16[128,256]{1,0:T(8,128)(2,1)S(1)}, u32[]{:S(2)}, u32[]{:S(2)}) collective-permute-start(bf16[128,256]{1,0:T(8,128)(2,1)} %get-tuple-element.32), channel_id=1, source_target_pairs={{0,8},{4,12},{8,16},{12,20},{16,24},{20,28},{24,32},{28,36},{32,40... | collective-permute-start | bytes 196616 | tf_op jit(solution)/shard_map/ppermute | solution.py:427
  8.9 1.3 %collective-permute-start.3 = (bf16[2,128,256]{2,1,0:T(8,128)(2,1)}, bf16[2,128,256]{2,1,0:T(8,128)(2,1)S(1)}, u32[]{:S(2)}, u32[]{:S(2)}) collective-permute-start(bf16[2,128,256]{2,1,0:T(8,128)(2,1)} %get-tuple-element.31), channel_id=1, source_target_pairs={{0,64},{4,68},{8,72},{12,76},{16,80},{20,84},{24,88},{28,92},{32,9... | collective-permute-start | bytes 393224 | tf_op jit(solution)/shard_map/ppermute | solution.py:70
  10.9 2.8 %collective-permute-start.5 = (bf16[2,128,256]{2,1,0:T(8,128)(2,1)}, bf16[2,128,256]{2,1,0:T(8,128)(2,1)S(1)}, u32[]{:S(2)}, u32[]{:S(2)}) collective-permute-start(bf16[2,128,256]{2,1,0:T(8,128)(2,1)} %get-tuple-element.31), channel_id=1, source_target_pairs={{0,16},{4,20},{8,24},{12,28},{16,0},{20,4},{24,8},{28,12},{32,48},... | collective-permute-start | bytes 393224 | tf_op jit(solution)/shard_map/ppermute | solution.py:60
  14.0 3.3 %collective-permute-start.11 = (bf16[2,128,256]{2,1,0:T(8,128)(2,1)}, bf16[2,128,256]{2,1,0:T(8,128)(2,1)S(1)}, u32[]{:S(2)}, u32[]{:S(2)}) collective-permute-start(bf16[2,128,256]{2,1,0:T(8,128)(2,1)} %get-tuple-element.31), channel_id=1, source_target_pairs={{0,32},{4,36},{8,40},{12,44},{16,48},{20,52},{24,56},{28,60},{32,6... | collective-permute-start | bytes 393224 | tf_op jit(solution)/shard_map/ppermute | solution.py:70
  18.2 1.9 %collective-permute-done.3 = bf16[2,128,256]{2,1,0:T(8,128)(2,1)S(1)} collective-permute-done((bf16[2,128,256]{2,1,0:T(8,128)(2,1)}, bf16[2,128,256]{2,1,0:T(8,128)(2,1)S(1)}, u32[]{:S(2)}, u32[]{:S(2)}) %collective-permute-start.3) | collective-permute-done | bytes 131104 | tf_op jit(solution)/shard_map/ppermute | solution.py:70
  20.1 2.7 %collective-permute-start.6 = (bf16[4,128,256]{2,1,0:T(8,128)(2,1)S(1)}, bf16[4,128,256]{2,1,0:T(8,128)(2,1)S(1)}, u32[]{:S(2)}, u32[]{:S(2)}) collective-permute-start(bf16[4,128,256]{2,1,0:T(8,128)(2,1)S(1)} %get-tuple-element.61), channel_id=1, source_target_pairs={{0,32},{4,36},{8,40},{12,44},{16,48},{20,52},{24,56},{28,60},{32,6... | collective-permute-start | bytes 786440 | tf_op jit(solution)/shard_map/ppermute | solution.py:70
  22.8 1.3 %collective-permute-start.9 = (bf16[4,128,256]{2,1,0:T(8,128)(2,1)S(1)}, bf16[4,128,256]{2,1,0:T(8,128)(2,1)S(1)}, u32[]{:S(2)}, u32[]{:S(2)}) collective-permute-start(bf16[4,128,256]{2,1,0:T(8,128)(2,1)S(1)} %get-tuple-element.62), channel_id=1, source_target_pairs={{0,224},{4,228},{8,232},{12,236},{16,240},{20,244},{24,248},{28,25... | collective-permute-start | bytes 786440 | tf_op jit(solution)/shard_map/ppermute | solution.py:76
  24.2 1.3 %collective-permute-start.13 = (bf16[8,128,256]{2,1,0:T(8,128)(2,1)S(1)}, bf16[8,128,256]{2,1,0:T(8,128)(2,1)S(1)}, u32[]{:S(2)}, u32[]{:S(2)}) collective-permute-start(bf16[8,128,256]{2,1,0:T(8,128)(2,1)S(1)} %constant_dynamic-update-slice_fusion.rest_0_), channel_id=1, source_target_pairs={{0,24},{4,28},{8,0},{12,4},{16,8},{20,12},{24,16},{28,20},{32,56},... | collective-permute-start | bytes 1572872 | tf_op jit(solution)/shard_map/ppermute | solution.py:60
  26.6 2.1 %collective-permute-done.6.rest_0_ = bf16[4,128,256]{2,1,0:T(8,128)(2,1)S(1)} collective-permute-done((bf16[4,128,256]{2,1,0:T(8,128)(2,1)S(1)}, bf16[4,128,256]{2,1,0:T(8,128)(2,1)S(1)}, u32[]{:S(2)}, u32[]{:S(2)}) %collective-permute-start.6) | collective-permute-done | bytes 262176 | tf_op jit(solution)/shard_map/ppermute | solution.py:70
  28.7 3.7 %collective-permute-start.7 = (bf16[4,128,256]{2,1,0:T(8,128)(2,1)S(1)}, bf16[4,128,256]{2,1,0:T(8,128)(2,1)S(1)}, u32[]{:S(2)}, u32[]{:S(2)}) collective-permute-start(bf16[4,128,256]{2,1,0:T(8,128)(2,1)S(1)} %collective-permute-done.6.rest_0_), channel_id=1, source_target_pairs={{32,64},{36,68},{40,72},{44,76},{48,80},{52,84},{56,88},{60,92},{6... | collective-permute-start | bytes 786440 | tf_op jit(solution)/shard_map/ppermute | solution.py:70
  32.4 2.2 %collective-permute-start.10 = (bf16[4,128,256]{2,1,0:T(8,128)(2,1)S(1)}, bf16[4,128,256]{2,1,0:T(8,128)(2,1)S(1)}, u32[]{:S(2)}, u32[]{:S(2)}) collective-permute-start(bf16[4,128,256]{2,1,0:T(8,128)(2,1)S(1)} %collective-permute-done.9.rest_3_), channel_id=1, source_target_pairs={{0,224},{4,228},{8,232},{12,236},{16,240},{20,244},{24,248},{28,25... | collective-permute-start | bytes 786440 | tf_op jit(solution)/shard_map/ppermute | solution.py:76
  36.5 5.4 %near_part.1 = (bf16[4,512,256]{2,1,0:T(8,128)(2,1)S(1)}, f32[4,512,256]{2,1,0:T(8,128)S(1)}, s32[256]{0:T(256)S(1)}, s32[16]{0:T(128)S(1)}) custom-call(s32[3]{0:T(128)S(1)} %copy-done.6, s32[8,16]{1,0:T(8,128)S(1)} %copy-done.7, s32[8]{0:T(128)S(1)} %copy-done.10, s32[8,8]{1,0:T(8,128)S(1)} %copy-done.9, s32[32]{0:T(128)S(1)} %copy-done.11, ...), custom_call_target="tpu_custom_call" | custom-call | flops 5000000000 | bytes 100000 | tf_op jit(solution)/shard_map/near_part/pallas_call | solution.py:387
  42.7 3.9 %collective-permute-start.15 = (bf16[8,128,256]{2,1,0:T(8,128)(2,1)S(1)}, bf16[8,128,256]{2,1,0:T(8,128)(2,1)S(1)}, u32[]{:S(2)}, u32[]{:S(2)}) collective-permute-start(bf16[8,128,256]{2,1,0:T(8,128)(2,1)S(1)} %pad_maximum_fusion), channel_id=1, source_target_pairs={{96,120},{100,124},{104,96},{108,100},{112,104},{116,108},{120,112... | collective-permute-start | bytes 1572872 | tf_op jit(solution)/shard_map/ppermute | solution.py:60
  46.6 2.0 %collective-permute-start.14 = (bf16[8,128,256]{2,1,0:T(8,128)(2,1)S(1)}, bf16[8,128,256]{2,1,0:T(8,128)(2,1)S(1)}, u32[]{:S(2)}, u32[]{:S(2)}) collective-permute-start(bf16[8,128,256]{2,1,0:T(8,128)(2,1)S(1)} %pad_maximum_fusion), channel_id=1, source_target_pairs={{96,104},{100,108},{104,112},{108,116},{112,120},{116,124},{120,96... | collective-permute-start | bytes 1572872 | tf_op jit(solution)/shard_map/ppermute | solution.py:60
  48.6 1.3 %collective-permute-start.16 = (bf16[4,128,256]{2,1,0:T(8,128)(2,1)S(1)}, bf16[4,128,256]{2,1,0:T(8,128)(2,1)S(1)}, u32[]{:S(2)}, u32[]{:S(2)}) collective-permute-start(bf16[4,128,256]{2,1,0:T(8,128)(2,1)S(1)} %pad_maximum_fusion.4), channel_id=1, source_target_pairs={{32,96},{36,100},{40,104},{44,108},{48,112},{52,116},{56,120},{60,... | collective-permute-start | bytes 786440 | tf_op jit(solution)/shard_map/ppermute | solution.py:70
  50.0 3.5 %far_part.3 = (bf16[4,512,256]{2,1,0:T(8,128)(2,1)S(1)}, f32[4,512,256]{2,1,0:T(8,128)S(1)}) custom-call(s32[3]{0:T(128)S(1)} %copy-done.6, s32[256]{0:T(256)S(1)} %get-tuple-element.34.lists, s32[16]{0:T(128)S(1)} %get-tuple-element.35.counts, bf16[4,512,256]{2,1,0:T(8,128)(2,1)S(1)} %get-tuple-element.36.qa_in, ...), custom_call_target="tpu_custom_call" | custom-call | flops 6000000000 | bytes 100000 | tf_op jit(solution)/shard_map/far_part/pallas_call | solution.py:387
  53.4 6.9 %collective-permute-start.17 = (bf16[2,128,256]{2,1,0:T(8,128)(2,1)S(1)}, bf16[2,128,256]{2,1,0:T(8,128)(2,1)S(1)}, u32[]{:S(2)}, u32[]{:S(2)}) collective-permute-start(bf16[2,128,256]{2,1,0:T(8,128)(2,1)S(1)} %slice.27), channel_id=1, source_target_pairs={{0,224},{4,228},{8,232},{12,236},{16,240},{20,244},{24,248},{28,25... | collective-permute-start | bytes 393224 | tf_op jit(solution)/shard_map/ppermute | solution.py:76
  61.7 4.1 %far_part.4 = (bf16[4,512,256]{2,1,0:T(8,128)(2,1)S(1)}, f32[4,512,256]{2,1,0:T(8,128)S(1)}) custom-call(s32[3]{0:T(128)S(1)} %copy-done.6, s32[256]{0:T(256)S(1)} %get-tuple-element.34.lists, s32[16]{0:T(128)S(1)} %get-tuple-element.35.counts, bf16[4,512,256]{2,1,0:T(8,128)(2,1)S(1)} %get-tuple-element.40.qa_in, ...), custom_call_target="tpu_custom_call" | custom-call | flops 6000000000 | bytes 100000 | tf_op jit(solution)/shard_map/far_part/pallas_call | solution.py:387
  65.8 4.5 %far_part.5 = (bf16[256,512]{1,0:T(8,128)(2,1)S(1)}, bf16[256,512]{1,0:T(8,128)(2,1)S(1)}) custom-call(s32[3]{0:T(128)S(1)} %copy-done.6, s32[256]{0:T(256)S(1)} %get-tuple-element.34.lists, s32[16]{0:T(128)S(1)} %get-tuple-element.35.counts, bf16[4,512,256]{2,1,0:T(8,128)(2,1)S(1)} %get-tuple-element.44.qa_in, f32[4,512,256]{2,1,0:T(8,128)S(1)} %get-tuple-element.45.acc_in, ...), custom_call_target="tpu_custom_call" | custom-call | flops 6000000000 | bytes 100000 | tf_op jit(solution)/shard_map/far_part/pallas_call | solution.py:387
  70.4 1.3 %own_part.3.part = f32[2,256,512]{2,1,0:T(8,128)S(1)} custom-call(s32[3]{0:T(128)S(1)} %copy-done.6, bf16[256,512]{1,0:T(8,128)(2,1)S(1)} %get-tuple-element.47.ctx, bf16[1024,4096]{1,0:T(8,128)(2,1)S(1)} %bitcast.4), custom_call_target="tpu_custom_call" | custom-call | flops 1000000 | bytes 1000 | tf_op jit(solution)/shard_map/own_part/pallas_call | solution.py:387
  71.9 1.3 %sib_part.3 = (bf16[256,512]{1,0:T(8,128)(2,1)S(1)}, bf16[256,512]{1,0:T(8,128)(2,1)S(1)}) custom-call(s32[3]{0:T(128)S(1)} %copy-done.6, bf16[256,512]{1,0:T(8,128)(2,1)S(1)} %collective-permute-done.18.ctx_sib.ctx, f32[2,256,512]{2,1,0:T(8,128)S(1)} %own_part.3.part, bf16[1024,4096]{1,0:T(8,128)(2,1)S(1)} %bitcast.4), custom_call_target="tpu_custom_call" | custom-call | flops 1000000 | bytes 1000 | tf_op jit(solution)/shard_map/sib_part/pallas_call | solution.py:387
  73.2 1.7 %collective-permute-start.20 = (bf16[256,512]{1,0:T(8,128)(2,1)S(1)}, bf16[256,512]{1,0:T(8,128)(2,1)S(1)}, u32[]{:S(2)}, u32[]{:S(2)}) collective-permute-start(bf16[256,512]{1,0:T(8,128)(2,1)S(1)} %get-tuple-element.52), channel_id=1, source_target_pairs={{0,1},{1,2},{2,3},{3,0},{4,5},{5,6},{6,7},{7,4},{8,9},{9,10},{10,1... | collective-permute-start | bytes 786440 | tf_op jit(solution)/shard_map/ppermute | solution.py:84
  74.9 1.7 %collective-permute-start.23 = (bf16[256,512]{1,0:T(8,128)(2,1)S(1)}, bf16[256,512]{1,0:T(8,128)(2,1)S(1)}, u32[]{:S(2)}, u32[]{:S(2)}) collective-permute-start(bf16[256,512]{1,0:T(8,128)(2,1)S(1)} %get-tuple-element.56), channel_id=1, source_target_pairs={{0,3},{1,0},{2,1},{3,2},{4,7},{5,4},{6,5},{7,6},{8,11},{9,8},{10,9... | collective-permute-start | bytes 786440 | tf_op jit(solution)/shard_map/ppermute | solution.py:84
  76.6 1.3 %own_part.2.part = f32[2,256,512]{2,1,0:T(8,128)S(1)} custom-call(s32[3]{0:T(128)S(1)} %copy-done.6, bf16[256,512]{1,0:T(8,128)(2,1)S(1)} %get-tuple-element.47.ctx, bf16[1024,4096]{1,0:T(8,128)(2,1)S(1)} %bitcast.4), custom_call_target="tpu_custom_call" | custom-call | flops 1000000 | bytes 1000 | tf_op jit(solution)/shard_map/own_part/pallas_call | solution.py:387
  78.0 1.3 %sib_part.2 = (bf16[256,512]{1,0:T(8,128)(2,1)S(1)}, bf16[256,512]{1,0:T(8,128)(2,1)S(1)}) custom-call(s32[3]{0:T(128)S(1)} %copy-done.6, bf16[256,512]{1,0:T(8,128)(2,1)S(1)} %collective-permute-done.18.ctx_sib.ctx, f32[2,256,512]{2,1,0:T(8,128)S(1)} %own_part.2.part, bf16[1024,4096]{1,0:T(8,128)(2,1)S(1)} %bitcast.4), custom_call_target="tpu_custom_call" | custom-call | flops 1000000 | bytes 1000 | tf_op jit(solution)/shard_map/sib_part/pallas_call | solution.py:387
  79.3 1.8 %collective-permute-start.19 = (bf16[256,512]{1,0:T(8,128)(2,1)S(1)}, bf16[256,512]{1,0:T(8,128)(2,1)S(1)}, u32[]{:S(2)}, u32[]{:S(2)}) collective-permute-start(bf16[256,512]{1,0:T(8,128)(2,1)S(1)} %get-tuple-element.50), channel_id=1, source_target_pairs={{0,3},{1,0},{2,1},{3,2},{4,7},{5,4},{6,5},{7,6},{8,11},{9,8},{10,9... | collective-permute-start | bytes 786440 | tf_op jit(solution)/shard_map/ppermute | solution.py:84
  81.1 3.2 %other_shares.1 = (f32[256,512]{1,0:T(8,128)S(1)}, f32[256,512]{1,0:T(8,128)S(1)}, f32[256,512]{1,0:T(8,128)S(1)}, f32[256,512]{1,0:T(8,128)S(1)}) custom-call(s32[3]{0:T(128)S(1)} %copy-done.6, bf16[256,512]{1,0:T(8,128)(2,1)S(1)} %get-tuple-element.47.ctx, bf16[256,512]{1,0:T(8,128)(2,1)S(1)} %collective-permute-done.18.ctx_sib.ctx, ...), custom_call_target="tpu_custom_call" | custom-call | flops 1000000 | bytes 1000 | tf_op jit(solution)/shard_map/other_shares/pallas_call | solution.py:387
  85.2 2.9 %collective-permute-start.24 = (bf16[256,512]{1,0:T(8,128)(2,1)S(1)}, bf16[256,512]{1,0:T(8,128)(2,1)S(1)}, u32[]{:S(2)}, u32[]{:S(2)}) collective-permute-start(bf16[256,512]{1,0:T(8,128)(2,1)S(1)} %add_convert_fusion.1), channel_id=1, source_target_pairs={{0,3},{1,0},{2,1},{3,2},{4,7},{5,4},{6,5},{7,6},{8,11},{9,8},{10,9... | collective-permute-start | bytes 786440 | tf_op jit(solution)/shard_map/ppermute | solution.py:84
  88.1 1.6 %collective-permute-done.19 = bf16[256,512]{1,0:T(8,128)(2,1)S(1)} collective-permute-done((bf16[256,512]{1,0:T(8,128)(2,1)S(1)}, bf16[256,512]{1,0:T(8,128)(2,1)S(1)}, u32[]{:S(2)}, u32[]{:S(2)}) %collective-permute-start.19) | collective-permute-done | bytes 262176 | tf_op jit(solution)/shard_map/ppermute | solution.py:84
  89.7 5.2 %collective-permute-done.21 = bf16[256,512]{1,0:T(8,128)(2,1)S(1)} collective-permute-done((bf16[256,512]{1,0:T(8,128)(2,1)S(1)}, bf16[256,512]{1,0:T(8,128)(2,1)S(1)}, u32[]{:S(2)}, u32[]{:S(2)}) %collective-permute-start.21) | collective-permute-done | bytes 262176 | tf_op jit(solution)/shard_map/ppermute | solution.py:84
  95.0 4.0 %collective-permute-done.22 = bf16[256,512]{1,0:T(8,128)(2,1)S(1)} collective-permute-done((bf16[256,512]{1,0:T(8,128)(2,1)S(1)}, bf16[256,512]{1,0:T(8,128)(2,1)S(1)}, u32[]{:S(2)}, u32[]{:S(2)}) %collective-permute-start.22) | collective-permute-done | bytes 262176 | tf_op jit(solution)/shard_map/ppermute | solution.py:84
  (75 shorter events, 12.2 us)
Async XLA Ops:
  0.0 34.6 %copy-start.11 = (s32[32]{0:T(128)S(1)}, s32[32]{0:T(128)}, u32[]{:S(2)}) copy-start(s32[32]{0:T(128)} %constant.24.clone.table) | copy-start | bytes 388
  0.0 34.6 %copy-start = (bf16[256,256]{1,0:T(8,128)(2,1)S(1)}, bf16[256,256]{1,0:T(8,128)(2,1)}, u32[]{:S(2)}) copy-start(bf16[256,256]{1,0:T(8,128)(2,1)} %k_ref.3) | copy-start | bytes 393220
  0.0 34.6 %copy-start.1 = (bf16[256,256]{1,0:T(8,128)(2,1)S(1)}, bf16[256,256]{1,0:T(8,128)(2,1)}, u32[]{:S(2)}) copy-start(bf16[256,256]{1,0:T(8,128)(2,1)} %v_ref.3) | copy-start | bytes 393220
  0.0 34.6 %copy-start.7 = (s32[8,16]{1,0:T(8,128)S(1)}, s32[8,16]{1,0:T(8,128)}, u32[]{:S(2)}) copy-start(s32[8,16]{1,0:T(8,128)} %blocks.1) | copy-start | bytes 1540
  0.0 34.6 %copy-start.8 = (bf16[256,1024]{1,0:T(8,128)(2,1)S(1)}, bf16[256,1024]{1,0:T(8,128)(2,1)}, u32[]{:S(2)}) copy-start(bf16[256,1024]{1,0:T(8,128)(2,1)} %q_ref.1) | copy-start | bytes 1572868
  0.0 34.6 %copy-start.9 = (s32[8,8]{1,0:T(8,128)S(1)}, s32[8,8]{1,0:T(8,128)}, u32[]{:S(2)}) copy-start(s32[8,8]{1,0:T(8,128)} %slash.1) | copy-start | bytes 772
  0.0 34.6 %copy-start.10 = (s32[8]{0:T(128)S(1)}, s32[8]{0:T(128)}, u32[]{:S(2)}) copy-start(s32[8]{0:T(128)} %window.1) | copy-start | bytes 100
  0.1 1.6 %collective-permute-start.1 = (bf16[256,256]{1,0:T(8,128)(2,1)}, bf16[256,256]{1,0:T(8,128)(2,1)S(1)}, u32[]{:S(2)}, u32[]{:S(2)}) collective-permute-start(bf16[256,256]{1,0:T(8,128)(2,1)} %k_ref.3), channel_id=1, source_target_pairs={{0,4},{4,0},{8,12},{12,8},{16,20},{20,16},{24,28},{28,24},{32,36},... | collective-permute-start | bytes 393224 | tf_op jit(solution)/shard_map/ppermute | solution.py:80
  0.2 1.7 %collective-permute-start.2 = (bf16[256,256]{1,0:T(8,128)(2,1)}, bf16[256,256]{1,0:T(8,128)(2,1)S(1)}, u32[]{:S(2)}, u32[]{:S(2)}) collective-permute-start(bf16[256,256]{1,0:T(8,128)(2,1)} %v_ref.3), channel_id=1, source_target_pairs={{0,4},{4,0},{8,12},{12,8},{16,20},{20,16},{24,28},{28,24},{32,36},... | collective-permute-start | bytes 393224 | tf_op jit(solution)/shard_map/ppermute | solution.py:80
  5.5 8.5 %collective-permute-start.4 = (bf16[128,256]{1,0:T(8,128)(2,1)}, bf16[128,256]{1,0:T(8,128)(2,1)S(1)}, u32[]{:S(2)}, u32[]{:S(2)}) collective-permute-start(bf16[128,256]{1,0:T(8,128)(2,1)} %get-tuple-element.32), channel_id=1, source_target_pairs={{0,8},{4,12},{8,16},{12,20},{16,24},{20,28},{24,32},{28,36},{32,40... | collective-permute-start | bytes 196616 | tf_op jit(solution)/shard_map/ppermute | solution.py:427
  8.9 11.1 %collective-permute-start.3 = (bf16[2,128,256]{2,1,0:T(8,128)(2,1)}, bf16[2,128,256]{2,1,0:T(8,128)(2,1)S(1)}, u32[]{:S(2)}, u32[]{:S(2)}) collective-permute-start(bf16[2,128,256]{2,1,0:T(8,128)(2,1)} %get-tuple-element.31), channel_id=1, source_target_pairs={{0,64},{4,68},{8,72},{12,76},{16,80},{20,84},{24,88},{28,92},{32,9... | collective-permute-start | bytes 393224 | tf_op jit(solution)/shard_map/ppermute | solution.py:70
  10.2 9.8 %collective-permute-start.8 = (bf16[2,128,256]{2,1,0:T(8,128)(2,1)}, bf16[2,128,256]{2,1,0:T(8,128)(2,1)S(1)}, u32[]{:S(2)}, u32[]{:S(2)}) collective-permute-start(bf16[2,128,256]{2,1,0:T(8,128)(2,1)} %get-tuple-element.31), channel_id=1, source_target_pairs={{0,224},{4,228},{8,232},{12,236},{16,240},{20,244},{24,248},{28,25... | collective-permute-start | bytes 393224 | tf_op jit(solution)/shard_map/ppermute | solution.py:76
  10.9 9.2 %collective-permute-start.5 = (bf16[2,128,256]{2,1,0:T(8,128)(2,1)}, bf16[2,128,256]{2,1,0:T(8,128)(2,1)S(1)}, u32[]{:S(2)}, u32[]{:S(2)}) collective-permute-start(bf16[2,128,256]{2,1,0:T(8,128)(2,1)} %get-tuple-element.31), channel_id=1, source_target_pairs={{0,16},{4,20},{8,24},{12,28},{16,0},{20,4},{24,8},{28,12},{32,48},... | collective-permute-start | bytes 393224 | tf_op jit(solution)/shard_map/ppermute | solution.py:60
  13.7 20.9 %collective-permute-start = (bf16[256,1024]{1,0:T(8,128)(2,1)}, bf16[256,1024]{1,0:T(8,128)(2,1)S(1)}, u32[]{:S(2)}, u32[]{:S(2)}) collective-permute-start(bf16[256,1024]{1,0:T(8,128)(2,1)} %q_ref.1), channel_id=1, source_target_pairs={{0,4},{4,0},{8,12},{12,8},{16,20},{20,16},{24,28},{28,24},{32,36},... | collective-permute-start | bytes 1572872 | tf_op jit(solution)/shard_map/ppermute | solution.py:80
  14.0 10.1 %collective-permute-start.11 = (bf16[2,128,256]{2,1,0:T(8,128)(2,1)}, bf16[2,128,256]{2,1,0:T(8,128)(2,1)S(1)}, u32[]{:S(2)}, u32[]{:S(2)}) collective-permute-start(bf16[2,128,256]{2,1,0:T(8,128)(2,1)} %get-tuple-element.31), channel_id=1, source_target_pairs={{0,32},{4,36},{8,40},{12,44},{16,48},{20,52},{24,56},{28,60},{32,6... | collective-permute-start | bytes 393224 | tf_op jit(solution)/shard_map/ppermute | solution.py:70
  20.1 8.6 %collective-permute-start.6 = (bf16[4,128,256]{2,1,0:T(8,128)(2,1)S(1)}, bf16[4,128,256]{2,1,0:T(8,128)(2,1)S(1)}, u32[]{:S(2)}, u32[]{:S(2)}) collective-permute-start(bf16[4,128,256]{2,1,0:T(8,128)(2,1)S(1)} %get-tuple-element.61), channel_id=1, source_target_pairs={{0,32},{4,36},{8,40},{12,44},{16,48},{20,52},{24,56},{28,60},{32,6... | collective-permute-start | bytes 786440 | tf_op jit(solution)/shard_map/ppermute | solution.py:70
  22.8 9.6 %collective-permute-start.9 = (bf16[4,128,256]{2,1,0:T(8,128)(2,1)S(1)}, bf16[4,128,256]{2,1,0:T(8,128)(2,1)S(1)}, u32[]{:S(2)}, u32[]{:S(2)}) collective-permute-start(bf16[4,128,256]{2,1,0:T(8,128)(2,1)S(1)} %get-tuple-element.62), channel_id=1, source_target_pairs={{0,224},{4,228},{8,232},{12,236},{16,240},{20,244},{24,248},{28,25... | collective-permute-start | bytes 786440 | tf_op jit(solution)/shard_map/ppermute | solution.py:76
  24.2 25.8 %collective-permute-start.13 = (bf16[8,128,256]{2,1,0:T(8,128)(2,1)S(1)}, bf16[8,128,256]{2,1,0:T(8,128)(2,1)S(1)}, u32[]{:S(2)}, u32[]{:S(2)}) collective-permute-start(bf16[8,128,256]{2,1,0:T(8,128)(2,1)S(1)} %constant_dynamic-update-slice_fusion.rest_0_), channel_id=1, source_target_pairs={{0,24},{4,28},{8,0},{12,4},{16,8},{20,12},{24,16},{28,20},{32,56},... | collective-permute-start | bytes 1572872 | tf_op jit(solution)/shard_map/ppermute | solution.py:60
  25.5 24.5 %collective-permute-start.12 = (bf16[8,128,256]{2,1,0:T(8,128)(2,1)S(1)}, bf16[8,128,256]{2,1,0:T(8,128)(2,1)S(1)}, u32[]{:S(2)}, u32[]{:S(2)}) collective-permute-start(bf16[8,128,256]{2,1,0:T(8,128)(2,1)S(1)} %constant_dynamic-update-slice_fusion.rest_0_), channel_id=1, source_target_pairs={{0,8},{4,12},{8,16},{12,20},{16,24},{20,28},{24,0},{28,4},{32,40},... | collective-permute-start | bytes 1572872 | tf_op jit(solution)/shard_map/ppermute | solution.py:60
  28.7 13.9 %collective-permute-start.7 = (bf16[4,128,256]{2,1,0:T(8,128)(2,1)S(1)}, bf16[4,128,256]{2,1,0:T(8,128)(2,1)S(1)}, u32[]{:S(2)}, u32[]{:S(2)}) collective-permute-start(bf16[4,128,256]{2,1,0:T(8,128)(2,1)S(1)} %collective-permute-done.6.rest_0_), channel_id=1, source_target_pairs={{32,64},{36,68},{40,72},{44,76},{48,80},{52,84},{56,88},{60,92},{6... | collective-permute-start | bytes 786440 | tf_op jit(solution)/shard_map/ppermute | solution.py:70
  32.4 10.2 %collective-permute-start.10 = (bf16[4,128,256]{2,1,0:T(8,128)(2,1)S(1)}, bf16[4,128,256]{2,1,0:T(8,128)(2,1)S(1)}, u32[]{:S(2)}, u32[]{:S(2)}) collective-permute-start(bf16[4,128,256]{2,1,0:T(8,128)(2,1)S(1)} %collective-permute-done.9.rest_3_), channel_id=1, source_target_pairs={{0,224},{4,228},{8,232},{12,236},{16,240},{20,244},{24,248},{28,25... | collective-permute-start | bytes 786440 | tf_op jit(solution)/shard_map/ppermute | solution.py:76
  42.7 17.7 %collective-permute-start.15 = (bf16[8,128,256]{2,1,0:T(8,128)(2,1)S(1)}, bf16[8,128,256]{2,1,0:T(8,128)(2,1)S(1)}, u32[]{:S(2)}, u32[]{:S(2)}) collective-permute-start(bf16[8,128,256]{2,1,0:T(8,128)(2,1)S(1)} %pad_maximum_fusion), channel_id=1, source_target_pairs={{96,120},{100,124},{104,96},{108,100},{112,104},{116,108},{120,112... | collective-permute-start | bytes 1572872 | tf_op jit(solution)/shard_map/ppermute | solution.py:60
  46.6 15.1 %collective-permute-start.14 = (bf16[8,128,256]{2,1,0:T(8,128)(2,1)S(1)}, bf16[8,128,256]{2,1,0:T(8,128)(2,1)S(1)}, u32[]{:S(2)}, u32[]{:S(2)}) collective-permute-start(bf16[8,128,256]{2,1,0:T(8,128)(2,1)S(1)} %pad_maximum_fusion), channel_id=1, source_target_pairs={{96,104},{100,108},{104,112},{108,116},{112,120},{116,124},{120,96... | collective-permute-start | bytes 1572872 | tf_op jit(solution)/shard_map/ppermute | solution.py:60
  48.6 17.1 %collective-permute-start.16 = (bf16[4,128,256]{2,1,0:T(8,128)(2,1)S(1)}, bf16[4,128,256]{2,1,0:T(8,128)(2,1)S(1)}, u32[]{:S(2)}, u32[]{:S(2)}) collective-permute-start(bf16[4,128,256]{2,1,0:T(8,128)(2,1)S(1)} %pad_maximum_fusion.4), channel_id=1, source_target_pairs={{32,96},{36,100},{40,104},{44,108},{48,112},{52,116},{56,120},{60,... | collective-permute-start | bytes 786440 | tf_op jit(solution)/shard_map/ppermute | solution.py:70
  53.4 12.3 %collective-permute-start.17 = (bf16[2,128,256]{2,1,0:T(8,128)(2,1)S(1)}, bf16[2,128,256]{2,1,0:T(8,128)(2,1)S(1)}, u32[]{:S(2)}, u32[]{:S(2)}) collective-permute-start(bf16[2,128,256]{2,1,0:T(8,128)(2,1)S(1)} %slice.27), channel_id=1, source_target_pairs={{0,224},{4,228},{8,232},{12,236},{16,240},{20,244},{24,248},{28,25... | collective-permute-start | bytes 393224 | tf_op jit(solution)/shard_map/ppermute | solution.py:76
  70.3 1.6 %collective-permute-start.18 = (bf16[256,512]{1,0:T(8,128)(2,1)S(1)}, bf16[256,512]{1,0:T(8,128)(2,1)S(1)}, u32[]{:S(2)}, u32[]{:S(2)}) collective-permute-start(bf16[256,512]{1,0:T(8,128)(2,1)S(1)} %get-tuple-element.48), channel_id=1, source_target_pairs={{0,4},{4,0},{8,12},{12,8},{16,20},{20,16},{24,28},{28,24},{32,36},... | collective-permute-start | bytes 786440 | tf_op jit(solution)/shard_map/ppermute | solution.py:80
  73.2 11.0 %collective-permute-start.20 = (bf16[256,512]{1,0:T(8,128)(2,1)S(1)}, bf16[256,512]{1,0:T(8,128)(2,1)S(1)}, u32[]{:S(2)}, u32[]{:S(2)}) collective-permute-start(bf16[256,512]{1,0:T(8,128)(2,1)S(1)} %get-tuple-element.52), channel_id=1, source_target_pairs={{0,1},{1,2},{2,3},{3,0},{4,5},{5,6},{6,7},{7,4},{8,9},{9,10},{10,1... | collective-permute-start | bytes 786440 | tf_op jit(solution)/shard_map/ppermute | solution.py:84
  74.9 10.3 %collective-permute-start.23 = (bf16[256,512]{1,0:T(8,128)(2,1)S(1)}, bf16[256,512]{1,0:T(8,128)(2,1)S(1)}, u32[]{:S(2)}, u32[]{:S(2)}) collective-permute-start(bf16[256,512]{1,0:T(8,128)(2,1)S(1)} %get-tuple-element.56), channel_id=1, source_target_pairs={{0,3},{1,0},{2,1},{3,2},{4,7},{5,4},{6,5},{7,6},{8,11},{9,8},{10,9... | collective-permute-start | bytes 786440 | tf_op jit(solution)/shard_map/ppermute | solution.py:84
  79.3 10.4 %collective-permute-start.19 = (bf16[256,512]{1,0:T(8,128)(2,1)S(1)}, bf16[256,512]{1,0:T(8,128)(2,1)S(1)}, u32[]{:S(2)}, u32[]{:S(2)}) collective-permute-start(bf16[256,512]{1,0:T(8,128)(2,1)S(1)} %get-tuple-element.50), channel_id=1, source_target_pairs={{0,3},{1,0},{2,1},{3,2},{4,7},{5,4},{6,5},{7,6},{8,11},{9,8},{10,9... | collective-permute-start | bytes 786440 | tf_op jit(solution)/shard_map/ppermute | solution.py:84
  84.3 10.5 %collective-permute-start.21 = (bf16[256,512]{1,0:T(8,128)(2,1)S(1)}, bf16[256,512]{1,0:T(8,128)(2,1)S(1)}, u32[]{:S(2)}, u32[]{:S(2)}) collective-permute-start(bf16[256,512]{1,0:T(8,128)(2,1)S(1)} %add_convert_fusion.3), channel_id=1, source_target_pairs={{0,1},{1,2},{2,3},{3,0},{4,5},{5,6},{6,7},{7,4},{8,9},{9,10},{10,1... | collective-permute-start | bytes 786440 | tf_op jit(solution)/shard_map/ppermute | solution.py:84
  84.7 14.2 %collective-permute-start.22 = (bf16[256,512]{1,0:T(8,128)(2,1)S(1)}, bf16[256,512]{1,0:T(8,128)(2,1)S(1)}, u32[]{:S(2)}, u32[]{:S(2)}) collective-permute-start(bf16[256,512]{1,0:T(8,128)(2,1)S(1)} %get-tuple-element.54), channel_id=1, source_target_pairs={{0,1},{1,2},{2,3},{3,0},{4,5},{5,6},{6,7},{7,4},{8,9},{9,10},{10,1... | collective-permute-start | bytes 786440 | tf_op jit(solution)/shard_map/ppermute | solution.py:84
  85.2 13.7 %collective-permute-start.24 = (bf16[256,512]{1,0:T(8,128)(2,1)S(1)}, bf16[256,512]{1,0:T(8,128)(2,1)S(1)}, u32[]{:S(2)}, u32[]{:S(2)}) collective-permute-start(bf16[256,512]{1,0:T(8,128)(2,1)S(1)} %add_convert_fusion.1), channel_id=1, source_target_pairs={{0,3},{1,0},{2,1},{3,2},{4,7},{5,4},{6,5},{7,6},{8,11},{9,8},{10,9... | collective-permute-start | bytes 786440 | tf_op jit(solution)/shard_map/ppermute | solution.py:84
  (7 other events, 45.7 us)

commit v7 on v6

--- a/solution.py
+++ b/solution.py
@@ -37,10 +37,11 @@
     put(0, 8, first, -1)
     put(0, 16, first, 1)
     put(0, 24, (0,), 2)
-    for at, dz in ((0, -3), (4, -4), (12, 2), (16, 3)):
-        put(2, at, (dz,), 0)
-    for at, dz in ((2, -1), (6, -2), (8, -3), (10, -4), (14, 1), (18, 2), (20, 3)):
-        put(2, at, (dz,), 2)
+    for at, dz in ((26, -3), (30, -4), (34, 2), (38, 3)):
+        put(0, at, (dz,), 0)
+    for at, dz in ((28, -1), (32, -2), (36, 1), (40, 2)):
+        put(0, at, (dz,), 2)
+    put(1, 16, (-3, -4, 3), 2)
     put(1, 0, second, -1)
     put(1, 8, second, 1)
     return table.reshape(-1)
@@ -468,7 +469,7 @@
             pltpu.SMEM((3 * (GROUP * PICKS + AT_ONCE),), I32),
             pltpu.SemaphoreType.DMA((len(sizes),)),
         ]
-        final = n == 2
+        final = n == 1
         outs = [shape(wide, BF16), shape(wide, F32)]
         if final:
             scratch = [pltpu.VMEM(wide, BF16), pltpu.VMEM(wide, F32)] + scratch
@@ -492,12 +493,10 @@
     )[0]
     second, acc, crossed = lax.optimization_barrier((second, acc, crossed))
     right2, left2 = along_x(second, 1, 3), along_x(second, -1, 3)
-    qa, acc = far(0, [first, right1, left1, opposite], qa, acc)
-    down3, acc = lax.optimization_barrier((down3, acc))
-    up5 = up(jnp.concatenate([up3[2:], up4[2:]], axis=0), 1, 2)
+    qa, acc = far(0, [first, right1, left1, opposite, up3, up4, down2, down3], qa, acc)
+    up5, up6 = up(up4[2:], 2), up(up4[2:], 2, 2)
     down4 = down(down3[2:], (3,))
-    qa, acc = far(1, [right2, left2], qa, acc)
-    ctx_mine, ctx_other = far(2, [up3, up4, up5, down2, down3, down4], qa, acc)
+    ctx_mine, ctx_other = far(1, [right2, left2, up5, up6, down4], qa, acc)
     ctx_sib = swap_cores(ctx_other)
 
     half_rows, half = rows // 2, out_weight.shape[1] // 8

time: 101 us -> 99.1 us (0.981)
  starting transfers between devices: 47.4 us -> 51.8 us
  waiting for transfers between devices: 17.6 us -> 13.5 us
  Pallas kernels: 28.4 us -> 26.8 us
    ppermute x5 -> x6, starting transfers between devices: 12.3 us -> 17.2 us  [up(): return lax.ppermute(value, 'seq', pairs)]
    ppermute x4, starting transfers between devices: 11.1 us -> 8.41 us  [down(): return lax.ppermute(value, 'seq', pairs)]
    ppermute x5 -> x6, waiting for transfers between devices: 4 us -> 1.76 us  [up(): return lax.ppermute(value, 'seq', pairs)]
    ppermute x5, starting transfers between devices: 11.1 us -> 13.2 us  [along_x(): return lax.ppermute(value, 'seq', pairs)]
    pallas_call x10 -> x9, Pallas kernels: 28.4 us -> 26.8 us  [call(): pl.pallas_call(kernel, out_shape=outs, in_specs=[spec(s) for s in spaces]...]
    ppermute x5, waiting for transfers between devices: 1.28 us -> 0.01 us  [along_x(): return lax.ppermute(value, 'seq', pairs)]
  transfers between devices with their start and end apart: 25 -> 26, of which waited for: 11 -> 8; matrix products, arithmetic and copies ran while one was open for 2% -> 2% of each run, Pallas kernels for 20% -> 18%
where the time goes in v7:
time: 99.1 us; the launch traced here: 98.7 us
  starting transfers between devices  51.8 us (52%)
  Pallas kernels  26.8 us (27%)
  waiting for transfers between devices  13.5 us (14%)
  local copies, waits for them, and re-layouts  3.98 us (4%)
  other arithmetic  1.99 us (2%)
    pallas_call x9, Pallas kernels, call(): pl.pallas_call(kernel, out_shape=outs, in_specs=[spec(s) for s in spaces]...  26.8 us
    ppermute x6, starting transfers between devices, up(): return lax.ppermute(value, 'seq', pairs)  17.2 us
    ppermute x5, starting transfers between devices, along_x(): return lax.ppermute(value, 'seq', pairs)  13.2 us
    ppermute x6, waiting for transfers between devices, tp_shift(): return lax.ppermute(value, 'tp', [(i, (i + step) % 4) for i in range(4)])  10.8 us
    ppermute x6, starting transfers between devices, tp_shift(): return lax.ppermute(value, 'tp', [(i, (i + step) % 4) for i in range(4)])  8.81 us
    ppermute x4, starting transfers between devices, down(): return lax.ppermute(value, 'seq', pairs)  8.41 us
    unnamed x31, local copies, waits for them, and re-layouts  3.91 us
    ppermute x1, starting transfers between devices, local(): lax.ppermute(tail, 'seq', [(i, i + 2) for i in range(2 * NX * NZ - 2)])  3.4 us
  transfers between devices with their start and end apart: 26, of which 8 were waited for; matrix products, arithmetic and copies ran while one was open for 2% of the time, Pallas kernels for 18%

profile of v7, /device:TPU:192, one launch (start us, length us, event | category | flops | bytes accessed | tf_op | source)
XLA Modules:
  0.0 98.7 jit_solution(2179920444172352051)
XLA Ops:
  3.0 2.5 %pick.1 = (bf16[2,128,256]{2,1,0:T(8,128)(2,1)}, bf16[128,256]{1,0:T(8,128)(2,1)}) custom-call(s32[3]{0:T(128)} %pad_add_fusion.scal, s32[8,16]{1,0:T(8,128)} %blocks.1, bf16[256,256]{1,0:T(8,128)(2,1)} %k_ref.3, bf16[256,256]{1,0:T(8,128)(2,1)} %v_ref.3, bf16[256,256]{1,0:T(8,128)(2,1)} %copy-done.2, bf16[256,256]{1,0:T(8,128)(2,1)} %copy-done.4), custom_call_target="tpu_custom_call" | custom-call | bytes 1000000 | tf_op jit(solution)/shard_map/pick/pallas_call | solution.py:388
  5.5 3.4 %collective-permute-start.4 = (bf16[128,256]{1,0:T(8,128)(2,1)}, bf16[128,256]{1,0:T(8,128)(2,1)S(1)}, u32[]{:S(2)}, u32[]{:S(2)}) collective-permute-start(bf16[128,256]{1,0:T(8,128)(2,1)} %get-tuple-element.28), channel_id=1, source_target_pairs={{0,8},{4,12},{8,16},{12,20},{16,24},{20,28},{24,32},{28,36},{32,40... | collective-permute-start | bytes 196616 | tf_op jit(solution)/shard_map/ppermute | solution.py:428
  8.9 1.3 %collective-permute-start.3 = (bf16[2,128,256]{2,1,0:T(8,128)(2,1)}, bf16[2,128,256]{2,1,0:T(8,128)(2,1)S(1)}, u32[]{:S(2)}, u32[]{:S(2)}) collective-permute-start(bf16[2,128,256]{2,1,0:T(8,128)(2,1)} %get-tuple-element.27), channel_id=1, source_target_pairs={{0,64},{4,68},{8,72},{12,76},{16,80},{20,84},{24,88},{28,92},{32,9... | collective-permute-start | bytes 393224 | tf_op jit(solution)/shard_map/ppermute | solution.py:71
  10.2 2.8 %collective-permute-start.5 = (bf16[2,128,256]{2,1,0:T(8,128)(2,1)}, bf16[2,128,256]{2,1,0:T(8,128)(2,1)S(1)}, u32[]{:S(2)}, u32[]{:S(2)}) collective-permute-start(bf16[2,128,256]{2,1,0:T(8,128)(2,1)} %get-tuple-element.27), channel_id=1, source_target_pairs={{0,16},{4,20},{8,24},{12,28},{16,0},{20,4},{24,8},{28,12},{32,48},... | collective-permute-start | bytes 393224 | tf_op jit(solution)/shard_map/ppermute | solution.py:61
  14.0 3.4 %collective-permute-start.11 = (bf16[2,128,256]{2,1,0:T(8,128)(2,1)}, bf16[2,128,256]{2,1,0:T(8,128)(2,1)S(1)}, u32[]{:S(2)}, u32[]{:S(2)}) collective-permute-start(bf16[2,128,256]{2,1,0:T(8,128)(2,1)} %get-tuple-element.27), channel_id=1, source_target_pairs={{0,32},{4,36},{8,40},{12,44},{16,48},{20,52},{24,56},{28,60},{32,6... | collective-permute-start | bytes 393224 | tf_op jit(solution)/shard_map/ppermute | solution.py:71
  18.3 1.8 %collective-permute-done.3 = bf16[2,128,256]{2,1,0:T(8,128)(2,1)S(1)} collective-permute-done((bf16[2,128,256]{2,1,0:T(8,128)(2,1)}, bf16[2,128,256]{2,1,0:T(8,128)(2,1)S(1)}, u32[]{:S(2)}, u32[]{:S(2)}) %collective-permute-start.3) | collective-permute-done | bytes 131104 | tf_op jit(solution)/shard_map/ppermute | solution.py:71
  20.1 1.3 %collective-permute-start.9 = (bf16[4,128,256]{2,1,0:T(8,128)(2,1)S(1)}, bf16[4,128,256]{2,1,0:T(8,128)(2,1)S(1)}, u32[]{:S(2)}, u32[]{:S(2)}) collective-permute-start(bf16[4,128,256]{2,1,0:T(8,128)(2,1)S(1)} %get-tuple-element.54), channel_id=1, source_target_pairs={{0,224},{4,228},{8,232},{12,236},{16,240},{20,244},{24,248},{28,25... | collective-permute-start | bytes 786440 | tf_op jit(solution)/shard_map/ppermute | solution.py:77
  21.4 4.8 %collective-permute-start.6 = (bf16[4,128,256]{2,1,0:T(8,128)(2,1)S(1)}, bf16[4,128,256]{2,1,0:T(8,128)(2,1)S(1)}, u32[]{:S(2)}, u32[]{:S(2)}) collective-permute-start(bf16[4,128,256]{2,1,0:T(8,128)(2,1)S(1)} %get-tuple-element.53), channel_id=1, source_target_pairs={{0,32},{4,36},{8,40},{12,44},{16,48},{20,52},{24,56},{28,60},{32,6... | collective-permute-start | bytes 786440 | tf_op jit(solution)/shard_map/ppermute | solution.py:71
  26.3 1.4 %collective-permute-start.12 = (bf16[8,128,256]{2,1,0:T(8,128)(2,1)S(1)}, bf16[8,128,256]{2,1,0:T(8,128)(2,1)S(1)}, u32[]{:S(2)}, u32[]{:S(2)}) collective-permute-start(bf16[8,128,256]{2,1,0:T(8,128)(2,1)S(1)} %constant_dynamic-update-slice_fusion.rest_0_), channel_id=1, source_target_pairs={{0,8},{4,12},{8,16},{12,20},{16,24},{20,28},{24,0},{28,4},{32,40},... | collective-permute-start | bytes 1572872 | tf_op jit(solution)/shard_map/ppermute | solution.py:61
  27.7 1.9 %collective-permute-start.13 = (bf16[8,128,256]{2,1,0:T(8,128)(2,1)S(1)}, bf16[8,128,256]{2,1,0:T(8,128)(2,1)S(1)}, u32[]{:S(2)}, u32[]{:S(2)}) collective-permute-start(bf16[8,128,256]{2,1,0:T(8,128)(2,1)S(1)} %constant_dynamic-update-slice_fusion.rest_0_), channel_id=1, source_target_pairs={{0,24},{4,28},{8,0},{12,4},{16,8},{20,12},{24,16},{28,20},{32,56},... | collective-permute-start | bytes 1572872 | tf_op jit(solution)/shard_map/ppermute | solution.py:61
  29.6 1.9 %collective-permute-start.10 = (bf16[4,128,256]{2,1,0:T(8,128)(2,1)S(1)}, bf16[4,128,256]{2,1,0:T(8,128)(2,1)S(1)}, u32[]{:S(2)}, u32[]{:S(2)}) collective-permute-start(bf16[4,128,256]{2,1,0:T(8,128)(2,1)S(1)} %collective-permute-done.9.rest_6_), channel_id=1, source_target_pairs={{0,224},{4,228},{8,232},{12,236},{16,240},{20,244},{24,248},{28,25... | collective-permute-start | bytes 786440 | tf_op jit(solution)/shard_map/ppermute | solution.py:77
  31.6 4.5 %collective-permute-start.7 = (bf16[4,128,256]{2,1,0:T(8,128)(2,1)S(1)}, bf16[4,128,256]{2,1,0:T(8,128)(2,1)S(1)}, u32[]{:S(2)}, u32[]{:S(2)}) collective-permute-start(bf16[4,128,256]{2,1,0:T(8,128)(2,1)S(1)} %collective-permute-done.6.rest_4_), channel_id=1, source_target_pairs={{32,64},{36,68},{40,72},{44,76},{48,80},{52,84},{56,88},{60,92},{6... | collective-permute-start | bytes 786440 | tf_op jit(solution)/shard_map/ppermute | solution.py:71
  38.0 5.4 %near_part.1 = (bf16[4,512,256]{2,1,0:T(8,128)(2,1)S(1)}, f32[4,512,256]{2,1,0:T(8,128)S(1)}, s32[256]{0:T(256)S(1)}, s32[16]{0:T(128)S(1)}) custom-call(s32[3]{0:T(128)S(1)} %copy-done.6, s32[8,16]{1,0:T(8,128)S(1)} %copy-done.7, s32[8]{0:T(128)S(1)} %copy-done.10, s32[8,8]{1,0:T(8,128)S(1)} %copy-done.9, s32[32]{0:T(128)S(1)} %copy-done.11, ...), custom_call_target="tpu_custom_call" | custom-call | flops 5000000000 | bytes 100000 | tf_op jit(solution)/shard_map/near_part/pallas_call | solution.py:388
  43.7 2.9 %collective-permute-start.14 = (bf16[8,128,256]{2,1,0:T(8,128)(2,1)S(1)}, bf16[8,128,256]{2,1,0:T(8,128)(2,1)S(1)}, u32[]{:S(2)}, u32[]{:S(2)}) collective-permute-start(bf16[8,128,256]{2,1,0:T(8,128)(2,1)S(1)} %pad_maximum_fusion), channel_id=1, source_target_pairs={{96,104},{100,108},{104,112},{108,116},{112,120},{116,124},{120,96... | collective-permute-start | bytes 1572872 | tf_op jit(solution)/shard_map/ppermute | solution.py:61
  46.6 4.1 %collective-permute-start.15 = (bf16[8,128,256]{2,1,0:T(8,128)(2,1)S(1)}, bf16[8,128,256]{2,1,0:T(8,128)(2,1)S(1)}, u32[]{:S(2)}, u32[]{:S(2)}) collective-permute-start(bf16[8,128,256]{2,1,0:T(8,128)(2,1)S(1)} %pad_maximum_fusion), channel_id=1, source_target_pairs={{96,120},{100,124},{104,96},{108,100},{112,104},{116,108},{120,112... | collective-permute-start | bytes 1572872 | tf_op jit(solution)/shard_map/ppermute | solution.py:61
  50.7 1.9 %collective-permute-start.16 = (bf16[2,128,256]{2,1,0:T(8,128)(2,1)S(1)}, bf16[2,128,256]{2,1,0:T(8,128)(2,1)S(1)}, u32[]{:S(2)}, u32[]{:S(2)}) collective-permute-start(bf16[2,128,256]{2,1,0:T(8,128)(2,1)S(1)} %get-tuple-element.51), channel_id=1, source_target_pairs={{64,96},{68,100},{72,104},{76,108},{80,112},{84,116},{88,120},{92,... | collective-permute-start | bytes 393224 | tf_op jit(solution)/shard_map/ppermute | solution.py:71
  52.7 1.3 %collective-permute-start.17 = (bf16[2,128,256]{2,1,0:T(8,128)(2,1)S(1)}, bf16[2,128,256]{2,1,0:T(8,128)(2,1)S(1)}, u32[]{:S(2)}, u32[]{:S(2)}) collective-permute-start(bf16[2,128,256]{2,1,0:T(8,128)(2,1)S(1)} %get-tuple-element.51), channel_id=1, source_target_pairs={{64,128},{68,132},{72,136},{76,140},{80,144},{84,148},{88,152},{92... | collective-permute-start | bytes 393224 | tf_op jit(solution)/shard_map/ppermute | solution.py:71
  54.0 4.6 %collective-permute-start.18 = (bf16[2,128,256]{2,1,0:T(8,128)(2,1)S(1)}, bf16[2,128,256]{2,1,0:T(8,128)(2,1)S(1)}, u32[]{:S(2)}, u32[]{:S(2)}) collective-permute-start(bf16[2,128,256]{2,1,0:T(8,128)(2,1)S(1)} %get-tuple-element.49), channel_id=1, source_target_pairs={{0,224},{4,228},{8,232},{12,236},{16,240},{20,244},{24,248},{28,25... | collective-permute-start | bytes 393224 | tf_op jit(solution)/shard_map/ppermute | solution.py:77
  58.5 5.6 %far_part.2 = (bf16[4,512,256]{2,1,0:T(8,128)(2,1)S(1)}, f32[4,512,256]{2,1,0:T(8,128)S(1)}) custom-call(s32[3]{0:T(128)S(1)} %copy-done.6, s32[256]{0:T(256)S(1)} %get-tuple-element.30.lists, s32[16]{0:T(128)S(1)} %get-tuple-element.31.counts, bf16[4,512,256]{2,1,0:T(8,128)(2,1)S(1)} %get-tuple-element.32.qa_in, ...), custom_call_target="tpu_custom_call" | custom-call | flops 6000000000 | bytes 100000 | tf_op jit(solution)/shard_map/far_part/pallas_call | solution.py:388
  64.2 4.8 %far_part.3 = (bf16[256,512]{1,0:T(8,128)(2,1)S(1)}, bf16[256,512]{1,0:T(8,128)(2,1)S(1)}) custom-call(s32[3]{0:T(128)S(1)} %copy-done.6, s32[256]{0:T(256)S(1)} %get-tuple-element.30.lists, s32[16]{0:T(128)S(1)} %get-tuple-element.31.counts, bf16[4,512,256]{2,1,0:T(8,128)(2,1)S(1)} %get-tuple-element.36.qa_in, f32[4,512,256]{2,1,0:T(8,128)S(1)} %get-tuple-element.37.acc_in, ...), custom_call_target="tpu_custom_call" | custom-call | flops 6000000000 | bytes 100000 | tf_op jit(solution)/shard_map/far_part/pallas_call | solution.py:388
  69.2 1.3 %own_part.3.part = f32[2,256,512]{2,1,0:T(8,128)S(1)} custom-call(s32[3]{0:T(128)S(1)} %copy-done.6, bf16[256,512]{1,0:T(8,128)(2,1)S(1)} %get-tuple-element.39.ctx, bf16[1024,4096]{1,0:T(8,128)(2,1)S(1)} %bitcast.4), custom_call_target="tpu_custom_call" | custom-call | flops 1000000 | bytes 1000 | tf_op jit(solution)/shard_map/own_part/pallas_call | solution.py:388
  70.7 1.3 %sib_part.3 = (bf16[256,512]{1,0:T(8,128)(2,1)S(1)}, bf16[256,512]{1,0:T(8,128)(2,1)S(1)}) custom-call(s32[3]{0:T(128)S(1)} %copy-done.6, bf16[256,512]{1,0:T(8,128)(2,1)S(1)} %collective-permute-done.19.ctx_sib.ctx, f32[2,256,512]{2,1,0:T(8,128)S(1)} %own_part.3.part, bf16[1024,4096]{1,0:T(8,128)(2,1)S(1)} %bitcast.4), custom_call_target="tpu_custom_call" | custom-call | flops 1000000 | bytes 1000 | tf_op jit(solution)/shard_map/sib_part/pallas_call | solution.py:388
  72.0 1.7 %collective-permute-start.21 = (bf16[256,512]{1,0:T(8,128)(2,1)S(1)}, bf16[256,512]{1,0:T(8,128)(2,1)S(1)}, u32[]{:S(2)}, u32[]{:S(2)}) collective-permute-start(bf16[256,512]{1,0:T(8,128)(2,1)S(1)} %get-tuple-element.44), channel_id=1, source_target_pairs={{0,1},{1,2},{2,3},{3,0},{4,5},{5,6},{6,7},{7,4},{8,9},{9,10},{10,1... | collective-permute-start | bytes 786440 | tf_op jit(solution)/shard_map/ppermute | solution.py:85
  73.6 1.7 %collective-permute-start.24 = (bf16[256,512]{1,0:T(8,128)(2,1)S(1)}, bf16[256,512]{1,0:T(8,128)(2,1)S(1)}, u32[]{:S(2)}, u32[]{:S(2)}) collective-permute-start(bf16[256,512]{1,0:T(8,128)(2,1)S(1)} %get-tuple-element.48), channel_id=1, source_target_pairs={{0,3},{1,0},{2,1},{3,2},{4,7},{5,4},{6,5},{7,6},{8,11},{9,8},{10,9... | collective-permute-start | bytes 786440 | tf_op jit(solution)/shard_map/ppermute | solution.py:85
  75.3 1.3 %own_part.2.part = f32[2,256,512]{2,1,0:T(8,128)S(1)} custom-call(s32[3]{0:T(128)S(1)} %copy-done.6, bf16[256,512]{1,0:T(8,128)(2,1)S(1)} %get-tuple-element.39.ctx, bf16[1024,4096]{1,0:T(8,128)(2,1)S(1)} %bitcast.4), custom_call_target="tpu_custom_call" | custom-call | flops 1000000 | bytes 1000 | tf_op jit(solution)/shard_map/own_part/pallas_call | solution.py:388
  76.6 1.3 %sib_part.2 = (bf16[256,512]{1,0:T(8,128)(2,1)S(1)}, bf16[256,512]{1,0:T(8,128)(2,1)S(1)}) custom-call(s32[3]{0:T(128)S(1)} %copy-done.6, bf16[256,512]{1,0:T(8,128)(2,1)S(1)} %collective-permute-done.19.ctx_sib.ctx, f32[2,256,512]{2,1,0:T(8,128)S(1)} %own_part.2.part, bf16[1024,4096]{1,0:T(8,128)(2,1)S(1)} %bitcast.4), custom_call_target="tpu_custom_call" | custom-call | flops 1000000 | bytes 1000 | tf_op jit(solution)/shard_map/sib_part/pallas_call | solution.py:388
  78.0 1.9 %collective-permute-start.20 = (bf16[256,512]{1,0:T(8,128)(2,1)S(1)}, bf16[256,512]{1,0:T(8,128)(2,1)S(1)}, u32[]{:S(2)}, u32[]{:S(2)}) collective-permute-start(bf16[256,512]{1,0:T(8,128)(2,1)S(1)} %get-tuple-element.42), channel_id=1, source_target_pairs={{0,3},{1,0},{2,1},{3,2},{4,7},{5,4},{6,5},{7,6},{8,11},{9,8},{10,9... | collective-permute-start | bytes 786440 | tf_op jit(solution)/shard_map/ppermute | solution.py:85
  79.8 3.2 %other_shares.1 = (f32[256,512]{1,0:T(8,128)S(1)}, f32[256,512]{1,0:T(8,128)S(1)}, f32[256,512]{1,0:T(8,128)S(1)}, f32[256,512]{1,0:T(8,128)S(1)}) custom-call(s32[3]{0:T(128)S(1)} %copy-done.6, bf16[256,512]{1,0:T(8,128)(2,1)S(1)} %get-tuple-element.39.ctx, bf16[256,512]{1,0:T(8,128)(2,1)S(1)} %collective-permute-done.19.ctx_sib.ctx, ...), custom_call_target="tpu_custom_call" | custom-call | flops 1000000 | bytes 1000 | tf_op jit(solution)/shard_map/other_shares/pallas_call | solution.py:388
  84.0 2.8 %collective-permute-start.25 = (bf16[256,512]{1,0:T(8,128)(2,1)S(1)}, bf16[256,512]{1,0:T(8,128)(2,1)S(1)}, u32[]{:S(2)}, u32[]{:S(2)}) collective-permute-start(bf16[256,512]{1,0:T(8,128)(2,1)S(1)} %add_convert_fusion.1), channel_id=1, source_target_pairs={{0,3},{1,0},{2,1},{3,2},{4,7},{5,4},{6,5},{7,6},{8,11},{9,8},{10,9... | collective-permute-start | bytes 786440 | tf_op jit(solution)/shard_map/ppermute | solution.py:85
  86.8 1.6 %collective-permute-done.20 = bf16[256,512]{1,0:T(8,128)(2,1)S(1)} collective-permute-done((bf16[256,512]{1,0:T(8,128)(2,1)S(1)}, bf16[256,512]{1,0:T(8,128)(2,1)S(1)}, u32[]{:S(2)}, u32[]{:S(2)}) %collective-permute-start.20) | collective-permute-done | bytes 262176 | tf_op jit(solution)/shard_map/ppermute | solution.py:85
  88.4 5.2 %collective-permute-done.22 = bf16[256,512]{1,0:T(8,128)(2,1)S(1)} collective-permute-done((bf16[256,512]{1,0:T(8,128)(2,1)S(1)}, bf16[256,512]{1,0:T(8,128)(2,1)S(1)}, u32[]{:S(2)}, u32[]{:S(2)}) %collective-permute-start.22) | collective-permute-done | bytes 262176 | tf_op jit(solution)/shard_map/ppermute | solution.py:85
  93.7 4.0 %collective-permute-done.23 = bf16[256,512]{1,0:T(8,128)(2,1)S(1)} collective-permute-done((bf16[256,512]{1,0:T(8,128)(2,1)S(1)}, bf16[256,512]{1,0:T(8,128)(2,1)S(1)}, u32[]{:S(2)}, u32[]{:S(2)}) %collective-permute-start.23) | collective-permute-done | bytes 262176 | tf_op jit(solution)/shard_map/ppermute | solution.py:85
  (74 shorter events, 9.2 us)
Async XLA Ops:
  0.0 36.1 %copy-start = (bf16[256,256]{1,0:T(8,128)(2,1)S(1)}, bf16[256,256]{1,0:T(8,128)(2,1)}, u32[]{:S(2)}) copy-start(bf16[256,256]{1,0:T(8,128)(2,1)} %k_ref.3) | copy-start | bytes 393220
  0.0 36.1 %copy-start.1 = (bf16[256,256]{1,0:T(8,128)(2,1)S(1)}, bf16[256,256]{1,0:T(8,128)(2,1)}, u32[]{:S(2)}) copy-start(bf16[256,256]{1,0:T(8,128)(2,1)} %v_ref.3) | copy-start | bytes 393220
  0.0 36.1 %copy-start.7 = (s32[8,16]{1,0:T(8,128)S(1)}, s32[8,16]{1,0:T(8,128)}, u32[]{:S(2)}) copy-start(s32[8,16]{1,0:T(8,128)} %blocks.1) | copy-start | bytes 1540
  0.0 36.1 %copy-start.8 = (bf16[256,1024]{1,0:T(8,128)(2,1)S(1)}, bf16[256,1024]{1,0:T(8,128)(2,1)}, u32[]{:S(2)}) copy-start(bf16[256,1024]{1,0:T(8,128)(2,1)} %q_ref.1) | copy-start | bytes 1572868
  0.0 36.1 %copy-start.10 = (s32[8]{0:T(128)S(1)}, s32[8]{0:T(128)}, u32[]{:S(2)}) copy-start(s32[8]{0:T(128)} %window.1) | copy-start | bytes 100
  0.0 36.1 %copy-start.9 = (s32[8,8]{1,0:T(8,128)S(1)}, s32[8,8]{1,0:T(8,128)}, u32[]{:S(2)}) copy-start(s32[8,8]{1,0:T(8,128)} %slash.1) | copy-start | bytes 772
  0.1 1.6 %collective-permute-start.1 = (bf16[256,256]{1,0:T(8,128)(2,1)}, bf16[256,256]{1,0:T(8,128)(2,1)S(1)}, u32[]{:S(2)}, u32[]{:S(2)}) collective-permute-start(bf16[256,256]{1,0:T(8,128)(2,1)} %k_ref.3), channel_id=1, source_target_pairs={{0,4},{4,0},{8,12},{12,8},{16,20},{20,16},{24,28},{28,24},{32,36},... | collective-permute-start | bytes 393224 | tf_op jit(solution)/shard_map/ppermute | solution.py:81
  0.2 1.7 %collective-permute-start.2 = (bf16[256,256]{1,0:T(8,128)(2,1)}, bf16[256,256]{1,0:T(8,128)(2,1)S(1)}, u32[]{:S(2)}, u32[]{:S(2)}) collective-permute-start(bf16[256,256]{1,0:T(8,128)(2,1)} %v_ref.3), channel_id=1, source_target_pairs={{0,4},{4,0},{8,12},{12,8},{16,20},{20,16},{24,28},{28,24},{32,36},... | collective-permute-start | bytes 393224 | tf_op jit(solution)/shard_map/ppermute | solution.py:81
  5.5 8.5 %collective-permute-start.4 = (bf16[128,256]{1,0:T(8,128)(2,1)}, bf16[128,256]{1,0:T(8,128)(2,1)S(1)}, u32[]{:S(2)}, u32[]{:S(2)}) collective-permute-start(bf16[128,256]{1,0:T(8,128)(2,1)} %get-tuple-element.28), channel_id=1, source_target_pairs={{0,8},{4,12},{8,16},{12,20},{16,24},{20,28},{24,32},{28,36},{32,40... | collective-permute-start | bytes 196616 | tf_op jit(solution)/shard_map/ppermute | solution.py:428
  8.9 11.1 %collective-permute-start.3 = (bf16[2,128,256]{2,1,0:T(8,128)(2,1)}, bf16[2,128,256]{2,1,0:T(8,128)(2,1)S(1)}, u32[]{:S(2)}, u32[]{:S(2)}) collective-permute-start(bf16[2,128,256]{2,1,0:T(8,128)(2,1)} %get-tuple-element.27), channel_id=1, source_target_pairs={{0,64},{4,68},{8,72},{12,76},{16,80},{20,84},{24,88},{28,92},{32,9... | collective-permute-start | bytes 393224 | tf_op jit(solution)/shard_map/ppermute | solution.py:71
  10.2 9.8 %collective-permute-start.5 = (bf16[2,128,256]{2,1,0:T(8,128)(2,1)}, bf16[2,128,256]{2,1,0:T(8,128)(2,1)S(1)}, u32[]{:S(2)}, u32[]{:S(2)}) collective-permute-start(bf16[2,128,256]{2,1,0:T(8,128)(2,1)} %get-tuple-element.27), channel_id=1, source_target_pairs={{0,16},{4,20},{8,24},{12,28},{16,0},{20,4},{24,8},{28,12},{32,48},... | collective-permute-start | bytes 393224 | tf_op jit(solution)/shard_map/ppermute | solution.py:61
  13.0 7.0 %collective-permute-start.8 = (bf16[2,128,256]{2,1,0:T(8,128)(2,1)}, bf16[2,128,256]{2,1,0:T(8,128)(2,1)S(1)}, u32[]{:S(2)}, u32[]{:S(2)}) collective-permute-start(bf16[2,128,256]{2,1,0:T(8,128)(2,1)} %get-tuple-element.27), channel_id=1, source_target_pairs={{0,224},{4,228},{8,232},{12,236},{16,240},{20,244},{24,248},{28,25... | collective-permute-start | bytes 393224 | tf_op jit(solution)/shard_map/ppermute | solution.py:77
  13.7 22.4 %collective-permute-start = (bf16[256,1024]{1,0:T(8,128)(2,1)}, bf16[256,1024]{1,0:T(8,128)(2,1)S(1)}, u32[]{:S(2)}, u32[]{:S(2)}) collective-permute-start(bf16[256,1024]{1,0:T(8,128)(2,1)} %q_ref.1), channel_id=1, source_target_pairs={{0,4},{4,0},{8,12},{12,8},{16,20},{20,16},{24,28},{28,24},{32,36},... | collective-permute-start | bytes 1572872 | tf_op jit(solution)/shard_map/ppermute | solution.py:81
  14.0 12.2 %collective-permute-start.11 = (bf16[2,128,256]{2,1,0:T(8,128)(2,1)}, bf16[2,128,256]{2,1,0:T(8,128)(2,1)S(1)}, u32[]{:S(2)}, u32[]{:S(2)}) collective-permute-start(bf16[2,128,256]{2,1,0:T(8,128)(2,1)} %get-tuple-element.27), channel_id=1, source_target_pairs={{0,32},{4,36},{8,40},{12,44},{16,48},{20,52},{24,56},{28,60},{32,6... | collective-permute-start | bytes 393224 | tf_op jit(solution)/shard_map/ppermute | solution.py:71
  20.1 9.5 %collective-permute-start.9 = (bf16[4,128,256]{2,1,0:T(8,128)(2,1)S(1)}, bf16[4,128,256]{2,1,0:T(8,128)(2,1)S(1)}, u32[]{:S(2)}, u32[]{:S(2)}) collective-permute-start(bf16[4,128,256]{2,1,0:T(8,128)(2,1)S(1)} %get-tuple-element.54), channel_id=1, source_target_pairs={{0,224},{4,228},{8,232},{12,236},{16,240},{20,244},{24,248},{28,25... | collective-permute-start | bytes 786440 | tf_op jit(solution)/shard_map/ppermute | solution.py:77
  21.4 10.1 %collective-permute-start.6 = (bf16[4,128,256]{2,1,0:T(8,128)(2,1)S(1)}, bf16[4,128,256]{2,1,0:T(8,128)(2,1)S(1)}, u32[]{:S(2)}, u32[]{:S(2)}) collective-permute-start(bf16[4,128,256]{2,1,0:T(8,128)(2,1)S(1)} %get-tuple-element.53), channel_id=1, source_target_pairs={{0,32},{4,36},{8,40},{12,44},{16,48},{20,52},{24,56},{28,60},{32,6... | collective-permute-start | bytes 786440 | tf_op jit(solution)/shard_map/ppermute | solution.py:71
  26.3 26.4 %collective-permute-start.12 = (bf16[8,128,256]{2,1,0:T(8,128)(2,1)S(1)}, bf16[8,128,256]{2,1,0:T(8,128)(2,1)S(1)}, u32[]{:S(2)}, u32[]{:S(2)}) collective-permute-start(bf16[8,128,256]{2,1,0:T(8,128)(2,1)S(1)} %constant_dynamic-update-slice_fusion.rest_0_), channel_id=1, source_target_pairs={{0,8},{4,12},{8,16},{12,20},{16,24},{20,28},{24,0},{28,4},{32,40},... | collective-permute-start | bytes 1572872 | tf_op jit(solution)/shard_map/ppermute | solution.py:61
  27.7 26.2 %collective-permute-start.13 = (bf16[8,128,256]{2,1,0:T(8,128)(2,1)S(1)}, bf16[8,128,256]{2,1,0:T(8,128)(2,1)S(1)}, u32[]{:S(2)}, u32[]{:S(2)}) collective-permute-start(bf16[8,128,256]{2,1,0:T(8,128)(2,1)S(1)} %constant_dynamic-update-slice_fusion.rest_0_), channel_id=1, source_target_pairs={{0,24},{4,28},{8,0},{12,4},{16,8},{20,12},{24,16},{28,20},{32,56},... | collective-permute-start | bytes 1572872 | tf_op jit(solution)/shard_map/ppermute | solution.py:61
  29.6 13.9 %collective-permute-start.10 = (bf16[4,128,256]{2,1,0:T(8,128)(2,1)S(1)}, bf16[4,128,256]{2,1,0:T(8,128)(2,1)S(1)}, u32[]{:S(2)}, u32[]{:S(2)}) collective-permute-start(bf16[4,128,256]{2,1,0:T(8,128)(2,1)S(1)} %collective-permute-done.9.rest_6_), channel_id=1, source_target_pairs={{0,224},{4,228},{8,232},{12,236},{16,240},{20,244},{24,248},{28,25... | collective-permute-start | bytes 786440 | tf_op jit(solution)/shard_map/ppermute | solution.py:77
  31.6 12.0 %collective-permute-start.7 = (bf16[4,128,256]{2,1,0:T(8,128)(2,1)S(1)}, bf16[4,128,256]{2,1,0:T(8,128)(2,1)S(1)}, u32[]{:S(2)}, u32[]{:S(2)}) collective-permute-start(bf16[4,128,256]{2,1,0:T(8,128)(2,1)S(1)} %collective-permute-done.6.rest_4_), channel_id=1, source_target_pairs={{32,64},{36,68},{40,72},{44,76},{48,80},{52,84},{56,88},{60,92},{6... | collective-permute-start | bytes 786440 | tf_op jit(solution)/shard_map/ppermute | solution.py:71
  43.7 20.5 %collective-permute-start.14 = (bf16[8,128,256]{2,1,0:T(8,128)(2,1)S(1)}, bf16[8,128,256]{2,1,0:T(8,128)(2,1)S(1)}, u32[]{:S(2)}, u32[]{:S(2)}) collective-permute-start(bf16[8,128,256]{2,1,0:T(8,128)(2,1)S(1)} %pad_maximum_fusion), channel_id=1, source_target_pairs={{96,104},{100,108},{104,112},{108,116},{112,120},{116,124},{120,96... | collective-permute-start | bytes 1572872 | tf_op jit(solution)/shard_map/ppermute | solution.py:61
  46.6 17.6 %collective-permute-start.15 = (bf16[8,128,256]{2,1,0:T(8,128)(2,1)S(1)}, bf16[8,128,256]{2,1,0:T(8,128)(2,1)S(1)}, u32[]{:S(2)}, u32[]{:S(2)}) collective-permute-start(bf16[8,128,256]{2,1,0:T(8,128)(2,1)S(1)} %pad_maximum_fusion), channel_id=1, source_target_pairs={{96,120},{100,124},{104,96},{108,100},{112,104},{116,108},{120,112... | collective-permute-start | bytes 1572872 | tf_op jit(solution)/shard_map/ppermute | solution.py:61
  50.7 13.4 %collective-permute-start.16 = (bf16[2,128,256]{2,1,0:T(8,128)(2,1)S(1)}, bf16[2,128,256]{2,1,0:T(8,128)(2,1)S(1)}, u32[]{:S(2)}, u32[]{:S(2)}) collective-permute-start(bf16[2,128,256]{2,1,0:T(8,128)(2,1)S(1)} %get-tuple-element.51), channel_id=1, source_target_pairs={{64,96},{68,100},{72,104},{76,108},{80,112},{84,116},{88,120},{92,... | collective-permute-start | bytes 393224 | tf_op jit(solution)/shard_map/ppermute | solution.py:71
  52.7 11.5 %collective-permute-start.17 = (bf16[2,128,256]{2,1,0:T(8,128)(2,1)S(1)}, bf16[2,128,256]{2,1,0:T(8,128)(2,1)S(1)}, u32[]{:S(2)}, u32[]{:S(2)}) collective-permute-start(bf16[2,128,256]{2,1,0:T(8,128)(2,1)S(1)} %get-tuple-element.51), channel_id=1, source_target_pairs={{64,128},{68,132},{72,136},{76,140},{80,144},{84,148},{88,152},{92... | collective-permute-start | bytes 393224 | tf_op jit(solution)/shard_map/ppermute | solution.py:71
  54.0 10.2 %collective-permute-start.18 = (bf16[2,128,256]{2,1,0:T(8,128)(2,1)S(1)}, bf16[2,128,256]{2,1,0:T(8,128)(2,1)S(1)}, u32[]{:S(2)}, u32[]{:S(2)}) collective-permute-start(bf16[2,128,256]{2,1,0:T(8,128)(2,1)S(1)} %get-tuple-element.49), channel_id=1, source_target_pairs={{0,224},{4,228},{8,232},{12,236},{16,240},{20,244},{24,248},{28,25... | collective-permute-start | bytes 393224 | tf_op jit(solution)/shard_map/ppermute | solution.py:77
  69.0 1.6 %collective-permute-start.19 = (bf16[256,512]{1,0:T(8,128)(2,1)S(1)}, bf16[256,512]{1,0:T(8,128)(2,1)S(1)}, u32[]{:S(2)}, u32[]{:S(2)}) collective-permute-start(bf16[256,512]{1,0:T(8,128)(2,1)S(1)} %get-tuple-element.40), channel_id=1, source_target_pairs={{0,4},{4,0},{8,12},{12,8},{16,20},{20,16},{24,28},{28,24},{32,36},... | collective-permute-start | bytes 786440 | tf_op jit(solution)/shard_map/ppermute | solution.py:81
  72.0 11.0 %collective-permute-start.21 = (bf16[256,512]{1,0:T(8,128)(2,1)S(1)}, bf16[256,512]{1,0:T(8,128)(2,1)S(1)}, u32[]{:S(2)}, u32[]{:S(2)}) collective-permute-start(bf16[256,512]{1,0:T(8,128)(2,1)S(1)} %get-tuple-element.44), channel_id=1, source_target_pairs={{0,1},{1,2},{2,3},{3,0},{4,5},{5,6},{6,7},{7,4},{8,9},{9,10},{10,1... | collective-permute-start | bytes 786440 | tf_op jit(solution)/shard_map/ppermute | solution.py:85
  73.6 10.3 %collective-permute-start.24 = (bf16[256,512]{1,0:T(8,128)(2,1)S(1)}, bf16[256,512]{1,0:T(8,128)(2,1)S(1)}, u32[]{:S(2)}, u32[]{:S(2)}) collective-permute-start(bf16[256,512]{1,0:T(8,128)(2,1)S(1)} %get-tuple-element.48), channel_id=1, source_target_pairs={{0,3},{1,0},{2,1},{3,2},{4,7},{5,4},{6,5},{7,6},{8,11},{9,8},{10,9... | collective-permute-start | bytes 786440 | tf_op jit(solution)/shard_map/ppermute | solution.py:85
  78.0 10.5 %collective-permute-start.20 = (bf16[256,512]{1,0:T(8,128)(2,1)S(1)}, bf16[256,512]{1,0:T(8,128)(2,1)S(1)}, u32[]{:S(2)}, u32[]{:S(2)}) collective-permute-start(bf16[256,512]{1,0:T(8,128)(2,1)S(1)} %get-tuple-element.42), channel_id=1, source_target_pairs={{0,3},{1,0},{2,1},{3,2},{4,7},{5,4},{6,5},{7,6},{8,11},{9,8},{10,9... | collective-permute-start | bytes 786440 | tf_op jit(solution)/shard_map/ppermute | solution.py:85
  83.1 10.5 %collective-permute-start.22 = (bf16[256,512]{1,0:T(8,128)(2,1)S(1)}, bf16[256,512]{1,0:T(8,128)(2,1)S(1)}, u32[]{:S(2)}, u32[]{:S(2)}) collective-permute-start(bf16[256,512]{1,0:T(8,128)(2,1)S(1)} %add_convert_fusion.3), channel_id=1, source_target_pairs={{0,1},{1,2},{2,3},{3,0},{4,5},{5,6},{6,7},{7,4},{8,9},{9,10},{10,1... | collective-permute-start | bytes 786440 | tf_op jit(solution)/shard_map/ppermute | solution.py:85
  83.4 14.3 %collective-permute-start.23 = (bf16[256,512]{1,0:T(8,128)(2,1)S(1)}, bf16[256,512]{1,0:T(8,128)(2,1)S(1)}, u32[]{:S(2)}, u32[]{:S(2)}) collective-permute-start(bf16[256,512]{1,0:T(8,128)(2,1)S(1)} %get-tuple-element.46), channel_id=1, source_target_pairs={{0,1},{1,2},{2,3},{3,0},{4,5},{5,6},{6,7},{7,4},{8,9},{9,10},{10,1... | collective-permute-start | bytes 786440 | tf_op jit(solution)/shard_map/ppermute | solution.py:85
  84.0 13.7 %collective-permute-start.25 = (bf16[256,512]{1,0:T(8,128)(2,1)S(1)}, bf16[256,512]{1,0:T(8,128)(2,1)S(1)}, u32[]{:S(2)}, u32[]{:S(2)}) collective-permute-start(bf16[256,512]{1,0:T(8,128)(2,1)S(1)} %add_convert_fusion.1), channel_id=1, source_target_pairs={{0,3},{1,0},{2,1},{3,2},{4,7},{5,4},{6,5},{7,6},{8,11},{9,8},{10,9... | collective-permute-start | bytes 786440 | tf_op jit(solution)/shard_map/ppermute | solution.py:85
  (8 other events, 83.9 us)

commit v8 on v7

--- a/solution.py
+++ b/solution.py
@@ -525,15 +525,20 @@
     opp0, opp1 = sib_part((0, 1), own_part((0, 1)))
     via_before = tp_shift(opp0, 1)
     via_after = tp_shift(opp1, -1)
-    after1, before0 = sib_part((3, 4), own_part((3, 4)))
+
+    def both(tiles, out):
+        bufs, sems = w_scratch(len(tiles))
+        return call(
+            functools.partial(both_parts_kernel, tiles), "both_parts", [out] * len(tiles),
+            (scal, ctx_mine, ctx_sib, out_weight), [smem, vmem, vmem, anywhere],
+            bufs * 2 + sems * 2, flops=1_000_000, moved=1_000,
+        )
+
+    after1, before0 = both((3, 4), tile_bf)
     direct1 = tp_shift(after1, 1)
     direct0 = tp_shift(before0, -1)
-    bufs, sems = w_scratch(4)
-    after0, before1, own0, own1 = call(
-        functools.partial(both_parts_kernel, (2, 5, 6, 7)), "other_shares", [tile_f] * 4,
-        (scal, ctx_mine, ctx_sib, out_weight), [smem, vmem, vmem, anywhere],
-        bufs * 2 + sems * 2, flops=1_000_000, moved=1_000,
-    )
+    after0, before1 = both((2, 5), tile_f)
+    own0, own1 = both((6, 7), tile_f)
     summed0 = tp_shift((after0 + via_before.astype(F32)).astype(BF16), 1)
     summed1 = tp_shift((before1 + via_after.astype(F32)).astype(BF16), -1)
     return jnp.concatenate(

time: 99.1 us -> 98.1 us (0.990)
  transfers between devices with their start and end apart: 26 -> 26, of which waited for: 8 -> 9; matrix products, arithmetic and copies ran while one was open for 2% -> 2% of each run, Pallas kernels for 18% -> 18%
where the time goes in v8:
time: 98.1 us; the launch traced here: 97.6 us
  starting transfers between devices  52 us (53%)
  Pallas kernels  26.6 us (27%)
  waiting for transfers between devices  12.6 us (13%)
  local copies, waits for them, and re-layouts  3.99 us (4%)
  other arithmetic  1.93 us (2%)
    pallas_call x9, Pallas kernels, call(): pl.pallas_call(kernel, out_shape=outs, in_specs=[spec(s) for s in spaces]...  26.6 us
    ppermute x6, starting transfers between devices, up(): return lax.ppermute(value, 'seq', pairs)  17.2 us
    ppermute x5, starting transfers between devices, along_x(): return lax.ppermute(value, 'seq', pairs)  13.2 us
    ppermute x6, waiting for transfers between devices, tp_shift(): return lax.ppermute(value, 'tp', [(i, (i + step) % 4) for i in range(4)])  9.82 us
    ppermute x6, starting transfers between devices, tp_shift(): return lax.ppermute(value, 'tp', [(i, (i + step) % 4) for i in range(4)])  8.98 us
    ppermute x4, starting transfers between devices, down(): return lax.ppermute(value, 'seq', pairs)  8.41 us
    unnamed x31, local copies, waits for them, and re-layouts  3.92 us
    ppermute x1, starting transfers between devices, local(): lax.ppermute(tail, 'seq', [(i, i + 2) for i in range(2 * NX * NZ - 2)])  3.4 us
  transfers between devices with their start and end apart: 26, of which 9 were waited for; matrix products, arithmetic and copies ran while one was open for 2% of the time, Pallas kernels for 18%

profile of v8, /device:TPU:192, one launch (start us, length us, event | category | flops | bytes accessed | tf_op | source)
XLA Modules:
  0.0 97.6 jit_solution(10174181096521490309)
XLA Ops:
  3.0 2.5 %pick.1 = (bf16[2,128,256]{2,1,0:T(8,128)(2,1)}, bf16[128,256]{1,0:T(8,128)(2,1)}) custom-call(s32[3]{0:T(128)} %pad_add_fusion.scal, s32[8,16]{1,0:T(8,128)} %blocks.1, bf16[256,256]{1,0:T(8,128)(2,1)} %k_ref.3, bf16[256,256]{1,0:T(8,128)(2,1)} %v_ref.3, bf16[256,256]{1,0:T(8,128)(2,1)} %copy-done.2, bf16[256,256]{1,0:T(8,128)(2,1)} %copy-done.4), custom_call_target="tpu_custom_call" | custom-call | bytes 1000000 | tf_op jit(solution)/shard_map/pick/pallas_call | solution.py:388
  5.5 3.4 %collective-permute-start.4 = (bf16[128,256]{1,0:T(8,128)(2,1)}, bf16[128,256]{1,0:T(8,128)(2,1)S(1)}, u32[]{:S(2)}, u32[]{:S(2)}) collective-permute-start(bf16[128,256]{1,0:T(8,128)(2,1)} %get-tuple-element.28), channel_id=1, source_target_pairs={{0,8},{4,12},{8,16},{12,20},{16,24},{20,28},{24,32},{28,36},{32,40... | collective-permute-start | bytes 196616 | tf_op jit(solution)/shard_map/ppermute | solution.py:428
  8.9 1.3 %collective-permute-start.3 = (bf16[2,128,256]{2,1,0:T(8,128)(2,1)}, bf16[2,128,256]{2,1,0:T(8,128)(2,1)S(1)}, u32[]{:S(2)}, u32[]{:S(2)}) collective-permute-start(bf16[2,128,256]{2,1,0:T(8,128)(2,1)} %get-tuple-element.27), channel_id=1, source_target_pairs={{0,64},{4,68},{8,72},{12,76},{16,80},{20,84},{24,88},{28,92},{32,9... | collective-permute-start | bytes 393224 | tf_op jit(solution)/shard_map/ppermute | solution.py:71
  10.2 2.8 %collective-permute-start.5 = (bf16[2,128,256]{2,1,0:T(8,128)(2,1)}, bf16[2,128,256]{2,1,0:T(8,128)(2,1)S(1)}, u32[]{:S(2)}, u32[]{:S(2)}) collective-permute-start(bf16[2,128,256]{2,1,0:T(8,128)(2,1)} %get-tuple-element.27), channel_id=1, source_target_pairs={{0,16},{4,20},{8,24},{12,28},{16,0},{20,4},{24,8},{28,12},{32,48},... | collective-permute-start | bytes 393224 | tf_op jit(solution)/shard_map/ppermute | solution.py:61
  14.0 3.4 %collective-permute-start.11 = (bf16[2,128,256]{2,1,0:T(8,128)(2,1)}, bf16[2,128,256]{2,1,0:T(8,128)(2,1)S(1)}, u32[]{:S(2)}, u32[]{:S(2)}) collective-permute-start(bf16[2,128,256]{2,1,0:T(8,128)(2,1)} %get-tuple-element.27), channel_id=1, source_target_pairs={{0,32},{4,36},{8,40},{12,44},{16,48},{20,52},{24,56},{28,60},{32,6... | collective-permute-start | bytes 393224 | tf_op jit(solution)/shard_map/ppermute | solution.py:71
  18.3 1.8 %collective-permute-done.3 = bf16[2,128,256]{2,1,0:T(8,128)(2,1)S(1)} collective-permute-done((bf16[2,128,256]{2,1,0:T(8,128)(2,1)}, bf16[2,128,256]{2,1,0:T(8,128)(2,1)S(1)}, u32[]{:S(2)}, u32[]{:S(2)}) %collective-permute-start.3) | collective-permute-done | bytes 131104 | tf_op jit(solution)/shard_map/ppermute | solution.py:71
  20.1 1.3 %collective-permute-start.9 = (bf16[4,128,256]{2,1,0:T(8,128)(2,1)S(1)}, bf16[4,128,256]{2,1,0:T(8,128)(2,1)S(1)}, u32[]{:S(2)}, u32[]{:S(2)}) collective-permute-start(bf16[4,128,256]{2,1,0:T(8,128)(2,1)S(1)} %get-tuple-element.54), channel_id=1, source_target_pairs={{0,224},{4,228},{8,232},{12,236},{16,240},{20,244},{24,248},{28,25... | collective-permute-start | bytes 786440 | tf_op jit(solution)/shard_map/ppermute | solution.py:77
  21.4 4.8 %collective-permute-start.6 = (bf16[4,128,256]{2,1,0:T(8,128)(2,1)S(1)}, bf16[4,128,256]{2,1,0:T(8,128)(2,1)S(1)}, u32[]{:S(2)}, u32[]{:S(2)}) collective-permute-start(bf16[4,128,256]{2,1,0:T(8,128)(2,1)S(1)} %get-tuple-element.53), channel_id=1, source_target_pairs={{0,32},{4,36},{8,40},{12,44},{16,48},{20,52},{24,56},{28,60},{32,6... | collective-permute-start | bytes 786440 | tf_op jit(solution)/shard_map/ppermute | solution.py:71
  26.3 1.4 %collective-permute-start.12 = (bf16[8,128,256]{2,1,0:T(8,128)(2,1)S(1)}, bf16[8,128,256]{2,1,0:T(8,128)(2,1)S(1)}, u32[]{:S(2)}, u32[]{:S(2)}) collective-permute-start(bf16[8,128,256]{2,1,0:T(8,128)(2,1)S(1)} %constant_dynamic-update-slice_fusion.rest_0_), channel_id=1, source_target_pairs={{0,8},{4,12},{8,16},{12,20},{16,24},{20,28},{24,0},{28,4},{32,40},... | collective-permute-start | bytes 1572872 | tf_op jit(solution)/shard_map/ppermute | solution.py:61
  27.8 1.9 %collective-permute-start.13 = (bf16[8,128,256]{2,1,0:T(8,128)(2,1)S(1)}, bf16[8,128,256]{2,1,0:T(8,128)(2,1)S(1)}, u32[]{:S(2)}, u32[]{:S(2)}) collective-permute-start(bf16[8,128,256]{2,1,0:T(8,128)(2,1)S(1)} %constant_dynamic-update-slice_fusion.rest_0_), channel_id=1, source_target_pairs={{0,24},{4,28},{8,0},{12,4},{16,8},{20,12},{24,16},{28,20},{32,56},... | collective-permute-start | bytes 1572872 | tf_op jit(solution)/shard_map/ppermute | solution.py:61
  29.6 1.9 %collective-permute-start.10 = (bf16[4,128,256]{2,1,0:T(8,128)(2,1)S(1)}, bf16[4,128,256]{2,1,0:T(8,128)(2,1)S(1)}, u32[]{:S(2)}, u32[]{:S(2)}) collective-permute-start(bf16[4,128,256]{2,1,0:T(8,128)(2,1)S(1)} %collective-permute-done.9.rest_6_), channel_id=1, source_target_pairs={{0,224},{4,228},{8,232},{12,236},{16,240},{20,244},{24,248},{28,25... | collective-permute-start | bytes 786440 | tf_op jit(solution)/shard_map/ppermute | solution.py:77
  31.6 4.5 %collective-permute-start.7 = (bf16[4,128,256]{2,1,0:T(8,128)(2,1)S(1)}, bf16[4,128,256]{2,1,0:T(8,128)(2,1)S(1)}, u32[]{:S(2)}, u32[]{:S(2)}) collective-permute-start(bf16[4,128,256]{2,1,0:T(8,128)(2,1)S(1)} %collective-permute-done.6.rest_4_), channel_id=1, source_target_pairs={{32,64},{36,68},{40,72},{44,76},{48,80},{52,84},{56,88},{60,92},{6... | collective-permute-start | bytes 786440 | tf_op jit(solution)/shard_map/ppermute | solution.py:71
  38.0 5.5 %near_part.1 = (bf16[4,512,256]{2,1,0:T(8,128)(2,1)S(1)}, f32[4,512,256]{2,1,0:T(8,128)S(1)}, s32[256]{0:T(256)S(1)}, s32[16]{0:T(128)S(1)}) custom-call(s32[3]{0:T(128)S(1)} %copy-done.6, s32[8,16]{1,0:T(8,128)S(1)} %copy-done.7, s32[8]{0:T(128)S(1)} %copy-done.10, s32[8,8]{1,0:T(8,128)S(1)} %copy-done.9, s32[32]{0:T(128)S(1)} %copy-done.11, ...), custom_call_target="tpu_custom_call" | custom-call | flops 5000000000 | bytes 100000 | tf_op jit(solution)/shard_map/near_part/pallas_call | solution.py:388
  43.7 2.9 %collective-permute-start.14 = (bf16[8,128,256]{2,1,0:T(8,128)(2,1)S(1)}, bf16[8,128,256]{2,1,0:T(8,128)(2,1)S(1)}, u32[]{:S(2)}, u32[]{:S(2)}) collective-permute-start(bf16[8,128,256]{2,1,0:T(8,128)(2,1)S(1)} %pad_maximum_fusion), channel_id=1, source_target_pairs={{96,104},{100,108},{104,112},{108,116},{112,120},{116,124},{120,96... | collective-permute-start | bytes 1572872 | tf_op jit(solution)/shard_map/ppermute | solution.py:61
  46.6 4.1 %collective-permute-start.15 = (bf16[8,128,256]{2,1,0:T(8,128)(2,1)S(1)}, bf16[8,128,256]{2,1,0:T(8,128)(2,1)S(1)}, u32[]{:S(2)}, u32[]{:S(2)}) collective-permute-start(bf16[8,128,256]{2,1,0:T(8,128)(2,1)S(1)} %pad_maximum_fusion), channel_id=1, source_target_pairs={{96,120},{100,124},{104,96},{108,100},{112,104},{116,108},{120,112... | collective-permute-start | bytes 1572872 | tf_op jit(solution)/shard_map/ppermute | solution.py:61
  50.7 1.9 %collective-permute-start.16 = (bf16[2,128,256]{2,1,0:T(8,128)(2,1)S(1)}, bf16[2,128,256]{2,1,0:T(8,128)(2,1)S(1)}, u32[]{:S(2)}, u32[]{:S(2)}) collective-permute-start(bf16[2,128,256]{2,1,0:T(8,128)(2,1)S(1)} %get-tuple-element.51), channel_id=1, source_target_pairs={{64,96},{68,100},{72,104},{76,108},{80,112},{84,116},{88,120},{92,... | collective-permute-start | bytes 393224 | tf_op jit(solution)/shard_map/ppermute | solution.py:71
  52.7 1.3 %collective-permute-start.17 = (bf16[2,128,256]{2,1,0:T(8,128)(2,1)S(1)}, bf16[2,128,256]{2,1,0:T(8,128)(2,1)S(1)}, u32[]{:S(2)}, u32[]{:S(2)}) collective-permute-start(bf16[2,128,256]{2,1,0:T(8,128)(2,1)S(1)} %get-tuple-element.51), channel_id=1, source_target_pairs={{64,128},{68,132},{72,136},{76,140},{80,144},{84,148},{88,152},{92... | collective-permute-start | bytes 393224 | tf_op jit(solution)/shard_map/ppermute | solution.py:71
  54.0 4.6 %collective-permute-start.18 = (bf16[2,128,256]{2,1,0:T(8,128)(2,1)S(1)}, bf16[2,128,256]{2,1,0:T(8,128)(2,1)S(1)}, u32[]{:S(2)}, u32[]{:S(2)}) collective-permute-start(bf16[2,128,256]{2,1,0:T(8,128)(2,1)S(1)} %get-tuple-element.49), channel_id=1, source_target_pairs={{0,224},{4,228},{8,232},{12,236},{16,240},{20,244},{24,248},{28,25... | collective-permute-start | bytes 393224 | tf_op jit(solution)/shard_map/ppermute | solution.py:77
  58.5 5.6 %far_part.2 = (bf16[4,512,256]{2,1,0:T(8,128)(2,1)S(1)}, f32[4,512,256]{2,1,0:T(8,128)S(1)}) custom-call(s32[3]{0:T(128)S(1)} %copy-done.6, s32[256]{0:T(256)S(1)} %get-tuple-element.30.lists, s32[16]{0:T(128)S(1)} %get-tuple-element.31.counts, bf16[4,512,256]{2,1,0:T(8,128)(2,1)S(1)} %get-tuple-element.32.qa_in, ...), custom_call_target="tpu_custom_call" | custom-call | flops 6000000000 | bytes 100000 | tf_op jit(solution)/shard_map/far_part/pallas_call | solution.py:388
  64.3 4.8 %far_part.3 = (bf16[256,512]{1,0:T(8,128)(2,1)S(1)}, bf16[256,512]{1,0:T(8,128)(2,1)S(1)}) custom-call(s32[3]{0:T(128)S(1)} %copy-done.6, s32[256]{0:T(256)S(1)} %get-tuple-element.30.lists, s32[16]{0:T(128)S(1)} %get-tuple-element.31.counts, bf16[4,512,256]{2,1,0:T(8,128)(2,1)S(1)} %get-tuple-element.36.qa_in, f32[4,512,256]{2,1,0:T(8,128)S(1)} %get-tuple-element.37.acc_in, ...), custom_call_target="tpu_custom_call" | custom-call | flops 6000000000 | bytes 100000 | tf_op jit(solution)/shard_map/far_part/pallas_call | solution.py:388
  69.2 1.3 %own_part.1.part = f32[2,256,512]{2,1,0:T(8,128)S(1)} custom-call(s32[3]{0:T(128)S(1)} %copy-done.6, bf16[256,512]{1,0:T(8,128)(2,1)S(1)} %get-tuple-element.39.ctx, bf16[1024,4096]{1,0:T(8,128)(2,1)S(1)} %bitcast.4), custom_call_target="tpu_custom_call" | custom-call | flops 1000000 | bytes 1000 | tf_op jit(solution)/shard_map/own_part/pallas_call | solution.py:388
  70.7 1.3 %sib_part.1 = (bf16[256,512]{1,0:T(8,128)(2,1)S(1)}, bf16[256,512]{1,0:T(8,128)(2,1)S(1)}) custom-call(s32[3]{0:T(128)S(1)} %copy-done.6, bf16[256,512]{1,0:T(8,128)(2,1)S(1)} %collective-permute-done.19.ctx_sib.ctx, f32[2,256,512]{2,1,0:T(8,128)S(1)} %own_part.1.part, bf16[1024,4096]{1,0:T(8,128)(2,1)S(1)} %bitcast.4), custom_call_target="tpu_custom_call" | custom-call | flops 1000000 | bytes 1000 | tf_op jit(solution)/shard_map/sib_part/pallas_call | solution.py:388
  72.0 1.7 %collective-permute-start.21 = (bf16[256,512]{1,0:T(8,128)(2,1)S(1)}, bf16[256,512]{1,0:T(8,128)(2,1)S(1)}, u32[]{:S(2)}, u32[]{:S(2)}) collective-permute-start(bf16[256,512]{1,0:T(8,128)(2,1)S(1)} %get-tuple-element.44), channel_id=1, source_target_pairs={{0,1},{1,2},{2,3},{3,0},{4,5},{5,6},{6,7},{7,4},{8,9},{9,10},{10,1... | collective-permute-start | bytes 786440 | tf_op jit(solution)/shard_map/ppermute | solution.py:85
  73.7 1.7 %collective-permute-start.24 = (bf16[256,512]{1,0:T(8,128)(2,1)S(1)}, bf16[256,512]{1,0:T(8,128)(2,1)S(1)}, u32[]{:S(2)}, u32[]{:S(2)}) collective-permute-start(bf16[256,512]{1,0:T(8,128)(2,1)S(1)} %get-tuple-element.48), channel_id=1, source_target_pairs={{0,3},{1,0},{2,1},{3,2},{4,7},{5,4},{6,5},{7,6},{8,11},{9,8},{10,9... | collective-permute-start | bytes 786440 | tf_op jit(solution)/shard_map/ppermute | solution.py:85
  75.3 1.9 %both_parts.4 = (bf16[256,512]{1,0:T(8,128)(2,1)S(1)}, bf16[256,512]{1,0:T(8,128)(2,1)S(1)}) custom-call(s32[3]{0:T(128)S(1)} %copy-done.6, bf16[256,512]{1,0:T(8,128)(2,1)S(1)} %get-tuple-element.39.ctx, bf16[256,512]{1,0:T(8,128)(2,1)S(1)} %collective-permute-done.19.ctx_sib.ctx, bf16[1024,4096]{1,0:T(8,128)(2,1)S(1)} %bitcast.4), custom_call_target="tpu_custom_call" | custom-call | flops 1000000 | bytes 1000 | tf_op jit(solution)/shard_map/both_parts/pallas_call | solution.py:388
  77.2 1.9 %collective-permute-start.20 = (bf16[256,512]{1,0:T(8,128)(2,1)S(1)}, bf16[256,512]{1,0:T(8,128)(2,1)S(1)}, u32[]{:S(2)}, u32[]{:S(2)}) collective-permute-start(bf16[256,512]{1,0:T(8,128)(2,1)S(1)} %get-tuple-element.42), channel_id=1, source_target_pairs={{0,3},{1,0},{2,1},{3,2},{4,7},{5,4},{6,5},{7,6},{8,11},{9,8},{10,9... | collective-permute-start | bytes 786440 | tf_op jit(solution)/shard_map/ppermute | solution.py:85
  79.0 1.9 %both_parts.5 = (f32[256,512]{1,0:T(8,128)S(1)}, f32[256,512]{1,0:T(8,128)S(1)}) custom-call(s32[3]{0:T(128)S(1)} %copy-done.6, bf16[256,512]{1,0:T(8,128)(2,1)S(1)} %get-tuple-element.39.ctx, bf16[256,512]{1,0:T(8,128)(2,1)S(1)} %collective-permute-done.19.ctx_sib.ctx, bf16[1024,4096]{1,0:T(8,128)(2,1)S(1)} %bitcast.4), custom_call_target="tpu_custom_call" | custom-call | flops 1000000 | bytes 1000 | tf_op jit(solution)/shard_map/both_parts/pallas_call | solution.py:388
  82.4 2.5 %collective-permute-start.23 = (bf16[256,512]{1,0:T(8,128)(2,1)S(1)}, bf16[256,512]{1,0:T(8,128)(2,1)S(1)}, u32[]{:S(2)}, u32[]{:S(2)}) collective-permute-start(bf16[256,512]{1,0:T(8,128)(2,1)S(1)} %get-tuple-element.46), channel_id=1, source_target_pairs={{0,1},{1,2},{2,3},{3,0},{4,5},{5,6},{6,7},{7,4},{8,9},{9,10},{10,1... | collective-permute-start | bytes 786440 | tf_op jit(solution)/shard_map/ppermute | solution.py:85
  85.8 1.9 %both_parts.3 = (f32[256,512]{1,0:T(8,128)S(1)}, f32[256,512]{1,0:T(8,128)S(1)}) custom-call(s32[3]{0:T(128)S(1)} %copy-done.6, bf16[256,512]{1,0:T(8,128)(2,1)S(1)} %get-tuple-element.39.ctx, bf16[256,512]{1,0:T(8,128)(2,1)S(1)} %collective-permute-done.19.ctx_sib.ctx, bf16[1024,4096]{1,0:T(8,128)(2,1)S(1)} %bitcast.4), custom_call_target="tpu_custom_call" | custom-call | flops 1000000 | bytes 1000 | tf_op jit(solution)/shard_map/both_parts/pallas_call | solution.py:388
  87.7 1.3 %collective-permute-done.20 = bf16[256,512]{1,0:T(8,128)(2,1)S(1)} collective-permute-done((bf16[256,512]{1,0:T(8,128)(2,1)S(1)}, bf16[256,512]{1,0:T(8,128)(2,1)S(1)}, u32[]{:S(2)}, u32[]{:S(2)}) %collective-permute-start.20) | collective-permute-done | bytes 262176 | tf_op jit(solution)/shard_map/ppermute | solution.py:85
  88.9 3.5 %collective-permute-done.22 = bf16[256,512]{1,0:T(8,128)(2,1)S(1)} collective-permute-done((bf16[256,512]{1,0:T(8,128)(2,1)S(1)}, bf16[256,512]{1,0:T(8,128)(2,1)S(1)}, u32[]{:S(2)}, u32[]{:S(2)}) %collective-permute-start.22) | collective-permute-done | bytes 262176 | tf_op jit(solution)/shard_map/ppermute | solution.py:85
  92.6 4.1 %collective-permute-done.23 = bf16[256,512]{1,0:T(8,128)(2,1)S(1)} collective-permute-done((bf16[256,512]{1,0:T(8,128)(2,1)S(1)}, bf16[256,512]{1,0:T(8,128)(2,1)S(1)}, u32[]{:S(2)}, u32[]{:S(2)}) %collective-permute-start.23) | collective-permute-done | bytes 262176 | tf_op jit(solution)/shard_map/ppermute | solution.py:85
  (74 shorter events, 10.7 us)
Async XLA Ops:
  0.0 36.1 %copy-start = (bf16[256,256]{1,0:T(8,128)(2,1)S(1)}, bf16[256,256]{1,0:T(8,128)(2,1)}, u32[]{:S(2)}) copy-start(bf16[256,256]{1,0:T(8,128)(2,1)} %k_ref.3) | copy-start | bytes 393220
  0.0 36.1 %copy-start.1 = (bf16[256,256]{1,0:T(8,128)(2,1)S(1)}, bf16[256,256]{1,0:T(8,128)(2,1)}, u32[]{:S(2)}) copy-start(bf16[256,256]{1,0:T(8,128)(2,1)} %v_ref.3) | copy-start | bytes 393220
  0.0 36.2 %copy-start.7 = (s32[8,16]{1,0:T(8,128)S(1)}, s32[8,16]{1,0:T(8,128)}, u32[]{:S(2)}) copy-start(s32[8,16]{1,0:T(8,128)} %blocks.1) | copy-start | bytes 1540
  0.0 36.2 %copy-start.8 = (bf16[256,1024]{1,0:T(8,128)(2,1)S(1)}, bf16[256,1024]{1,0:T(8,128)(2,1)}, u32[]{:S(2)}) copy-start(bf16[256,1024]{1,0:T(8,128)(2,1)} %q_ref.1) | copy-start | bytes 1572868
  0.0 36.1 %copy-start.10 = (s32[8]{0:T(128)S(1)}, s32[8]{0:T(128)}, u32[]{:S(2)}) copy-start(s32[8]{0:T(128)} %window.1) | copy-start | bytes 100
  0.0 36.1 %copy-start.9 = (s32[8,8]{1,0:T(8,128)S(1)}, s32[8,8]{1,0:T(8,128)}, u32[]{:S(2)}) copy-start(s32[8,8]{1,0:T(8,128)} %slash.1) | copy-start | bytes 772
  0.1 1.6 %collective-permute-start.1 = (bf16[256,256]{1,0:T(8,128)(2,1)}, bf16[256,256]{1,0:T(8,128)(2,1)S(1)}, u32[]{:S(2)}, u32[]{:S(2)}) collective-permute-start(bf16[256,256]{1,0:T(8,128)(2,1)} %k_ref.3), channel_id=1, source_target_pairs={{0,4},{4,0},{8,12},{12,8},{16,20},{20,16},{24,28},{28,24},{32,36},... | collective-permute-start | bytes 393224 | tf_op jit(solution)/shard_map/ppermute | solution.py:81
  0.2 1.7 %collective-permute-start.2 = (bf16[256,256]{1,0:T(8,128)(2,1)}, bf16[256,256]{1,0:T(8,128)(2,1)S(1)}, u32[]{:S(2)}, u32[]{:S(2)}) collective-permute-start(bf16[256,256]{1,0:T(8,128)(2,1)} %v_ref.3), channel_id=1, source_target_pairs={{0,4},{4,0},{8,12},{12,8},{16,20},{20,16},{24,28},{28,24},{32,36},... | collective-permute-start | bytes 393224 | tf_op jit(solution)/shard_map/ppermute | solution.py:81
  5.5 8.5 %collective-permute-start.4 = (bf16[128,256]{1,0:T(8,128)(2,1)}, bf16[128,256]{1,0:T(8,128)(2,1)S(1)}, u32[]{:S(2)}, u32[]{:S(2)}) collective-permute-start(bf16[128,256]{1,0:T(8,128)(2,1)} %get-tuple-element.28), channel_id=1, source_target_pairs={{0,8},{4,12},{8,16},{12,20},{16,24},{20,28},{24,32},{28,36},{32,40... | collective-permute-start | bytes 196616 | tf_op jit(solution)/shard_map/ppermute | solution.py:428
  8.9 11.1 %collective-permute-start.3 = (bf16[2,128,256]{2,1,0:T(8,128)(2,1)}, bf16[2,128,256]{2,1,0:T(8,128)(2,1)S(1)}, u32[]{:S(2)}, u32[]{:S(2)}) collective-permute-start(bf16[2,128,256]{2,1,0:T(8,128)(2,1)} %get-tuple-element.27), channel_id=1, source_target_pairs={{0,64},{4,68},{8,72},{12,76},{16,80},{20,84},{24,88},{28,92},{32,9... | collective-permute-start | bytes 393224 | tf_op jit(solution)/shard_map/ppermute | solution.py:71
  10.2 9.8 %collective-permute-start.5 = (bf16[2,128,256]{2,1,0:T(8,128)(2,1)}, bf16[2,128,256]{2,1,0:T(8,128)(2,1)S(1)}, u32[]{:S(2)}, u32[]{:S(2)}) collective-permute-start(bf16[2,128,256]{2,1,0:T(8,128)(2,1)} %get-tuple-element.27), channel_id=1, source_target_pairs={{0,16},{4,20},{8,24},{12,28},{16,0},{20,4},{24,8},{28,12},{32,48},... | collective-permute-start | bytes 393224 | tf_op jit(solution)/shard_map/ppermute | solution.py:61
  13.1 7.0 %collective-permute-start.8 = (bf16[2,128,256]{2,1,0:T(8,128)(2,1)}, bf16[2,128,256]{2,1,0:T(8,128)(2,1)S(1)}, u32[]{:S(2)}, u32[]{:S(2)}) collective-permute-start(bf16[2,128,256]{2,1,0:T(8,128)(2,1)} %get-tuple-element.27), channel_id=1, source_target_pairs={{0,224},{4,228},{8,232},{12,236},{16,240},{20,244},{24,248},{28,25... | collective-permute-start | bytes 393224 | tf_op jit(solution)/shard_map/ppermute | solution.py:77
  13.7 22.4 %collective-permute-start = (bf16[256,1024]{1,0:T(8,128)(2,1)}, bf16[256,1024]{1,0:T(8,128)(2,1)S(1)}, u32[]{:S(2)}, u32[]{:S(2)}) collective-permute-start(bf16[256,1024]{1,0:T(8,128)(2,1)} %q_ref.1), channel_id=1, source_target_pairs={{0,4},{4,0},{8,12},{12,8},{16,20},{20,16},{24,28},{28,24},{32,36},... | collective-permute-start | bytes 1572872 | tf_op jit(solution)/shard_map/ppermute | solution.py:81
  14.0 12.2 %collective-permute-start.11 = (bf16[2,128,256]{2,1,0:T(8,128)(2,1)}, bf16[2,128,256]{2,1,0:T(8,128)(2,1)S(1)}, u32[]{:S(2)}, u32[]{:S(2)}) collective-permute-start(bf16[2,128,256]{2,1,0:T(8,128)(2,1)} %get-tuple-element.27), channel_id=1, source_target_pairs={{0,32},{4,36},{8,40},{12,44},{16,48},{20,52},{24,56},{28,60},{32,6... | collective-permute-start | bytes 393224 | tf_op jit(solution)/shard_map/ppermute | solution.py:71
  20.1 9.5 %collective-permute-start.9 = (bf16[4,128,256]{2,1,0:T(8,128)(2,1)S(1)}, bf16[4,128,256]{2,1,0:T(8,128)(2,1)S(1)}, u32[]{:S(2)}, u32[]{:S(2)}) collective-permute-start(bf16[4,128,256]{2,1,0:T(8,128)(2,1)S(1)} %get-tuple-element.54), channel_id=1, source_target_pairs={{0,224},{4,228},{8,232},{12,236},{16,240},{20,244},{24,248},{28,25... | collective-permute-start | bytes 786440 | tf_op jit(solution)/shard_map/ppermute | solution.py:77
  21.4 10.1 %collective-permute-start.6 = (bf16[4,128,256]{2,1,0:T(8,128)(2,1)S(1)}, bf16[4,128,256]{2,1,0:T(8,128)(2,1)S(1)}, u32[]{:S(2)}, u32[]{:S(2)}) collective-permute-start(bf16[4,128,256]{2,1,0:T(8,128)(2,1)S(1)} %get-tuple-element.53), channel_id=1, source_target_pairs={{0,32},{4,36},{8,40},{12,44},{16,48},{20,52},{24,56},{28,60},{32,6... | collective-permute-start | bytes 786440 | tf_op jit(solution)/shard_map/ppermute | solution.py:71
  26.3 26.4 %collective-permute-start.12 = (bf16[8,128,256]{2,1,0:T(8,128)(2,1)S(1)}, bf16[8,128,256]{2,1,0:T(8,128)(2,1)S(1)}, u32[]{:S(2)}, u32[]{:S(2)}) collective-permute-start(bf16[8,128,256]{2,1,0:T(8,128)(2,1)S(1)} %constant_dynamic-update-slice_fusion.rest_0_), channel_id=1, source_target_pairs={{0,8},{4,12},{8,16},{12,20},{16,24},{20,28},{24,0},{28,4},{32,40},... | collective-permute-start | bytes 1572872 | tf_op jit(solution)/shard_map/ppermute | solution.py:61
  27.8 26.2 %collective-permute-start.13 = (bf16[8,128,256]{2,1,0:T(8,128)(2,1)S(1)}, bf16[8,128,256]{2,1,0:T(8,128)(2,1)S(1)}, u32[]{:S(2)}, u32[]{:S(2)}) collective-permute-start(bf16[8,128,256]{2,1,0:T(8,128)(2,1)S(1)} %constant_dynamic-update-slice_fusion.rest_0_), channel_id=1, source_target_pairs={{0,24},{4,28},{8,0},{12,4},{16,8},{20,12},{24,16},{28,20},{32,56},... | collective-permute-start | bytes 1572872 | tf_op jit(solution)/shard_map/ppermute | solution.py:61
  29.6 13.9 %collective-permute-start.10 = (bf16[4,128,256]{2,1,0:T(8,128)(2,1)S(1)}, bf16[4,128,256]{2,1,0:T(8,128)(2,1)S(1)}, u32[]{:S(2)}, u32[]{:S(2)}) collective-permute-start(bf16[4,128,256]{2,1,0:T(8,128)(2,1)S(1)} %collective-permute-done.9.rest_6_), channel_id=1, source_target_pairs={{0,224},{4,228},{8,232},{12,236},{16,240},{20,244},{24,248},{28,25... | collective-permute-start | bytes 786440 | tf_op jit(solution)/shard_map/ppermute | solution.py:77
  31.6 12.0 %collective-permute-start.7 = (bf16[4,128,256]{2,1,0:T(8,128)(2,1)S(1)}, bf16[4,128,256]{2,1,0:T(8,128)(2,1)S(1)}, u32[]{:S(2)}, u32[]{:S(2)}) collective-permute-start(bf16[4,128,256]{2,1,0:T(8,128)(2,1)S(1)} %collective-permute-done.6.rest_4_), channel_id=1, source_target_pairs={{32,64},{36,68},{40,72},{44,76},{48,80},{52,84},{56,88},{60,92},{6... | collective-permute-start | bytes 786440 | tf_op jit(solution)/shard_map/ppermute | solution.py:71
  43.7 20.5 %collective-permute-start.14 = (bf16[8,128,256]{2,1,0:T(8,128)(2,1)S(1)}, bf16[8,128,256]{2,1,0:T(8,128)(2,1)S(1)}, u32[]{:S(2)}, u32[]{:S(2)}) collective-permute-start(bf16[8,128,256]{2,1,0:T(8,128)(2,1)S(1)} %pad_maximum_fusion), channel_id=1, source_target_pairs={{96,104},{100,108},{104,112},{108,116},{112,120},{116,124},{120,96... | collective-permute-start | bytes 1572872 | tf_op jit(solution)/shard_map/ppermute | solution.py:61
  46.6 17.6 %collective-permute-start.15 = (bf16[8,128,256]{2,1,0:T(8,128)(2,1)S(1)}, bf16[8,128,256]{2,1,0:T(8,128)(2,1)S(1)}, u32[]{:S(2)}, u32[]{:S(2)}) collective-permute-start(bf16[8,128,256]{2,1,0:T(8,128)(2,1)S(1)} %pad_maximum_fusion), channel_id=1, source_target_pairs={{96,120},{100,124},{104,96},{108,100},{112,104},{116,108},{120,112... | collective-permute-start | bytes 1572872 | tf_op jit(solution)/shard_map/ppermute | solution.py:61
  50.7 13.4 %collective-permute-start.16 = (bf16[2,128,256]{2,1,0:T(8,128)(2,1)S(1)}, bf16[2,128,256]{2,1,0:T(8,128)(2,1)S(1)}, u32[]{:S(2)}, u32[]{:S(2)}) collective-permute-start(bf16[2,128,256]{2,1,0:T(8,128)(2,1)S(1)} %get-tuple-element.51), channel_id=1, source_target_pairs={{64,96},{68,100},{72,104},{76,108},{80,112},{84,116},{88,120},{92,... | collective-permute-start | bytes 393224 | tf_op jit(solution)/shard_map/ppermute | solution.py:71
  52.7 11.5 %collective-permute-start.17 = (bf16[2,128,256]{2,1,0:T(8,128)(2,1)S(1)}, bf16[2,128,256]{2,1,0:T(8,128)(2,1)S(1)}, u32[]{:S(2)}, u32[]{:S(2)}) collective-permute-start(bf16[2,128,256]{2,1,0:T(8,128)(2,1)S(1)} %get-tuple-element.51), channel_id=1, source_target_pairs={{64,128},{68,132},{72,136},{76,140},{80,144},{84,148},{88,152},{92... | collective-permute-start | bytes 393224 | tf_op jit(solution)/shard_map/ppermute | solution.py:71
  54.0 10.2 %collective-permute-start.18 = (bf16[2,128,256]{2,1,0:T(8,128)(2,1)S(1)}, bf16[2,128,256]{2,1,0:T(8,128)(2,1)S(1)}, u32[]{:S(2)}, u32[]{:S(2)}) collective-permute-start(bf16[2,128,256]{2,1,0:T(8,128)(2,1)S(1)} %get-tuple-element.49), channel_id=1, source_target_pairs={{0,224},{4,228},{8,232},{12,236},{16,240},{20,244},{24,248},{28,25... | collective-permute-start | bytes 393224 | tf_op jit(solution)/shard_map/ppermute | solution.py:77
  69.0 1.6 %collective-permute-start.19 = (bf16[256,512]{1,0:T(8,128)(2,1)S(1)}, bf16[256,512]{1,0:T(8,128)(2,1)S(1)}, u32[]{:S(2)}, u32[]{:S(2)}) collective-permute-start(bf16[256,512]{1,0:T(8,128)(2,1)S(1)} %get-tuple-element.40), channel_id=1, source_target_pairs={{0,4},{4,0},{8,12},{12,8},{16,20},{20,16},{24,28},{28,24},{32,36},... | collective-permute-start | bytes 786440 | tf_op jit(solution)/shard_map/ppermute | solution.py:81
  72.0 9.9 %collective-permute-start.21 = (bf16[256,512]{1,0:T(8,128)(2,1)S(1)}, bf16[256,512]{1,0:T(8,128)(2,1)S(1)}, u32[]{:S(2)}, u32[]{:S(2)}) collective-permute-start(bf16[256,512]{1,0:T(8,128)(2,1)S(1)} %get-tuple-element.44), channel_id=1, source_target_pairs={{0,1},{1,2},{2,3},{3,0},{4,5},{5,6},{6,7},{7,4},{8,9},{9,10},{10,1... | collective-permute-start | bytes 786440 | tf_op jit(solution)/shard_map/ppermute | solution.py:85
  73.7 11.3 %collective-permute-start.24 = (bf16[256,512]{1,0:T(8,128)(2,1)S(1)}, bf16[256,512]{1,0:T(8,128)(2,1)S(1)}, u32[]{:S(2)}, u32[]{:S(2)}) collective-permute-start(bf16[256,512]{1,0:T(8,128)(2,1)S(1)} %get-tuple-element.48), channel_id=1, source_target_pairs={{0,3},{1,0},{2,1},{3,2},{4,7},{5,4},{6,5},{7,6},{8,11},{9,8},{10,9... | collective-permute-start | bytes 786440 | tf_op jit(solution)/shard_map/ppermute | solution.py:85
  77.2 11.8 %collective-permute-start.20 = (bf16[256,512]{1,0:T(8,128)(2,1)S(1)}, bf16[256,512]{1,0:T(8,128)(2,1)S(1)}, u32[]{:S(2)}, u32[]{:S(2)}) collective-permute-start(bf16[256,512]{1,0:T(8,128)(2,1)S(1)} %get-tuple-element.42), channel_id=1, source_target_pairs={{0,3},{1,0},{2,1},{3,2},{4,7},{5,4},{6,5},{7,6},{8,11},{9,8},{10,9... | collective-permute-start | bytes 786440 | tf_op jit(solution)/shard_map/ppermute | solution.py:85
  81.9 10.5 %collective-permute-start.22 = (bf16[256,512]{1,0:T(8,128)(2,1)S(1)}, bf16[256,512]{1,0:T(8,128)(2,1)S(1)}, u32[]{:S(2)}, u32[]{:S(2)}) collective-permute-start(bf16[256,512]{1,0:T(8,128)(2,1)S(1)} %add_convert_fusion.3), channel_id=1, source_target_pairs={{0,1},{1,2},{2,3},{3,0},{4,5},{5,6},{6,7},{7,4},{8,9},{9,10},{10,1... | collective-permute-start | bytes 786440 | tf_op jit(solution)/shard_map/ppermute | solution.py:85
  82.4 14.2 %collective-permute-start.23 = (bf16[256,512]{1,0:T(8,128)(2,1)S(1)}, bf16[256,512]{1,0:T(8,128)(2,1)S(1)}, u32[]{:S(2)}, u32[]{:S(2)}) collective-permute-start(bf16[256,512]{1,0:T(8,128)(2,1)S(1)} %get-tuple-element.46), channel_id=1, source_target_pairs={{0,1},{1,2},{2,3},{3,0},{4,5},{5,6},{6,7},{7,4},{8,9},{9,10},{10,1... | collective-permute-start | bytes 786440 | tf_op jit(solution)/shard_map/ppermute | solution.py:85
  85.0 11.7 %collective-permute-start.25 = (bf16[256,512]{1,0:T(8,128)(2,1)S(1)}, bf16[256,512]{1,0:T(8,128)(2,1)S(1)}, u32[]{:S(2)}, u32[]{:S(2)}) collective-permute-start(bf16[256,512]{1,0:T(8,128)(2,1)S(1)} %add_convert_fusion.1), channel_id=1, source_target_pairs={{0,3},{1,0},{2,1},{3,2},{4,7},{5,4},{6,5},{7,6},{8,11},{9,8},{10,9... | collective-permute-start | bytes 786440 | tf_op jit(solution)/shard_map/ppermute | solution.py:85
  (8 other events, 84.0 us)
